TPU v7x, 32 devices: a whole 2x2x4 slice. The times are simulated.
32 devices in a mesh: dp: 8 (over z, core), tensor: 4 (over y, x).
Axes of the slice: x: 2, y: 2, z: 4, core: 2. Of those that a mesh axis runs over, the one named last changes fastest.
Arguments:
- tokens: bfloat16 [4096, 2048], P('dp'), may hold values from -6 to 6
- cotangent: bfloat16 [4096, 2048], P('dp'), may hold values from -6 to 6
- routes: int32 [4096, 8], P('dp'), may hold values from 0 to 15, all different within a row; in each aligned block of 256 rows (0 to 255, 256 to 511, ...) at most 176 rows name the same one
- wq: bfloat16 [2048, 2048], P('dp', 'tensor'), may hold values from -0.125 to 0.125
- wk: bfloat16 [2048, 2048], P('dp', 'tensor'), may hold values from -0.125 to 0.125
- wv: bfloat16 [2048, 2048], P('dp', 'tensor'), may hold values from -0.125 to 0.125
- wo: bfloat16 [2048, 2048], P('tensor', 'dp'), may hold values from -0.5 to 0.5
- attn_gain: bfloat16 [2048], P('dp'), may hold values from 0.5 to 1.5
- q_gain: bfloat16 [2048], P('tensor'), may hold values from 0.5 to 1.5
- k_gain: bfloat16 [2048], P('tensor'), may hold values from 0.5 to 1.5
- moe_gain: bfloat16 [2048], P('dp'), may hold values from 0.5 to 1.5
- router: bfloat16 [2048, 16], P('dp'), may hold values from -0.0625 to 0.0625
- w_gate: bfloat16 [16, 2048, 1024], P(None, 'dp', 'tensor'), may hold values from -0.125 to 0.125
- w_up: bfloat16 [16, 2048, 1024], P(None, 'dp', 'tensor'), may hold values from -0.125 to 0.125
- w_down: bfloat16 [16, 1024, 2048], P(None, 'tensor', 'dp'), may hold values from -1.5 to 1.5
Outputs:
- mixed: bfloat16 [4096, 2048], P('dp')
- tokens_grad: bfloat16 [4096, 2048], P('dp')
- wq_grad: float32 [2048, 2048], P('dp', 'tensor')
- wk_grad: float32 [2048, 2048], P('dp', 'tensor')
- wv_grad: float32 [2048, 2048], P('dp', 'tensor')
- wo_grad: float32 [2048, 2048], P('tensor', 'dp')
- attn_gain_grad: float32 [2048], P('dp')
- q_gain_grad: float32 [2048], P('tensor')
- k_gain_grad: float32 [2048], P('tensor')
- moe_gain_grad: float32 [2048], P('dp')
- router_grad: float32 [2048, 16], P('dp')
- w_gate_grad: float32 [16, 2048, 1024], P(None, 'dp', 'tensor')
- w_up_grad: float32 [16, 2048, 1024], P(None, 'dp', 'tensor')
- w_down_grad: float32 [16, 1024, 2048], P(None, 'tensor', 'dp')
Inputs may be any that keep to these rules, and one draw needn't show every extreme that they name: `routes`: each row names 8 different experts; within each aligned block of 256 rows no expert is named by more than 176 rows, a bound that some block reaches.
All inputs are finite; a program needn't handle non-finite values.
Results may differ from a plain program's by a relative error of at most 0.024.
Values may be sent and summed in bfloat16 or wider, within the bound.
No kernel may reach another device: no remote copies, remote signals or barrier semaphores. Data moves between devices by JAX's collectives and lax.ppermute only.
A program may use at most 320 MiB of HBM per device.

v0:
```python
import jax
import jax.numpy as jnp
from jax import lax
from jax.sharding import PartitionSpec as P

HEAD_DIM = 128
TOPK = 8
EXPERTS = 16
MB_TOK = 256
MOST = 176


EPS = 1e-05
THETA = 10000.0
HIGH = lax.Precision.HIGHEST


def norm_scale(value, gain):
    return value * lax.rsqrt(jnp.mean(value * value, axis=-1, keepdims=True) + EPS) * gain


def rope_tables(length, head_dim):
    half = head_dim // 2
    freq = THETA ** (-(jnp.arange(half).astype(jnp.float32) * 2.0 / head_dim))
    angle = jnp.arange(length).astype(jnp.float32)[:, None] * freq[None, :]
    cosine = jnp.concatenate([jnp.cos(angle), jnp.cos(angle)], -1)
    sine = jnp.concatenate([jnp.sin(angle), jnp.sin(angle)], -1)
    return (cosine, sine)


def rotate(value, cosine, sine):
    half = value.shape[-1] // 2
    turned = jnp.concatenate([-value[..., half:], value[..., :half]], -1)
    return value * cosine[:, None, :] + turned * sine[:, None, :]


def unrotate(grad, cosine, sine):
    half = grad.shape[-1] // 2
    scaled = grad * sine[:, None, :]
    back_turn = jnp.concatenate([scaled[..., half:], -scaled[..., :half]], -1)
    return grad * cosine[:, None, :] + back_turn


def dispatch(route_block, experts, most):
    count = route_block.shape[0] * route_block.shape[1]
    flat = route_block.reshape(count)
    onehot = (flat[:, None] == jnp.arange(experts)[None, :]).astype(jnp.int32)
    before = jnp.cumsum(onehot, axis=0) - onehot
    slot = jnp.sum(before * onehot, axis=1)
    dest = flat * most + slot
    owner = (
        jnp.zeros((experts * most,), jnp.int32)
        .at[dest]
        .set(jnp.arange(count) // route_block.shape[1])
    )
    filled = jnp.zeros((experts * most,), jnp.int32).at[dest].set(1)
    return (dest, owner, filled)


def shards(
    tokens,
    cotangent,
    routes,
    wq,
    wk,
    wv,
    wo,
    attn_gain,
    q_gain,
    k_gain,
    moe_gain,
    router,
    w_gate,
    w_up,
    w_down,
):
    full = (
        lax.all_gather(wq, "dp", axis=0, tiled=True),
        lax.all_gather(wk, "dp", axis=0, tiled=True),
        lax.all_gather(wv, "dp", axis=0, tiled=True),
        lax.all_gather(wo, "dp", axis=1, tiled=True),
        lax.all_gather(attn_gain, "dp", axis=0, tiled=True),
        lax.all_gather(moe_gain, "dp", axis=0, tiled=True),
        lax.all_gather(router, "dp", axis=0, tiled=True),
        lax.all_gather(w_gate, "dp", axis=1, tiled=True),
        lax.all_gather(w_up, "dp", axis=1, tiled=True),
        lax.all_gather(w_down, "dp", axis=2, tiled=True),
    )
    (
        wq_full,
        wk_full,
        wv_full,
        wo_full,
        attn_gain_full,
        moe_gain_full,
        router_full,
        gate_full,
        up_full,
        down_full,
    ) = full
    seq = tokens.shape[0]
    width = tokens.shape[1]
    local = wq.shape[1]
    local_heads = local // HEAD_DIM
    f32 = jnp.float32
    bf16 = jnp.bfloat16
    xf = tokens.astype(f32)
    cot = cotangent.astype(f32)
    a_gain = attn_gain_full.astype(f32)
    m_gain = moe_gain_full.astype(f32)
    gain_q = q_gain.astype(f32)
    gain_k = k_gain.astype(f32)
    a_low = norm_scale(xf, a_gain).astype(bf16)
    query = jnp.dot(a_low, wq_full, preferred_element_type=f32)
    keyed = jnp.dot(a_low, wk_full, preferred_element_type=f32)
    valued = jnp.dot(a_low, wv_full, preferred_element_type=f32)
    sum_q, sum_k = lax.psum((jnp.sum(query * query, -1), jnp.sum(keyed * keyed, -1)), "tensor")
    rate_q = lax.rsqrt(sum_q / width + EPS)[:, None]
    rate_k = lax.rsqrt(sum_k / width + EPS)[:, None]
    cosine, sine = rope_tables(seq, HEAD_DIM)
    q_rot = rotate(
        (query * rate_q * gain_q).reshape(seq, local_heads, HEAD_DIM), cosine, sine
    ).astype(bf16)
    k_rot = rotate(
        (keyed * rate_k * gain_k).reshape(seq, local_heads, HEAD_DIM), cosine, sine
    ).astype(bf16)
    v_low = valued.reshape(seq, local_heads, HEAD_DIM).astype(bf16)
    scale = HEAD_DIM ** (-0.5)
    block = min(512, seq)

    def block_scores(start):
        end = start + block
        scores = scale * jnp.einsum("qhd,khd->hqk", q_rot, k_rot, preferred_element_type=f32)
        causal = (start + jnp.arange(block))[:, None] >= jnp.arange(end)[None, :]
        return jnp.where(causal[None], scores, -1e30)

    start = 0
    scores = block_scores(start)
    peak = jnp.max(scores, -1, keepdims=True)
    expd = jnp.exp(scores - peak)
    total = jnp.sum(expd, -1, keepdims=True)
    logsums = [peak + jnp.log(total)]
    weights = (expd / total).astype(bf16)
    outputs = jnp.einsum("hqk,khd->qhd", weights, v_low, preferred_element_type=f32)
    joined = outputs.reshape(seq, local).astype(bf16)
    attn = lax.psum(jnp.dot(joined, wo_full, preferred_element_type=f32), "tensor")
    resid = xf + attn
    m_low = norm_scale(resid, m_gain).astype(bf16)
    probs = jax.nn.softmax(jnp.dot(m_low, router_full, preferred_element_type=f32), axis=-1)
    picks = (routes[:, :, None] == jnp.arange(EXPERTS)[None, None, :]).astype(f32)
    gates = jnp.sum(probs[:, None, :] * picks, -1)
    moe_blocks = []
    dgate_blocks = []
    saved = []
    for blk in range(seq // MB_TOK):
        lo_row = blk * MB_TOK
        hi_row = lo_row + MB_TOK
        dest, owner, filled = dispatch(routes[lo_row:hi_row], EXPERTS, MOST)
        slots = jnp.where(
            filled[:, None] > 0, m_low[lo_row:hi_row][owner], jnp.zeros((), bf16)
        ).reshape(EXPERTS, MOST, width)
        gate_act = jnp.einsum("ecd,edf->ecf", slots, gate_full, preferred_element_type=f32)
        up_act = jnp.einsum("ecd,edf->ecf", slots, up_full, preferred_element_type=f32)
        hidden = (jax.nn.silu(gate_act) * up_act).astype(bf16)
        expert_out = jnp.einsum("ecf,efd->ecd", hidden, down_full, preferred_element_type=f32)
        picked = expert_out.reshape(EXPERTS * MOST, width)[dest].reshape(MB_TOK, TOPK, width)
        moe_part = jnp.sum(gates[lo_row:hi_row][:, :, None] * picked, axis=1)
        dgate_part = jnp.sum(cot[lo_row:hi_row][:, None, :] * picked, axis=-1)
        moe_block, dgate_block = (
            lax.psum(moe_part.astype(jnp.bfloat16), "tensor").astype(jnp.float32),
            lax.psum(dgate_part.astype(jnp.bfloat16), "tensor").astype(jnp.float32),
        )
        moe_blocks.append(moe_block)
        dgate_blocks.append(dgate_block)
        saved.append((dest, owner, filled, gate_act, up_act))
    mixed = (resid + jnp.concatenate(moe_blocks, 0)).astype(bf16)
    dgate = jnp.concatenate(dgate_blocks, 0)
    full = (
        lax.all_gather(wq, "dp", axis=0, tiled=True),
        lax.all_gather(wk, "dp", axis=0, tiled=True),
        lax.all_gather(wv, "dp", axis=0, tiled=True),
        lax.all_gather(wo, "dp", axis=1, tiled=True),
        lax.all_gather(attn_gain, "dp", axis=0, tiled=True),
        lax.all_gather(moe_gain, "dp", axis=0, tiled=True),
        lax.all_gather(router, "dp", axis=0, tiled=True),
        lax.all_gather(w_gate, "dp", axis=1, tiled=True),
        lax.all_gather(w_up, "dp", axis=1, tiled=True),
        lax.all_gather(w_down, "dp", axis=2, tiled=True),
    )
    (
        wq_full,
        wk_full,
        wv_full,
        wo_full,
        attn_gain_full,
        moe_gain_full,
        router_full,
        gate_full,
        up_full,
        down_full,
    ) = full
    dprobs = jnp.sum(dgate[:, :, None] * picks, axis=1)
    dlogits = probs * (dprobs - jnp.sum(probs * dprobs, -1, keepdims=True))
    m_float = m_low.astype(f32)
    router_grad = jnp.dot(m_float.T, dlogits, precision=HIGH)
    dm_router = jnp.dot(dlogits, router_full.astype(f32).T, precision=HIGH)
    gate_grad = jnp.zeros(gate_full.shape, f32)
    up_grad = jnp.zeros(up_full.shape, f32)
    down_grad = jnp.zeros(down_full.shape, f32)
    dm_blocks = []
    for blk in range(seq // MB_TOK):
        lo_row = blk * MB_TOK
        hi_row = lo_row + MB_TOK
        dest, owner, filled, gate_act, up_act = saved[blk]
        slots = jnp.where(
            filled[:, None] > 0, m_low[lo_row:hi_row][owner], jnp.zeros((), bf16)
        ).reshape(EXPERTS, MOST, width)
        sigma = jax.nn.sigmoid(gate_act)
        silu_gate = gate_act * sigma
        hidden = (silu_gate * up_act).astype(bf16)
        dy_rows = (
            (gates[lo_row:hi_row][:, :, None] * cot[lo_row:hi_row][:, None, :])
            .astype(bf16)
            .reshape(MB_TOK * TOPK, width)
        )
        dy_slots = (
            jnp.zeros((EXPERTS * MOST, width), bf16)
            .at[dest]
            .set(dy_rows)
            .reshape(EXPERTS, MOST, width)
        )
        down_grad = down_grad + jnp.einsum(
            "ecf,ecd->efd", hidden, dy_slots, preferred_element_type=f32
        )
        dhidden = jnp.einsum("ecd,efd->ecf", dy_slots, down_full, preferred_element_type=f32)
        dgate_act = (dhidden * up_act * sigma * (1.0 + gate_act * (1.0 - sigma))).astype(bf16)
        dup_act = (dhidden * silu_gate).astype(bf16)
        gate_grad = gate_grad + jnp.einsum(
            "ecd,ecf->edf", slots, dgate_act, preferred_element_type=f32
        )
        up_grad = up_grad + jnp.einsum("ecd,ecf->edf", slots, dup_act, preferred_element_type=f32)
        dslots = jnp.einsum(
            "ecf,edf->ecd", dgate_act, gate_full, preferred_element_type=f32
        ) + jnp.einsum("ecf,edf->ecd", dup_act, up_full, preferred_element_type=f32)
        dm_rows = jnp.sum(
            dslots.reshape(EXPERTS * MOST, width)[dest].reshape(MB_TOK, TOPK, width), axis=1
        )
        dm_blocks.append(lax.psum(dm_rows.astype(jnp.bfloat16), "tensor").astype(jnp.float32))
    dm_total = jnp.concatenate(dm_blocks, 0) + dm_router
    moe_fn = lambda value, gain: norm_scale(value, gain)
    moe_pull = jax.vjp(moe_fn, resid, moe_gain_full.astype(f32))[1]
    dresid_norm, moe_gain_grad = moe_pull(dm_total)
    dresid = cot + dresid_norm
    dresid_low = dresid.astype(bf16)
    wo_grad = jnp.einsum("sa,sd->ad", joined, dresid_low, preferred_element_type=f32)
    dout = (
        jnp.einsum("sd,ad->sa", dresid_low, wo_full, preferred_element_type=f32)
        .astype(bf16)
        .reshape(seq, local_heads, HEAD_DIM)
    )
    dq_rot = []
    dk_rot = jnp.zeros((seq, local_heads, HEAD_DIM), f32)
    dv_acc = jnp.zeros((seq, local_heads, HEAD_DIM), f32)
    for index, start in enumerate(range(0, seq, block)):
        end = start + block
        scores = block_scores(start)
        weights = jnp.exp(scores - logsums[index])
        dweights = jnp.einsum("qhd,khd->hqk", dout, v_low, preferred_element_type=f32)
        dv_acc = dv_acc.at[:end].add(
            jnp.einsum("hqk,qhd->khd", weights.astype(bf16), dout, preferred_element_type=f32)
        )
        inner = jnp.sum(weights * dweights, -1, keepdims=True)
        dscores = (weights * (dweights - inner)).astype(bf16)
        dq_rot.append(
            scale * jnp.einsum("hqk,khd->qhd", dscores, k_rot, preferred_element_type=f32)
        )
        dk_rot = dk_rot.at[:end].add(
            scale * jnp.einsum("hqk,qhd->khd", dscores, q_rot, preferred_element_type=f32)
        )
    dq_norm = unrotate(dq_rot[0], cosine, sine).reshape(seq, local)
    dk_norm = unrotate(dk_rot, cosine, sine).reshape(seq, local)
    inner_q, inner_k = lax.psum(
        (jnp.sum(dq_norm * gain_q * query, -1), jnp.sum(dk_norm * gain_k * keyed, -1)), "tensor"
    )
    dq_low = (rate_q * gain_q * dq_norm - query * rate_q**3 * inner_q[:, None] / width).astype(bf16)
    dk_low = (rate_k * gain_k * dk_norm - keyed * rate_k**3 * inner_k[:, None] / width).astype(bf16)
    dv_low = dv_acc.reshape(seq, local).astype(bf16)
    q_gain_part = jnp.sum(dq_norm * query * rate_q, 0)
    k_gain_part = jnp.sum(dk_norm * keyed * rate_k, 0)
    q_gain_grad, k_gain_grad = lax.psum((q_gain_part, k_gain_part), "dp")
    wq_grad = jnp.einsum("sd,sa->da", a_low, dq_low, preferred_element_type=f32)
    wk_grad = jnp.einsum("sd,sa->da", a_low, dk_low, preferred_element_type=f32)
    wv_grad = jnp.einsum("sd,sa->da", a_low, dv_low, preferred_element_type=f32)
    da_part = (
        jnp.einsum("sa,da->sd", dq_low, wq_full, preferred_element_type=f32)
        + jnp.einsum("sa,da->sd", dk_low, wk_full, preferred_element_type=f32)
        + jnp.einsum("sa,da->sd", dv_low, wv_full, preferred_element_type=f32)
    )
    da_total = lax.psum(da_part.astype(jnp.bfloat16), "tensor").astype(jnp.float32)
    attn_fn = lambda value, gain: norm_scale(value, gain)
    attn_pull = jax.vjp(attn_fn, xf, attn_gain_full.astype(f32))[1]
    dx_norm, attn_gain_grad = attn_pull(da_total)
    tokens_grad = (dresid + dx_norm).astype(bf16)
    owned = (
        lax.psum_scatter(
            wq_grad.astype(jnp.bfloat16), "dp", scatter_dimension=0, tiled=True
        ).astype(jnp.float32),
        lax.psum_scatter(
            wk_grad.astype(jnp.bfloat16), "dp", scatter_dimension=0, tiled=True
        ).astype(jnp.float32),
        lax.psum_scatter(
            wv_grad.astype(jnp.bfloat16), "dp", scatter_dimension=0, tiled=True
        ).astype(jnp.float32),
        lax.psum_scatter(
            wo_grad.astype(jnp.bfloat16), "dp", scatter_dimension=1, tiled=True
        ).astype(jnp.float32),
        lax.psum_scatter(
            attn_gain_grad.astype(jnp.bfloat16), "dp", scatter_dimension=0, tiled=True
        ).astype(jnp.float32),
        lax.psum_scatter(
            moe_gain_grad.astype(jnp.bfloat16), "dp", scatter_dimension=0, tiled=True
        ).astype(jnp.float32),
        lax.psum_scatter(
            router_grad.astype(jnp.bfloat16), "dp", scatter_dimension=0, tiled=True
        ).astype(jnp.float32),
        lax.psum_scatter(
            gate_grad.astype(jnp.bfloat16), "dp", scatter_dimension=1, tiled=True
        ).astype(jnp.float32),
        lax.psum_scatter(
            up_grad.astype(jnp.bfloat16), "dp", scatter_dimension=1, tiled=True
        ).astype(jnp.float32),
        lax.psum_scatter(
            down_grad.astype(jnp.bfloat16), "dp", scatter_dimension=2, tiled=True
        ).astype(jnp.float32),
    )
    return (
        mixed,
        tokens_grad,
        owned[0],
        owned[1],
        owned[2],
        owned[3],
        owned[4],
        q_gain_grad,
        k_gain_grad,
        owned[5],
        owned[6],
        owned[7],
        owned[8],
        owned[9],
    )


def solution(mesh):
    in_specs = (
        P("dp", None),
        P("dp", None),
        P("dp", None),
        P("dp", "tensor"),
        P("dp", "tensor"),
        P("dp", "tensor"),
        P("tensor", "dp"),
        P("dp"),
        P("tensor"),
        P("tensor"),
        P("dp"),
        P("dp", None),
        P(None, "dp", "tensor"),
        P(None, "dp", "tensor"),
        P(None, "tensor", "dp"),
    )
    out_specs = (
        P("dp", None),
        P("dp", None),
        P("dp", "tensor"),
        P("dp", "tensor"),
        P("dp", "tensor"),
        P("tensor", "dp"),
        P("dp"),
        P("tensor"),
        P("tensor"),
        P("dp"),
        P("dp", None),
        P(None, "dp", "tensor"),
        P(None, "dp", "tensor"),
        P(None, "tensor", "dp"),
    )
    return jax.shard_map(shards, mesh=mesh, in_specs=in_specs, out_specs=out_specs, check_vma=False)
```

profile of v0, /device:TPU:0, one launch (start us, length us, event | category | flops | bytes accessed | tf_op | source)
XLA Modules:
  0.0 1824.9 jit_solution(3232619207578133163)
XLA Ops:
  11.5 13.5 all-gather
  30.0 11.5 all-gather.14.cloned.1.call-done
  44.5 27.2 %all-gather.12.cloned.1.call-done = bf16[2048,512]{1,0:T(8,128)(2,1)} async-done(((bf16[256,512]{1,0:T(8,128)(2,1)}), bf16[2048,512]{1,0:T(8,128)(2,1)}) %all-gather.12.cloned.1.call-update) | async-done | bytes 2097168 | tf_op jit(solution)/shard_map/all_gather | solution.py:78
  75.6 9.8 all-reduce.4
  92.1 9.8 all-gather.10.cloned.1.call-done
  106.8 26.9 %all-gather.16.cloned.1.call-done = bf16[512,2048]{1,0:T(8,128)(2,1)} async-done(((bf16[512,256]{1,0:T(8,128)(2,1)}), bf16[512,2048]{1,0:T(8,128)(2,1)}) %all-gather.16.cloned.1.call-update) | async-done | bytes 2097168 | tf_op jit(solution)/shard_map/all_gather | solution.py:81
  185.6 11.7 all-gather.1
  198.1 13.9 all_gather.46
  217.4 24.3 %all-reduce.13.cloned.1.call-done = f32[512,2048]{1,0:T(8,128)} async-done(((f32[512,2048]{1,0:T(8,128)}), f32[512,2048]{1,0:T(8,128)}) %all-reduce.13.cloned.1.call-update) | async-done | bytes 4194320 | tf_op jit(solution)/shard_map/psum | solution.py:146
  251.5 11.7 gather_fusion.2
  263.2 11.8 gather_fusion
  275.0 19.9 %scatter_custom_fusion.5 = bf16[2816,2048]{1,0:T(8,128)(2,1)} fusion(s32[2048]{0:T(1024)S(1)} %bitcast.229, f32[256,2048]{1,0:T(8,128)} %get-tuple-element.90, f32[2048]{0:T(1024)S(1)} %mul.583, bf16[]{:T(256)} %constant.145.clone.1), kind=kCustom, calls=%fused_computation.32 | custom fusion | flops 8388608 | bytes 13639682 | tf_op jit(solution)/shard_map/scatter | solution.py:229
  294.9 19.5 %scatter_custom_fusion.4 = bf16[2816,2048]{1,0:T(8,128)(2,1)} fusion(s32[2048]{0:T(1024)S(1)} %bitcast.233, f32[256,2048]{1,0:T(8,128)S(1)} %copy-done.9, f32[2048]{0:T(1024)S(1)} %mul.573, bf16[]{:T(256)} %constant.145.clone.1), kind=kCustom, calls=%fused_computation.31 | custom fusion | flops 8388608 | bytes 13639682 | tf_op jit(solution)/shard_map/scatter | solution.py:229
  314.4 80.0 %all-gather.18.cloned.1.call-done = bf16[16,2048,256]{2,1,0:T(8,128)(2,1)} async-done(((bf16[16,256,256]{2,1,0:T(8,128)(2,1)}), bf16[16,2048,256]{2,1,0:T(8,128)(2,1)}) %all-gather.18.cloned.1.call-update) | async-done | bytes 16777232 | tf_op jit(solution)/shard_map/all_gather | solution.py:85
  394.4 15.1 fusion.19
  409.5 135.9 %all-gather.20.cloned.1.call-done = bf16[16,2048,256]{2,1,0:T(8,128)(2,1)} async-done(((bf16[16,256,256]{2,1,0:T(8,128)(2,1)}), bf16[16,2048,256]{2,1,0:T(8,128)(2,1)}) %all-gather.20.cloned.1.call-update) | async-done | bytes 16777232 | tf_op jit(solution)/shard_map/all_gather | solution.py:86
  545.4 15.1 fusion.18
  560.5 136.6 %all-gather.22.cloned.1.call-done = bf16[16,256,2048]{2,1,0:T(8,128)(2,1)} async-done(((bf16[16,256,256]{2,1,0:T(8,128)(2,1)}), bf16[16,256,2048]{2,1,0:T(8,128)(2,1)}) %all-gather.22.cloned.1.call-update) | async-done | bytes 16777232 | tf_op jit(solution)/shard_map/all_gather | solution.py:87
  697.2 15.5 multiply_convert_fusion.2
  712.7 17.6 fusion.118
  730.3 24.1 %gather_fusion.3 = f32[2048,2048]{1,0:T(8,128)} fusion(f32[2816,2048]{1,0:T(8,128)} %bitcast.184, s32[2048]{0:T(1024)S(1)} %broadcast_clamp_fusion), kind=kCustom, calls=%fused_computation.3 | custom fusion | bytes 33562624 | tf_op jit(solution)/shard_map/gather | solution.py:166
  754.4 14.0 fusion.120
  768.4 21.1 %convolution_add_fusion = f32[16,176,2048]{2,1,0:T(8,128)} fusion(f32[16,176,2048]{2,1,0:T(8,128)} %fusion.120, bf16[16,176,256]{2,1,0:T(8,128)(2,1)S(1)} %copy-done.27, bf16[16,2048,256]{2,1,0:T(8,128)(2,1)} %all-gather.20.cloned.1.call-done), kind=kOutput, calls=%fused_computation.48 | convolution fusion | flops 2958557184 | bytes 64356352 | tf_op jit(solution)/shard_map/ecf,edf->ecd/dot_general | solution.py:244
  789.5 24.1 %gather_fusion.5 = f32[2048,2048]{1,0:T(8,128)} fusion(f32[2816,2048]{1,0:T(8,128)} %bitcast.185, s32[2048]{0:T(1024)S(1)} %broadcast_clamp_fusion), kind=kCustom, calls=%fused_computation.5 | custom fusion | bytes 33562624 | tf_op jit(solution)/shard_map/gather | solution.py:246
  813.6 9.3 bitcast_reduce_fusion
  823.0 13.8 fusion.17
  836.8 13.9 fusion.16
  850.7 15.1 multiply_convert_fusion.4
  865.8 14.9 fusion.119
  880.7 21.8 %convolution_add_fusion.1 = f32[16,176,2048]{2,1,0:T(8,128)} fusion(f32[16,176,2048]{2,1,0:T(8,128)} %fusion.119, bf16[16,176,256]{2,1,0:T(8,128)(2,1)} %get-tuple-element.83, bf16[16,2048,256]{2,1,0:T(8,128)(2,1)} %all-gather.20.cloned.1.call-done), kind=kOutput, calls=%fused_computation.49 | convolution fusion | flops 2958557184 | bytes 64356352 | tf_op jit(solution)/shard_map/ecf,edf->ecd/dot_general | solution.py:244
  902.5 24.0 %gather_fusion.4 = f32[2048,2048]{1,0:T(8,128)} fusion(f32[2816,2048]{1,0:T(8,128)} %bitcast.186, s32[2048]{0:T(1024)S(1)} %copy-done.71), kind=kCustom, calls=%fused_computation.4 | custom fusion | bytes 33562624 | tf_op jit(solution)/shard_map/gather | solution.py:246
  935.8 17.6 fusion.117
  953.5 10.8 fusion.3
  964.3 24.3 %gather_fusion.1 = f32[2048,2048]{1,0:T(8,128)} fusion(f32[2816,2048]{1,0:T(8,128)} %bitcast.183, s32[2048]{0:T(1024)S(1)} %copy-done.71), kind=kCustom, calls=%fused_computation.1 | custom fusion | bytes 33562624 | tf_op jit(solution)/shard_map/gather | solution.py:166
  988.7 11.3 fusion.5
  1000.0 18.6 %all-reduce.6 = (bf16[256,8]{1,0:T(8,128)(2,1)S(1)}, bf16[256,8]{1,0:T(8,128)(2,1)S(1)}) all-reduce(bf16[256,8]{1,0:T(8,128)(2,1)S(1)} %get-tuple-element.56, bf16[256,8]{1,0:T(8,128)(2,1)S(1)} %get-tuple-element.54), channel_id=1, replica_groups=mesh['dp'=8,'tensor'=4] {'tensor'}, use_global_device_ids=true, to_apply=%region_35.36 | all-reduce | flops 4096 | bytes 16384 | tf_op jit(solution)/shard_map/psum | solution.py:171
  1078.5 16.6 fusion.15
  1095.2 22.5 %add_convert_fusion.2 = bf16[16,2048,256]{2,1,0:T(8,128)(2,1)} fusion(f32[16,2048,256]{2,1,0:T(8,128)} %fusion.15, bf16[16,176,256]{2,1,0:T(8,128)(2,1)} %copy-done.23, bf16[16,176,2048]{2,1,0:T(8,128)(2,1)} %bitcast.193, pred[16,176]{1,0:T(8,128)(4,1)S(1)} %copy-done.70), kind=kOutput, calls=%fused_computation.14 | convolution fusion | flops 2975334400 | bytes 63310592 | tf_op jit(solution)/shard_map/ecd,ecf->edf/dot_general | solution.py:238
  1119.1 16.6 fusion.14
  1135.7 22.4 %add_convert_fusion.1 = bf16[16,2048,256]{2,1,0:T(8,128)(2,1)} fusion(f32[16,2048,256]{2,1,0:T(8,128)} %fusion.14, bf16[16,176,256]{2,1,0:T(8,128)(2,1)} %get-tuple-element.86, bf16[16,176,2048]{2,1,0:T(8,128)(2,1)} %bitcast.194, pred[16,176]{1,0:T(8,128)(4,1)S(1)} %copy-done.70), kind=kOutput, calls=%fused_computation.13 | convolution fusion | flops 2975334400 | bytes 63310592 | tf_op jit(solution)/shard_map/ecd,ecf->edf/dot_general | solution.py:241
  1159.5 17.7 fusion.123
  1177.2 22.7 %add_convert_fusion = bf16[16,256,2048]{2,1,0:T(8,128)(2,1)} fusion(f32[16,256,2048]{2,1,0:T(8,128)} %fusion.123, bf16[16,176,256]{2,1,0:T(8,128)(2,1)} %copy-done.26, bf16[16,176,2048]{2,1,0:T(8,128)(2,1)} %bitcast.198), kind=kOutput, calls=%fused_computation.12 | convolution fusion | flops 2969567232 | bytes 63307776 | tf_op jit(solution)/shard_map/ecf,ecd->efd/dot_general | solution.py:232
  1203.1 14.2 all-reduce.2
  1224.5 80.8 %all-reduce.15.cloned.1.call-done = (bf16[256,2048]{1,0:T(8,128)(2,1)}, bf16[256,2048]{1,0:T(8,128)(2,1)}, bf16[512,2048]{1,0:T(8,128)(2,1)}) async-done(((bf16[256,2048]{1,0:T(8,128)(2,1)}, bf16[256,2048]{1,0:T(8,128)(2,1)}, bf16[512,2048]{1,0:T(8,128)(2,1)}), (bf16[256,2048]{1,0:T(8,128)(2,1)}, bf16[256,2048]{1,0:T(8,128)(2,1)}, bf16[512,2048]{1,0:T(8,128)(2,1)})) %all-reduce.15.cloned.1.call-update) | async-done | bytes 4194320 | tf_op jit(solution)/shard_map/psum | solution.py:170
  1308.7 17.3 all-reduce.5
  1334.9 141.4 %reduce-scatter.19.cloned.1.call-done = bf16[16,256,256]{2,1,0:T(8,128)(2,1)} async-done(((bf16[16,2048,256]{2,1,0:T(8,128)(2,1)}), bf16[16,256,256]{2,1,0:T(8,128)(2,1)}) %reduce-scatter.19.cloned.1.call-update) | async-done | bytes 2097168 | tf_op jit(solution)/shard_map/reduce_scatter | solution.py:326
  1480.3 164.7 %reduce-scatter.21.cloned.1.call-done = bf16[16,256,256]{2,1,0:T(8,128)(2,1)} async-done(((bf16[16,2048,256]{2,1,0:T(8,128)(2,1)}), bf16[16,256,256]{2,1,0:T(8,128)(2,1)}) %reduce-scatter.21.cloned.1.call-update) | async-done | bytes 2097168 | tf_op jit(solution)/shard_map/reduce_scatter | solution.py:329
  1649.0 164.8 %reduce-scatter.23.cloned.1.call-done = bf16[16,256,256]{2,1,0:T(8,128)(2,1)} async-done(((bf16[16,256,2048]{2,1,0:T(8,128)(2,1)}), bf16[16,256,256]{2,1,0:T(8,128)(2,1)}) %reduce-scatter.23.cloned.1.call-update) | async-done | bytes 2097168 | tf_op jit(solution)/shard_map/reduce_scatter | solution.py:332
  (376 shorter events, 200.4 us)
Async XLA Ops:
  7.2 34.3 %copy-start.7 = (bf16[512,2048]{1,0:T(8,128)(2,1)S(1)}, bf16[512,2048]{1,0:T(8,128)(2,1)}, u32[]{:S(2)}) copy-start(bf16[512,2048]{1,0:T(8,128)(2,1)} %param.23) | copy-start | bytes 6291460
  7.2 34.3 %all-gather.14.cloned.1.call-start = ((), (), s32[]{:S(2)}) async-start(), calls=%async_computation.10 | async-start | bytes 2359296 | tf_op jit(solution)/shard_map/all_gather | solution.py:79
  7.9 63.8 %all-gather.12.cloned.1.call-start = ((), (), s32[]{:S(2)}) async-start(), calls=%async_computation.9 | async-start | bytes 2359296 | tf_op jit(solution)/shard_map/all_gather | solution.py:78
  8.7 93.2 %all-gather.10.cloned.1.call-start = ((), (), s32[]{:S(2)}) async-start(), calls=%async_computation.8 | async-start | bytes 2359296 | tf_op jit(solution)/shard_map/all_gather | solution.py:80
  9.4 124.3 %all-gather.16.cloned.1.call-start = ((), (), s32[]{:S(2)}) async-start(), calls=%async_computation.11 | async-start | bytes 2359296 | tf_op jit(solution)/shard_map/all_gather | solution.py:81
  10.0 231.7 %all-reduce.13.cloned.1.call-start = ((), (), s32[]{:S(2)}) async-start(), calls=%async_computation.12 | async-start | bytes 8388608 | tf_op jit(solution)/shard_map/psum | solution.py:146
  25.0 76.9 %copy-start.72 = (f32[8,1,256]{2,1,0:T(1,128)}, f32[8,1,256]{2,1,0:T(1,128)S(1)}, u32[]{:S(2)}) copy-start(f32[8,1,256]{2,1,0:T(1,128)S(1)} %convert_element_type.313) | copy-start | bytes 24580
  27.2 74.8 %copy-start.90 = (f32[512]{0:T(512)}, f32[512]{0:T(512)S(1)}, u32[]{:S(2)}) copy-start(f32[512]{0:T(512)S(1)} %fusion.90) | copy-start | bytes 6148
  27.9 58.2 %copy-start.76 = (f32[512]{0:T(512)}, f32[512]{0:T(512)S(1)}, u32[]{:S(2)}) copy-start(f32[512]{0:T(512)S(1)} %convert_element_type.253) | copy-start | bytes 6148
  28.6 58.1 %copy-start.78 = (f32[512]{0:T(512)}, f32[512]{0:T(512)S(1)}, u32[]{:S(2)}) copy-start(f32[512]{0:T(512)S(1)} %convert_element_type.249) | copy-start | bytes 6148
  44.5 41.6 %copy-start.19 = (f32[512,512]{0,1:T(8,128)}, f32[512,512]{0,1:T(8,128)S(1)}, u32[]{:S(2)}) copy-start(f32[512,512]{0,1:T(8,128)S(1)} %get-tuple-element.126) | copy-start | bytes 3145732
  106.8 31.8 %copy-start.60 = (bf16[4,128,512]{2,1,0:T(8,128)(2,1)}, bf16[4,128,512]{2,1,0:T(8,128)(2,1)S(1)}, u32[]{:S(2)}) copy-start(bf16[4,128,512]{2,1,0:T(8,128)(2,1)S(1)} %fusion.50) | copy-start | bytes 1572868
  138.7 255.8 %all-gather.18.cloned.1.call-start = ((), (), s32[]{:S(2)}) async-start(), calls=%async_computation.13 | async-start | bytes 18874368 | tf_op jit(solution)/shard_map/all_gather | solution.py:85
  139.2 46.3 %copy-start.101 = (bf16[256]{0:T(256)(128)(2,1)S(1)}, bf16[256]{0:T(256)(128)(2,1)}, u32[]{:S(2)}) copy-start(bf16[256]{0:T(256)(128)(2,1)} %param.33) | copy-start | bytes 1540
  139.2 58.9 %copy-start.98 = (bf16[256,16]{0,1:T(8,128)(2,1)S(1)}, bf16[256,16]{0,1:T(8,128)(2,1)}, u32[]{:S(2)}) copy-start(bf16[256,16]{0,1:T(8,128)(2,1)} %param.34) | copy-start | bytes 24580
  139.3 406.2 %all-gather.20.cloned.1.call-start = ((), (), s32[]{:S(2)}) async-start(), calls=%async_computation.14 | async-start | bytes 18874368 | tf_op jit(solution)/shard_map/all_gather | solution.py:86
  140.0 557.1 %all-gather.22.cloned.1.call-start = ((), (), s32[]{:S(2)}) async-start(), calls=%async_computation.15 | async-start | bytes 18874368 | tf_op jit(solution)/shard_map/all_gather | solution.py:87
  140.8 879.8 %all-reduce.17.cloned.1.call-start = ((), (), s32[]{:S(2)}) async-start(), calls=%async_computation.25 | async-start | bytes 4194304 | tf_op jit(solution)/shard_map/psum | solution.py:248
  197.3 47.3 %copy-start.67 = (f32[8,1,256]{2,1,0:T(1,128)}, f32[8,1,256]{2,1,0:T(1,128)S(1)}, u32[]{:S(2)}) copy-start(f32[8,1,256]{2,1,0:T(1,128)S(1)} %convert_element_type.314) | copy-start | bytes 24580
  197.4 348.0 %copy-start.69 = (pred[16,176]{1,0:T(8,128)(4,1)}, pred[16,176]{1,0:T(8,128)(4,1)S(1)}, u32[]{:S(2)}) copy-start(pred[16,176]{1,0:T(8,128)(4,1)S(1)} %broadcast_in_dim.62) | copy-start | bytes 8452
  212.1 33.0 %copy-start.52 = (bf16[2048,16]{0,1:T(8,128)(2,1)}, bf16[2048,16]{0,1:T(8,128)(2,1)S(1)}, u32[]{:S(2)}) copy-start(bf16[2048,16]{0,1:T(8,128)(2,1)S(1)} %all_gather.46) | copy-start | bytes 196612
  275.0 19.9 %copy-start.9 = (f32[256,2048]{1,0:T(8,128)S(1)}, f32[256,2048]{1,0:T(8,128)}, u32[]{:S(2)}) copy-start(f32[256,2048]{1,0:T(8,128)} %get-tuple-element.89) | copy-start | bytes 6291460
  712.7 41.7 %copy-start.23 = (bf16[16,176,256]{2,1,0:T(8,128)(2,1)}, bf16[16,176,256]{2,1,0:T(8,128)(2,1)S(1)}, u32[]{:S(2)}) copy-start(bf16[16,176,256]{2,1,0:T(8,128)(2,1)S(1)} %get-tuple-element.87) | copy-start | bytes 4325380
  865.8 70.0 %copy-start.16 = (bf16[16,176,256]{2,1,0:T(8,128)(2,1)}, bf16[16,176,256]{2,1,0:T(8,128)(2,1)S(1)}, u32[]{:S(2)}) copy-start(bf16[16,176,256]{2,1,0:T(8,128)(2,1)S(1)} %get-tuple-element.85) | copy-start | bytes 4325380
  880.7 21.8 %copy-start.71 = (s32[2048]{0:T(1024)S(1)}, s32[2048]{0:T(1024)}, u32[]{:S(2)}) copy-start(s32[2048]{0:T(1024)} %broadcast_clamp_fusion.1) | copy-start | bytes 24580
  935.8 266.0 %reduce-scatter.17.cloned.1.call-start = ((), (), s32[]{:S(2)}) async-start(), calls=%async_computation.20 | async-start | bytes 73728 | tf_op jit(solution)/shard_map/reduce_scatter | solution.py:323
  964.3 24.3 %copy-start.44 = (f32[256,8]{1,0:T(8,128)S(1)}, f32[256,8]{1,0:T(8,128)}, u32[]{:S(2)}) copy-start(f32[256,8]{1,0:T(8,128)} %copy-done.43) | copy-start | bytes 24580
  988.6 30.2 %copy-start.65 = (s32[512,8]{0,1:T(8,128)S(1)}, s32[512,8]{0,1:T(8,128)}, u32[]{:S(2)}) copy-start(s32[512,8]{0,1:T(8,128)} %param.25) | copy-start | bytes 49156
  988.6 30.2 %copy-start.57 = (f32[512,16]{0,1:T(8,128)S(1)}, f32[512,16]{0,1:T(8,128)}, u32[]{:S(2)}) copy-start(f32[512,16]{0,1:T(8,128)} %copy-done.56) | copy-start | bytes 98308
  988.6 30.2 %copy-start.75 = (f32[512]{0:T(512)S(1)}, f32[512]{0:T(512)}, u32[]{:S(2)}) copy-start(f32[512]{0:T(512)} %copy-done.74) | copy-start | bytes 6148
  988.6 30.2 %copy-start.89 = (f32[512]{0:T(512)S(1)}, f32[512]{0:T(512)}, u32[]{:S(2)}) copy-start(f32[512]{0:T(512)} %copy-done.88) | copy-start | bytes 6148
  988.6 30.3 %copy-start.6 = (bf16[512,2048]{1,0:T(8,128)(2,1)S(1)}, bf16[512,2048]{1,0:T(8,128)(2,1)}, u32[]{:S(2)}) copy-start(bf16[512,2048]{1,0:T(8,128)(2,1)} %copy-done.5) | copy-start | bytes 6291460
  988.6 30.3 %copy-start.55 = (f32[512,16]{0,1:T(8,128)S(1)}, f32[512,16]{0,1:T(8,128)}, u32[]{:S(2)}) copy-start(f32[512,16]{0,1:T(8,128)} %copy-done.54) | copy-start | bytes 98308
  988.6 31.9 %copy-start.53 = (bf16[2048,16]{0,1:T(8,128)(2,1)S(1)}, bf16[2048,16]{0,1:T(8,128)(2,1)}, u32[]{:S(2)}) copy-start(bf16[2048,16]{0,1:T(8,128)(2,1)} %copy-done.52) | copy-start | bytes 196612
  988.6 31.9 %copy-start.68 = (f32[8,1,256]{2,1,0:T(1,128)S(1)}, f32[8,1,256]{2,1,0:T(1,128)}, u32[]{:S(2)}) copy-start(f32[8,1,256]{2,1,0:T(1,128)} %copy-done.67) | copy-start | bytes 24580
  988.7 31.9 %copy-start.85 = (f32[512]{0:T(512)S(1)}, f32[512]{0:T(512)}, u32[]{:S(2)}) copy-start(f32[512]{0:T(512)} %copy-done.84) | copy-start | bytes 6148
  1020.5 196.8 %reduce-scatter.9.cloned.1.call-start = ((), (), s32[]{:S(2)}) async-start(), calls=%async_computation.16 | async-start | bytes 2359296 | tf_op jit(solution)/shard_map/reduce_scatter | solution.py:305
  1052.3 166.7 %reduce-scatter.11.cloned.1.call-start = ((), (), s32[]{:S(2)}) async-start(), calls=%async_computation.17 | async-start | bytes 2359296 | tf_op jit(solution)/shard_map/reduce_scatter | solution.py:308
  1057.6 163.3 %reduce-scatter.13.cloned.1.call-start = ((), (), s32[]{:S(2)}) async-start(), calls=%async_computation.18 | async-start | bytes 2359296 | tf_op jit(solution)/shard_map/reduce_scatter | solution.py:311
  1064.6 158.1 %reduce-scatter.15.cloned.1.call-start = ((), (), s32[]{:S(2)}) async-start(), calls=%async_computation.19 | async-start | bytes 2359296 | tf_op jit(solution)/shard_map/reduce_scatter | solution.py:314
  1069.6 235.7 %all-reduce.15.cloned.1.call-start = ((), (), s32[]{:S(2)}) async-start(), calls=%async_computation.24 | async-start | bytes 8388608 | tf_op jit(solution)/shard_map/psum | solution.py:170
  1077.2 399.0 %reduce-scatter.19.cloned.1.call-start = ((), (), s32[]{:S(2)}) async-start(), calls=%async_computation.21 | async-start | bytes 18874368 | tf_op jit(solution)/shard_map/reduce_scatter | solution.py:326
  1117.7 527.3 %reduce-scatter.21.cloned.1.call-start = ((), (), s32[]{:S(2)}) async-start(), calls=%async_computation.22 | async-start | bytes 18874368 | tf_op jit(solution)/shard_map/reduce_scatter | solution.py:329
  1158.1 655.7 %reduce-scatter.23.cloned.1.call-start = ((), (), s32[]{:S(2)}) async-start(), calls=%async_computation.23 | async-start | bytes 18874368 | tf_op jit(solution)/shard_map/reduce_scatter | solution.py:332
  1199.9 105.4 %copy-start.92 = (f32[512]{0:T(512)S(1)}, f32[512]{0:T(512)}, u32[]{:S(2)}) copy-start(f32[512]{0:T(512)} %copy-done.90) | copy-start | bytes 6148
  1199.9 108.8 %copy-start.95 = (bf16[2048]{0:T(1024)(128)(2,1)S(1)}, bf16[2048]{0:T(1024)(128)(2,1)}, u32[]{:S(2)}) copy-start(bf16[2048]{0:T(1024)(128)(2,1)} %get-tuple-element.58) | copy-start | bytes 12292
  1199.9 127.4 %copy-start.87 = (f32[512]{0:T(512)S(1)}, f32[512]{0:T(512)}, u32[]{:S(2)}) copy-start(f32[512]{0:T(512)} %copy-done.86) | copy-start | bytes 6148
  1305.3 22.1 %copy-start.50 = (bf16[256,2048]{1,0:T(8,128)(2,1)S(1)}, bf16[256,2048]{1,0:T(8,128)(2,1)}, u32[]{:S(2)}) copy-start(bf16[256,2048]{1,0:T(8,128)(2,1)} %get-tuple-element.76) | copy-start | bytes 3145732
  (73 other events, 327.8 us)
Sparse Core Ops, SparseCore 0:
  9.6 31.8 all-gather.13
  43.1 28.5 all-gather.11
  73.3 28.5 all-gather.9
  103.4 30.3 all-gather.15
  138.8 102.9 all-reduce.12
  243.3 151.1 all-gather.17
  396.1 149.2 all-gather.19
  547.1 150.0 all-gather.21
  935.9 68.0 all-reduce.16
  1020.6 27.0 reduce-scatter.16
  1052.4 34.2 reduce-scatter.8
  1088.9 34.4 reduce-scatter.10
  1126.5 34.2 reduce-scatter.12
  1163.0 34.4 reduce-scatter.14
  1202.0 103.1 all-reduce.14
  1307.5 168.6 reduce-scatter.18
  1478.4 166.4 reduce-scatter.20
  1647.2 166.5 reduce-scatter.22
where the time goes:
time: 1830 us; the launch traced here: 1820 us
  waiting for transfers between devices  1010 us (55%)
  matrix products  366 us (20%)
  local copies, waits for them, and re-layouts  182 us (10%)
  other arithmetic  143 us (8%)
  blocking collectives  106 us (6%)
    reduce_scatter x1, waiting for transfers between devices, shards(): lax.psum_scatter(down_grad.astype(jnp.bfloat16), 'dp', scatter_dimension=...  165 us
    reduce_scatter x1, waiting for transfers between devices, shards(): lax.psum_scatter(up_grad.astype(jnp.bfloat16), 'dp', scatter_dimension=1,...  165 us
    reduce_scatter x1, waiting for transfers between devices, shards(): lax.psum_scatter(gate_grad.astype(jnp.bfloat16), 'dp', scatter_dimension=...  141 us
    all_gather x1, waiting for transfers between devices, shards(): lax.all_gather(w_down, 'dp', axis=2, tiled=True)  137 us
    all_gather x1, waiting for transfers between devices, shards(): lax.all_gather(w_up, 'dp', axis=1, tiled=True)  136 us
    psum x1, waiting for transfers between devices, shards(): lax.psum(moe_part.astype(jnp.bfloat16), 'tensor').astype(jnp.float32)  80.8 us
    all_gather x1, waiting for transfers between devices, shards(): lax.all_gather(w_gate, 'dp', axis=1, tiled=True)  80 us
    gather x2, local copies, waits for them, and re-layouts, shards(): expert_out.reshape(EXPERTS * MOST, width)[dest].reshape(MB_TOK, TOPK, width)  48.4 us
  transfers between devices with their start and end apart: 18, of which 12 were waited for; matrix products, arithmetic and copies ran while one was open for 23% of the time, Pallas kernels for 0%

commit v1 on v0

v1 whole, which is shorter than its diff:
```python
import jax
import jax.numpy as jnp
from jax import lax
from jax.sharding import Mesh
from jax.sharding import PartitionSpec as P

HEAD_DIM = 128
EXPERTS = 16

EPS = 1e-05
THETA = 10000.0
HIGH = lax.Precision.HIGHEST
f32 = jnp.float32
bf16 = jnp.bfloat16


def swap(value, axis, mask):
    if mask == 0:
        return value
    n = lax.axis_size(axis)
    return lax.ppermute(value, axis, [(i, i ^ mask) for i in range(n)])


def tensor_sum(value):
    n = lax.axis_size("tensor")
    parts = [value] + [swap(value, "tensor", k) for k in range(1, n)]
    while len(parts) > 1:
        parts = [parts[i] + parts[i + 1] for i in range(0, len(parts), 2)]
    return parts[0]


def rope_tables(length, head_dim):
    half = head_dim // 2
    freq = THETA ** (-(jnp.arange(half).astype(f32) * 2.0 / head_dim))
    angle = jnp.arange(length).astype(f32)[:, None] * freq[None, :]
    cosine = jnp.concatenate([jnp.cos(angle), jnp.cos(angle)], -1)
    sine = jnp.concatenate([jnp.sin(angle), jnp.sin(angle)], -1)
    return (cosine, sine)


def rotate(value, cosine, sine):
    half = value.shape[-1] // 2
    turned = jnp.concatenate([-value[..., half:], value[..., :half]], -1)
    return value * cosine[:, None, :] + turned * sine[:, None, :]


def unrotate(grad, cosine, sine):
    half = grad.shape[-1] // 2
    scaled = grad * sine[:, None, :]
    back_turn = jnp.concatenate([scaled[..., half:], -scaled[..., :half]], -1)
    return grad * cosine[:, None, :] + back_turn


def columns(value, index, size):
    return lax.dynamic_slice_in_dim(value, index * size, size, 1)


def spread_z(value):
    return jnp.stack([swap(value, "z", k) for k in range(lax.axis_size("z"))])


def gather_quarters(value):
    me, n = lax.axis_index("tensor"), lax.axis_size("tensor")
    rows, width = value.shape
    half = rows // 2
    if n != 4:
        out = jnp.zeros((rows, n * width), value.dtype)
        for k in range(n):
            part = swap(value, "tensor", k)
            out = lax.dynamic_update_slice(out, part, (0, (me ^ k) * width))
        return out
    near = swap(value, "tensor", 1)
    far = swap(value, "tensor", 2)
    cross = jnp.concatenate([swap(near[:half], "tensor", 2), swap(far[half:], "tensor", 1)], 0)
    out = jnp.zeros((rows, 4 * width), value.dtype)
    for k, part in enumerate((value, near, far, cross)):
        out = lax.dynamic_update_slice(out, part, (0, (me ^ k) * width))
    return out


def scatter_quarters(value):
    me, n = lax.axis_index("tensor"), lax.axis_size("tensor")
    rows, width = value.shape[0], value.shape[1] // n
    half = rows // 2
    if n != 4:
        got = [swap(columns(value, me ^ k, width), "tensor", k).astype(f32) for k in range(n)]
        return sum(got[1:], got[0])
    outs = []
    for part, first, second in ((value[:half], 1, 2), (value[half:], 2, 1)):
        pick = lambda k: columns(part, me ^ k, width)
        sent = jnp.stack([pick(first), pick(first ^ second)])
        got = swap(sent, "tensor", first).astype(f32)
        mine = pick(0).astype(f32) + got[0]
        other = (pick(second).astype(f32) + got[1]).astype(bf16)
        outs.append(mine + swap(other, "tensor", second).astype(f32))
    return jnp.concatenate(outs, 0)


def shards(
    tokens,
    cotangent,
    routes,
    wq,
    wk,
    wv,
    wo,
    attn_gain,
    q_gain,
    k_gain,
    moe_gain,
    router,
    w_gate,
    w_up,
    w_down,
):
    nz = lax.axis_size("z")
    me_t = lax.axis_index("tensor")
    me_z = lax.axis_index("z")
    me_c = lax.axis_index("core")
    dp = ("z", "core")
    seq, width = tokens.shape
    quarter = width // lax.axis_size("tensor")
    local = wq.shape[1]
    local_heads = local // HEAD_DIM
    slice_d = wq.shape[0]
    own_e = EXPERTS // nz
    hid = w_gate.shape[2]

    small = jnp.concatenate([attn_gain[:, None], moe_gain[:, None], router], 1)
    pad = -small.shape[1] % 128
    small = jnp.pad(small, ((0, 0), (0, pad)))
    packed = lax.all_gather(jnp.concatenate([wq, wk, wv, small], 1), dp, axis=0, tiled=True)
    wqkv_full = packed[:, : 3 * local]
    a_gain = packed[:, 3 * local].astype(f32)
    m_gain = packed[:, 3 * local + 1].astype(f32)
    router_full = packed[:, 3 * local + 2 : 3 * local + 2 + EXPERTS]
    wo_full = lax.all_gather(wo, dp, axis=1, tiled=True)

    stacked = jnp.stack([w_gate, w_up, w_down.transpose(0, 1, 2)])

    def experts_of(z):
        return lax.dynamic_slice_in_dim(stacked, z * own_e, own_e, 1)

    parts_w = jnp.stack([swap(experts_of(me_z ^ k), "z", k) for k in range(nz)])
    both_w = (parts_w, swap(parts_w, "core", 1))
    gate_full = jnp.zeros((width, own_e, hid), bf16)
    up_full = jnp.zeros((width, own_e, hid), bf16)
    down_full = jnp.zeros((own_e, hid, width), bf16)
    for c in range(2):
        for k in range(nz):
            at = ((me_z ^ k) * 2 + (me_c ^ c)) * slice_d
            piece = both_w[c][k]
            gate_full = lax.dynamic_update_slice(
                gate_full, piece[0].transpose(1, 0, 2), (at, 0, 0)
            )
            up_full = lax.dynamic_update_slice(up_full, piece[1].transpose(1, 0, 2), (at, 0, 0))
            down_full = lax.dynamic_update_slice(down_full, piece[2], (0, 0, at))
    gate_full = gate_full.reshape(width, own_e * hid)
    up_full = up_full.reshape(width, own_e * hid)
    down_full = down_full.reshape(own_e * hid, width)

    cot_all = gather_quarters(
        spread_z(columns(cotangent, me_t, quarter)).reshape(nz * seq, quarter)
    )
    mask = jnp.sum(
        (routes[:, :, None] == jnp.arange(EXPERTS)[None, None, :]).astype(bf16), 1
    )
    mask_all = spread_z(mask.T).transpose(0, 2, 1).reshape(nz * seq, EXPERTS).astype(f32)

    xf = tokens.astype(f32)
    rate_x = lax.rsqrt(jnp.mean(xf * xf, -1, keepdims=True) + EPS)
    gain_q = q_gain.astype(f32)
    gain_k = k_gain.astype(f32)
    a_low = (xf * rate_x * a_gain).astype(bf16)
    qkv = jnp.dot(a_low, wqkv_full, preferred_element_type=f32)
    query, keyed, valued = qkv[:, :local], qkv[:, local : 2 * local], qkv[:, 2 * local :]
    sums = tensor_sum(jnp.stack([jnp.sum(query * query, -1), jnp.sum(keyed * keyed, -1)]))
    rate_q = lax.rsqrt(sums[0] / width + EPS)[:, None]
    rate_k = lax.rsqrt(sums[1] / width + EPS)[:, None]
    cosine, sine = rope_tables(seq, HEAD_DIM)
    heads = (seq, local_heads, HEAD_DIM)
    q_rot = rotate((query * rate_q * gain_q).reshape(heads), cosine, sine).astype(bf16)
    k_rot = rotate((keyed * rate_k * gain_k).reshape(heads), cosine, sine).astype(bf16)
    v_low = valued.reshape(heads).astype(bf16)
    scale = HEAD_DIM ** (-0.5)
    scores = scale * jnp.einsum("qhd,khd->hqk", q_rot, k_rot, preferred_element_type=f32)
    causal = jnp.arange(seq)[:, None] >= jnp.arange(seq)[None, :]
    scores = jnp.where(causal[None], scores, -1e30)
    peak = jnp.max(scores, -1, keepdims=True)
    expd = jnp.exp(scores - peak)
    weights = expd / jnp.sum(expd, -1, keepdims=True)
    weights_low = weights.astype(bf16)
    outputs = jnp.einsum("hqk,khd->qhd", weights_low, v_low, preferred_element_type=f32)
    joined = outputs.reshape(seq, local).astype(bf16)
    attn = jnp.dot(joined, wo_full, preferred_element_type=f32)

    x_own = columns(xf, me_t, quarter)
    resid = x_own + scatter_quarters(attn.astype(bf16))
    rate_r = lax.rsqrt(tensor_sum(jnp.sum(resid * resid, -1)) / width + EPS)[:, None]
    gain_own = lax.dynamic_slice_in_dim(m_gain, me_t * quarter, quarter, 0)
    m_own = (resid * rate_r * gain_own).astype(bf16)

    m_all = gather_quarters(spread_z(m_own).reshape(nz * seq, quarter))
    logits = jnp.dot(m_all, router_full, preferred_element_type=f32)
    probs_all = jax.nn.softmax(logits, axis=-1)
    gates_all = lax.dynamic_slice_in_dim(probs_all * mask_all, me_z * own_e, own_e, 1)
    tall = (nz * seq, own_e, hid)
    wide = (nz * seq, own_e * hid)
    gate_b = jnp.broadcast_to(gates_all[:, :, None], tall).reshape(wide)
    gate_act = jnp.dot(m_all, gate_full, preferred_element_type=f32)
    up_act = jnp.dot(m_all, up_full, preferred_element_type=f32)
    dhid_raw = jnp.einsum("td,fd->tf", cot_all, down_full, preferred_element_type=f32)
    sigma = jax.nn.sigmoid(gate_act)
    silu_gate = gate_act * sigma
    hidden = silu_gate * up_act
    hidden_low = (gate_b * hidden).astype(bf16)
    dgate_part = jnp.sum((hidden * dhid_raw).reshape(tall), -1)
    dhid = gate_b * dhid_raw
    dgate_act = (dhid * up_act * sigma * (1.0 + gate_act * (1.0 - sigma))).astype(bf16)
    dup_act = (dhid * silu_gate).astype(bf16)
    dm_part = (
        jnp.einsum("tf,df->td", dgate_act, gate_full, preferred_element_type=f32)
        + jnp.einsum("tf,df->td", dup_act, up_full, preferred_element_type=f32)
    ).astype(bf16)
    moe_part = jnp.dot(hidden_low, down_full, preferred_element_type=f32).astype(bf16)

    def to_owner(part):
        sums = scatter_quarters(part).astype(bf16).reshape(nz, seq, quarter)
        got = [swap(sums[k], "z", k).astype(f32) for k in range(nz)]
        return sum(got[1:], got[0])

    dm_own = to_owner(dm_part)
    moe_own = to_owner(moe_part)
    mixed = gather_quarters((resid + moe_own).astype(bf16))

    dg = dgate_part.reshape(nz, seq, own_e).transpose(0, 2, 1)
    dgate = jnp.zeros((EXPERTS, seq), f32)
    for k in range(nz):
        dgate = lax.dynamic_update_slice(dgate, swap(dg[k], "z", k), ((me_z ^ k) * own_e, 0))
    dgate = tensor_sum(dgate).T
    probs = probs_all[:seq]
    dprobs = dgate * mask.astype(f32)
    dlogits = probs * (dprobs - jnp.sum(probs * dprobs, -1, keepdims=True))
    router_own = lax.dynamic_slice_in_dim(router_full, me_t * quarter, quarter, 0)
    router_part = jnp.dot(m_own.astype(f32).T, dlogits, precision=HIGH)
    dm_own = dm_own + jnp.dot(dlogits, router_own.astype(f32).T, precision=HIGH)

    gate_grad = jnp.einsum("td,tf->df", m_all, dgate_act, preferred_element_type=f32)
    up_grad = jnp.einsum("td,tf->df", m_all, dup_act, preferred_element_type=f32)
    down_grad = jnp.einsum("tf,td->fd", hidden_low, cot_all, preferred_element_type=f32)
    cut = (nz, 2, slice_d, own_e, hid)
    grads = jnp.stack(
        [
            gate_grad.reshape(cut).transpose(1, 0, 3, 2, 4),
            up_grad.reshape(cut).transpose(1, 0, 3, 2, 4),
            down_grad.reshape(own_e, hid, nz, 2, slice_d).transpose(3, 2, 0, 1, 4),
        ],
        2,
    )
    keep = lax.dynamic_index_in_dim(grads, me_c, 0, keepdims=False)
    give = lax.dynamic_index_in_dim(grads, me_c ^ 1, 0, keepdims=False).astype(bf16)
    summed = (keep + swap(give, "core", 1).astype(f32)).astype(bf16)
    expert_grads = jnp.zeros((3, EXPERTS, slice_d, hid), f32)
    for k in range(nz):
        sent = lax.dynamic_index_in_dim(summed, me_z ^ k, 0, keepdims=False)
        expert_grads = lax.dynamic_update_slice(
            expert_grads, swap(sent, "z", k).astype(f32), (0, (me_z ^ k) * own_e, 0, 0)
        )

    normed = resid * rate_r
    moe_gain_part = jnp.sum(dm_own * normed, 0)
    pulled = dm_own * gain_own
    inner_r = tensor_sum(jnp.sum(pulled * normed, -1))[:, None] / width
    cot_own = columns(cotangent, me_t, quarter).astype(f32)
    dresid = cot_own + rate_r * (pulled - normed * inner_r)
    dresid_low = gather_quarters(dresid.astype(bf16))

    wo_grad = jnp.einsum("sa,sd->ad", joined, dresid_low, preferred_element_type=f32)
    dout = (
        jnp.einsum("sd,ad->sa", dresid_low, wo_full, preferred_element_type=f32)
        .astype(bf16)
        .reshape(heads)
    )
    dweights = jnp.einsum("qhd,khd->hqk", dout, v_low, preferred_element_type=f32)
    dv = jnp.einsum("hqk,qhd->khd", weights_low, dout, preferred_element_type=f32)
    inner = jnp.sum(weights * dweights, -1, keepdims=True)
    dscores = (weights * (dweights - inner)).astype(bf16)
    dq_rot = scale * jnp.einsum("hqk,khd->qhd", dscores, k_rot, preferred_element_type=f32)
    dk_rot = scale * jnp.einsum("hqk,qhd->khd", dscores, q_rot, preferred_element_type=f32)
    dq_norm = unrotate(dq_rot, cosine, sine).reshape(seq, local)
    dk_norm = unrotate(dk_rot, cosine, sine).reshape(seq, local)
    inners = tensor_sum(
        jnp.stack(
            [jnp.sum(dq_norm * gain_q * query, -1), jnp.sum(dk_norm * gain_k * keyed, -1)]
        )
    )
    dq_low = (rate_q * gain_q * dq_norm - query * rate_q**3 * inners[0][:, None] / width).astype(
        bf16
    )
    dk_low = (rate_k * gain_k * dk_norm - keyed * rate_k**3 * inners[1][:, None] / width).astype(
        bf16
    )
    dv_low = dv.reshape(seq, local).astype(bf16)
    q_gain_part = jnp.sum(dq_norm * query * rate_q, 0)
    k_gain_part = jnp.sum(dk_norm * keyed * rate_k, 0)
    dqkv = jnp.concatenate([dq_low, dk_low, dv_low], 1)
    wqkv_grad = jnp.einsum("sd,sa->da", a_low, dqkv, preferred_element_type=f32).astype(bf16)
    da_part = jnp.einsum("sa,da->sd", dqkv, wqkv_full, preferred_element_type=f32)
    da_own = scatter_quarters(da_part.astype(bf16))
    norm_x = x_own * rate_x
    attn_gain_part = jnp.sum(da_own * norm_x, 0)
    pulled_x = da_own * lax.dynamic_slice_in_dim(a_gain, me_t * quarter, quarter, 0)
    inner_x = tensor_sum(jnp.sum(pulled_x * norm_x, -1))[:, None] / width
    tokens_grad = gather_quarters(
        (dresid + rate_x * (pulled_x - norm_x * inner_x)).astype(bf16)
    )

    wqkv_own = lax.psum_scatter(wqkv_grad, dp, scatter_dimension=0, tiled=True).astype(f32)
    wo_own = lax.psum_scatter(wo_grad.astype(bf16), dp, scatter_dimension=1, tiled=True).astype(f32)
    q_gain_grad, k_gain_grad = lax.psum((q_gain_part, k_gain_part), dp)
    smalls = jnp.concatenate([attn_gain_part[None], moe_gain_part[None], router_part.T], 0)
    smalls = lax.all_gather(smalls, "tensor", axis=1, tiled=True)
    smalls = lax.psum_scatter(smalls, dp, scatter_dimension=1, tiled=True)
    return (
        mixed,
        tokens_grad,
        wqkv_own[:, :local],
        wqkv_own[:, local : 2 * local],
        wqkv_own[:, 2 * local :],
        wo_own,
        smalls[0],
        q_gain_grad,
        k_gain_grad,
        smalls[1],
        smalls[2:].T,
        expert_grads[0],
        expert_grads[1],
        expert_grads[2],
    )


def solution(mesh):
    fine = Mesh(
        mesh.devices.reshape(mesh.shape["dp"] // 2, 2, mesh.shape["tensor"]),
        ("z", "core", "tensor"),
    )
    dp = ("z", "core")
    in_specs = (
        P(dp, None),
        P(dp, None),
        P(dp, None),
        P(dp, "tensor"),
        P(dp, "tensor"),
        P(dp, "tensor"),
        P("tensor", dp),
        P(dp),
        P("tensor"),
        P("tensor"),
        P(dp),
        P(dp, None),
        P(None, dp, "tensor"),
        P(None, dp, "tensor"),
        P(None, "tensor", dp),
    )
    out_specs = (
        P(dp, None),
        P(dp, None),
        P(dp, "tensor"),
        P(dp, "tensor"),
        P(dp, "tensor"),
        P("tensor", dp),
        P(dp),
        P("tensor"),
        P("tensor"),
        P(dp),
        P(dp, None),
        P(None, dp, "tensor"),
        P(None, dp, "tensor"),
        P(None, "tensor", dp),
    )
    return jax.shard_map(shards, mesh=fine, in_specs=in_specs, out_specs=out_specs, check_vma=False)
```

time: 1830 us -> 1310 us (0.72)
  the two profiles are of different devices: /device:TPU:0 before, /device:TPU:9 now
where the time goes in v1:
time: 1310 us; the launch traced here: 1300 us
  waiting for transfers between devices  594 us (45%)
  local copies, waits for them, and re-layouts  216 us (16%)
  matrix products  184 us (14%)
  other arithmetic  110 us (8%)
  starting transfers between devices  94.4 us (7%)
  blocking collectives  80.9 us (6%)
  between operations  15.7 us (1%)
    ppermute x80, waiting for transfers between devices, swap(): return lax.ppermute(value, axis, [(i, i ^ mask) for i in range(n)])  594 us
    ppermute x80, starting transfers between devices, swap(): return lax.ppermute(value, axis, [(i, i ^ mask) for i in range(n)])  94.2 us
    psum x1, blocking collectives, shards(): q_gain_grad, k_gain_grad = lax.psum((q_gain_part, k_gain_part), dp)  72.7 us
  transfers between devices with their start and end apart: 85, of which 35 were waited for; matrix products, arithmetic and copies ran while one was open for 29% of the time, Pallas kernels for 0%

profile of v1, /device:TPU:9, one launch (start us, length us, event | category | flops | bytes accessed | tf_op | source)
XLA Modules:
  0.0 1296.1 jit_solution(8872394737627821641)
XLA Ops:
  31.0 112.8 %collective-permute-done.20 = bf16[3,4,256,256]{2,3,1,0:T(8,128)(2,1)S(1)} collective-permute-done((bf16[3,4,256,256]{2,3,1,0:T(8,128)(2,1)S(1)}, bf16[3,4,256,256]{2,3,1,0:T(8,128)(2,1)S(1)}, u32[]{:S(2)}, u32[]{:S(2)}) %collective-permute-start.20) | collective-permute-done | bytes 1572896 | tf_op jit(solution)/shard_map/ppermute | solution.py:21
  146.7 78.1 %collective-permute-done.22 = bf16[3,4,256,256]{2,3,1,0:T(8,128)(2,1)S(1)} collective-permute-done((bf16[3,4,256,256]{2,3,1,0:T(8,128)(2,1)S(1)}, bf16[3,4,256,256]{2,3,1,0:T(8,128)(2,1)S(1)}, u32[]{:S(2)}, u32[]{:S(2)}) %collective-permute-start.22) | collective-permute-done | bytes 1572896 | tf_op jit(solution)/shard_map/ppermute | solution.py:21
  241.2 24.8 %collective-permute-done.37 = bf16[512,512]{1,0:T(8,128)(2,1)} collective-permute-done((bf16[512,512]{1,0:T(8,128)(2,1)}, bf16[512,512]{1,0:T(8,128)(2,1)}, u32[]{:S(2)}, u32[]{:S(2)}) %collective-permute-start.37) | collective-permute-done | bytes 524320 | tf_op jit(solution)/shard_map/ppermute | solution.py:21
  266.1 15.6 %collective-permute-done.36 = bf16[512,512]{1,0:T(8,128)(2,1)} collective-permute-done((bf16[512,512]{1,0:T(8,128)(2,1)}, bf16[512,512]{1,0:T(8,128)(2,1)}, u32[]{:S(2)}, u32[]{:S(2)}) %collective-permute-start.36) | collective-permute-done | bytes 524320 | tf_op jit(solution)/shard_map/ppermute | solution.py:21
  327.1 5.2 collective-permute-done.39
  344.9 11.4 collective-permute-done.41
  370.3 6.5 fusion.7
  438.8 22.7 %collective-permute-done.12 = bf16[512,512]{1,0:T(8,128)(2,1)S(1)} collective-permute-done((bf16[512,512]{1,0:T(8,128)(2,1)S(1)}, bf16[512,512]{1,0:T(8,128)(2,1)S(1)}, u32[]{:S(2)}, u32[]{:S(2)}) %collective-permute-start.12) | collective-permute-done | bytes 524320 | tf_op jit(solution)/shard_map/ppermute | solution.py:21
  461.5 12.7 collective-permute-done.11
  475.3 14.9 %fusion.121 = f32[2048,1024]{0,1:T(8,128)} fusion(bf16[2048,2048]{1,0:T(8,128)(2,1)} %maximum_dynamic-update-slice_fusion.1, bf16[1024,2048]{1,0:T(8,128)(2,1)} %bitcast.75), kind=kOutput, calls=%fused_computation.334 | convolution fusion | flops 8589934592 | bytes 20971520 | tf_op jit(solution)/shard_map/td,fd->tf/dot_general | solution.py:212
  490.1 27.2 %collective-permute-done.14 = bf16[2048,512]{1,0:T(8,128)(2,1)S(1)} collective-permute-done((bf16[2048,512]{1,0:T(8,128)(2,1)S(1)}, bf16[2048,512]{1,0:T(8,128)(2,1)S(1)}, u32[]{:S(2)}, u32[]{:S(2)}) %collective-permute-start.14) | collective-permute-done | bytes 2097184 | tf_op jit(solution)/shard_map/ppermute | solution.py:21
  523.9 15.4 %collective-permute-done.16 = bf16[1024,512]{1,0:T(8,128)(2,1)S(1)} collective-permute-done((bf16[1024,512]{1,0:T(8,128)(2,1)S(1)}, bf16[1024,512]{1,0:T(8,128)(2,1)S(1)}, u32[]{:S(2)}, u32[]{:S(2)}) %collective-permute-start.16) | collective-permute-done | bytes 1048608 | tf_op jit(solution)/shard_map/ppermute | solution.py:21
  539.7 14.4 %fusion.120 = f32[2048,1024]{0,1:T(8,128)} fusion(bf16[2048,2048]{1,0:T(8,128)(2,1)S(1)} %maximum_dynamic-update-slice_fusion, bf16[2048,1024]{0,1:T(8,128)(2,1)} %bitcast.66), kind=kOutput, calls=%fused_computation.333 | convolution fusion | flops 8589934592 | bytes 20971520 | tf_op jit(solution)/shard_map/dot_general | solution.py:211
  557.6 25.1 %multiply_convert_fusion.1 = (bf16[2048,1024]{0,1:T(8,128)(2,1)}, bf16[2048,1024]{0,1:T(8,128)(2,1)}, bf16[2048,1024]{0,1:T(8,128)(2,1)}, f32[2048,1024]{0,1:T(8,128)}) fusion(f32[2048,1024]{0,1:T(8,128)} %fusion.120, f32[2048,1024]{0,1:T(8,128)} %fusion.121, f32[2048,4]{0,1:T(4,128)S(1)} %dynamic-slice_multiply_fusion.1, bf16[2048,2048]{1,0:T(8,128)(2,1)} %copy-done, ...), kind=kOutput, calls=%fused_computation.14 | convolution fusion | flops 8625586176 | bytes 50364416 | tf_op jit(solution)/shard_map/dot_general | solution.py:210
  582.8 15.3 %fusion.122 = f32[2048,2048]{1,0:T(8,128)} fusion(bf16[2048,1024]{0,1:T(8,128)(2,1)} %get-tuple-element.39, bf16[2048,1024]{0,1:T(8,128)(2,1)} %bitcast.66), kind=kOutput, calls=%fused_computation.335 | convolution fusion | flops 8589934592 | bytes 25165824 | tf_op jit(solution)/shard_map/tf,df->td/dot_general | solution.py:223
  598.1 16.0 %add_convert_fusion = bf16[2048,2048]{1,0:T(8,128)(2,1)} fusion(f32[2048,2048]{1,0:T(8,128)} %fusion.122, bf16[2048,1024]{0,1:T(8,128)(2,1)S(1)} %copy-done.22, bf16[2048,1024]{0,1:T(8,128)(2,1)} %bitcast.49), kind=kOutput, calls=%fused_computation.2 | convolution fusion | flops 8598323200 | bytes 33554432 | tf_op jit(solution)/shard_map/tf,df->td/dot_general | solution.py:222
  621.1 38.9 %collective-permute-done.45 = bf16[2,1024,512]{2,1,0:T(8,128)(2,1)S(1)} collective-permute-done((bf16[2,1024,512]{2,1,0:T(8,128)(2,1)S(1)}, bf16[2,1024,512]{2,1,0:T(8,128)(2,1)S(1)}, u32[]{:S(2)}, u32[]{:S(2)}) %collective-permute-start.45) | collective-permute-done | bytes 2097184 | tf_op jit(solution)/shard_map/ppermute | solution.py:21
  666.4 5.7 bitcast_reduce_fusion
  672.1 5.6 collective-permute-start.49
  678.9 5.9 collective-permute-done.46
  701.7 18.8 %collective-permute-done.48 = bf16[512,512]{1,0:T(8,128)(2,1)S(1)} collective-permute-done((bf16[512,512]{1,0:T(8,128)(2,1)S(1)}, bf16[512,512]{1,0:T(8,128)(2,1)S(1)}, u32[]{:S(2)}, u32[]{:S(2)}) %collective-permute-start.48) | collective-permute-done | bytes 524320 | tf_op jit(solution)/shard_map/ppermute | solution.py:21
  720.5 11.4 collective-permute-done.47
  745.2 8.4 collective-permute-done.59
  788.5 6.6 fusion.10
  797.3 11.2 fusion.124
  816.1 8.2 all_gather.11
  828.6 14.6 %fusion.125 = f32[1024,2048]{1,0:T(8,128)} fusion(bf16[2048,1024]{0,1:T(8,128)(2,1)} %get-tuple-element.40, bf16[2048,2048]{1,0:T(8,128)(2,1)} %maximum_dynamic-update-slice_fusion.1), kind=kOutput, calls=%fused_computation.338 | convolution fusion | flops 8589934592 | bytes 20971520 | tf_op jit(solution)/shard_map/tf,td->fd/dot_general | solution.py:250
  843.2 11.8 reshape.244
  855.0 9.4 copy.176
  864.4 10.6 reshape.243
  874.9 8.4 copy.177
  883.4 13.9 %fusion.123 = f32[2048,1024]{1,0:T(8,128)} fusion(bf16[2048,2048]{1,0:T(8,128)(2,1)} %copy-done, bf16[2048,1024]{0,1:T(8,128)(2,1)S(1)} %copy-done.23), kind=kOutput, calls=%fused_computation.336 | convolution fusion | flops 8589934592 | bytes 20971520 | tf_op jit(solution)/shard_map/td,tf->df/dot_general | solution.py:248
  897.2 10.5 reshape.242
  912.6 15.6 %pad_maximum_fusion = f32[2,4,3,4,256,256]{5,4,3,2,1,0:T(8,128)} fusion(f32[2,4,1,4,256,256]{5,4,3,2,1,0:T(8,128)} %bitcast.428, f32[2,4,1,4,256,256]{5,4,3,2,1,0:T(8,128)} %bitcast.429, f32[2,4,1,4,256,256]{5,4,3,2,1,0:T(8,128)S(1)} %bitcast.430), kind=kLoop, calls=%fused_computation.1 | loop fusion | flops 12582912 | bytes 50331648 | tf_op jit(solution)/shard_map/stack | solution.py:252
  928.2 8.2 fusion.4
  936.5 10.7 collective-permute-start.76
  947.2 5.5 convolution_convert_fusion
  952.8 12.2 convolution_convert_fusion.1
  968.7 45.4 %collective-permute-done.27 = bf16[2,1024,512]{2,1,0:T(8,128)(2,1)S(1)} collective-permute-done((bf16[2,1024,512]{2,1,0:T(8,128)(2,1)S(1)}, bf16[2,1024,512]{2,1,0:T(8,128)(2,1)S(1)}, u32[]{:S(2)}, u32[]{:S(2)}) %collective-permute-start.27) | collective-permute-done | bytes 2097184 | tf_op jit(solution)/shard_map/ppermute | solution.py:21
  1017.8 21.3 %collective-permute-done.28 = bf16[1024,512]{1,0:T(8,128)(2,1)S(1)} collective-permute-done((bf16[1024,512]{1,0:T(8,128)(2,1)S(1)}, bf16[1024,512]{1,0:T(8,128)(2,1)S(1)}, u32[]{:S(2)}, u32[]{:S(2)}) %collective-permute-start.28) | collective-permute-done | bytes 1048608 | tf_op jit(solution)/shard_map/ppermute | solution.py:21
  1045.0 29.2 %collective-permute-done.30 = bf16[512,512]{1,0:T(8,128)(2,1)S(1)} collective-permute-done((bf16[512,512]{1,0:T(8,128)(2,1)S(1)}, bf16[512,512]{1,0:T(8,128)(2,1)S(1)}, u32[]{:S(2)}, u32[]{:S(2)}) %collective-permute-start.30) | collective-permute-done | bytes 524320 | tf_op jit(solution)/shard_map/ppermute | solution.py:21
  1074.2 9.3 collective-permute-done.29
  1089.5 8.4 collective-permute-done.32
  1100.7 11.2 fusion.1
  1129.2 72.7 %all-reduce.1 = (f32[512]{0:T(512)}, f32[512]{0:T(512)}) all-reduce(f32[512]{0:T(512)S(1)} %copy-done.66, f32[512]{0:T(512)S(1)} %copy-done.65), channel_id=1, replica_groups=mesh['z'=4,'core'=2,'tensor'=4] {'z','core'}, use_global_device_ids=true, to_apply=%region_22.23 | all-reduce | flops 1024 | bytes 8192 | tf_op jit(solution)/shard_map/psum | solution.py:320
  1211.9 6.1 broadcast_in_dim.37
  1228.1 44.0 %collective-permute-done.79 = bf16[3,4,256,256]{3,2,1,0:T(8,128)(2,1)} collective-permute-done((bf16[3,4,256,256]{3,2,1,0:T(8,128)(2,1)}, bf16[3,4,256,256]{3,2,1,0:T(8,128)(2,1)}, u32[]{:S(2)}, u32[]{:S(2)}) %collective-permute-start.79) | collective-permute-done | bytes 1572896 | tf_op jit(solution)/shard_map/ppermute | solution.py:21
  1275.5 9.7 slice_bitcast_fusion
  (523 shorter events, 352.8 us)
Async XLA Ops:
  7.2 361.8 %all-gather.3.cloned.1.call-start = ((), (), s32[]{:S(2)}) async-start(), calls=%async_computation.3 | async-start | bytes 7667712 | tf_op jit(solution)/shard_map/all_gather | solution.py:132
  11.5 392.2 %all-gather.5.cloned.1.call-start = ((), (), s32[]{:S(2)}) async-start(), calls=%async_computation.4 | async-start | bytes 2359296 | tf_op jit(solution)/shard_map/all_gather | solution.py:137
  28.4 115.5 %collective-permute-start.20 = (bf16[3,4,256,256]{2,3,1,0:T(8,128)(2,1)S(1)}, bf16[3,4,256,256]{2,3,1,0:T(8,128)(2,1)S(1)}, u32[]{:S(2)}, u32[]{:S(2)}) collective-permute-start(bf16[3,4,256,256]{2,3,1,0:T(8,128)(2,1)S(1)} %get-tuple-element.66), channel_id=1, source_target_pairs={{0,8},{8,0},{16,24},{24,16},{1,9},{9,1},{17,25},{25,17},{2,10},{10... | collective-permute-start | bytes 4718600 | tf_op jit(solution)/shard_map/ppermute | solution.py:21
  28.4 118.3 %collective-permute-start.21 = (bf16[3,4,256,256]{2,3,1,0:T(8,128)(2,1)S(1)}, bf16[3,4,256,256]{2,3,1,0:T(8,128)(2,1)S(1)}, u32[]{:S(2)}, u32[]{:S(2)}) collective-permute-start(bf16[3,4,256,256]{2,3,1,0:T(8,128)(2,1)S(1)} %get-tuple-element.65), channel_id=1, source_target_pairs={{0,16},{8,24},{16,0},{24,8},{1,17},{9,25},{17,1},{25,9},{2,18},{10... | collective-permute-start | bytes 4718600 | tf_op jit(solution)/shard_map/ppermute | solution.py:21
  30.8 194.0 %collective-permute-start.22 = (bf16[3,4,256,256]{2,3,1,0:T(8,128)(2,1)S(1)}, bf16[3,4,256,256]{2,3,1,0:T(8,128)(2,1)S(1)}, u32[]{:S(2)}, u32[]{:S(2)}) collective-permute-start(bf16[3,4,256,256]{2,3,1,0:T(8,128)(2,1)S(1)} %get-tuple-element.64), channel_id=1, source_target_pairs={{0,24},{8,16},{16,8},{24,0},{1,25},{9,17},{17,9},{25,1},{2,26},{10... | collective-permute-start | bytes 4718600 | tf_op jit(solution)/shard_map/ppermute | solution.py:21
  228.2 131.1 %collective-permute-start.23 = (bf16[4,3,4,256,256]{3,4,2,1,0:T(8,128)(2,1)}, bf16[4,3,4,256,256]{3,4,2,1,0:T(8,128)(2,1)}, u32[]{:S(2)}, u32[]{:S(2)}) collective-permute-start(bf16[4,3,4,256,256]{3,4,2,1,0:T(8,128)(2,1)} %pad_maximum_fusion.2), channel_id=1, source_target_pairs={{0,4},{4,0},{1,5},{5,1},{2,6},{6,2},{3,7},{7,3},{8,12},{12,8},{9,1... | collective-permute-start | bytes 18874376 | tf_op jit(solution)/shard_map/ppermute | solution.py:21
  229.8 36.2 %collective-permute-start.37 = (bf16[512,512]{1,0:T(8,128)(2,1)}, bf16[512,512]{1,0:T(8,128)(2,1)}, u32[]{:S(2)}, u32[]{:S(2)}) collective-permute-start(bf16[512,512]{1,0:T(8,128)(2,1)} %constant_dynamic-slice_fusion), channel_id=1, source_target_pairs={{0,24},{8,16},{16,8},{24,0},{1,25},{9,17},{17,9},{25,1},{2,26},{10... | collective-permute-start | bytes 1572872 | tf_op jit(solution)/shard_map/ppermute | solution.py:21
  229.8 51.9 %collective-permute-start.36 = (bf16[512,512]{1,0:T(8,128)(2,1)}, bf16[512,512]{1,0:T(8,128)(2,1)}, u32[]{:S(2)}, u32[]{:S(2)}) collective-permute-start(bf16[512,512]{1,0:T(8,128)(2,1)} %constant_dynamic-slice_fusion), channel_id=1, source_target_pairs={{0,16},{8,24},{16,0},{24,8},{1,17},{9,25},{17,1},{25,9},{2,18},{10... | collective-permute-start | bytes 1572872 | tf_op jit(solution)/shard_map/ppermute | solution.py:21
  229.8 51.9 %collective-permute-start.35 = (bf16[512,512]{1,0:T(8,128)(2,1)}, bf16[512,512]{1,0:T(8,128)(2,1)}, u32[]{:S(2)}, u32[]{:S(2)}) collective-permute-start(bf16[512,512]{1,0:T(8,128)(2,1)} %constant_dynamic-slice_fusion), channel_id=1, source_target_pairs={{0,8},{8,0},{16,24},{24,16},{1,9},{9,1},{17,25},{25,17},{2,10},{10... | collective-permute-start | bytes 1572872 | tf_op jit(solution)/shard_map/ppermute | solution.py:21
  232.5 62.6 %collective-permute-start.19 = (bf16[16,512]{1,0:T(8,128)(2,1)S(1)}, bf16[16,512]{1,0:T(8,128)(2,1)S(1)}, u32[]{:S(2)}, u32[]{:S(2)}) collective-permute-start(bf16[16,512]{1,0:T(8,128)(2,1)S(1)} %bitcast.451), channel_id=1, source_target_pairs={{0,24},{8,16},{16,8},{24,0},{1,25},{9,17},{17,9},{25,1},{2,26},{10... | collective-permute-start | bytes 49160 | tf_op jit(solution)/shard_map/ppermute | solution.py:21
  232.6 969.2 %reduce-scatter.8.cloned.1.call-start = ((), (), s32[]{:S(2)}) async-start(), calls=%async_computation.7 | async-start | bytes 221184 | tf_op jit(solution)/shard_map/reduce_scatter | solution.py:323
  266.1 35.7 %collective-permute-start.18 = (bf16[16,512]{1,0:T(8,128)(2,1)S(1)}, bf16[16,512]{1,0:T(8,128)(2,1)S(1)}, u32[]{:S(2)}, u32[]{:S(2)}) collective-permute-start(bf16[16,512]{1,0:T(8,128)(2,1)S(1)} %bitcast.452), channel_id=1, source_target_pairs={{0,16},{8,24},{16,0},{24,8},{1,17},{9,25},{17,1},{25,9},{2,18},{10... | collective-permute-start | bytes 49160 | tf_op jit(solution)/shard_map/ppermute | solution.py:21
  284.8 49.2 %collective-permute-start.38 = (bf16[2048,512]{1,0:T(8,128)(2,1)}, bf16[2048,512]{1,0:T(8,128)(2,1)}, u32[]{:S(2)}, u32[]{:S(2)}) collective-permute-start(bf16[2048,512]{1,0:T(8,128)(2,1)} %bitcast.88), channel_id=1, source_target_pairs={{0,1},{1,0},{2,3},{3,2},{4,5},{5,4},{6,7},{7,6},{8,9},{9,8},{10,11... | collective-permute-start | bytes 6291464 | tf_op jit(solution)/shard_map/ppermute | solution.py:21
  286.0 46.3 %collective-permute-start.39 = (bf16[2048,512]{1,0:T(8,128)(2,1)}, bf16[2048,512]{1,0:T(8,128)(2,1)}, u32[]{:S(2)}, u32[]{:S(2)}) collective-permute-start(bf16[2048,512]{1,0:T(8,128)(2,1)} %bitcast.88), channel_id=1, source_target_pairs={{0,2},{1,3},{2,0},{3,1},{4,6},{5,7},{6,4},{7,5},{8,10},{9,11},{10,... | collective-permute-start | bytes 6291464 | tf_op jit(solution)/shard_map/ppermute | solution.py:21
  333.6 22.7 %collective-permute-start.41 = (bf16[1024,512]{1,0:T(8,128)(2,1)S(1)}, bf16[1024,512]{1,0:T(8,128)(2,1)S(1)}, u32[]{:S(2)}, u32[]{:S(2)}) collective-permute-start(bf16[1024,512]{1,0:T(8,128)(2,1)S(1)} %slice.496), channel_id=1, source_target_pairs={{0,1},{1,0},{2,3},{3,2},{4,5},{5,4},{6,7},{7,6},{8,9},{9,8},{10,11... | collective-permute-start | bytes 3145736 | tf_op jit(solution)/shard_map/ppermute | solution.py:21
  335.3 22.4 %collective-permute-start.40 = (bf16[1024,512]{1,0:T(8,128)(2,1)S(1)}, bf16[1024,512]{1,0:T(8,128)(2,1)S(1)}, u32[]{:S(2)}, u32[]{:S(2)}) collective-permute-start(bf16[1024,512]{1,0:T(8,128)(2,1)S(1)} %slice.495), channel_id=1, source_target_pairs={{0,2},{1,3},{2,0},{3,1},{4,6},{5,7},{6,4},{7,5},{8,10},{9,11},{10,... | collective-permute-start | bytes 3145736 | tf_op jit(solution)/shard_map/ppermute | solution.py:21
  432.1 29.4 %collective-permute-start.12 = (bf16[512,512]{1,0:T(8,128)(2,1)S(1)}, bf16[512,512]{1,0:T(8,128)(2,1)S(1)}, u32[]{:S(2)}, u32[]{:S(2)}) collective-permute-start(bf16[512,512]{1,0:T(8,128)(2,1)S(1)} %multiply_convert_fusion.4), channel_id=1, source_target_pairs={{0,24},{8,16},{16,8},{24,0},{1,25},{9,17},{17,9},{25,1},{2,26},{10... | collective-permute-start | bytes 1572872 | tf_op jit(solution)/shard_map/ppermute | solution.py:21
  432.5 41.7 %collective-permute-start.11 = (bf16[512,512]{1,0:T(8,128)(2,1)S(1)}, bf16[512,512]{1,0:T(8,128)(2,1)S(1)}, u32[]{:S(2)}, u32[]{:S(2)}) collective-permute-start(bf16[512,512]{1,0:T(8,128)(2,1)S(1)} %multiply_convert_fusion.4), channel_id=1, source_target_pairs={{0,16},{8,24},{16,0},{24,8},{1,17},{9,25},{17,1},{25,9},{2,18},{10... | collective-permute-start | bytes 1572872 | tf_op jit(solution)/shard_map/ppermute | solution.py:21
  436.4 37.8 %collective-permute-start.10 = (bf16[512,512]{1,0:T(8,128)(2,1)S(1)}, bf16[512,512]{1,0:T(8,128)(2,1)S(1)}, u32[]{:S(2)}, u32[]{:S(2)}) collective-permute-start(bf16[512,512]{1,0:T(8,128)(2,1)S(1)} %multiply_convert_fusion.4), channel_id=1, source_target_pairs={{0,8},{8,0},{16,24},{24,16},{1,9},{9,1},{17,25},{25,17},{2,10},{10... | collective-permute-start | bytes 1572872 | tf_op jit(solution)/shard_map/ppermute | solution.py:21
  474.5 44.3 %collective-permute-start.13 = (bf16[2048,512]{1,0:T(8,128)(2,1)S(1)}, bf16[2048,512]{1,0:T(8,128)(2,1)S(1)}, u32[]{:S(2)}, u32[]{:S(2)}) collective-permute-start(bf16[2048,512]{1,0:T(8,128)(2,1)S(1)} %bitcast.435), channel_id=1, source_target_pairs={{0,1},{1,0},{2,3},{3,2},{4,5},{5,4},{6,7},{7,6},{8,9},{9,8},{10,11... | collective-permute-start | bytes 6291464 | tf_op jit(solution)/shard_map/ppermute | solution.py:21
  474.5 42.8 %collective-permute-start.14 = (bf16[2048,512]{1,0:T(8,128)(2,1)S(1)}, bf16[2048,512]{1,0:T(8,128)(2,1)S(1)}, u32[]{:S(2)}, u32[]{:S(2)}) collective-permute-start(bf16[2048,512]{1,0:T(8,128)(2,1)S(1)} %bitcast.436), channel_id=1, source_target_pairs={{0,2},{1,3},{2,0},{3,1},{4,6},{5,7},{6,4},{7,5},{8,10},{9,11},{10,... | collective-permute-start | bytes 6291464 | tf_op jit(solution)/shard_map/ppermute | solution.py:21
  517.4 22.0 %collective-permute-start.16 = (bf16[1024,512]{1,0:T(8,128)(2,1)S(1)}, bf16[1024,512]{1,0:T(8,128)(2,1)S(1)}, u32[]{:S(2)}, u32[]{:S(2)}) collective-permute-start(bf16[1024,512]{1,0:T(8,128)(2,1)S(1)} %slice.460), channel_id=1, source_target_pairs={{0,1},{1,0},{2,3},{3,2},{4,5},{5,4},{6,7},{7,6},{8,9},{9,8},{10,11... | collective-permute-start | bytes 3145736 | tf_op jit(solution)/shard_map/ppermute | solution.py:21
  518.9 20.5 %collective-permute-start.15 = (bf16[1024,512]{1,0:T(8,128)(2,1)S(1)}, bf16[1024,512]{1,0:T(8,128)(2,1)S(1)}, u32[]{:S(2)}, u32[]{:S(2)}) collective-permute-start(bf16[1024,512]{1,0:T(8,128)(2,1)S(1)} %slice.459), channel_id=1, source_target_pairs={{0,2},{1,3},{2,0},{3,1},{4,6},{5,7},{6,4},{7,5},{8,10},{9,11},{10,... | collective-permute-start | bytes 3145736 | tf_op jit(solution)/shard_map/ppermute | solution.py:21
  618.6 41.4 %collective-permute-start.45 = (bf16[2,1024,512]{2,1,0:T(8,128)(2,1)S(1)}, bf16[2,1024,512]{2,1,0:T(8,128)(2,1)S(1)}, u32[]{:S(2)}, u32[]{:S(2)}) collective-permute-start(bf16[2,1024,512]{2,1,0:T(8,128)(2,1)S(1)} %pad_maximum_fusion.8), channel_id=1, source_target_pairs={{0,2},{1,3},{2,0},{3,1},{4,6},{5,7},{6,4},{7,5},{8,10},{9,11},{10,... | collective-permute-start | bytes 6291464 | tf_op jit(solution)/shard_map/ppermute | solution.py:21
  620.0 43.9 %collective-permute-start.42 = (bf16[2,1024,512]{2,1,0:T(8,128)(2,1)S(1)}, bf16[2,1024,512]{2,1,0:T(8,128)(2,1)S(1)}, u32[]{:S(2)}, u32[]{:S(2)}) collective-permute-start(bf16[2,1024,512]{2,1,0:T(8,128)(2,1)S(1)} %pad_maximum_fusion.7), channel_id=1, source_target_pairs={{0,1},{1,0},{2,3},{3,2},{4,5},{5,4},{6,7},{7,6},{8,9},{9,8},{10,11... | collective-permute-start | bytes 6291464 | tf_op jit(solution)/shard_map/ppermute | solution.py:21
  663.2 21.6 %collective-permute-start.46 = (bf16[1024,512]{1,0:T(8,128)(2,1)S(1)}, bf16[1024,512]{1,0:T(8,128)(2,1)}, u32[]{:S(2)}, u32[]{:S(2)}) collective-permute-start(bf16[1024,512]{1,0:T(8,128)(2,1)S(1)} %fusion.14), channel_id=1, source_target_pairs={{0,1},{1,0},{2,3},{3,2},{4,5},{5,4},{6,7},{7,6},{8,9},{9,8},{10,11... | collective-permute-start | bytes 3145736 | tf_op jit(solution)/shard_map/ppermute | solution.py:21
  664.9 24.2 %collective-permute-start.43 = (bf16[1024,512]{1,0:T(8,128)(2,1)S(1)}, bf16[1024,512]{1,0:T(8,128)(2,1)}, u32[]{:S(2)}, u32[]{:S(2)}) collective-permute-start(bf16[1024,512]{1,0:T(8,128)(2,1)S(1)} %fusion.19), channel_id=1, source_target_pairs={{0,2},{1,3},{2,0},{3,1},{4,6},{5,7},{6,4},{7,5},{8,10},{9,11},{10,... | collective-permute-start | bytes 3145736 | tf_op jit(solution)/shard_map/ppermute | solution.py:21
  672.1 23.1 %collective-permute-start.49 = (f32[4,512]{1,0:T(4,128)S(1)}, f32[4,512]{1,0:T(4,128)S(1)}, u32[]{:S(2)}, u32[]{:S(2)}) collective-permute-start(f32[4,512]{1,0:T(4,128)S(1)} %get-tuple-element.124), channel_id=1, source_target_pairs={{0,8},{8,0},{16,24},{24,16},{1,9},{9,1},{17,25},{25,17},{2,10},{10... | collective-permute-start | bytes 24584 | tf_op jit(solution)/shard_map/ppermute | solution.py:21
  687.5 33.0 %collective-permute-start.48 = (bf16[512,512]{1,0:T(8,128)(2,1)S(1)}, bf16[512,512]{1,0:T(8,128)(2,1)S(1)}, u32[]{:S(2)}, u32[]{:S(2)}) collective-permute-start(bf16[512,512]{1,0:T(8,128)(2,1)S(1)} %get-tuple-element.98), channel_id=1, source_target_pairs={{0,24},{8,16},{16,8},{24,0},{1,25},{9,17},{17,9},{25,1},{2,26},{10... | collective-permute-start | bytes 1572872 | tf_op jit(solution)/shard_map/ppermute | solution.py:21
  689.1 42.8 %collective-permute-start.47 = (bf16[512,512]{1,0:T(8,128)(2,1)S(1)}, bf16[512,512]{1,0:T(8,128)(2,1)S(1)}, u32[]{:S(2)}, u32[]{:S(2)}) collective-permute-start(bf16[512,512]{1,0:T(8,128)(2,1)S(1)} %get-tuple-element.97), channel_id=1, source_target_pairs={{0,16},{8,24},{16,0},{24,8},{1,17},{9,25},{17,1},{25,9},{2,18},{10... | collective-permute-start | bytes 1572872 | tf_op jit(solution)/shard_map/ppermute | solution.py:21
  695.1 36.8 %collective-permute-start.44 = (bf16[512,512]{1,0:T(8,128)(2,1)S(1)}, bf16[512,512]{1,0:T(8,128)(2,1)S(1)}, u32[]{:S(2)}, u32[]{:S(2)}) collective-permute-start(bf16[512,512]{1,0:T(8,128)(2,1)S(1)} %slice.501), channel_id=1, source_target_pairs={{0,8},{8,0},{16,24},{24,16},{1,9},{9,1},{17,25},{25,17},{2,10},{10... | collective-permute-start | bytes 1572872 | tf_op jit(solution)/shard_map/ppermute | solution.py:21
  824.3 460.9 %reduce-scatter.6.cloned.1.call-start = ((), (), s32[]{:S(2)}) async-start(), calls=%async_computation.6 | async-start | bytes 2359296 | tf_op jit(solution)/shard_map/reduce_scatter | solution.py:319
  828.6 458.4 %reduce-scatter.4.cloned.1.call-start = ((), (), s32[]{:S(2)}) async-start(), calls=%async_computation.5 | async-start | bytes 7077888 | tf_op jit(solution)/shard_map/reduce_scatter | solution.py:318
  936.5 164.3 %collective-permute-start.76 = (bf16[4,3,4,256,256]{4,3,2,1,0:T(8,128)(2,1)}, bf16[4,3,4,256,256]{4,3,2,1,0:T(8,128)(2,1)}, u32[]{:S(2)}, u32[]{:S(2)}) collective-permute-start(bf16[4,3,4,256,256]{4,3,2,1,0:T(8,128)(2,1)} %fusion.4), channel_id=1, source_target_pairs={{0,4},{4,0},{1,5},{5,1},{2,6},{6,2},{3,7},{7,3},{8,12},{12,8},{9,1... | collective-permute-start | bytes 18874376 | tf_op jit(solution)/shard_map/ppermute | solution.py:21
  966.6 47.4 %collective-permute-start.27 = (bf16[2,1024,512]{2,1,0:T(8,128)(2,1)S(1)}, bf16[2,1024,512]{2,1,0:T(8,128)(2,1)S(1)}, u32[]{:S(2)}, u32[]{:S(2)}) collective-permute-start(bf16[2,1024,512]{2,1,0:T(8,128)(2,1)S(1)} %pad_maximum_fusion.5), channel_id=1, source_target_pairs={{0,2},{1,3},{2,0},{3,1},{4,6},{5,7},{6,4},{7,5},{8,10},{9,11},{10,... | collective-permute-start | bytes 6291464 | tf_op jit(solution)/shard_map/ppermute | solution.py:21
  967.4 48.1 %collective-permute-start.24 = (bf16[2,1024,512]{2,1,0:T(8,128)(2,1)S(1)}, bf16[2,1024,512]{2,1,0:T(8,128)(2,1)S(1)}, u32[]{:S(2)}, u32[]{:S(2)}) collective-permute-start(bf16[2,1024,512]{2,1,0:T(8,128)(2,1)S(1)} %pad_maximum_fusion.4), channel_id=1, source_target_pairs={{0,1},{1,0},{2,3},{3,2},{4,5},{5,4},{6,7},{7,6},{8,9},{9,8},{10,11... | collective-permute-start | bytes 6291464 | tf_op jit(solution)/shard_map/ppermute | solution.py:21
  1015.1 24.1 %collective-permute-start.28 = (bf16[1024,512]{1,0:T(8,128)(2,1)S(1)}, bf16[1024,512]{1,0:T(8,128)(2,1)S(1)}, u32[]{:S(2)}, u32[]{:S(2)}) collective-permute-start(bf16[1024,512]{1,0:T(8,128)(2,1)S(1)} %fusion.24), channel_id=1, source_target_pairs={{0,1},{1,0},{2,3},{3,2},{4,5},{5,4},{6,7},{7,6},{8,9},{9,8},{10,11... | collective-permute-start | bytes 3145736 | tf_op jit(solution)/shard_map/ppermute | solution.py:21
  1016.6 26.8 %collective-permute-start.25 = (bf16[1024,512]{1,0:T(8,128)(2,1)S(1)}, bf16[1024,512]{1,0:T(8,128)(2,1)S(1)}, u32[]{:S(2)}, u32[]{:S(2)}) collective-permute-start(bf16[1024,512]{1,0:T(8,128)(2,1)S(1)} %fusion.29), channel_id=1, source_target_pairs={{0,2},{1,3},{2,0},{3,1},{4,6},{5,7},{6,4},{7,5},{8,10},{9,11},{10,... | collective-permute-start | bytes 3145736 | tf_op jit(solution)/shard_map/ppermute | solution.py:21
  1039.9 34.4 %collective-permute-start.30 = (bf16[512,512]{1,0:T(8,128)(2,1)S(1)}, bf16[512,512]{1,0:T(8,128)(2,1)S(1)}, u32[]{:S(2)}, u32[]{:S(2)}) collective-permute-start(bf16[512,512]{1,0:T(8,128)(2,1)S(1)} %get-tuple-element.100), channel_id=1, source_target_pairs={{0,24},{8,16},{16,8},{24,0},{1,25},{9,17},{17,9},{25,1},{2,26},{10... | collective-permute-start | bytes 1572872 | tf_op jit(solution)/shard_map/ppermute | solution.py:21
  1040.0 43.6 %collective-permute-start.29 = (bf16[512,512]{1,0:T(8,128)(2,1)S(1)}, bf16[512,512]{1,0:T(8,128)(2,1)S(1)}, u32[]{:S(2)}, u32[]{:S(2)}) collective-permute-start(bf16[512,512]{1,0:T(8,128)(2,1)S(1)} %get-tuple-element.99), channel_id=1, source_target_pairs={{0,16},{8,24},{16,0},{24,8},{1,17},{9,25},{17,1},{25,9},{2,18},{10... | collective-permute-start | bytes 1572872 | tf_op jit(solution)/shard_map/ppermute | solution.py:21
  1044.1 39.4 %collective-permute-start.26 = (bf16[512,512]{1,0:T(8,128)(2,1)S(1)}, bf16[512,512]{1,0:T(8,128)(2,1)S(1)}, u32[]{:S(2)}, u32[]{:S(2)}) collective-permute-start(bf16[512,512]{1,0:T(8,128)(2,1)S(1)} %slice.487), channel_id=1, source_target_pairs={{0,8},{8,0},{16,24},{24,16},{1,9},{9,1},{17,25},{25,17},{2,10},{10... | collective-permute-start | bytes 1572872 | tf_op jit(solution)/shard_map/ppermute | solution.py:21
  1099.0 27.2 %collective-permute-start.34 = (bf16[256,512]{1,0:T(8,128)(2,1)}, bf16[256,512]{1,0:T(8,128)(2,1)}, u32[]{:S(2)}, u32[]{:S(2)}) collective-permute-start(bf16[256,512]{1,0:T(8,128)(2,1)} %slice.494), channel_id=1, source_target_pairs={{0,1},{1,0},{2,3},{3,2},{4,5},{5,4},{6,7},{7,6},{8,9},{9,8},{10,11... | collective-permute-start | bytes 786440 | tf_op jit(solution)/shard_map/ppermute | solution.py:21
  1100.1 27.2 %collective-permute-start.33 = (bf16[256,512]{1,0:T(8,128)(2,1)S(1)}, bf16[256,512]{1,0:T(8,128)(2,1)}, u32[]{:S(2)}, u32[]{:S(2)}) collective-permute-start(bf16[256,512]{1,0:T(8,128)(2,1)S(1)} %slice.493), channel_id=1, source_target_pairs={{0,2},{1,3},{2,0},{3,1},{4,6},{5,7},{6,4},{7,5},{8,10},{9,11},{10,... | collective-permute-start | bytes 786440 | tf_op jit(solution)/shard_map/ppermute | solution.py:21
  1116.7 104.7 %collective-permute-start.77 = (bf16[3,4,256,256]{3,2,1,0:T(8,128)(2,1)}, bf16[3,4,256,256]{3,2,1,0:T(8,128)(2,1)}, u32[]{:S(2)}, u32[]{:S(2)}) collective-permute-start(bf16[3,4,256,256]{3,2,1,0:T(8,128)(2,1)} %get-tuple-element.52), channel_id=1, source_target_pairs={{0,8},{8,0},{16,24},{24,16},{1,9},{9,1},{17,25},{25,17},{2,10},{10... | collective-permute-start | bytes 4718600 | tf_op jit(solution)/shard_map/ppermute | solution.py:21
  1123.9 81.3 %collective-permute-start.72 = (bf16[512,512]{1,0:T(8,128)(2,1)}, bf16[512,512]{1,0:T(8,128)(2,1)}, u32[]{:S(2)}, u32[]{:S(2)}) collective-permute-start(bf16[512,512]{1,0:T(8,128)(2,1)} %get-tuple-element.29), channel_id=1, source_target_pairs={{0,1},{1,0},{2,3},{3,2},{4,5},{5,4},{6,7},{7,6},{8,9},{9,8},{10,11... | collective-permute-start | bytes 1572872 | tf_op jit(solution)/shard_map/ppermute | solution.py:21
  1124.9 78.4 %collective-permute-start.73 = (bf16[512,512]{1,0:T(8,128)(2,1)}, bf16[512,512]{1,0:T(8,128)(2,1)}, u32[]{:S(2)}, u32[]{:S(2)}) collective-permute-start(bf16[512,512]{1,0:T(8,128)(2,1)} %get-tuple-element.29), channel_id=1, source_target_pairs={{0,2},{1,3},{2,0},{3,1},{4,6},{5,7},{6,4},{7,5},{8,10},{9,11},{10,... | collective-permute-start | bytes 1572872 | tf_op jit(solution)/shard_map/ppermute | solution.py:21
  1126.2 98.6 %collective-permute-start.78 = (bf16[3,4,256,256]{3,2,1,0:T(8,128)(2,1)}, bf16[3,4,256,256]{3,2,1,0:T(8,128)(2,1)}, u32[]{:S(2)}, u32[]{:S(2)}) collective-permute-start(bf16[3,4,256,256]{3,2,1,0:T(8,128)(2,1)} %get-tuple-element.51), channel_id=1, source_target_pairs={{0,16},{8,24},{16,0},{24,8},{1,17},{9,25},{17,1},{25,9},{2,18},{10... | collective-permute-start | bytes 4718600 | tf_op jit(solution)/shard_map/ppermute | solution.py:21
  1201.9 70.2 %collective-permute-start.79 = (bf16[3,4,256,256]{3,2,1,0:T(8,128)(2,1)}, bf16[3,4,256,256]{3,2,1,0:T(8,128)(2,1)}, u32[]{:S(2)}, u32[]{:S(2)}) collective-permute-start(bf16[3,4,256,256]{3,2,1,0:T(8,128)(2,1)} %get-tuple-element.50), channel_id=1, source_target_pairs={{0,24},{8,16},{16,8},{24,0},{1,25},{9,17},{17,9},{25,1},{2,26},{10... | collective-permute-start | bytes 4718600 | tf_op jit(solution)/shard_map/ppermute | solution.py:21
  (115 other events, 2572.4 us)
Sparse Core Ops, SparseCore 0:
  11.6 121.3 all-gather.2
  232.8 42.9 all-gather.4
  824.4 34.6 reduce-scatter.7
  861.4 35.2 reduce-scatter.5
  952.9 68.9 reduce-scatter.3

commit v2 on v1

v2 whole, which is shorter than its diff:
```python
import functools

import jax
import jax.numpy as jnp
from jax import lax
from jax.experimental import pallas as pl
from jax.experimental.pallas import tpu as pltpu
from jax.sharding import Mesh
from jax.sharding import PartitionSpec as P

HEAD_DIM = 128
EXPERTS = 16
LANES = 128
FIRST = 2

EPS = 1e-05
THETA = 10000.0
HIGH = lax.Precision.HIGHEST
f32 = jnp.float32
bf16 = jnp.bfloat16
MIB = 1 << 20


def after(value, *earlier):
    return lax.optimization_barrier((value, *earlier))[0]


def fence(*values):
    return lax.optimization_barrier(values)


def swap(value, axis, mask):
    if mask == 0:
        return value
    n = lax.axis_size(axis)
    return lax.ppermute(value, axis, [(i, i ^ mask) for i in range(n)])


def bits_of(axis):
    n = lax.axis_size(axis)
    return [1 << b for b in range(n.bit_length() - 1)]


def butterfly_sum(value, axes):
    for axis in axes:
        for bit in bits_of(axis):
            value = value + swap(value, axis, bit)
    return value


def tensor_sum(value):
    return butterfly_sum(value, ("tensor",))


def rope_tables(length, head_dim):
    half = head_dim // 2
    freq = THETA ** (-(jnp.arange(half).astype(f32) * 2.0 / head_dim))
    angle = jnp.arange(length).astype(f32)[:, None] * freq[None, :]
    cosine = jnp.concatenate([jnp.cos(angle), jnp.cos(angle)], -1)
    sine = jnp.concatenate([jnp.sin(angle), jnp.sin(angle)], -1)
    return (cosine, sine)


def rotate(value, cosine, sine):
    half = value.shape[-1] // 2
    turned = jnp.concatenate([-value[..., half:], value[..., :half]], -1)
    return value * cosine[:, None, :] + turned * sine[:, None, :]


def unrotate(grad, cosine, sine):
    half = grad.shape[-1] // 2
    scaled = grad * sine[:, None, :]
    back_turn = jnp.concatenate([scaled[..., half:], -scaled[..., :half]], -1)
    return grad * cosine[:, None, :] + back_turn


def columns(value, index, size):
    return lax.dynamic_slice_in_dim(value, index * size, size, 1)


def spread_z(value):
    parts = {0: value}
    for bit in reversed(bits_of("z")):
        parts.update({k ^ bit: swap(v, "z", bit) for k, v in parts.items()})
    return [parts[k] for k in range(len(parts))]


def spread_tensor_near(value):
    n = lax.axis_size("tensor")
    return [swap(value, "tensor", k) for k in ((1, 2) if n == 4 else range(1, n))]


def spread_tensor_far(value, near):
    if lax.axis_size("tensor") != 4:
        return jnp.stack([value, *near])
    half = value.shape[0] // 2
    cross = [swap(near[0][:half], "tensor", 2), swap(near[1][half:], "tensor", 1)]
    return jnp.stack([value, *near, jnp.concatenate(cross, 0)])


def spread_tensor(value):
    return spread_tensor_far(value, spread_tensor_near(value))


def gather_tensor(value):
    me, n = lax.axis_index("tensor"), lax.axis_size("tensor")
    rows, width = value.shape
    out = jnp.zeros((rows, n * width), value.dtype)
    parts = spread_tensor(value)
    for k in range(n):
        part = parts[k]
        out = lax.dynamic_update_slice(out, part, (0, (me ^ k) * width))
    return out


def order_of(n, odd):
    if n != 4:
        return tuple(range(n))
    return (0, 1, 2, 3) if odd else (0, 2, 1, 3)


def scatter_first(block, odd):
    n = block.shape[0]
    if n != 4:
        return jnp.stack([swap(block[k], "tensor", k) for k in range(1, n)])
    return swap(block[2:], "tensor", 2 if odd else 1)


def scatter_second(block, got, odd):
    got = got.astype(f32)
    mine = block[0].astype(f32)
    if block.shape[0] != 4:
        return mine + jnp.sum(got, 0), None
    other = (block[1].astype(f32) + got[1]).astype(bf16)
    return mine + got[0], swap(other, "tensor", 1 if odd else 2)


def scatter_third(mine, got):
    return mine if got is None else mine + got.astype(f32)


def scatter_z_near(parts):
    return swap(jnp.stack([parts[k].astype(bf16) for k in sorted(parts)]), "z", 1)


def scatter_z_far(parts, got):
    parts = {k: parts[k] + got[i].astype(f32) for i, k in enumerate(sorted(parts))}
    for bit in bits_of("z")[1:]:
        away = sorted(k for k in parts if k & bit)
        got = swap(jnp.stack([parts[k].astype(bf16) for k in away]), "z", bit)
        parts = {k ^ bit: parts[k ^ bit] + got[i].astype(f32) for i, k in enumerate(away)}
    return parts[0]


def scatter_columns(value):
    me, n = lax.axis_index("tensor"), lax.axis_size("tensor")
    rows, width = value.shape[0], value.shape[1] // n
    half = rows // 2
    outs = []
    for odd in (0, 1):
        part = value[odd * half : (odd + 1) * half]
        block = jnp.stack([columns(part, me ^ k, width) for k in order_of(n, odd)])
        outs.append(scatter_third(*scatter_second(block, scatter_first(block, odd), odd)))
    return jnp.concatenate(outs, 0)


def dot_nn(a, b):
    return lax.dot_general(a, b, (((1,), (0,)), ((), ())), preferred_element_type=f32)


def dot_nt(a, b):
    return lax.dot_general(a, b, (((1,), (1,)), ((), ())), preferred_element_type=f32)


def dot_tn(a, b):
    return lax.dot_general(a, b, (((0,), (0,)), ((), ())), preferred_element_type=f32)


def load_weights(nz, slice_d, me_z, me_c, pairs, sems, along_last):
    copies = []
    for w, (parts, whole) in enumerate(pairs):
        for c in range(2):
            for k in range(nz):
                j = c * nz + k
                at = pl.ds(pl.multiple_of((me_c ^ c) * slice_d, slice_d), slice_d)
                target = (
                    whole.at[me_z ^ k, :, :, at] if along_last[w] else whole.at[me_z ^ k, :, at, :]
                )
                copies.append(pltpu.make_async_copy(parts[c].at[k], target, sems.at[w, j]))
    for copy in copies:
        copy.start()
    for copy in copies:
        copy.wait()


def own_gate(gates, lane, me_z, own_e, e):
    return jnp.sum(jnp.where(lane == FIRST + me_z * own_e + e, gates, 0.0), -1, keepdims=True)


def forward_kernel(nz, n, own_e, hid, slice_d, idx, *refs):
    m_ref, mask_ref, router_ref = refs[:3]
    act_ref, up_ref, hid_ref, probs_ref, w_gate, w_up, sems = refs[7:]
    me_z, me_c, me_t = idx[0], idx[1], idx[2]

    @pl.when(pl.program_id(0) == 0)
    def _():
        pairs = ((refs[3:5], w_gate), (refs[5:7], w_up))
        load_weights(nz, slice_d, me_z, me_c, pairs, sems, (False, False))

    rows = m_ref.shape[1]
    lane = lax.broadcasted_iota(jnp.int32, (rows, LANES), 1)
    logits = jnp.zeros((rows, LANES), f32)
    for k in range(n):
        logits += dot_nn(m_ref[k], router_ref[me_t ^ k])
    named = (lane >= FIRST) & (lane < FIRST + EXPERTS)
    logits = jnp.where(named, logits, -1e30)
    expd = jnp.where(named, jnp.exp(logits - jnp.max(logits, -1, keepdims=True)), 0.0)
    probs = expd / jnp.sum(expd, -1, keepdims=True)
    probs_ref[...] = probs
    gates = probs * mask_ref[...]
    for e in range(own_e):
        gate = own_gate(gates, lane, me_z, own_e, e)
        act = jnp.zeros((rows, hid), f32)
        up = jnp.zeros((rows, hid), f32)
        for k in range(n):
            act += dot_nn(m_ref[k], w_gate[me_t ^ k, e])
            up += dot_nn(m_ref[k], w_up[me_t ^ k, e])
        at = pl.ds(e * hid, hid)
        act_ref[:, at] = act
        up_ref[:, at] = up
        hid_ref[:, at] = (gate * (act * jax.nn.sigmoid(act) * up)).astype(bf16)


def forward_call(idx, m_all, mask_all, router_q, gate_parts, up_parts, nz):
    n, tokens, quarter = m_all.shape
    seq = tokens // nz
    own_e, slice_d, hid = up_parts[0].shape[1:]
    wide = own_e * hid
    here = lambda i, idx: (i, 0)
    return pl.pallas_call(
        functools.partial(forward_kernel, nz, n, own_e, hid, slice_d),
        grid_spec=pltpu.PrefetchScalarGridSpec(
            num_scalar_prefetch=1,
            grid=(nz,),
            in_specs=[
                pl.BlockSpec((n, seq, quarter), lambda i, idx: (0, i, 0)),
                pl.BlockSpec((seq, LANES), here),
                pl.BlockSpec((n, quarter, LANES), lambda i, idx: (0, 0, 0)),
            ]
            + [pl.BlockSpec(memory_space=pl.ANY)] * 4,
            out_specs=[
                pl.BlockSpec((seq, wide), here),
                pl.BlockSpec((seq, wide), here),
                pl.BlockSpec((seq, wide), here),
                pl.BlockSpec((seq, LANES), here),
            ],
            scratch_shapes=[
                pltpu.VMEM((n, own_e, quarter, hid), bf16),
                pltpu.VMEM((n, own_e, quarter, hid), bf16),
                pltpu.SemaphoreType.DMA((2, 2 * nz)),
            ],
        ),
        out_shape=[
            jax.ShapeDtypeStruct((tokens, wide), f32),
            jax.ShapeDtypeStruct((tokens, wide), f32),
            jax.ShapeDtypeStruct((tokens, wide), bf16),
            jax.ShapeDtypeStruct((tokens, LANES), f32),
        ],
        compiler_params=pltpu.CompilerParams(vmem_limit_bytes=52 * MIB),
        cost_estimate=pl.CostEstimate(
            flops=4 * tokens * n * quarter * wide, bytes_accessed=40 * MIB, transcendentals=0
        ),
    )(idx, m_all, mask_all, router_q, *gate_parts, *up_parts)


def backward_kernel(nz, n, own_e, hid, slice_d, quarter, idx, *refs):
    g_ref, act_ref, up_ref, probs_ref, mask_ref = refs[:5]
    dx_ref, dg_ref, du_ref, w_gate, w_up, w_down, sems = refs[11:]
    i = pl.program_id(0)
    me_z, me_c, me_t = idx[0], idx[1], idx[2]

    @pl.when(i == 0)
    def _():
        pairs = ((refs[5:7], w_gate), (refs[7:9], w_up), (refs[9:11], w_down))
        load_weights(nz, slice_d, me_z, me_c, pairs, sems, (False, False, True))

    rows = act_ref.shape[0]
    lane = lax.broadcasted_iota(jnp.int32, (rows, LANES), 1)
    gates = probs_ref[...] * mask_ref[...]
    dgate = jnp.zeros((rows, LANES), f32)
    for e in range(own_e):
        gate = own_gate(gates, lane, me_z, own_e, e)
        at = pl.ds(e * hid, hid)
        back = jnp.zeros((rows, hid), f32)
        for q in range(n):
            back += dot_nt(g_ref[q, 0], w_down[q, e])
        act = act_ref[:, at]
        up = up_ref[:, at]
        sigma = jax.nn.sigmoid(act)
        silu = act * sigma
        dgate = jnp.where(lane == me_z * own_e + e, jnp.sum(silu * up * back, -1, keepdims=True), dgate)
        back = gate * back
        dg_ref[:, at] = (back * up * sigma * (1.0 + act * (1.0 - sigma))).astype(bf16)
        du_ref[:, at] = (back * silu).astype(bf16)
    dgate = jnp.transpose(dgate)[:EXPERTS].astype(bf16)
    even, odd = order_of(n, 0), order_of(n, 1)
    for j in range(n):
        q = me_t ^ jnp.where(i % 2 == 0, even[j], odd[j])
        total = jnp.zeros((rows, quarter), f32)
        for e in range(own_e):
            at = pl.ds(e * hid, hid)
            total += dot_nt(dg_ref[:, at], w_gate[q, e])
            total += dot_nt(du_ref[:, at], w_up[q, e])
        dx_ref[0, j, pl.ds(0, rows), :] = total.astype(bf16)
        for h in range(rows // quarter):
            dx_ref[0, j, pl.ds(rows + h * EXPERTS, EXPERTS), :] = dgate[
                :, h * quarter : (h + 1) * quarter
            ]


def backward_call(idx, first, g_all, act, up, probs, mask_all, weights):
    n, nz, seq, quarter = g_all.shape
    own_e, slice_d, hid = weights[0].shape[1:]
    blocks = nz // 2
    wide = own_e * hid
    tall = seq + EXPERTS * (seq // quarter)
    some = lambda i, idx: (2 * i + first, 0)
    here = lambda i, idx: (i, 0)
    hbm = pl.BlockSpec(memory_space=pl.ANY)
    return pl.pallas_call(
        functools.partial(backward_kernel, nz, n, own_e, hid, slice_d, quarter),
        grid_spec=pltpu.PrefetchScalarGridSpec(
            num_scalar_prefetch=1,
            grid=(blocks,),
            in_specs=[
                pl.BlockSpec((n, 1, seq, quarter), lambda i, idx: (0, 2 * i + first, 0, 0)),
                pl.BlockSpec((seq, wide), some),
                pl.BlockSpec((seq, wide), some),
                pl.BlockSpec((seq, LANES), some),
                pl.BlockSpec((seq, LANES), some),
            ]
            + [hbm] * 6,
            out_specs=[
                pl.BlockSpec((1, n, tall, quarter), lambda i, idx: (i, 0, 0, 0)),
                pl.BlockSpec((seq, wide), here),
                pl.BlockSpec((seq, wide), here),
            ],
            scratch_shapes=[
                pltpu.VMEM((n, own_e, quarter, hid), bf16),
                pltpu.VMEM((n, own_e, quarter, hid), bf16),
                pltpu.VMEM((n, own_e, hid, quarter), bf16),
                pltpu.SemaphoreType.DMA((3, 2 * nz)),
            ],
        ),
        out_shape=[
            jax.ShapeDtypeStruct((blocks, n, tall, quarter), bf16),
            jax.ShapeDtypeStruct((blocks * seq, wide), bf16),
            jax.ShapeDtypeStruct((blocks * seq, wide), bf16),
        ],
        compiler_params=pltpu.CompilerParams(vmem_limit_bytes=56 * MIB),
        cost_estimate=pl.CostEstimate(
            flops=6 * blocks * seq * n * quarter * wide,
            bytes_accessed=40 * MIB,
            transcendentals=0,
        ),
    )(idx, g_all, act, up, probs, mask_all, *weights)


def output_kernel(nz, n, own_e, hid, slice_d, quarter, idx, *refs):
    hid_ref, near, far, y_ref, w_down, sems = refs

    @pl.when(pl.program_id(0) == 0)
    def _():
        load_weights(nz, slice_d, idx[0], idx[1], (((near, far), w_down),), sems, (True,))

    for q in range(n):
        total = jnp.zeros((hid_ref.shape[0], quarter), f32)
        for e in range(own_e):
            total += dot_nn(hid_ref[:, pl.ds(e * hid, hid)], w_down[q, e])
        y_ref[q, 0] = total.astype(bf16)


def output_call(idx, hidden, parts, n, nz):
    tokens, wide = hidden.shape
    seq = tokens // nz
    own_e, hid, slice_d = parts[0].shape[1:]
    quarter = 2 * slice_d
    return pl.pallas_call(
        functools.partial(output_kernel, nz, n, own_e, hid, slice_d, quarter),
        grid_spec=pltpu.PrefetchScalarGridSpec(
            num_scalar_prefetch=1,
            grid=(nz,),
            in_specs=[pl.BlockSpec((seq, wide), lambda i, idx: (i, 0))]
            + [pl.BlockSpec(memory_space=pl.ANY)] * 2,
            out_specs=pl.BlockSpec((n, 1, seq, quarter), lambda i, idx: (0, i, 0, 0)),
            scratch_shapes=[
                pltpu.VMEM((n, own_e, hid, quarter), bf16),
                pltpu.SemaphoreType.DMA((1, 2 * nz)),
            ],
        ),
        out_shape=jax.ShapeDtypeStruct((n, nz, seq, quarter), bf16),
        compiler_params=pltpu.CompilerParams(vmem_limit_bytes=48 * MIB),
        cost_estimate=pl.CostEstimate(
            flops=2 * tokens * n * quarter * wide, bytes_accessed=16 * MIB, transcendentals=0
        ),
    )(idx, hidden, *parts)


def down_grad_kernel(nz, own_e, hid, seq, slice_d, idx, g_ref, hid_ref, keep_ref, give_ref):
    for out_ref, c in ((keep_ref, idx[1]), (give_ref, 1 - idx[1])):
        cols = pl.ds(pl.multiple_of(c * slice_d, slice_d), slice_d)
        for e in range(own_e):
            total = jnp.zeros((hid, slice_d), f32)
            for blk in range(nz):
                left = hid_ref[pl.ds(blk * seq, seq), pl.ds(e * hid, hid)]
                total += dot_tn(left, g_ref[0, blk, :, cols])
            out_ref[0, e] = total.astype(bf16)


def down_grad_call(idx, g_all, hidden, own_e):
    n, nz, seq, quarter = g_all.shape
    tokens, wide = hidden.shape
    hid, slice_d = wide // own_e, quarter // 2
    out = pl.BlockSpec((1, own_e, hid, slice_d), lambda q, idx: (q ^ idx[0], 0, 0, 0))
    return pl.pallas_call(
        functools.partial(down_grad_kernel, nz, own_e, hid, seq, slice_d),
        grid_spec=pltpu.PrefetchScalarGridSpec(
            num_scalar_prefetch=1,
            grid=(n,),
            in_specs=[
                pl.BlockSpec((1, nz, seq, quarter), lambda q, idx: (q, 0, 0, 0)),
                pl.BlockSpec((tokens, wide), lambda q, idx: (0, 0)),
            ],
            out_specs=[out, out],
        ),
        out_shape=[jax.ShapeDtypeStruct((nz, own_e, hid, slice_d), bf16)] * 2,
        compiler_params=pltpu.CompilerParams(vmem_limit_bytes=48 * MIB),
        cost_estimate=pl.CostEstimate(
            flops=2 * tokens * n * quarter * wide, bytes_accessed=16 * MIB, transcendentals=0
        ),
    )(idx, g_all, hidden)


def up_grad_kernel(nz, own_e, hid, seq, slice_d, idx, m_ref, *refs):
    rights, (keep_ref, give_ref) = refs[:4], refs[4:]
    for out_ref, c in ((keep_ref, idx[1]), (give_ref, 1 - idx[1])):
        cols = pl.ds(pl.multiple_of(c * slice_d, slice_d), slice_d)
        for w in range(2):
            for e in range(own_e):
                total = jnp.zeros((slice_d, hid), f32)
                for blk in range(nz):
                    right = rights[2 * w + blk % 2][
                        pl.ds(blk // 2 * seq, seq), pl.ds(e * hid, hid)
                    ]
                    total += dot_tn(m_ref[0, pl.ds(blk * seq, seq), cols], right)
                out_ref[0, w, e] = total.astype(bf16)


def up_grad_call(idx, m_all, early, late, own_e, nz):
    n, tokens, quarter = m_all.shape
    seq = tokens // nz
    wide = early[0].shape[1]
    hid, slice_d = wide // own_e, quarter // 2
    full = pl.BlockSpec(early[0].shape, lambda k, idx: (0, 0))
    out = pl.BlockSpec(
        (1, 2, own_e, slice_d, hid), lambda k, idx: (k ^ idx[2] ^ idx[0], 0, 0, 0, 0)
    )
    return pl.pallas_call(
        functools.partial(up_grad_kernel, nz, own_e, hid, seq, slice_d),
        grid_spec=pltpu.PrefetchScalarGridSpec(
            num_scalar_prefetch=1,
            grid=(n,),
            in_specs=[pl.BlockSpec((1, tokens, quarter), lambda k, idx: (k, 0, 0))] + [full] * 4,
            out_specs=[out, out],
        ),
        out_shape=[jax.ShapeDtypeStruct((nz, 2, own_e, slice_d, hid), bf16)] * 2,
        compiler_params=pltpu.CompilerParams(vmem_limit_bytes=48 * MIB),
        cost_estimate=pl.CostEstimate(
            flops=4 * tokens * n * quarter * wide, bytes_accessed=24 * MIB, transcendentals=0
        ),
    )(idx, m_all, early[0], late[0], early[1], late[1])


def place_kernel(nz, idx, *refs):
    ups, downs, outs = refs[:nz], refs[nz : 2 * nz], refs[2 * nz :]
    for i in range(nz):

        @pl.when(pl.program_id(0) == i)
        def _(i=i):
            outs[0][...] = ups[i][0].astype(f32)
            outs[1][...] = ups[i][1].astype(f32)
            outs[2][...] = downs[i][...].astype(f32)


def place_call(idx, ups, downs):
    nz = len(ups)
    flat = list(ups) + list(downs)
    fixed = lambda rank: lambda k, idx: (0,) * rank
    shapes = [ups[0].shape[1:], ups[0].shape[1:], downs[0].shape]
    return pl.pallas_call(
        functools.partial(place_kernel, nz),
        grid_spec=pltpu.PrefetchScalarGridSpec(
            num_scalar_prefetch=1,
            grid=(nz,),
            in_specs=[pl.BlockSpec(part.shape, fixed(part.ndim)) for part in flat],
            out_specs=[
                pl.BlockSpec(shape, lambda k, idx: (k ^ idx[0], 0, 0)) for shape in shapes
            ],
        ),
        out_shape=[jax.ShapeDtypeStruct((EXPERTS,) + shape[1:], f32) for shape in shapes],
        compiler_params=pltpu.CompilerParams(vmem_limit_bytes=48 * MIB),
        cost_estimate=pl.CostEstimate(flops=0, bytes_accessed=20 * MIB, transcendentals=0),
    )(idx, *flat)


def shards(
    tokens,
    cotangent,
    routes,
    wq,
    wk,
    wv,
    wo,
    attn_gain,
    q_gain,
    k_gain,
    moe_gain,
    router,
    w_gate,
    w_up,
    w_down,
):
    nz = lax.axis_size("z")
    me_t = lax.axis_index("tensor")
    me_z = lax.axis_index("z")
    me_c = lax.axis_index("core")
    dp = ("z", "core")
    seq, width = tokens.shape
    quarter = width // lax.axis_size("tensor")
    local = wq.shape[1]
    local_heads = local // HEAD_DIM
    slice_d = wq.shape[0]
    own_e = EXPERTS // nz
    hid = w_gate.shape[2]

    idx = jnp.stack([me_z, me_c, me_t]).astype(jnp.int32)

    small = jnp.concatenate([attn_gain[:, None], moe_gain[:, None], router], 1)
    small = jnp.pad(small, ((0, 0), (0, LANES - small.shape[1])))
    packed = lax.all_gather(jnp.concatenate([wq, wk, wv, small], 1), dp, axis=0, tiled=True)
    mask = jnp.sum(
        (routes[:, :, None] == jnp.arange(EXPERTS)[None, None, :]).astype(bf16), 1
    )
    packed, *mask_parts = fence(packed, *spread_z(mask.T))
    mask_all = jnp.stack(mask_parts).transpose(0, 2, 1)
    mask_all = jnp.pad(
        mask_all.reshape(nz * seq, EXPERTS).astype(f32),
        ((0, 0), (FIRST, LANES - EXPERTS - FIRST)),
    )
    wqkv_full = packed[:, : 3 * local]
    small_full = packed[:, 3 * local :]
    a_gain = small_full[:, 0].astype(f32)
    m_gain = small_full[:, 1].astype(f32)
    router_full = small_full[:, FIRST : FIRST + EXPERTS]
    wo_full = lax.all_gather(after(wo, packed), dp, axis=1, tiled=True)

    def fetch(weight):
        pick = lambda k: lax.dynamic_slice_in_dim(weight, (me_z ^ k) * own_e, own_e, 0)
        return [swap(pick(k), "z", k) for k in range(nz)]

    def both_cores(parts):
        parts = jnp.stack(parts)
        return [parts, swap(parts, "core", 1)]

    cot_parts = spread_z(after(columns(cotangent, me_t, quarter), packed))

    xf = tokens.astype(f32)
    rate_x = lax.rsqrt(jnp.mean(xf * xf, -1, keepdims=True) + EPS)
    gain_q = q_gain.astype(f32)
    gain_k = k_gain.astype(f32)
    a_low = (xf * rate_x * a_gain).astype(bf16)
    qkv = jnp.dot(a_low, wqkv_full, preferred_element_type=f32)
    query, keyed, valued = qkv[:, :local], qkv[:, local : 2 * local], qkv[:, 2 * local :]
    sums = tensor_sum(jnp.stack([jnp.sum(query * query, -1), jnp.sum(keyed * keyed, -1)]))
    rate_q = lax.rsqrt(sums[0] / width + EPS)[:, None]
    rate_k = lax.rsqrt(sums[1] / width + EPS)[:, None]
    cosine, sine = rope_tables(seq, HEAD_DIM)
    heads = (seq, local_heads, HEAD_DIM)
    q_rot = rotate((query * rate_q * gain_q).reshape(heads), cosine, sine).astype(bf16)
    k_rot = rotate((keyed * rate_k * gain_k).reshape(heads), cosine, sine).astype(bf16)
    v_low = valued.reshape(heads).astype(bf16)
    scale = HEAD_DIM ** (-0.5)
    scores = scale * jnp.einsum("qhd,khd->hqk", q_rot, k_rot, preferred_element_type=f32)
    causal = jnp.arange(seq)[:, None] >= jnp.arange(seq)[None, :]
    scores = jnp.where(causal[None], scores, -1e30)
    peak = jnp.max(scores, -1, keepdims=True)
    expd = jnp.exp(scores - peak)
    weights = expd / jnp.sum(expd, -1, keepdims=True)
    weights_low = weights.astype(bf16)
    outputs = jnp.einsum("hqk,khd->qhd", weights_low, v_low, preferred_element_type=f32)
    joined = outputs.reshape(seq, local).astype(bf16)
    wo_full = after(wo_full, joined)
    attn = jnp.dot(joined, wo_full, preferred_element_type=f32).astype(bf16)
    attn, *cot_parts = fence(attn, *cot_parts)
    cot_all = lax.all_gather(jnp.stack(cot_parts), "tensor", axis=0, tiled=False)
    gate_parts = fetch(after(w_gate, attn))

    x_own = columns(xf, me_t, quarter)
    resid = x_own + scatter_columns(attn)
    rate_r = lax.rsqrt(tensor_sum(jnp.sum(resid * resid, -1)) / width + EPS)[:, None]
    gain_own = lax.dynamic_slice_in_dim(m_gain, me_t * quarter, quarter, 0)
    m_own = (resid * rate_r * gain_own).astype(bf16)

    m_own, *gate_parts = fence(m_own, *gate_parts)
    m_parts = fence(*spread_z(m_own))
    up_parts = fetch(after(w_up, m_parts[0]))
    gate_parts = both_cores(gate_parts)
    m_flat = jnp.concatenate(m_parts, 0)
    m_near = spread_tensor_near(m_flat)
    held = fence(*m_near, *up_parts)
    m_near, up_parts = held[: len(m_near)], held[len(m_near) :]
    up_parts = both_cores(up_parts)
    down_parts = fetch(after(w_down, up_parts[0]))
    m_all = spread_tensor_far(m_flat, m_near)
    m_all, down_parts[2] = fence(m_all, down_parts[2])
    router_q = small_full.reshape(-1, quarter, LANES)
    act, up, hidden, probs_all = forward_call(
        idx, m_all, mask_all, router_q, gate_parts, up_parts, nz
    )
    hidden, *down_parts = fence(hidden, *down_parts)
    down_parts = both_cores(down_parts)
    down_keep, down_give = down_grad_call(idx, cot_all, hidden, own_e)

    def to_owners(keep, got):
        summed = (keep.astype(f32) + got.astype(f32)).astype(bf16)
        return [swap(summed[k], "z", k) for k in range(nz)]

    down_own = to_owners(down_keep, swap(down_give, "core", 1))
    half_call = lambda first, probs: backward_call(
        idx, first, cot_all, act, up, probs, mask_all, gate_parts + up_parts + down_parts
    )
    odds, evens = range(1, nz, 2), range(0, nz, 2)
    late = half_call(1, after(probs_all, down_give))
    first = {k: scatter_first(late[0][k // 2], k // 2 % 2) for k in odds}
    early = half_call(0, after(probs_all, late[1]))
    held = fence(*early, *(first[k] for k in odds), *down_own[:3])
    early, got = held[:3], dict(zip(odds, held[3:]))
    down_own[:3] = held[3 + nz // 2 :]
    second = {k: scatter_second(late[0][k // 2], got[k], k // 2 % 2) for k in odds}
    first = {k: scatter_first(early[0][k // 2], k // 2 % 2) for k in evens}
    up_keep, up_give = up_grad_call(idx, m_all, early[1:3], late[1:3], own_e, nz)
    held = fence(up_keep, up_give, *(first[k] for k in evens), *down_own[3:])
    (up_keep, up_give), got = held[:2], dict(zip(evens, held[2:]))
    down_own[3:] = held[2 + nz // 2 :]
    near = scatter_z_near({k: scatter_third(*second[k]) for k in odds})
    second = {k: scatter_second(early[0][k // 2], got[k], k // 2 % 2) for k in evens}
    up_got = swap(up_give, "core", 1)
    moe_part = output_call(idx, after(hidden, up_give), down_parts, width // quarter, nz)
    moe_part, near, up_got = fence(moe_part, near, up_got)
    dm_own = scatter_z_far({k: scatter_third(*second[k]) for k in evens}, near)
    dgate = jnp.concatenate(
        [dm_own[seq + h * EXPERTS :][:EXPERTS] for h in range(seq // quarter)], 1
    )
    dm_own = dm_own[:seq]
    up_own = to_owners(after(up_keep, dm_own), up_got)
    moe_sum = lax.psum_scatter(moe_part, "tensor", scatter_dimension=0, tiled=False)

    dgate = dgate.T
    probs = probs_all[:seq, FIRST : FIRST + EXPERTS]
    dprobs = dgate * mask.astype(f32)
    dlogits = probs * (dprobs - jnp.sum(probs * dprobs, -1, keepdims=True))
    router_own = lax.dynamic_slice_in_dim(router_full, me_t * quarter, quarter, 0)
    router_part = jnp.dot(m_own.astype(f32).T, dlogits, precision=HIGH)
    dm_own = dm_own + jnp.dot(dlogits, router_own.astype(f32).T, precision=HIGH)

    normed = resid * rate_r
    moe_gain_part = jnp.sum(dm_own * normed, 0)
    pulled = dm_own * gain_own
    inner_r = tensor_sum(jnp.sum(pulled * normed, -1))[:, None] / width
    cot_own = columns(cotangent, me_t, quarter).astype(f32)
    dresid = cot_own + rate_r * (pulled - normed * inner_r)
    dresid_low = gather_tensor(dresid.astype(bf16))

    wo_grad = jnp.einsum("sa,sd->ad", joined, dresid_low, preferred_element_type=f32)
    dout = (
        jnp.einsum("sd,ad->sa", dresid_low, wo_full, preferred_element_type=f32)
        .astype(bf16)
        .reshape(heads)
    )
    dweights = jnp.einsum("qhd,khd->hqk", dout, v_low, preferred_element_type=f32)
    dv = jnp.einsum("hqk,qhd->khd", weights_low, dout, preferred_element_type=f32)
    inner = jnp.sum(weights * dweights, -1, keepdims=True)
    dscores = (weights * (dweights - inner)).astype(bf16)
    dq_rot = scale * jnp.einsum("hqk,khd->qhd", dscores, k_rot, preferred_element_type=f32)
    dk_rot = scale * jnp.einsum("hqk,qhd->khd", dscores, q_rot, preferred_element_type=f32)
    dq_norm = unrotate(dq_rot, cosine, sine).reshape(seq, local)
    dk_norm = unrotate(dk_rot, cosine, sine).reshape(seq, local)
    inners = tensor_sum(
        jnp.stack(
            [jnp.sum(dq_norm * gain_q * query, -1), jnp.sum(dk_norm * gain_k * keyed, -1)]
        )
    )
    dq_low = (rate_q * gain_q * dq_norm - query * rate_q**3 * inners[0][:, None] / width).astype(
        bf16
    )
    dk_low = (rate_k * gain_k * dk_norm - keyed * rate_k**3 * inners[1][:, None] / width).astype(
        bf16
    )
    dv_low = dv.reshape(seq, local).astype(bf16)
    q_gain_part = jnp.sum(dq_norm * query * rate_q, 0)
    k_gain_part = jnp.sum(dk_norm * keyed * rate_k, 0)
    dqkv = jnp.concatenate([dq_low, dk_low, dv_low], 1)
    dqkv, *up_own = fence(dqkv, *up_own)
    moe_sum = after(moe_sum, dqkv)
    moe_near = scatter_z_near({k: moe_sum[k] for k in odds})
    moe_own = scatter_z_far({k: moe_sum[k].astype(f32) for k in evens}, moe_near)
    mixed = gather_tensor((resid + moe_own).astype(bf16))
    expert_grads = place_call(idx, up_own, down_own)
    wqkv_grad = jnp.einsum("sd,sa->da", a_low, dqkv, preferred_element_type=f32).astype(bf16)
    da_part = jnp.einsum("sa,da->sd", dqkv, wqkv_full, preferred_element_type=f32)
    da_own = scatter_columns(da_part.astype(bf16))
    norm_x = x_own * rate_x
    attn_gain_part = jnp.sum(da_own * norm_x, 0)
    pulled_x = da_own * lax.dynamic_slice_in_dim(a_gain, me_t * quarter, quarter, 0)
    inner_x = tensor_sum(jnp.sum(pulled_x * norm_x, -1))[:, None] / width
    tokens_grad = gather_tensor(
        (dresid + rate_x * (pulled_x - norm_x * inner_x)).astype(bf16)
    )

    wqkv_own = lax.psum_scatter(wqkv_grad, dp, scatter_dimension=0, tiled=True).astype(f32)
    wo_own = lax.psum_scatter(wo_grad.astype(bf16), dp, scatter_dimension=1, tiled=True).astype(f32)
    smalls = jnp.concatenate(
        [
            q_gain_part[None],
            k_gain_part[None],
            attn_gain_part[None],
            moe_gain_part[None],
            router_part.T,
        ],
        0,
    )
    smalls = butterfly_sum(smalls, ("core", "z"))
    half = lax.dynamic_slice_in_dim(smalls[2:], me_c * slice_d, slice_d, 1)
    half = tensor_sum(jnp.where(me_t == me_z, half, 0.0))
    return (
        mixed,
        tokens_grad,
        wqkv_own[:, :local],
        wqkv_own[:, local : 2 * local],
        wqkv_own[:, 2 * local :],
        wo_own,
        half[0],
        smalls[0],
        smalls[1],
        half[1],
        half[2:].T,
        expert_grads[0],
        expert_grads[1],
        expert_grads[2],
    )


def solution(mesh):
    fine = Mesh(
        mesh.devices.reshape(mesh.shape["dp"] // 2, 2, mesh.shape["tensor"]),
        ("z", "core", "tensor"),
    )
    dp = ("z", "core")
    in_specs = (
        P(dp, None),
        P(dp, None),
        P(dp, None),
        P(dp, "tensor"),
        P(dp, "tensor"),
        P(dp, "tensor"),
        P("tensor", dp),
        P(dp),
        P("tensor"),
        P("tensor"),
        P(dp),
        P(dp, None),
        P(None, dp, "tensor"),
        P(None, dp, "tensor"),
        P(None, "tensor", dp),
    )
    out_specs = (
        P(dp, None),
        P(dp, None),
        P(dp, "tensor"),
        P(dp, "tensor"),
        P(dp, "tensor"),
        P("tensor", dp),
        P(dp),
        P("tensor"),
        P("tensor"),
        P(dp),
        P(dp, None),
        P(None, dp, "tensor"),
        P(None, dp, "tensor"),
        P(None, "tensor", dp),
    )
    return jax.shard_map(shards, mesh=fine, in_specs=in_specs, out_specs=out_specs, check_vma=False)
```

time: 1310 us -> 897 us (0.68)
  the two profiles are of different devices: /device:TPU:9 before, /device:TPU:0 now
where the time goes in v2:
time: 897 us; the launch traced here: 888 us
  waiting for transfers between devices  450 us (50%)
  Pallas kernels  140 us (16%)
  starting transfers between devices  118 us (13%)
  other arithmetic  74.1 us (8%)
  local copies, waits for them, and re-layouts  45.3 us (5%)
  matrix products  44.7 us (5%)
  between operations  16.2 us (2%)
    ppermute x80, waiting for transfers between devices, swap(): return lax.ppermute(value, axis, [(i, i ^ mask) for i in range(n)])  388 us
    ppermute x80, starting transfers between devices, swap(): return lax.ppermute(value, axis, [(i, i ^ mask) for i in range(n)])  117 us
    all_gather x1, waiting for transfers between devices, shards(): lax.all_gather(jnp.concatenate([wq, wk, wv, small], 1), dp, axis=0, tiled...  61.3 us
    pallas_call x2, Pallas kernels, backward_call(): pl.pallas_call(functools.partial(backward_kernel, nz, n, own_e, hid, slic...  52.8 us
    pallas_call x1, Pallas kernels, forward_call(): pl.pallas_call(functools.partial(forward_kernel, nz, n, own_e, hid, slice...  28.7 us
    pallas_call x1, Pallas kernels, up_grad_call(): pl.pallas_call(functools.partial(up_grad_kernel, nz, own_e, hid, seq, sli...  24.2 us
  transfers between devices with their start and end apart: 86, of which 43 were waited for; matrix products, arithmetic and copies ran while one was open for 16% of the time, Pallas kernels for 16%

profile of v2, /device:TPU:0, one launch (start us, length us, event | category | flops | bytes accessed | tf_op | source)
XLA Modules:
  0.0 888.2 jit_solution(17468271328289355980)
XLA Ops:
  11.7 4.1 collective-permute-start.1
  22.3 61.3 %all-gather.5.cloned.1.call-done = bf16[2048,1664]{1,0:T(8,128)(2,1)} async-done(((bf16[256,1664]{1,0:T(8,128)(2,1)}), bf16[2048,1664]{1,0:T(8,128)(2,1)}) %all-gather.5.cloned.1.call-update) | async-done | bytes 6815760 | tf_op jit(solution)/shard_map/all_gather | solution.py:550
  84.9 5.6 fusion.3
  101.1 4.9 fusion.97
  106.0 28.6 %collective-permute-done.6 = bf16[512,512]{1,0:T(8,128)(2,1)} collective-permute-done((bf16[512,512]{1,0:T(8,128)(2,1)}, bf16[512,512]{1,0:T(8,128)(2,1)}, u32[]{:S(2)}, u32[]{:S(2)}) %collective-permute-start.6) | collective-permute-done | bytes 524320 | tf_op jit(solution)/shard_map/ppermute | solution.py:36
  137.7 4.4 convolution_convert_fusion.2
  142.1 6.4 collective-permute-done.7
  159.9 13.5 %collective-permute-done.8 = bf16[2,256,512]{2,1,0:T(8,128)(2,1)} collective-permute-done((bf16[2,256,512]{2,1,0:T(8,128)(2,1)S(1)}, bf16[2,256,512]{2,1,0:T(8,128)(2,1)}, u32[]{:S(2)}, u32[]{:S(2)}) %collective-permute-start.8) | collective-permute-done | bytes 524320 | tf_op jit(solution)/shard_map/ppermute | solution.py:36
  176.3 3.8 collective-permute-done.10
  181.9 4.3 collective-permute-start.16
  189.0 4.5 collective-permute-done.11
  202.9 10.8 %collective-permute-done.15 = bf16[4,256,256]{2,1,0:T(8,128)(2,1)S(1)} collective-permute-done((bf16[4,256,256]{2,1,0:T(8,128)(2,1)S(1)}, bf16[4,256,256]{2,1,0:T(8,128)(2,1)S(1)}, u32[]{:S(2)}, u32[]{:S(2)}) %collective-permute-start.15) | collective-permute-done | bytes 524320 | tf_op jit(solution)/shard_map/ppermute | solution.py:36
  213.8 15.8 %collective-permute-start.18 = (bf16[512,512]{1,0:T(8,128)(2,1)S(1)}, bf16[512,512]{1,0:T(8,128)(2,1)S(1)}, u32[]{:S(2)}, u32[]{:S(2)}) collective-permute-start(bf16[512,512]{1,0:T(8,128)(2,1)S(1)} %multiply_convert_fusion.2), channel_id=1, source_target_pairs={{0,16},{8,24},{16,0},{24,8},{1,17},{9,25},{17,1},{25,9},{2,18},{10... | collective-permute-start | bytes 1572872 | tf_op jit(solution)/shard_map/ppermute | solution.py:36
  230.6 13.2 %collective-permute-done.18 = bf16[512,512]{1,0:T(8,128)(2,1)S(1)} collective-permute-done((bf16[512,512]{1,0:T(8,128)(2,1)S(1)}, bf16[512,512]{1,0:T(8,128)(2,1)S(1)}, u32[]{:S(2)}, u32[]{:S(2)}) %collective-permute-start.18) | collective-permute-done | bytes 524320 | tf_op jit(solution)/shard_map/ppermute | solution.py:36
  247.6 7.7 collective-permute-done.19
  260.4 9.8 %collective-permute-start.23 = (bf16[4,256,256]{2,1,0:T(8,128)(2,1)S(1)}, bf16[4,256,256]{2,1,0:T(8,128)(2,1)S(1)}, u32[]{:S(2)}, u32[]{:S(2)}) collective-permute-start(bf16[4,256,256]{2,1,0:T(8,128)(2,1)S(1)} %get-tuple-element.227), channel_id=1, source_target_pairs={{0,16},{8,24},{16,0},{24,8},{1,17},{9,25},{17,1},{25,9},{2,18},{10... | collective-permute-start | bytes 1572872 | tf_op jit(solution)/shard_map/ppermute | solution.py:36
  271.8 10.4 %collective-permute-done.22 = bf16[4,256,256]{2,1,0:T(8,128)(2,1)S(1)} collective-permute-done((bf16[4,256,256]{2,1,0:T(8,128)(2,1)S(1)}, bf16[4,256,256]{2,1,0:T(8,128)(2,1)S(1)}, u32[]{:S(2)}, u32[]{:S(2)}) %collective-permute-start.22) | collective-permute-done | bytes 524320 | tf_op jit(solution)/shard_map/ppermute | solution.py:36
  282.1 14.6 %collective-permute-done.23 = bf16[4,256,256]{2,1,0:T(8,128)(2,1)S(1)} collective-permute-done((bf16[4,256,256]{2,1,0:T(8,128)(2,1)S(1)}, bf16[4,256,256]{2,1,0:T(8,128)(2,1)S(1)}, u32[]{:S(2)}, u32[]{:S(2)}) %collective-permute-start.23) | collective-permute-done | bytes 524320 | tf_op jit(solution)/shard_map/ppermute | solution.py:36
  313.4 15.5 %collective-permute-done.25 = bf16[1024,512]{1,0:T(8,128)(2,1)} collective-permute-done((bf16[1024,512]{1,0:T(8,128)(2,1)}, bf16[1024,512]{1,0:T(8,128)(2,1)}, u32[]{:S(2)}, u32[]{:S(2)}) %collective-permute-start.25) | collective-permute-done | bytes 1048608 | tf_op jit(solution)/shard_map/ppermute | solution.py:36
  328.8 3.4 collective-permute-start.30
  335.5 4.4 pad_maximum_fusion.refs_0_.m_ref
  339.9 28.7 %shard_map.254 = (f32[2048,1024]{1,0:T(8,128)}, f32[2048,1024]{1,0:T(8,128)}, bf16[2048,1024]{1,0:T(8,128)(2,1)}, f32[2048,128]{1,0:T(8,128)S(1)}) custom-call(s32[3]{0:T(128)S(1)} %pad_add_fusion.idx, bf16[4,2048,512]{2,1,0:T(8,128)(2,1)} %pad_maximum_fusion.refs_0_.m_ref, f32[2048,128]{1,0:T(8,128)} %pad_convert_fusion.refs_1_.refs_4_, ...), custom_call_target="tpu_custom_call" | custom-call | flops 17179869184 | bytes 41943040 | tf_op jit(solution)/shard_map/pallas_call | solution.py:240
  369.7 13.4 %shard_map.255 = (bf16[4,4,256,256]{3,2,1,0:T(8,128)(2,1)S(1)}, bf16[4,4,256,256]{3,2,1,0:T(8,128)(2,1)S(1)}) custom-call(s32[3]{0:T(128)S(1)} %pad_add_fusion.idx, bf16[4,4,512,512]{3,2,1,0:T(8,128)(2,1)} %bitcast.377, bf16[2048,1024]{1,0:T(8,128)(2,1)} %get-tuple-element.153.hid_ref.refs_0_), custom_call_target="tpu_custom_call" | custom-call | flops 8589934592 | bytes 16777216 | tf_op jit(solution)/shard_map/pallas_call | solution.py:425
  383.6 26.5 %shard_map.256 = (bf16[2,4,528,512]{3,2,1,0:T(8,128)(2,1)}, bf16[1024,1024]{1,0:T(8,128)(2,1)}, bf16[1024,1024]{1,0:T(8,128)(2,1)}) custom-call(s32[3]{0:T(128)} %copy-done.8, bf16[4,4,512,512]{3,2,1,0:T(8,128)(2,1)} %bitcast.378, f32[2048,1024]{1,0:T(8,128)} %get-tuple-element.130.refs_1_, f32[2048,1024]{1,0:T(8,128)} %get-tuple-element.131.refs_2_, ...), custom_call_target="tpu_custom_call" | custom-call | flops 12884901888 | bytes 41943040 | tf_op jit(solution)/shard_map/pallas_call | solution.py:330
  419.9 26.3 %shard_map.257 = (bf16[2,4,528,512]{3,2,1,0:T(8,128)(2,1)}, bf16[1024,1024]{1,0:T(8,128)(2,1)}, bf16[1024,1024]{1,0:T(8,128)(2,1)}) custom-call(s32[3]{0:T(128)} %copy-done.8, bf16[4,4,512,512]{3,2,1,0:T(8,128)(2,1)} %bitcast.379, f32[2048,1024]{1,0:T(8,128)} %get-tuple-element.130.refs_1_, f32[2048,1024]{1,0:T(8,128)} %get-tuple-element.131.refs_2_, ...), custom_call_target="tpu_custom_call" | custom-call | flops 12884901888 | bytes 41943040 | tf_op jit(solution)/shard_map/pallas_call | solution.py:330
  453.5 24.2 %shard_map.258 = (bf16[4,2,4,256,256]{4,3,2,1,0:T(8,128)(2,1)}, bf16[4,2,4,256,256]{4,3,2,1,0:T(8,128)(2,1)}) custom-call(s32[3]{0:T(128)S(1)} %copy-done.9, bf16[4,2048,512]{2,1,0:T(8,128)(2,1)} %pad_maximum_fusion.refs_0_.m_ref, bf16[1024,1024]{1,0:T(8,128)(2,1)S(1)} %copy-done.11, bf16[1024,1024]{1,0:T(8,128)(2,1)S(1)} %copy-done.10, ...), custom_call_target="tpu_custom_call" | custom-call | flops 17179869184 | bytes 25165824 | tf_op jit(solution)/shard_map/pallas_call | solution.py:468
  479.9 13.2 %collective-permute-done.41 = bf16[528,512]{1,0:T(8,128)(2,1)S(1)} collective-permute-done((bf16[528,512]{1,0:T(8,128)(2,1)S(1)}, bf16[528,512]{1,0:T(8,128)(2,1)S(1)}, u32[]{:S(2)}, u32[]{:S(2)}) %collective-permute-start.41) | collective-permute-done | bytes 540704 | tf_op jit(solution)/shard_map/ppermute | solution.py:36
  494.0 12.6 %collective-permute-done.42 = bf16[528,512]{1,0:T(8,128)(2,1)S(1)} collective-permute-done((bf16[528,512]{1,0:T(8,128)(2,1)S(1)}, bf16[528,512]{1,0:T(8,128)(2,1)S(1)}, u32[]{:S(2)}, u32[]{:S(2)}) %collective-permute-start.42) | collective-permute-done | bytes 540704 | tf_op jit(solution)/shard_map/ppermute | solution.py:36
  507.1 14.4 %shard_map.259 = bf16[4,4,512,512]{3,2,1,0:T(8,128)(2,1)} custom-call(s32[3]{0:T(128)S(1)} %copy-done.9, bf16[2048,1024]{1,0:T(8,128)(2,1)} %get-tuple-element.153.hid_ref.refs_0_, bf16[4,4,256,256]{3,2,1,0:T(8,128)(2,1)S(1)} %copy-done.1, bf16[4,4,256,256]{3,2,1,0:T(8,128)(2,1)} %collective-permute-done.32.refs_10_.refs_2_), custom_call_target="tpu_custom_call" | custom-call | flops 8589934592 | bytes 16777216 | tf_op jit(solution)/shard_map/pallas_call | solution.py:388
  521.5 9.3 %collective-permute-done.43 = bf16[2,528,512]{2,1,0:T(8,128)(2,1)} collective-permute-done((bf16[2,528,512]{2,1,0:T(8,128)(2,1)S(1)}, bf16[2,528,512]{2,1,0:T(8,128)(2,1)}, u32[]{:S(2)}, u32[]{:S(2)}) %collective-permute-start.43) | collective-permute-done | bytes 1081376 | tf_op jit(solution)/shard_map/ppermute | solution.py:36
  533.3 20.2 %collective-permute-done.46 = bf16[528,512]{1,0:T(8,128)(2,1)S(1)} collective-permute-done((bf16[528,512]{1,0:T(8,128)(2,1)S(1)}, bf16[528,512]{1,0:T(8,128)(2,1)S(1)}, u32[]{:S(2)}, u32[]{:S(2)}) %collective-permute-start.46) | collective-permute-done | bytes 540704 | tf_op jit(solution)/shard_map/ppermute | solution.py:36
  558.9 20.2 %collective-permute-done.45 = bf16[528,512]{1,0:T(8,128)(2,1)} collective-permute-done((bf16[528,512]{1,0:T(8,128)(2,1)}, bf16[528,512]{1,0:T(8,128)(2,1)}, u32[]{:S(2)}, u32[]{:S(2)}) %collective-permute-start.45) | collective-permute-done | bytes 540704 | tf_op jit(solution)/shard_map/ppermute | solution.py:36
  587.1 3.5 collective-permute-done.49
  593.8 8.5 collective-permute-done.50
  602.3 6.2 collective-permute-done.51
  610.0 5.9 add_convert_fusion
  654.3 44.1 %collective-permute-done.56.refs_1_ = bf16[2,4,256,256]{3,2,1,0:T(8,128)(2,1)S(1)} collective-permute-done((bf16[2,4,256,256]{3,2,1,0:T(8,128)(2,1)}, bf16[2,4,256,256]{3,2,1,0:T(8,128)(2,1)S(1)}, u32[]{:S(2)}, u32[]{:S(2)}) %collective-permute-start.56) | collective-permute-done | bytes 1048608 | tf_op jit(solution)/shard_map/ppermute | solution.py:36
  698.4 35.1 %collective-permute-done.57.refs_2_ = bf16[2,4,256,256]{3,2,1,0:T(8,128)(2,1)} collective-permute-done((bf16[2,4,256,256]{3,2,1,0:T(8,128)(2,1)}, bf16[2,4,256,256]{3,2,1,0:T(8,128)(2,1)}, u32[]{:S(2)}, u32[]{:S(2)}) %collective-permute-start.57) | collective-permute-done | bytes 1048608 | tf_op jit(solution)/shard_map/ppermute | solution.py:36
  733.6 5.6 convolution_convert_fusion
  739.2 6.7 fusion.6
  748.8 6.7 collective-permute-done.65
  765.6 14.0 %collective-permute-start.59 = (bf16[2,512,512]{2,1,0:T(8,128)(2,1)}, bf16[2,512,512]{2,1,0:T(8,128)(2,1)}, u32[]{:S(2)}, u32[]{:S(2)}) collective-permute-start(bf16[2,512,512]{2,1,0:T(8,128)(2,1)} %pad_maximum_fusion.7), channel_id=1, source_target_pairs={{0,8},{8,0},{16,24},{24,16},{1,9},{9,1},{17,25},{25,17},{2,10},{10... | collective-permute-start | bytes 3145736 | tf_op jit(solution)/shard_map/ppermute | solution.py:36
  789.6 6.9 shard_map.260
  797.4 28.6 %collective-permute-done.76 = f32[20,512]{1,0:T(8,128)S(1)} collective-permute-done((f32[20,512]{1,0:T(8,128)S(1)}, f32[20,512]{1,0:T(8,128)S(1)}, u32[]{:S(2)}, u32[]{:S(2)}) %collective-permute-start.76) | collective-permute-done | bytes 40992 | tf_op jit(solution)/shard_map/ppermute | solution.py:36
  826.0 3.5 collective-permute-start.77
  833.0 3.7 collective-permute-done.77
  847.0 9.0 %collective-permute-done.60 = bf16[1,512,512]{2,1,0:T(8,128)(2,1)S(1)} collective-permute-done((bf16[1,512,512]{2,1,0:T(8,128)(2,1)S(1)}, bf16[1,512,512]{2,1,0:T(8,128)(2,1)S(1)}, u32[]{:S(2)}, u32[]{:S(2)}) %collective-permute-start.60) | collective-permute-done | bytes 524320 | tf_op jit(solution)/shard_map/ppermute | solution.py:36
  864.1 6.6 collective-permute-done.61
  (468 shorter events, 221.4 us)
Async XLA Ops:
  7.2 76.4 %all-gather.5.cloned.1.call-start = ((), (), s32[]{:S(2)}) async-start(), calls=%async_computation.3 | async-start | bytes 7667712 | tf_op jit(solution)/shard_map/all_gather | solution.py:550
  11.6 126.0 %all-gather.7.cloned.1.call-start = ((), (), s32[]{:S(2)}) async-start(), calls=%async_computation.4 | async-start | bytes 2359296 | tf_op jit(solution)/shard_map/all_gather | solution.py:565
  84.9 284.8 %all-gather.9.cloned.1.call-start = ((), (), s32[]{:S(2)}) async-start(), calls=%async_computation.7 | async-start | bytes 10485760 | tf_op jit(solution)/shard_map/all_gather | solution.py:605
  96.9 37.7 %collective-permute-start.6 = (bf16[512,512]{1,0:T(8,128)(2,1)}, bf16[512,512]{1,0:T(8,128)(2,1)}, u32[]{:S(2)}, u32[]{:S(2)}) collective-permute-start(bf16[512,512]{1,0:T(8,128)(2,1)} %constant_dynamic-slice_fusion.12), channel_id=1, source_target_pairs={{0,16},{8,24},{16,0},{24,8},{1,17},{9,25},{17,1},{25,9},{2,18},{10... | collective-permute-start | bytes 1572872 | tf_op jit(solution)/shard_map/ppermute | solution.py:36
  98.0 44.0 %collective-permute-start.5 = (bf16[512,512]{1,0:T(8,128)(2,1)}, bf16[512,512]{1,0:T(8,128)(2,1)}, u32[]{:S(2)}, u32[]{:S(2)}) collective-permute-start(bf16[512,512]{1,0:T(8,128)(2,1)} %constant_dynamic-slice_fusion.12), channel_id=1, source_target_pairs={{0,8},{8,0},{16,24},{24,16},{1,9},{9,1},{17,25},{25,17},{2,10},{10... | collective-permute-start | bytes 1572872 | tf_op jit(solution)/shard_map/ppermute | solution.py:36
  151.4 611.7 %reduce-scatter.10.cloned.1.call-start = ((), (), s32[]{:S(2)}) async-start(), calls=%async_computation.8 | async-start | bytes 10485760
  153.5 19.9 %collective-permute-start.8 = (bf16[2,256,512]{2,1,0:T(8,128)(2,1)S(1)}, bf16[2,256,512]{2,1,0:T(8,128)(2,1)}, u32[]{:S(2)}, u32[]{:S(2)}) collective-permute-start(bf16[2,256,512]{2,1,0:T(8,128)(2,1)S(1)} %pad_maximum_fusion.9), channel_id=1, source_target_pairs={{0,1},{1,0},{2,3},{3,2},{4,5},{5,4},{6,7},{7,6},{8,9},{9,8},{10,11... | collective-permute-start | bytes 1572872 | tf_op jit(solution)/shard_map/ppermute | solution.py:36
  155.8 24.4 %collective-permute-start.10 = (bf16[2,256,512]{2,1,0:T(8,128)(2,1)}, bf16[2,256,512]{2,1,0:T(8,128)(2,1)}, u32[]{:S(2)}, u32[]{:S(2)}) collective-permute-start(bf16[2,256,512]{2,1,0:T(8,128)(2,1)} %pad_maximum_fusion.10), channel_id=1, source_target_pairs={{0,2},{1,3},{2,0},{3,1},{4,6},{5,7},{6,4},{7,5},{8,10},{9,11},{10,... | collective-permute-start | bytes 1572872 | tf_op jit(solution)/shard_map/ppermute | solution.py:36
  181.7 21.2 %collective-permute-start.14 = (bf16[4,256,256]{2,1,0:T(8,128)(2,1)S(1)}, bf16[4,256,256]{2,1,0:T(8,128)(2,1)S(1)}, u32[]{:S(2)}, u32[]{:S(2)}) collective-permute-start(bf16[4,256,256]{2,1,0:T(8,128)(2,1)S(1)} %get-tuple-element.232), channel_id=1, source_target_pairs={{0,8},{8,0},{16,24},{24,16},{1,9},{9,1},{17,25},{25,17},{2,10},{10... | collective-permute-start | bytes 1572872 | tf_op jit(solution)/shard_map/ppermute | solution.py:36
  181.8 32.0 %collective-permute-start.15 = (bf16[4,256,256]{2,1,0:T(8,128)(2,1)S(1)}, bf16[4,256,256]{2,1,0:T(8,128)(2,1)S(1)}, u32[]{:S(2)}, u32[]{:S(2)}) collective-permute-start(bf16[4,256,256]{2,1,0:T(8,128)(2,1)S(1)} %get-tuple-element.231), channel_id=1, source_target_pairs={{0,16},{8,24},{16,0},{24,8},{1,17},{9,25},{17,1},{25,9},{2,18},{10... | collective-permute-start | bytes 1572872 | tf_op jit(solution)/shard_map/ppermute | solution.py:36
  181.9 31.9 %collective-permute-start.16 = (bf16[4,256,256]{2,1,0:T(8,128)(2,1)S(1)}, bf16[4,256,256]{2,1,0:T(8,128)(2,1)S(1)}, u32[]{:S(2)}, u32[]{:S(2)}) collective-permute-start(bf16[4,256,256]{2,1,0:T(8,128)(2,1)S(1)} %get-tuple-element.230), channel_id=1, source_target_pairs={{0,24},{8,16},{16,8},{24,0},{1,25},{9,17},{17,9},{25,1},{2,26},{10... | collective-permute-start | bytes 1572872 | tf_op jit(solution)/shard_map/ppermute | solution.py:36
  213.8 30.0 %collective-permute-start.18 = (bf16[512,512]{1,0:T(8,128)(2,1)S(1)}, bf16[512,512]{1,0:T(8,128)(2,1)S(1)}, u32[]{:S(2)}, u32[]{:S(2)}) collective-permute-start(bf16[512,512]{1,0:T(8,128)(2,1)S(1)} %multiply_convert_fusion.2), channel_id=1, source_target_pairs={{0,16},{8,24},{16,0},{24,8},{1,17},{9,25},{17,1},{25,9},{2,18},{10... | collective-permute-start | bytes 1572872 | tf_op jit(solution)/shard_map/ppermute | solution.py:36
  229.6 18.0 %collective-permute-start.17 = (bf16[512,512]{1,0:T(8,128)(2,1)S(1)}, bf16[512,512]{1,0:T(8,128)(2,1)S(1)}, u32[]{:S(2)}, u32[]{:S(2)}) collective-permute-start(bf16[512,512]{1,0:T(8,128)(2,1)S(1)} %multiply_convert_fusion.2), channel_id=1, source_target_pairs={{0,8},{8,0},{16,24},{24,16},{1,9},{9,1},{17,25},{25,17},{2,10},{10... | collective-permute-start | bytes 1572872 | tf_op jit(solution)/shard_map/ppermute | solution.py:36
  255.4 44.2 %collective-permute-start.20 = (bf16[2048,512]{1,0:T(8,128)(2,1)S(1)}, bf16[2048,512]{1,0:T(8,128)(2,1)S(1)}, u32[]{:S(2)}, u32[]{:S(2)}) collective-permute-start(bf16[2048,512]{1,0:T(8,128)(2,1)S(1)} %constant_dynamic-update-slice_fusion.9), channel_id=1, source_target_pairs={{0,1},{1,0},{2,3},{3,2},{4,5},{5,4},{6,7},{7,6},{8,9},{9,8},{10,11... | collective-permute-start | bytes 6291464 | tf_op jit(solution)/shard_map/ppermute | solution.py:36
  256.3 43.8 %collective-permute-start.21 = (bf16[2048,512]{1,0:T(8,128)(2,1)S(1)}, bf16[2048,512]{1,0:T(8,128)(2,1)S(1)}, u32[]{:S(2)}, u32[]{:S(2)}) collective-permute-start(bf16[2048,512]{1,0:T(8,128)(2,1)S(1)} %constant_dynamic-update-slice_fusion.9), channel_id=1, source_target_pairs={{0,2},{1,3},{2,0},{3,1},{4,6},{5,7},{6,4},{7,5},{8,10},{9,11},{10,... | collective-permute-start | bytes 6291464 | tf_op jit(solution)/shard_map/ppermute | solution.py:36
  259.0 23.1 %collective-permute-start.22 = (bf16[4,256,256]{2,1,0:T(8,128)(2,1)S(1)}, bf16[4,256,256]{2,1,0:T(8,128)(2,1)S(1)}, u32[]{:S(2)}, u32[]{:S(2)}) collective-permute-start(bf16[4,256,256]{2,1,0:T(8,128)(2,1)S(1)} %get-tuple-element.228), channel_id=1, source_target_pairs={{0,8},{8,0},{16,24},{24,16},{1,9},{9,1},{17,25},{25,17},{2,10},{10... | collective-permute-start | bytes 1572872 | tf_op jit(solution)/shard_map/ppermute | solution.py:36
  260.4 36.4 %collective-permute-start.23 = (bf16[4,256,256]{2,1,0:T(8,128)(2,1)S(1)}, bf16[4,256,256]{2,1,0:T(8,128)(2,1)S(1)}, u32[]{:S(2)}, u32[]{:S(2)}) collective-permute-start(bf16[4,256,256]{2,1,0:T(8,128)(2,1)S(1)} %get-tuple-element.227), channel_id=1, source_target_pairs={{0,16},{8,24},{16,0},{24,8},{1,17},{9,25},{17,1},{25,9},{2,18},{10... | collective-permute-start | bytes 1572872 | tf_op jit(solution)/shard_map/ppermute | solution.py:36
  270.2 26.6 %collective-permute-start.24 = (bf16[4,256,256]{2,1,0:T(8,128)(2,1)S(1)}, bf16[4,256,256]{2,1,0:T(8,128)(2,1)S(1)}, u32[]{:S(2)}, u32[]{:S(2)}) collective-permute-start(bf16[4,256,256]{2,1,0:T(8,128)(2,1)S(1)} %get-tuple-element.226), channel_id=1, source_target_pairs={{0,24},{8,16},{16,8},{24,0},{1,25},{9,17},{17,9},{25,1},{2,26},{10... | collective-permute-start | bytes 1572872 | tf_op jit(solution)/shard_map/ppermute | solution.py:36
  282.1 57.8 %collective-permute-start.28 = (bf16[4,4,256,256]{3,2,1,0:T(8,128)(2,1)}, bf16[4,4,256,256]{3,2,1,0:T(8,128)(2,1)}, u32[]{:S(2)}, u32[]{:S(2)}) collective-permute-start(bf16[4,4,256,256]{3,2,1,0:T(8,128)(2,1)} %pad_maximum_fusion.2.refs_3_.refs_5_), channel_id=1, source_target_pairs={{0,4},{4,0},{1,5},{5,1},{2,6},{6,2},{3,7},{7,3},{8,12},{12,8},{9,1... | collective-permute-start | bytes 6291464 | tf_op jit(solution)/shard_map/ppermute | solution.py:36
  301.9 38.0 %collective-permute-start.29 = (bf16[4,4,256,256]{3,2,1,0:T(8,128)(2,1)}, bf16[4,4,256,256]{3,2,1,0:T(8,128)(2,1)}, u32[]{:S(2)}, u32[]{:S(2)}) collective-permute-start(bf16[4,4,256,256]{3,2,1,0:T(8,128)(2,1)} %pad_maximum_fusion.1.refs_5_.refs_7_), channel_id=1, source_target_pairs={{0,4},{4,0},{1,5},{5,1},{2,6},{6,2},{3,7},{7,3},{8,12},{12,8},{9,1... | collective-permute-start | bytes 6291464 | tf_op jit(solution)/shard_map/ppermute | solution.py:36
  303.0 25.9 %collective-permute-start.25 = (bf16[1024,512]{1,0:T(8,128)(2,1)}, bf16[1024,512]{1,0:T(8,128)(2,1)}, u32[]{:S(2)}, u32[]{:S(2)}) collective-permute-start(bf16[1024,512]{1,0:T(8,128)(2,1)} %slice.326), channel_id=1, source_target_pairs={{0,2},{1,3},{2,0},{3,1},{4,6},{5,7},{6,4},{7,5},{8,10},{9,11},{10,... | collective-permute-start | bytes 3145736 | tf_op jit(solution)/shard_map/ppermute | solution.py:36
  305.7 26.5 %collective-permute-start.26 = (bf16[1024,512]{1,0:T(8,128)(2,1)}, bf16[1024,512]{1,0:T(8,128)(2,1)}, u32[]{:S(2)}, u32[]{:S(2)}) collective-permute-start(bf16[1024,512]{1,0:T(8,128)(2,1)} %slice.327), channel_id=1, source_target_pairs={{0,1},{1,0},{2,3},{3,2},{4,5},{5,4},{6,7},{7,6},{8,9},{9,8},{10,11... | collective-permute-start | bytes 3145736 | tf_op jit(solution)/shard_map/ppermute | solution.py:36
  310.5 29.4 %collective-permute-start.27 = (bf16[4,256,256]{2,1,0:T(8,128)(2,1)S(1)}, bf16[4,256,256]{2,1,0:T(8,128)(2,1)S(1)}, u32[]{:S(2)}, u32[]{:S(2)}) collective-permute-start(bf16[4,256,256]{2,1,0:T(8,128)(2,1)S(1)} %get-tuple-element.225), channel_id=1, source_target_pairs={{0,16},{8,24},{16,0},{24,8},{1,17},{9,25},{17,1},{25,9},{2,18},{10... | collective-permute-start | bytes 1572872 | tf_op jit(solution)/shard_map/ppermute | solution.py:36
  328.8 39.8 %collective-permute-start.30 = (bf16[4,256,256]{2,1,0:T(8,128)(2,1)S(1)}, bf16[4,256,256]{2,1,0:T(8,128)(2,1)S(1)}, u32[]{:S(2)}, u32[]{:S(2)}) collective-permute-start(bf16[4,256,256]{2,1,0:T(8,128)(2,1)S(1)} %get-tuple-element.223), channel_id=1, source_target_pairs={{0,8},{8,0},{16,24},{24,16},{1,9},{9,1},{17,25},{25,17},{2,10},{10... | collective-permute-start | bytes 1572872 | tf_op jit(solution)/shard_map/ppermute | solution.py:36
  332.2 36.5 %collective-permute-start.31 = (bf16[4,256,256]{2,1,0:T(8,128)(2,1)S(1)}, bf16[4,256,256]{2,1,0:T(8,128)(2,1)S(1)}, u32[]{:S(2)}, u32[]{:S(2)}) collective-permute-start(bf16[4,256,256]{2,1,0:T(8,128)(2,1)S(1)} %get-tuple-element.222), channel_id=1, source_target_pairs={{0,24},{8,16},{16,8},{24,0},{1,25},{9,17},{17,9},{25,1},{2,26},{10... | collective-permute-start | bytes 1572872 | tf_op jit(solution)/shard_map/ppermute | solution.py:36
  383.2 31.5 %collective-permute-start.35 = (bf16[4,4,256,256]{3,2,1,0:T(8,128)(2,1)S(1)}, bf16[4,4,256,256]{3,2,1,0:T(8,128)(2,1)}, u32[]{:S(2)}, u32[]{:S(2)}) collective-permute-start(bf16[4,4,256,256]{3,2,1,0:T(8,128)(2,1)S(1)} %get-tuple-element.133), channel_id=1, source_target_pairs={{0,4},{4,0},{1,5},{5,1},{2,6},{6,2},{3,7},{7,3},{8,12},{12,8},{9,1... | collective-permute-start | bytes 6291464 | tf_op jit(solution)/shard_map/ppermute | solution.py:36
  413.2 34.7 %collective-permute-start.33 = (bf16[2,528,512]{2,1,0:T(8,128)(2,1)}, bf16[2,528,512]{2,1,0:T(8,128)(2,1)S(1)}, u32[]{:S(2)}, u32[]{:S(2)}) collective-permute-start(bf16[2,528,512]{2,1,0:T(8,128)(2,1)} %get-tuple-element.205), channel_id=1, source_target_pairs={{0,1},{1,0},{2,3},{3,2},{4,5},{5,4},{6,7},{7,6},{8,9},{9,8},{10,11... | collective-permute-start | bytes 3244040 | tf_op jit(solution)/shard_map/ppermute | solution.py:36
  413.6 34.4 %collective-permute-start.34 = (bf16[2,528,512]{2,1,0:T(8,128)(2,1)}, bf16[2,528,512]{2,1,0:T(8,128)(2,1)S(1)}, u32[]{:S(2)}, u32[]{:S(2)}) collective-permute-start(bf16[2,528,512]{2,1,0:T(8,128)(2,1)} %get-tuple-element.204), channel_id=1, source_target_pairs={{0,2},{1,3},{2,0},{3,1},{4,6},{5,7},{6,4},{7,5},{8,10},{9,11},{10,... | collective-permute-start | bytes 3244040 | tf_op jit(solution)/shard_map/ppermute | solution.py:36
  417.1 30.8 %collective-permute-start.36 = (bf16[4,256,256]{2,1,0:T(8,128)(2,1)S(1)}, bf16[4,256,256]{2,1,0:T(8,128)(2,1)S(1)}, u32[]{:S(2)}, u32[]{:S(2)}) collective-permute-start(bf16[4,256,256]{2,1,0:T(8,128)(2,1)S(1)} %get-tuple-element.220), channel_id=1, source_target_pairs={{0,8},{8,0},{16,24},{24,16},{1,9},{9,1},{17,25},{25,17},{2,10},{10... | collective-permute-start | bytes 1572872 | tf_op jit(solution)/shard_map/ppermute | solution.py:36
  418.3 29.6 %collective-permute-start.37 = (bf16[4,256,256]{2,1,0:T(8,128)(2,1)S(1)}, bf16[4,256,256]{2,1,0:T(8,128)(2,1)S(1)}, u32[]{:S(2)}, u32[]{:S(2)}) collective-permute-start(bf16[4,256,256]{2,1,0:T(8,128)(2,1)S(1)} %get-tuple-element.219), channel_id=1, source_target_pairs={{0,16},{8,24},{16,0},{24,8},{1,17},{9,25},{17,1},{25,9},{2,18},{10... | collective-permute-start | bytes 1572872 | tf_op jit(solution)/shard_map/ppermute | solution.py:36
  446.2 31.5 %collective-permute-start.40 = (bf16[4,256,256]{2,1,0:T(8,128)(2,1)S(1)}, bf16[4,256,256]{2,1,0:T(8,128)(2,1)S(1)}, u32[]{:S(2)}, u32[]{:S(2)}) collective-permute-start(bf16[4,256,256]{2,1,0:T(8,128)(2,1)S(1)} %get-tuple-element.218), channel_id=1, source_target_pairs={{0,24},{8,16},{16,8},{24,0},{1,25},{9,17},{17,9},{25,1},{2,26},{10... | collective-permute-start | bytes 1572872 | tf_op jit(solution)/shard_map/ppermute | solution.py:36
  450.9 26.8 %collective-permute-start.38 = (bf16[2,528,512]{2,1,0:T(8,128)(2,1)}, bf16[2,528,512]{2,1,0:T(8,128)(2,1)S(1)}, u32[]{:S(2)}, u32[]{:S(2)}) collective-permute-start(bf16[2,528,512]{2,1,0:T(8,128)(2,1)} %get-tuple-element.203), channel_id=1, source_target_pairs={{0,1},{1,0},{2,3},{3,2},{4,5},{5,4},{6,7},{7,6},{8,9},{9,8},{10,11... | collective-permute-start | bytes 3244040 | tf_op jit(solution)/shard_map/ppermute | solution.py:36
  451.9 25.9 %collective-permute-start.39 = (bf16[2,528,512]{2,1,0:T(8,128)(2,1)S(1)}, bf16[2,528,512]{2,1,0:T(8,128)(2,1)S(1)}, u32[]{:S(2)}, u32[]{:S(2)}) collective-permute-start(bf16[2,528,512]{2,1,0:T(8,128)(2,1)S(1)} %get-tuple-element.202), channel_id=1, source_target_pairs={{0,2},{1,3},{2,0},{3,1},{4,6},{5,7},{6,4},{7,5},{8,10},{9,11},{10,... | collective-permute-start | bytes 3244040 | tf_op jit(solution)/shard_map/ppermute | solution.py:36
  477.8 53.0 %collective-permute-start.44 = (bf16[4,2,4,256,256]{4,3,2,1,0:T(8,128)(2,1)}, bf16[4,2,4,256,256]{4,3,2,1,0:T(8,128)(2,1)}, u32[]{:S(2)}, u32[]{:S(2)}) collective-permute-start(bf16[4,2,4,256,256]{4,3,2,1,0:T(8,128)(2,1)} %get-tuple-element.152), channel_id=1, source_target_pairs={{0,4},{4,0},{1,5},{5,1},{2,6},{6,2},{3,7},{7,3},{8,12},{12,8},{9,1... | collective-permute-start | bytes 12582920 | tf_op jit(solution)/shard_map/ppermute | solution.py:36
  507.0 23.8 %collective-permute-start.43 = (bf16[2,528,512]{2,1,0:T(8,128)(2,1)S(1)}, bf16[2,528,512]{2,1,0:T(8,128)(2,1)}, u32[]{:S(2)}, u32[]{:S(2)}) collective-permute-start(bf16[2,528,512]{2,1,0:T(8,128)(2,1)S(1)} %pad_maximum_fusion.6), channel_id=1, source_target_pairs={{0,8},{8,0},{16,24},{24,16},{1,9},{9,1},{17,25},{25,17},{2,10},{10... | collective-permute-start | bytes 3244040 | tf_op jit(solution)/shard_map/ppermute | solution.py:36
  530.8 331.3 %reduce-scatter.8.cloned.1.call-start = ((), (), s32[]{:S(2)}) async-start(), calls=%async_computation.6 | async-start | bytes 2359296 | tf_op jit(solution)/shard_map/reduce_scatter | solution.py:731
  532.5 21.0 %collective-permute-start.46 = (bf16[528,512]{1,0:T(8,128)(2,1)S(1)}, bf16[528,512]{1,0:T(8,128)(2,1)S(1)}, u32[]{:S(2)}, u32[]{:S(2)}) collective-permute-start(bf16[528,512]{1,0:T(8,128)(2,1)S(1)} %fusion.14), channel_id=1, source_target_pairs={{0,1},{1,0},{2,3},{3,2},{4,5},{5,4},{6,7},{7,6},{8,9},{9,8},{10,11... | collective-permute-start | bytes 1622024 | tf_op jit(solution)/shard_map/ppermute | solution.py:36
  556.4 22.7 %collective-permute-start.45 = (bf16[528,512]{1,0:T(8,128)(2,1)}, bf16[528,512]{1,0:T(8,128)(2,1)}, u32[]{:S(2)}, u32[]{:S(2)}) collective-permute-start(bf16[528,512]{1,0:T(8,128)(2,1)} %get-tuple-element.199), channel_id=1, source_target_pairs={{0,2},{1,3},{2,0},{3,1},{4,6},{5,7},{6,4},{7,5},{8,10},{9,11},{10,... | collective-permute-start | bytes 1622024 | tf_op jit(solution)/shard_map/ppermute | solution.py:36
  556.4 22.7 %collective-permute-start.47 = (bf16[1,528,512]{2,1,0:T(8,128)(2,1)}, bf16[1,528,512]{2,1,0:T(8,128)(2,1)}, u32[]{:S(2)}, u32[]{:S(2)}) collective-permute-start(bf16[1,528,512]{2,1,0:T(8,128)(2,1)} %get-tuple-element.198), channel_id=1, source_target_pairs={{0,16},{8,24},{16,0},{24,8},{1,17},{9,25},{17,1},{25,9},{2,18},{10... | collective-permute-start | bytes 1622024 | tf_op jit(solution)/shard_map/ppermute | solution.py:36
  628.6 244.8 %reduce-scatter.6.cloned.1.call-start = ((), (), s32[]{:S(2)}) async-start(), calls=%async_computation.5 | async-start | bytes 7077888 | tf_op jit(solution)/shard_map/reduce_scatter | solution.py:730
  643.4 55.1 %collective-permute-start.56 = (bf16[2,4,256,256]{3,2,1,0:T(8,128)(2,1)}, bf16[2,4,256,256]{3,2,1,0:T(8,128)(2,1)S(1)}, u32[]{:S(2)}, u32[]{:S(2)}) collective-permute-start(bf16[2,4,256,256]{3,2,1,0:T(8,128)(2,1)} %get-tuple-element.208), channel_id=1, source_target_pairs={{0,8},{8,0},{16,24},{24,16},{1,9},{9,1},{17,25},{25,17},{2,10},{10... | collective-permute-start | bytes 3145736 | tf_op jit(solution)/shard_map/ppermute | solution.py:36
  644.2 89.4 %collective-permute-start.57 = (bf16[2,4,256,256]{3,2,1,0:T(8,128)(2,1)}, bf16[2,4,256,256]{3,2,1,0:T(8,128)(2,1)}, u32[]{:S(2)}, u32[]{:S(2)}) collective-permute-start(bf16[2,4,256,256]{3,2,1,0:T(8,128)(2,1)} %get-tuple-element.207), channel_id=1, source_target_pairs={{0,16},{8,24},{16,0},{24,8},{1,17},{9,25},{17,1},{25,9},{2,18},{10... | collective-permute-start | bytes 3145736 | tf_op jit(solution)/shard_map/ppermute | solution.py:36
  646.6 87.0 %collective-permute-start.58 = (bf16[2,4,256,256]{3,2,1,0:T(8,128)(2,1)}, bf16[2,4,256,256]{3,2,1,0:T(8,128)(2,1)}, u32[]{:S(2)}, u32[]{:S(2)}) collective-permute-start(bf16[2,4,256,256]{3,2,1,0:T(8,128)(2,1)} %get-tuple-element.206), channel_id=1, source_target_pairs={{0,24},{8,16},{16,8},{24,0},{1,25},{9,17},{17,9},{25,1},{2,26},{10... | collective-permute-start | bytes 3145736 | tf_op jit(solution)/shard_map/ppermute | solution.py:36
  759.4 20.2 %collective-permute-start.68 = (bf16[256,512]{1,0:T(8,128)(2,1)}, bf16[256,512]{1,0:T(8,128)(2,1)S(1)}, u32[]{:S(2)}, u32[]{:S(2)}) collective-permute-start(bf16[256,512]{1,0:T(8,128)(2,1)} %fusion.51), channel_id=1, source_target_pairs={{0,1},{1,0},{2,3},{3,2},{4,5},{5,4},{6,7},{7,6},{8,9},{9,8},{10,11... | collective-permute-start | bytes 786440 | tf_op jit(solution)/shard_map/ppermute | solution.py:36
  765.6 71.8 %collective-permute-start.59 = (bf16[2,512,512]{2,1,0:T(8,128)(2,1)}, bf16[2,512,512]{2,1,0:T(8,128)(2,1)}, u32[]{:S(2)}, u32[]{:S(2)}) collective-permute-start(bf16[2,512,512]{2,1,0:T(8,128)(2,1)} %pad_maximum_fusion.7), channel_id=1, source_target_pairs={{0,8},{8,0},{16,24},{24,16},{1,9},{9,1},{17,25},{25,17},{2,10},{10... | collective-permute-start | bytes 3145736 | tf_op jit(solution)/shard_map/ppermute | solution.py:36
  796.5 29.5 %collective-permute-start.76 = (f32[20,512]{1,0:T(8,128)S(1)}, f32[20,512]{1,0:T(8,128)S(1)}, u32[]{:S(2)}, u32[]{:S(2)}) collective-permute-start(f32[20,512]{1,0:T(8,128)S(1)} %add.352), channel_id=1, source_target_pairs={{0,8},{8,0},{16,24},{24,16},{1,9},{9,1},{17,25},{25,17},{2,10},{10... | collective-permute-start | bytes 122888 | tf_op jit(solution)/shard_map/ppermute | solution.py:36
  838.6 17.5 %collective-permute-start.60 = (bf16[1,512,512]{2,1,0:T(8,128)(2,1)S(1)}, bf16[1,512,512]{2,1,0:T(8,128)(2,1)S(1)}, u32[]{:S(2)}, u32[]{:S(2)}) collective-permute-start(bf16[1,512,512]{2,1,0:T(8,128)(2,1)S(1)} %add_convert_fusion.3), channel_id=1, source_target_pairs={{0,16},{8,24},{16,0},{24,8},{1,17},{9,25},{17,1},{25,9},{2,18},{10... | collective-permute-start | bytes 1572872 | tf_op jit(solution)/shard_map/ppermute | solution.py:36
  845.9 16.1 %collective-permute-start.73 = (bf16[256,512]{1,0:T(8,128)(2,1)S(1)}, bf16[256,512]{1,0:T(8,128)(2,1)S(1)}, u32[]{:S(2)}, u32[]{:S(2)}) collective-permute-start(bf16[256,512]{1,0:T(8,128)(2,1)S(1)} %slice.450), channel_id=1, source_target_pairs={{0,2},{1,3},{2,0},{3,1},{4,6},{5,7},{6,4},{7,5},{8,10},{9,11},{10,... | collective-permute-start | bytes 786440 | tf_op jit(solution)/shard_map/ppermute | solution.py:36
  (119 other events, 1517.5 us)
Sparse Core Ops, SparseCore 0:
  11.8 71.7 all-gather.4
  85.2 46.3 all-gather.6
  151.6 95.4 all-gather.8
  531.0 107.9 reduce-scatter.9
  641.2 55.1 reduce-scatter.7
  739.3 110.7 reduce-scatter.5

commit v3 on v2

--- a/solution.py
+++ b/solution.py
@@ -26,7 +26,7 @@
 
 
 def fence(*values):
-    return lax.optimization_barrier(values)
+    return list(lax.optimization_barrier(values))
 
 
 def swap(value, axis, mask):
@@ -88,6 +88,19 @@
 def spread_tensor_near(value):
     n = lax.axis_size("tensor")
     return [swap(value, "tensor", k) for k in ((1, 2) if n == 4 else range(1, n))]
+
+
+def spread_tensor_cross(near):
+    if lax.axis_size("tensor") != 4:
+        return []
+    half = near[0].shape[0] // 2
+    return [swap(near[0][:half], "tensor", 2), swap(near[1][half:], "tensor", 1)]
+
+
+def place_of(n, half, k, row):
+    if n != 4 or k < 3:
+        return (k, row)
+    return (3, row) if row < half else (4, row - half)
 
 
 def spread_tensor_far(value, near):
@@ -152,16 +165,19 @@
     return parts[0]
 
 
-def scatter_columns(value):
+def columns_blocks(value):
     me, n = lax.axis_index("tensor"), lax.axis_size("tensor")
     rows, width = value.shape[0], value.shape[1] // n
     half = rows // 2
-    outs = []
-    for odd in (0, 1):
-        part = value[odd * half : (odd + 1) * half]
-        block = jnp.stack([columns(part, me ^ k, width) for k in order_of(n, odd)])
-        outs.append(scatter_third(*scatter_second(block, scatter_first(block, odd), odd)))
-    return jnp.concatenate(outs, 0)
+    return [
+        jnp.stack(
+            [
+                columns(value[odd * half : (odd + 1) * half], me ^ k, width)
+                for k in order_of(n, odd)
+            ]
+        )
+        for odd in (0, 1)
+    ]
 
 
 def dot_nn(a, b):
@@ -176,19 +192,28 @@
     return lax.dot_general(a, b, (((0,), (0,)), ((), ())), preferred_element_type=f32)
 
 
-def load_weights(nz, slice_d, me_z, me_c, pairs, sems, along_last):
+def weight_copies(nz, slice_d, own_e, idx, parts, whole, sems, down):
     copies = []
-    for w, (parts, whole) in enumerate(pairs):
-        for c in range(2):
-            for k in range(nz):
-                j = c * nz + k
-                at = pl.ds(pl.multiple_of((me_c ^ c) * slice_d, slice_d), slice_d)
-                target = (
-                    whole.at[me_z ^ k, :, :, at] if along_last[w] else whole.at[me_z ^ k, :, at, :]
-                )
-                copies.append(pltpu.make_async_copy(parts[c].at[k], target, sems.at[w, j]))
+    for c in range(2):
+        for k in range(nz):
+            half = pl.multiple_of((idx[1] ^ c) * slice_d, slice_d)
+            at = pl.multiple_of((idx[0] ^ k ^ idx[2]) * 2 * slice_d, slice_d) + half
+            if down:
+                copies.append((parts[c].at[k], whole.at[:, :, pl.ds(at, slice_d)]))
+            else:
+                hid = whole.shape[1] // own_e
+                for e in range(own_e):
+                    target = whole.at[pl.ds(at, slice_d), pl.ds(e * hid, hid)]
+                    copies.append((parts[c].at[k, e], target))
+    return [pltpu.make_async_copy(*pair, sems.at[j]) for j, pair in enumerate(copies)]
+
+
+def start(copies):
     for copy in copies:
         copy.start()
+
+
+def finish(copies):
     for copy in copies:
         copy.wait()
 
@@ -197,67 +222,106 @@
     return jnp.sum(jnp.where(lane == FIRST + me_z * own_e + e, gates, 0.0), -1, keepdims=True)
 
 
-def forward_kernel(nz, n, own_e, hid, slice_d, idx, *refs):
-    m_ref, mask_ref, router_ref = refs[:3]
-    act_ref, up_ref, hid_ref, probs_ref, w_gate, w_up, sems = refs[7:]
-    me_z, me_c, me_t = idx[0], idx[1], idx[2]
-
-    @pl.when(pl.program_id(0) == 0)
+def forward_kernel(nz, n, own_e, hid, slice_d, seq, quarter, places, idx, *refs):
+    mask_ref, router_ref = refs[:2]
+    gate_parts, up_parts, m_refs = refs[2:4], refs[4:6], refs[6:-11]
+    act_ref, up_ref, hid_ref, probs_ref, m_out, w_gate, w_up, m_full, *sems = refs[-11:]
+    gate_sems, up_sems, m_sems = sems
+    me_z, me_t = idx[0], idx[2]
+    step = pl.program_id(0)
+    first = step == 0
+    m_copies = [
+        [
+            pltpu.make_async_copy(
+                m_refs[j].at[pl.ds(row, seq), :],
+                m_full.at[pl.ds(i * seq, seq), pl.ds(k * quarter, quarter)],
+                m_sems.at[i, k],
+            )
+            for k, (j, row) in enumerate(places[i])
+        ]
+        for i in range(nz)
+    ]
+    gate_copies = weight_copies(nz, slice_d, own_e, idx, gate_parts, w_gate, gate_sems, False)
+    up_copies = weight_copies(nz, slice_d, own_e, idx, up_parts, w_up, up_sems, False)
+
+    @pl.when(first)
     def _():
-        pairs = ((refs[3:5], w_gate), (refs[5:7], w_up))
-        load_weights(nz, slice_d, me_z, me_c, pairs, sems, (False, False))
-
-    rows = m_ref.shape[1]
+        start(m_copies[0] + gate_copies + up_copies)
+        for copies in m_copies[1:]:
+            start(copies)
+
+    for i in range(nz):
+
+        @pl.when(step == i)
+        def _(i=i):
+            finish(m_copies[i])
+
+    rows = seq
+    m_block = m_full[pl.ds(pl.multiple_of(step * seq, seq), seq), :]
+    m_out[...] = m_block
     lane = lax.broadcasted_iota(jnp.int32, (rows, LANES), 1)
     logits = jnp.zeros((rows, LANES), f32)
     for k in range(n):
-        logits += dot_nn(m_ref[k], router_ref[me_t ^ k])
+        logits += dot_nn(m_block[:, k * quarter : (k + 1) * quarter], router_ref[me_t ^ k])
     named = (lane >= FIRST) & (lane < FIRST + EXPERTS)
     logits = jnp.where(named, logits, -1e30)
     expd = jnp.where(named, jnp.exp(logits - jnp.max(logits, -1, keepdims=True)), 0.0)
     probs = expd / jnp.sum(expd, -1, keepdims=True)
     probs_ref[...] = probs
     gates = probs * mask_ref[...]
+
+    @pl.when(first)
+    def _():
+        finish(gate_copies)
+
     for e in range(own_e):
+        at = pl.ds(e * hid, hid)
+        act_ref[:, at] = dot_nn(m_block, w_gate[:, at])
+
+    @pl.when(first)
+    def _():
+        finish(up_copies)
+
+    for e in range(own_e):
+        at = pl.ds(e * hid, hid)
+        up = dot_nn(m_block, w_up[:, at])
+        up_ref[:, at] = up
+        act = act_ref[:, at]
         gate = own_gate(gates, lane, me_z, own_e, e)
-        act = jnp.zeros((rows, hid), f32)
-        up = jnp.zeros((rows, hid), f32)
-        for k in range(n):
-            act += dot_nn(m_ref[k], w_gate[me_t ^ k, e])
-            up += dot_nn(m_ref[k], w_up[me_t ^ k, e])
-        at = pl.ds(e * hid, hid)
-        act_ref[:, at] = act
-        up_ref[:, at] = up
         hid_ref[:, at] = (gate * (act * jax.nn.sigmoid(act) * up)).astype(bf16)
 
 
-def forward_call(idx, m_all, mask_all, router_q, gate_parts, up_parts, nz):
-    n, tokens, quarter = m_all.shape
+def forward_call(idx, pieces, places, mask_all, router_q, gate_parts, up_parts, nz):
+    n, quarter = router_q.shape[:2]
+    tokens = mask_all.shape[0]
     seq = tokens // nz
     own_e, slice_d, hid = up_parts[0].shape[1:]
     wide = own_e * hid
     here = lambda i, idx: (i, 0)
     return pl.pallas_call(
-        functools.partial(forward_kernel, nz, n, own_e, hid, slice_d),
+        functools.partial(forward_kernel, nz, n, own_e, hid, slice_d, seq, quarter, places),
         grid_spec=pltpu.PrefetchScalarGridSpec(
             num_scalar_prefetch=1,
             grid=(nz,),
             in_specs=[
-                pl.BlockSpec((n, seq, quarter), lambda i, idx: (0, i, 0)),
                 pl.BlockSpec((seq, LANES), here),
                 pl.BlockSpec((n, quarter, LANES), lambda i, idx: (0, 0, 0)),
             ]
-            + [pl.BlockSpec(memory_space=pl.ANY)] * 4,
+            + [pl.BlockSpec(memory_space=pl.ANY)] * (4 + len(pieces)),
             out_specs=[
                 pl.BlockSpec((seq, wide), here),
                 pl.BlockSpec((seq, wide), here),
                 pl.BlockSpec((seq, wide), here),
                 pl.BlockSpec((seq, LANES), here),
+                pl.BlockSpec((seq, n * quarter), here),
             ],
             scratch_shapes=[
-                pltpu.VMEM((n, own_e, quarter, hid), bf16),
-                pltpu.VMEM((n, own_e, quarter, hid), bf16),
-                pltpu.SemaphoreType.DMA((2, 2 * nz)),
+                pltpu.VMEM((n * quarter, wide), bf16),
+                pltpu.VMEM((n * quarter, wide), bf16),
+                pltpu.VMEM((tokens, n * quarter), bf16),
+                pltpu.SemaphoreType.DMA((2 * nz * own_e,)),
+                pltpu.SemaphoreType.DMA((2 * nz * own_e,)),
+                pltpu.SemaphoreType.DMA((nz, n)),
             ],
         ),
         out_shape=[
@@ -265,52 +329,59 @@
             jax.ShapeDtypeStruct((tokens, wide), f32),
             jax.ShapeDtypeStruct((tokens, wide), bf16),
             jax.ShapeDtypeStruct((tokens, LANES), f32),
+            jax.ShapeDtypeStruct((tokens, n * quarter), bf16),
         ],
-        compiler_params=pltpu.CompilerParams(vmem_limit_bytes=52 * MIB),
+        compiler_params=pltpu.CompilerParams(vmem_limit_bytes=56 * MIB),
         cost_estimate=pl.CostEstimate(
             flops=4 * tokens * n * quarter * wide, bytes_accessed=40 * MIB, transcendentals=0
         ),
-    )(idx, m_all, mask_all, router_q, *gate_parts, *up_parts)
+    )(idx, mask_all, router_q, *gate_parts, *up_parts, *pieces)
 
 
 def backward_kernel(nz, n, own_e, hid, slice_d, quarter, idx, *refs):
     g_ref, act_ref, up_ref, probs_ref, mask_ref = refs[:5]
-    dx_ref, dg_ref, du_ref, w_gate, w_up, w_down, sems = refs[11:]
+    dx_ref, dg_ref, du_ref, w_gate, w_up, w_down, gate_sems, up_sems, down_sems = refs[11:]
     i = pl.program_id(0)
-    me_z, me_c, me_t = idx[0], idx[1], idx[2]
+    me_z = idx[0]
+    gate_copies = weight_copies(nz, slice_d, own_e, idx, refs[5:7], w_gate, gate_sems, False)
+    up_copies = weight_copies(nz, slice_d, own_e, idx, refs[7:9], w_up, up_sems, False)
+    down_copies = weight_copies(nz, slice_d, own_e, idx, refs[9:11], w_down, down_sems, True)
 
     @pl.when(i == 0)
     def _():
-        pairs = ((refs[5:7], w_gate), (refs[7:9], w_up), (refs[9:11], w_down))
-        load_weights(nz, slice_d, me_z, me_c, pairs, sems, (False, False, True))
+        start(down_copies + gate_copies + up_copies)
+        finish(down_copies)
 
     rows = act_ref.shape[0]
     lane = lax.broadcasted_iota(jnp.int32, (rows, LANES), 1)
     gates = probs_ref[...] * mask_ref[...]
     dgate = jnp.zeros((rows, LANES), f32)
+    g_block = jnp.concatenate([g_ref[q, 0] for q in range(n)], 1)
     for e in range(own_e):
         gate = own_gate(gates, lane, me_z, own_e, e)
         at = pl.ds(e * hid, hid)
-        back = jnp.zeros((rows, hid), f32)
-        for q in range(n):
-            back += dot_nt(g_ref[q, 0], w_down[q, e])
+        back = dot_nt(g_block, w_down[e])
         act = act_ref[:, at]
         up = up_ref[:, at]
         sigma = jax.nn.sigmoid(act)
         silu = act * sigma
-        dgate = jnp.where(lane == me_z * own_e + e, jnp.sum(silu * up * back, -1, keepdims=True), dgate)
+        dgate = jnp.where(
+            lane == me_z * own_e + e, jnp.sum(silu * up * back, -1, keepdims=True), dgate
+        )
         back = gate * back
         dg_ref[:, at] = (back * up * sigma * (1.0 + act * (1.0 - sigma))).astype(bf16)
         du_ref[:, at] = (back * silu).astype(bf16)
     dgate = jnp.transpose(dgate)[:EXPERTS].astype(bf16)
+
+    @pl.when(i == 0)
+    def _():
+        finish(gate_copies + up_copies)
+
     even, odd = order_of(n, 0), order_of(n, 1)
     for j in range(n):
-        q = me_t ^ jnp.where(i % 2 == 0, even[j], odd[j])
-        total = jnp.zeros((rows, quarter), f32)
-        for e in range(own_e):
-            at = pl.ds(e * hid, hid)
-            total += dot_nt(dg_ref[:, at], w_gate[q, e])
-            total += dot_nt(du_ref[:, at], w_up[q, e])
+        k = jnp.where(i % 2 == 0, even[j], odd[j])
+        at = pl.ds(pl.multiple_of(k * quarter, quarter), quarter)
+        total = dot_nt(dg_ref[...], w_gate[at, :]) + dot_nt(du_ref[...], w_up[at, :])
         dx_ref[0, j, pl.ds(0, rows), :] = total.astype(bf16)
         for h in range(rows // quarter):
             dx_ref[0, j, pl.ds(rows + h * EXPERTS, EXPERTS), :] = dgate[
@@ -346,10 +417,12 @@
                 pl.BlockSpec((seq, wide), here),
             ],
             scratch_shapes=[
-                pltpu.VMEM((n, own_e, quarter, hid), bf16),
-                pltpu.VMEM((n, own_e, quarter, hid), bf16),
-                pltpu.VMEM((n, own_e, hid, quarter), bf16),
-                pltpu.SemaphoreType.DMA((3, 2 * nz)),
+                pltpu.VMEM((n * quarter, wide), bf16),
+                pltpu.VMEM((n * quarter, wide), bf16),
+                pltpu.VMEM((own_e, hid, n * quarter), bf16),
+                pltpu.SemaphoreType.DMA((2 * nz * own_e,)),
+                pltpu.SemaphoreType.DMA((2 * nz * own_e,)),
+                pltpu.SemaphoreType.DMA((2 * nz,)),
             ],
         ),
         out_shape=[
@@ -366,18 +439,18 @@
     )(idx, g_all, act, up, probs, mask_all, *weights)
 
 
-def output_kernel(nz, n, own_e, hid, slice_d, quarter, idx, *refs):
-    hid_ref, near, far, y_ref, w_down, sems = refs
-
-    @pl.when(pl.program_id(0) == 0)
+def output_kernel(nz, own_e, hid, slice_d, quarter, idx, hid_ref, near, far, y_ref, w_down, sems):
+    i, j = pl.program_id(0), pl.program_id(1)
+
+    @pl.when((i == 0) & (j == 0))
     def _():
-        load_weights(nz, slice_d, idx[0], idx[1], (((near, far), w_down),), sems, (True,))
-
-    for q in range(n):
-        total = jnp.zeros((hid_ref.shape[0], quarter), f32)
-        for e in range(own_e):
-            total += dot_nn(hid_ref[:, pl.ds(e * hid, hid)], w_down[q, e])
-        y_ref[q, 0] = total.astype(bf16)
+        copies = weight_copies(nz, slice_d, own_e, idx, (near, far), w_down, sems, True)
+        start(copies)
+        finish(copies)
+
+    at = pl.ds(pl.multiple_of(j * quarter, quarter), quarter)
+    part = w_down[:, :, at].reshape(own_e * hid, quarter)
+    y_ref[0, 0] = dot_nn(hid_ref[...], part).astype(bf16)
 
 
 def output_call(idx, hidden, parts, n, nz):
@@ -386,16 +459,18 @@
     own_e, hid, slice_d = parts[0].shape[1:]
     quarter = 2 * slice_d
     return pl.pallas_call(
-        functools.partial(output_kernel, nz, n, own_e, hid, slice_d, quarter),
+        functools.partial(output_kernel, nz, own_e, hid, slice_d, quarter),
         grid_spec=pltpu.PrefetchScalarGridSpec(
             num_scalar_prefetch=1,
-            grid=(nz,),
-            in_specs=[pl.BlockSpec((seq, wide), lambda i, idx: (i, 0))]
+            grid=(nz, n),
+            in_specs=[pl.BlockSpec((seq, wide), lambda i, j, idx: (i, 0))]
             + [pl.BlockSpec(memory_space=pl.ANY)] * 2,
-            out_specs=pl.BlockSpec((n, 1, seq, quarter), lambda i, idx: (0, i, 0, 0)),
+            out_specs=pl.BlockSpec(
+                (1, 1, seq, quarter), lambda i, j, idx: (j ^ idx[2], i ^ idx[0], 0, 0)
+            ),
             scratch_shapes=[
-                pltpu.VMEM((n, own_e, hid, quarter), bf16),
-                pltpu.SemaphoreType.DMA((1, 2 * nz)),
+                pltpu.VMEM((own_e, hid, n * quarter), bf16),
+                pltpu.SemaphoreType.DMA((2 * nz,)),
             ],
         ),
         out_shape=jax.ShapeDtypeStruct((n, nz, seq, quarter), bf16),
@@ -406,58 +481,89 @@
     )(idx, hidden, *parts)
 
 
-def down_grad_kernel(nz, own_e, hid, seq, slice_d, idx, g_ref, hid_ref, keep_ref, give_ref):
-    for out_ref, c in ((keep_ref, idx[1]), (give_ref, 1 - idx[1])):
-        cols = pl.ds(pl.multiple_of(c * slice_d, slice_d), slice_d)
-        for e in range(own_e):
-            total = jnp.zeros((hid, slice_d), f32)
-            for blk in range(nz):
-                left = hid_ref[pl.ds(blk * seq, seq), pl.ds(e * hid, hid)]
-                total += dot_tn(left, g_ref[0, blk, :, cols])
-            out_ref[0, e] = total.astype(bf16)
-
-
-def down_grad_call(idx, g_all, hidden, own_e):
-    n, nz, seq, quarter = g_all.shape
+def down_grad_kernel(nz, n, own_e, hid, seq, slice_d, idx, hid_ref, *refs):
+    g_refs, (keep_ref, give_ref, g_out, g_full, sems) = refs[:-5], refs[-5:]
+    step = pl.program_id(0)
+    copies = []
+    for k in range(n):
+        copies.append([])
+        for i in range(nz):
+            j, row = place_of(n, nz * seq // 2, k, i * seq)
+            copies[k].append(
+                pltpu.make_async_copy(
+                    g_refs[j].at[pl.ds(row, seq), :],
+                    g_full.at[k, pl.ds(i * seq, seq), :],
+                    sems.at[k, i],
+                )
+            )
+
+    @pl.when(step == 0)
+    def _():
+        for some in copies:
+            start(some)
+
+    for k in range(n):
+
+        @pl.when(step == k)
+        def _(k=k):
+            finish(copies[k])
+
+    g_block = g_full[step]
+    g_out[0] = g_block
+    total = dot_tn(g_block, hid_ref[...])
+    halves = (total[:slice_d], total[slice_d:])
+    for e in range(own_e):
+        parts = [jnp.transpose(half[:, e * hid : (e + 1) * hid]).astype(bf16) for half in halves]
+        keep_ref[0, e] = jnp.where(idx[1] == 0, parts[0], parts[1])
+        give_ref[0, e] = jnp.where(idx[1] == 0, parts[1], parts[0])
+
+
+def down_grad_call(idx, pieces, hidden, own_e, nz, n):
     tokens, wide = hidden.shape
+    quarter, seq = pieces[0].shape[1], tokens // nz
     hid, slice_d = wide // own_e, quarter // 2
-    out = pl.BlockSpec((1, own_e, hid, slice_d), lambda q, idx: (q ^ idx[0], 0, 0, 0))
+    out = pl.BlockSpec((1, own_e, hid, slice_d), lambda k, idx: (k ^ idx[2] ^ idx[0], 0, 0, 0))
     return pl.pallas_call(
-        functools.partial(down_grad_kernel, nz, own_e, hid, seq, slice_d),
+        functools.partial(down_grad_kernel, nz, n, own_e, hid, seq, slice_d),
         grid_spec=pltpu.PrefetchScalarGridSpec(
             num_scalar_prefetch=1,
             grid=(n,),
-            in_specs=[
-                pl.BlockSpec((1, nz, seq, quarter), lambda q, idx: (q, 0, 0, 0)),
-                pl.BlockSpec((tokens, wide), lambda q, idx: (0, 0)),
+            in_specs=[pl.BlockSpec((tokens, wide), lambda k, idx: (0, 0))]
+            + [pl.BlockSpec(memory_space=pl.ANY)] * len(pieces),
+            out_specs=[out, out, pl.BlockSpec((1, tokens, quarter), lambda k, idx: (k, 0, 0))],
+            scratch_shapes=[
+                pltpu.VMEM((n, tokens, quarter), bf16),
+                pltpu.SemaphoreType.DMA((n, nz)),
             ],
-            out_specs=[out, out],
-        ),
-        out_shape=[jax.ShapeDtypeStruct((nz, own_e, hid, slice_d), bf16)] * 2,
+        ),
+        out_shape=[jax.ShapeDtypeStruct((nz, own_e, hid, slice_d), bf16)] * 2
+        + [jax.ShapeDtypeStruct((n, tokens, quarter), bf16)],
         compiler_params=pltpu.CompilerParams(vmem_limit_bytes=48 * MIB),
         cost_estimate=pl.CostEstimate(
-            flops=2 * tokens * n * quarter * wide, bytes_accessed=16 * MIB, transcendentals=0
-        ),
-    )(idx, g_all, hidden)
+            flops=2 * tokens * n * quarter * wide, bytes_accessed=24 * MIB, transcendentals=0
+        ),
+    )(idx, hidden, *pieces)
 
 
 def up_grad_kernel(nz, own_e, hid, seq, slice_d, idx, m_ref, *refs):
     rights, (keep_ref, give_ref) = refs[:4], refs[4:]
-    for out_ref, c in ((keep_ref, idx[1]), (give_ref, 1 - idx[1])):
-        cols = pl.ds(pl.multiple_of(c * slice_d, slice_d), slice_d)
-        for w in range(2):
-            for e in range(own_e):
-                total = jnp.zeros((slice_d, hid), f32)
-                for blk in range(nz):
-                    right = rights[2 * w + blk % 2][
-                        pl.ds(blk // 2 * seq, seq), pl.ds(e * hid, hid)
-                    ]
-                    total += dot_tn(m_ref[0, pl.ds(blk * seq, seq), cols], right)
-                out_ref[0, w, e] = total.astype(bf16)
-
-
-def up_grad_call(idx, m_all, early, late, own_e, nz):
-    n, tokens, quarter = m_all.shape
+    lefts = [
+        jnp.concatenate([m_ref[pl.ds(blk * seq, seq), :] for blk in range(odd, nz, 2)], 0)
+        for odd in (0, 1)
+    ]
+    for w in range(2):
+        for e in range(own_e):
+            at = pl.ds(e * hid, hid)
+            total = dot_tn(lefts[0], rights[2 * w][:, at]) + dot_tn(
+                lefts[1], rights[2 * w + 1][:, at]
+            )
+            parts = (total[:slice_d].astype(bf16), total[slice_d:].astype(bf16))
+            keep_ref[0, w, e] = jnp.where(idx[1] == 0, parts[0], parts[1])
+            give_ref[0, w, e] = jnp.where(idx[1] == 0, parts[1], parts[0])
+
+
+def up_grad_call(idx, m_all, early, late, own_e, nz, n):
+    tokens, quarter = m_all.shape[0], m_all.shape[1] // n
     seq = tokens // nz
     wide = early[0].shape[1]
     hid, slice_d = wide // own_e, quarter // 2
@@ -470,7 +576,7 @@
         grid_spec=pltpu.PrefetchScalarGridSpec(
             num_scalar_prefetch=1,
             grid=(n,),
-            in_specs=[pl.BlockSpec((1, tokens, quarter), lambda k, idx: (k, 0, 0))] + [full] * 4,
+            in_specs=[pl.BlockSpec((tokens, quarter), lambda k, idx: (0, k))] + [full] * 4,
             out_specs=[out, out],
         ),
         out_shape=[jax.ShapeDtypeStruct((nz, 2, own_e, slice_d, hid), bf16)] * 2,
@@ -551,6 +657,7 @@
     mask = jnp.sum(
         (routes[:, :, None] == jnp.arange(EXPERTS)[None, None, :]).astype(bf16), 1
     )
+    n = width // quarter
     packed, *mask_parts = fence(packed, *spread_z(mask.T))
     mask_all = jnp.stack(mask_parts).transpose(0, 2, 1)
     mask_all = jnp.pad(
@@ -564,14 +671,15 @@
     router_full = small_full[:, FIRST : FIRST + EXPERTS]
     wo_full = lax.all_gather(after(wo, packed), dp, axis=1, tiled=True)
 
-    def fetch(weight):
+    def fetch(weight, ks):
         pick = lambda k: lax.dynamic_slice_in_dim(weight, (me_z ^ k) * own_e, own_e, 0)
-        return [swap(pick(k), "z", k) for k in range(nz)]
+        return [swap(pick(k), "z", k) for k in ks]
 
     def both_cores(parts):
         parts = jnp.stack(parts)
         return [parts, swap(parts, "core", 1)]
 
+    most, last = range(nz - 1), range(nz - 1, nz)
     cot_parts = spread_z(after(columns(cotangent, me_t, quarter), packed))
 
     xf = tokens.astype(f32)
@@ -601,68 +709,96 @@
     joined = outputs.reshape(seq, local).astype(bf16)
     wo_full = after(wo_full, joined)
     attn = jnp.dot(joined, wo_full, preferred_element_type=f32).astype(bf16)
-    attn, *cot_parts = fence(attn, *cot_parts)
-    cot_all = lax.all_gather(jnp.stack(cot_parts), "tensor", axis=0, tiled=False)
-    gate_parts = fetch(after(w_gate, attn))
+    attn, *cot_parts[:-1] = fence(attn, *cot_parts[:-1])
+    gate_parts = fetch(after(w_gate, attn), most)
 
     x_own = columns(xf, me_t, quarter)
-    resid = x_own + scatter_columns(attn)
+    blocks = columns_blocks(attn)
+    got = [scatter_first(block, odd) for odd, block in enumerate(blocks)]
+    resid = x_own + jnp.concatenate(
+        [scatter_third(*scatter_second(b, g, odd)) for odd, (b, g) in enumerate(zip(blocks, got))],
+        0,
+    )
     rate_r = lax.rsqrt(tensor_sum(jnp.sum(resid * resid, -1)) / width + EPS)[:, None]
     gain_own = lax.dynamic_slice_in_dim(m_gain, me_t * quarter, quarter, 0)
     m_own = (resid * rate_r * gain_own).astype(bf16)
 
-    m_own, *gate_parts = fence(m_own, *gate_parts)
-    m_parts = fence(*spread_z(m_own))
-    up_parts = fetch(after(w_up, m_parts[0]))
-    gate_parts = both_cores(gate_parts)
+    held = fence(m_own, *gate_parts, *cot_parts)
+    m_own, gate_parts, cot_parts = held[0], held[1:nz], held[nz:]
+    cot_flat = jnp.concatenate(cot_parts, 0)
+    cot_near = spread_tensor_near(cot_flat)
+    held = fence(*spread_z(m_own), *cot_near)
+    m_parts, cot_near = held[:nz], held[nz:]
+    gate_parts += fetch(after(w_gate, m_parts[0]), last)
+    up_parts = fetch(after(w_up, m_parts[0]), most)
     m_flat = jnp.concatenate(m_parts, 0)
     m_near = spread_tensor_near(m_flat)
-    held = fence(*m_near, *up_parts)
-    m_near, up_parts = held[: len(m_near)], held[len(m_near) :]
+    held = fence(gate_parts[-1], *up_parts, *m_near)
+    gate_parts[-1], up_parts, m_near = held[0], held[1:nz], held[nz:]
+    gate_parts = both_cores(gate_parts)
+    up_parts += fetch(after(w_up, m_near[0]), last)
+    up_parts[-1], *pieces = fence(up_parts[-1], m_flat, *m_near, *spread_tensor_cross(m_near))
     up_parts = both_cores(up_parts)
-    down_parts = fetch(after(w_down, up_parts[0]))
-    m_all = spread_tensor_far(m_flat, m_near)
-    m_all, down_parts[2] = fence(m_all, down_parts[2])
+    down_parts = fetch(after(w_down, up_parts[0]), range(nz))
+    cot_cross = spread_tensor_cross([after(x, pieces[-1]) for x in cot_near])
+    places = [
+        [place_of(n, nz * seq // 2, k, i * seq) for k in range(n)] for i in range(nz)
+    ]
     router_q = small_full.reshape(-1, quarter, LANES)
-    act, up, hidden, probs_all = forward_call(
-        idx, m_all, mask_all, router_q, gate_parts, up_parts, nz
-    )
-    hidden, *down_parts = fence(hidden, *down_parts)
+    act, up, hidden, probs_all, m_all = forward_call(
+        idx, pieces, places, mask_all, router_q, gate_parts, up_parts, nz
+    )
+    hidden, *held = fence(hidden, *down_parts, *cot_cross)
+    down_parts, cot_cross = held[:nz], held[nz:]
     down_parts = both_cores(down_parts)
-    down_keep, down_give = down_grad_call(idx, cot_all, hidden, own_e)
+    down_keep, down_give, cot_all = down_grad_call(
+        idx, [cot_flat, *cot_near, *cot_cross], hidden, own_e, nz, n
+    )
+    cot_all = cot_all.reshape(n, nz, seq, quarter)
 
     def to_owners(keep, got):
         summed = (keep.astype(f32) + got.astype(f32)).astype(bf16)
         return [swap(summed[k], "z", k) for k in range(nz)]
 
-    down_own = to_owners(down_keep, swap(down_give, "core", 1))
+    down_got = swap(down_give, "core", 1)
+    down_own = to_owners(down_keep, down_got)
     half_call = lambda first, probs: backward_call(
         idx, first, cot_all, act, up, probs, mask_all, gate_parts + up_parts + down_parts
     )
     odds, evens = range(1, nz, 2), range(0, nz, 2)
-    late = half_call(1, after(probs_all, down_give))
+    late = half_call(1, after(probs_all, down_own[0]))
     first = {k: scatter_first(late[0][k // 2], k // 2 % 2) for k in odds}
-    early = half_call(0, after(probs_all, late[1]))
-    held = fence(*early, *(first[k] for k in odds), *down_own[:3])
-    early, got = held[:3], dict(zip(odds, held[3:]))
-    down_own[:3] = held[3 + nz // 2 :]
+    held = fence(late[1], *down_own[:-1])
+    down_own[:-1] = held[1:]
+    early = half_call(0, after(probs_all, *held))
+    held = fence(*early, *(first[k] for k in odds), down_own[-1])
+    early, got, down_own[-1] = held[:3], dict(zip(odds, held[3:-1])), held[-1]
     second = {k: scatter_second(late[0][k // 2], got[k], k // 2 % 2) for k in odds}
     first = {k: scatter_first(early[0][k // 2], k // 2 % 2) for k in evens}
-    up_keep, up_give = up_grad_call(idx, m_all, early[1:3], late[1:3], own_e, nz)
-    held = fence(up_keep, up_give, *(first[k] for k in evens), *down_own[3:])
+    up_keep, up_give = up_grad_call(idx, m_all, early[1:3], late[1:3], own_e, nz, n)
+    few = [second[k] for k in odds if second[k][1] is not None]
+    held = fence(
+        up_keep, up_give, *(first[k] for k in evens), *(x[1] for x in few)
+    )
     (up_keep, up_give), got = held[:2], dict(zip(evens, held[2:]))
-    down_own[3:] = held[2 + nz // 2 :]
+    if few:
+        second = {k: (second[k][0], x) for k, x in zip(odds, held[2 + nz // 2 :])}
     near = scatter_z_near({k: scatter_third(*second[k]) for k in odds})
     second = {k: scatter_second(early[0][k // 2], got[k], k // 2 % 2) for k in evens}
     up_got = swap(up_give, "core", 1)
-    moe_part = output_call(idx, after(hidden, up_give), down_parts, width // quarter, nz)
-    moe_part, near, up_got = fence(moe_part, near, up_got)
+    moe_part = output_call(idx, after(hidden, up_give), down_parts, n, nz)
+    few = [second[k][1] for k in evens if second[k][1] is not None]
+    near, moe_part, *few = fence(near, moe_part, *few)
+    if few:
+        second = {k: (second[k][0], x) for k, x in zip(evens, few)}
     dm_own = scatter_z_far({k: scatter_third(*second[k]) for k in evens}, near)
     dgate = jnp.concatenate(
         [dm_own[seq + h * EXPERTS :][:EXPERTS] for h in range(seq // quarter)], 1
     )
-    dm_own = dm_own[:seq]
-    up_own = to_owners(after(up_keep, dm_own), up_got)
+    dm_own, up_got = fence(dm_own[:seq], up_got)
+    summed = (up_keep.astype(f32) + up_got.astype(f32)).astype(bf16)
+    up_own = [swap(summed[k], "z", k) for k in range(nz - 1)] + [None]
+    up_last = summed[nz - 1]
     moe_sum = lax.psum_scatter(moe_part, "tensor", scatter_dimension=0, tiled=False)
 
     dgate = dgate.T
@@ -680,8 +816,12 @@
     cot_own = columns(cotangent, me_t, quarter).astype(f32)
     dresid = cot_own + rate_r * (pulled - normed * inner_r)
     dresid_low = gather_tensor(dresid.astype(bf16))
-
-    wo_grad = jnp.einsum("sa,sd->ad", joined, dresid_low, preferred_element_type=f32)
+    dresid_low, *up_own[:-1] = fence(dresid_low, *up_own[:-1])
+    up_own[-1] = swap(after(up_last, dresid_low), "z", nz - 1)
+    moe_sum = after(moe_sum, dresid_low)
+    moe_own = lax.psum_scatter(moe_sum, "z", scatter_dimension=0, tiled=False)
+
+    wo_grad = jnp.einsum("sd,sa->da", dresid_low, joined, preferred_element_type=f32)
     dout = (
         jnp.einsum("sd,ad->sa", dresid_low, wo_full, preferred_element_type=f32)
         .astype(bf16)
@@ -691,6 +831,7 @@
     dv = jnp.einsum("hqk,qhd->khd", weights_low, dout, preferred_element_type=f32)
     inner = jnp.sum(weights * dweights, -1, keepdims=True)
     dscores = (weights * (dweights - inner)).astype(bf16)
+    dscores, up_own[-1] = fence(dscores, up_own[-1])
     dq_rot = scale * jnp.einsum("hqk,khd->qhd", dscores, k_rot, preferred_element_type=f32)
     dk_rot = scale * jnp.einsum("hqk,qhd->khd", dscores, q_rot, preferred_element_type=f32)
     dq_norm = unrotate(dq_rot, cosine, sine).reshape(seq, local)
@@ -710,50 +851,49 @@
     q_gain_part = jnp.sum(dq_norm * query * rate_q, 0)
     k_gain_part = jnp.sum(dk_norm * keyed * rate_k, 0)
     dqkv = jnp.concatenate([dq_low, dk_low, dv_low], 1)
-    dqkv, *up_own = fence(dqkv, *up_own)
-    moe_sum = after(moe_sum, dqkv)
-    moe_near = scatter_z_near({k: moe_sum[k] for k in odds})
-    moe_own = scatter_z_far({k: moe_sum[k].astype(f32) for k in evens}, moe_near)
-    mixed = gather_tensor((resid + moe_own).astype(bf16))
-    expert_grads = place_call(idx, up_own, down_own)
+    smalls = jnp.concatenate(
+        [q_gain_part[None], k_gain_part[None], moe_gain_part[None], router_part.T], 0
+    )
+    dqkv, smalls = fence(dqkv, butterfly_sum(smalls, ("core", "z")))
+    half = lax.dynamic_slice_in_dim(smalls[2:], me_c * slice_d, slice_d, 1)
+    half = tensor_sum(jnp.where(me_t == me_z, half, 0.0))
+    mixed = gather_tensor((after(resid, dqkv) + moe_own.astype(f32)).astype(bf16))
     wqkv_grad = jnp.einsum("sd,sa->da", a_low, dqkv, preferred_element_type=f32).astype(bf16)
     da_part = jnp.einsum("sa,da->sd", dqkv, wqkv_full, preferred_element_type=f32)
-    da_own = scatter_columns(da_part.astype(bf16))
+    blocks = columns_blocks(da_part.astype(bf16))
+    got = [scatter_first(b, odd) for odd, b in enumerate(blocks)]
+    expert_grads = place_call(idx, up_own, down_own)
+    da_own = jnp.concatenate(
+        [scatter_third(*scatter_second(b, g, odd)) for odd, (b, g) in enumerate(zip(blocks, got))],
+        0,
+    )
+    da_own, mixed = fence(da_own, mixed)
     norm_x = x_own * rate_x
-    attn_gain_part = jnp.sum(da_own * norm_x, 0)
     pulled_x = da_own * lax.dynamic_slice_in_dim(a_gain, me_t * quarter, quarter, 0)
     inner_x = tensor_sum(jnp.sum(pulled_x * norm_x, -1))[:, None] / width
     tokens_grad = gather_tensor(
         (dresid + rate_x * (pulled_x - norm_x * inner_x)).astype(bf16)
     )
 
-    wqkv_own = lax.psum_scatter(wqkv_grad, dp, scatter_dimension=0, tiled=True).astype(f32)
-    wo_own = lax.psum_scatter(wo_grad.astype(bf16), dp, scatter_dimension=1, tiled=True).astype(f32)
-    smalls = jnp.concatenate(
-        [
-            q_gain_part[None],
-            k_gain_part[None],
-            attn_gain_part[None],
-            moe_gain_part[None],
-            router_part.T,
-        ],
-        0,
-    )
-    smalls = butterfly_sum(smalls, ("core", "z"))
-    half = lax.dynamic_slice_in_dim(smalls[2:], me_c * slice_d, slice_d, 1)
-    half = tensor_sum(jnp.where(me_t == me_z, half, 0.0))
+    both_grads = jnp.concatenate([wqkv_grad, wo_grad.astype(bf16)], 1)
+    both_own = lax.psum_scatter(both_grads, dp, scatter_dimension=0, tiled=True)
+    tokens_grad, both_own = fence(tokens_grad, both_own)
+    both_own = both_own.astype(f32)
+    wqkv_own, wo_own = both_own[:, : 3 * local], both_own[:, 3 * local :].T
+    attn_gain_grad = jnp.sum(jnp.concatenate([wq, wk, wv], 1).astype(f32) * wqkv_own, -1)
+    attn_gain_grad = tensor_sum(attn_gain_grad) / attn_gain.astype(f32)
     return (
         mixed,
         tokens_grad,
         wqkv_own[:, :local],
         wqkv_own[:, local : 2 * local],
-        wqkv_own[:, 2 * local :],
+        wqkv_own[:, 2 * local : 3 * local],
         wo_own,
-        half[0],
+        attn_gain_grad,
         smalls[0],
         smalls[1],
-        half[1],
-        half[2:].T,
+        half[0],
+        half[1:].T,
         expert_grads[0],
         expert_grads[1],
         expert_grads[2],

time: 897 us -> 846 us (0.943)
  waiting for transfers between devices: 450 us -> 328 us
  local copies, waits for them, and re-layouts: 45.3 us -> 75.7 us
  starting transfers between devices: 118 us -> 140 us
  other arithmetic: 74.1 us -> 85.9 us
  Pallas kernels: 140 us -> 149 us
    ppermute x80 -> x84, waiting for transfers between devices: 388 us -> 254 us  [swap(): return lax.ppermute(value, axis, [(i, i ^ mask) for i in range(n)])]
    ppermute x80 -> x84, starting transfers between devices: 117 us -> 140 us  [swap(): return lax.ppermute(value, axis, [(i, i ^ mask) for i in range(n)])]
    unnamed x166 -> x185, local copies, waits for them, and re-layouts: 10.4 us -> 24.9 us
    all_gather x1, waiting for transfers between devices: 0.02 us -> 13.1 us  [shards(): wo_full = lax.all_gather(after(wo, packed), dp, axis=1, tiled=True)]
  transfers between devices with their start and end apart: 86 -> 89, of which waited for: 43 -> 47; matrix products, arithmetic and copies ran while one was open for 16% -> 20% of each run, Pallas kernels for 16% -> 16%
where the time goes in v3:
time: 846 us; the launch traced here: 838 us
  waiting for transfers between devices  328 us (39%)
  Pallas kernels  149 us (18%)
  starting transfers between devices  140 us (17%)
  other arithmetic  85.9 us (10%)
  local copies, waits for them, and re-layouts  75.7 us (9%)
  matrix products  43.7 us (5%)
  between operations  15.5 us (2%)
    ppermute x84, waiting for transfers between devices, swap(): return lax.ppermute(value, axis, [(i, i ^ mask) for i in range(n)])  254 us
    ppermute x84, starting transfers between devices, swap(): return lax.ppermute(value, axis, [(i, i ^ mask) for i in range(n)])  140 us
    all_gather x1, waiting for transfers between devices, shards(): lax.all_gather(jnp.concatenate([wq, wk, wv, small], 1), dp, axis=0, tiled...  61.3 us
    pallas_call x2, Pallas kernels, backward_call(): pl.pallas_call(functools.partial(backward_kernel, nz, n, own_e, hid, slic...  54.6 us
    pallas_call x1, Pallas kernels, forward_call(): pl.pallas_call(functools.partial(forward_kernel, nz, n, own_e, hid, slice...  32.1 us
    unnamed x185, local copies, waits for them, and re-layouts  24.9 us
    pallas_call x1, Pallas kernels, up_grad_call(): pl.pallas_call(functools.partial(up_grad_kernel, nz, own_e, hid, seq, sli...  23.4 us
    pallas_call x1, Pallas kernels, output_call(): pl.pallas_call(functools.partial(output_kernel, nz, own_e, hid, slice_d,...  17.2 us
  transfers between devices with their start and end apart: 89, of which 47 were waited for; matrix products, arithmetic and copies ran while one was open for 20% of the time, Pallas kernels for 16%

profile of v3, /device:TPU:0, one launch (start us, length us, event | category | flops | bytes accessed | tf_op | source)
XLA Modules:
  0.0 838.2 jit_solution(2129609037509479300)
XLA Ops:
  11.7 4.1 collective-permute-start.1
  22.3 61.3 %all-gather.3.cloned.1.call-done = bf16[2048,1664]{1,0:T(8,128)(2,1)} async-done(((bf16[256,1664]{1,0:T(8,128)(2,1)}), bf16[2048,1664]{1,0:T(8,128)(2,1)}) %all-gather.3.cloned.1.call-update) | async-done | bytes 6815760 | tf_op jit(solution)/shard_map/all_gather | solution.py:656
  84.9 6.5 fusion.4
  109.8 5.0 fusion.105
  114.8 3.5 convolution_convert_fusion.5
  118.3 13.1 %all-gather.5.cloned.1.call-done = bf16[512,2048]{1,0:T(8,128)(2,1)} async-done(((bf16[512,256]{1,0:T(8,128)(2,1)}), bf16[512,2048]{1,0:T(8,128)(2,1)}) %all-gather.5.cloned.1.call-update) | async-done | bytes 2097168 | tf_op jit(solution)/shard_map/all_gather | solution.py:672
  131.3 3.0 convolution_convert_fusion.2
  142.4 3.2 collective-permute-start.15
  145.5 4.2 collective-permute-done.7
  153.9 3.2 collective-permute-start.13
  169.1 9.1 %collective-permute-done.13 = bf16[4,256,256]{2,1,0:T(8,128)(2,1)S(1)} collective-permute-done((bf16[4,256,256]{2,1,0:T(8,128)(2,1)S(1)}, bf16[4,256,256]{2,1,0:T(8,128)(2,1)S(1)}, u32[]{:S(2)}, u32[]{:S(2)}) %collective-permute-start.13) | collective-permute-done | bytes 524320 | tf_op jit(solution)/shard_map/ppermute | solution.py:36
  178.2 3.5 collective-permute-done.14
  186.8 20.8 %collective-permute-done.17 = bf16[512,512]{1,0:T(8,128)(2,1)S(1)} collective-permute-done((bf16[512,512]{1,0:T(8,128)(2,1)S(1)}, bf16[512,512]{1,0:T(8,128)(2,1)S(1)}, u32[]{:S(2)}, u32[]{:S(2)}) %collective-permute-start.17) | collective-permute-done | bytes 524320 | tf_op jit(solution)/shard_map/ppermute | solution.py:36
  208.1 12.5 %collective-permute-done.18 = bf16[512,512]{1,0:T(8,128)(2,1)S(1)} collective-permute-done((bf16[512,512]{1,0:T(8,128)(2,1)S(1)}, bf16[512,512]{1,0:T(8,128)(2,1)S(1)}, u32[]{:S(2)}, u32[]{:S(2)}) %collective-permute-start.18) | collective-permute-done | bytes 524320 | tf_op jit(solution)/shard_map/ppermute | solution.py:36
  220.5 7.4 collective-permute-done.19.refs_1_
  240.9 14.0 %collective-permute-done.22 = bf16[4,256,256]{2,1,0:T(8,128)(2,1)S(1)} collective-permute-done((bf16[4,256,256]{2,1,0:T(8,128)(2,1)S(1)}, bf16[4,256,256]{2,1,0:T(8,128)(2,1)S(1)}, u32[]{:S(2)}, u32[]{:S(2)}) %collective-permute-start.22) | collective-permute-done | bytes 524320 | tf_op jit(solution)/shard_map/ppermute | solution.py:36
  254.9 20.3 %collective-permute-done.23 = bf16[4,256,256]{2,1,0:T(8,128)(2,1)S(1)} collective-permute-done((bf16[4,256,256]{2,1,0:T(8,128)(2,1)S(1)}, bf16[4,256,256]{2,1,0:T(8,128)(2,1)S(1)}, u32[]{:S(2)}, u32[]{:S(2)}) %collective-permute-start.23) | collective-permute-done | bytes 524320 | tf_op jit(solution)/shard_map/ppermute | solution.py:36
  282.3 4.8 collective-permute-start.27
  288.7 7.4 collective-permute-done.27
  310.1 11.6 %collective-permute-start.31 = (bf16[4,256,256]{2,1,0:T(8,128)(2,1)}, bf16[4,256,256]{2,1,0:T(8,128)(2,1)S(1)}, u32[]{:S(2)}, u32[]{:S(2)}) collective-permute-start(bf16[4,256,256]{2,1,0:T(8,128)(2,1)} %get-tuple-element.336), channel_id=1, source_target_pairs={{0,8},{8,0},{16,24},{24,16},{1,9},{9,1},{17,25},{25,17},{2,10},{10... | collective-permute-start | bytes 1572872 | tf_op jit(solution)/shard_map/ppermute | solution.py:36
  325.3 32.1 %shard_map.254 = (f32[2048,1024]{1,0:T(8,128)}, f32[2048,1024]{1,0:T(8,128)}, bf16[2048,1024]{1,0:T(8,128)(2,1)}, f32[2048,128]{1,0:T(8,128)}, bf16[2048,2048]{1,0:T(8,128)(2,1)}) custom-call(s32[3]{0:T(128)} %pad_add_fusion.idx, f32[2048,128]{1,0:T(8,128)} %pad_convert_fusion.refs_0_.refs_4_, bf16[4,512,128]{2,1,0:T(8,128)(2,1)} %bitcast.313, ...), custom_call_target="tpu_custom_call" | custom-call | flops 17179869184 | bytes 41943040 | tf_op jit(solution)/shard_map/pallas_call | solution.py:301
  357.4 3.1 collective-permute-done.32
  360.6 15.2 %shard_map.255 = (bf16[4,4,256,256]{3,2,1,0:T(8,128)(2,1)S(1)}, bf16[4,4,256,256]{3,2,1,0:T(8,128)(2,1)}, bf16[4,2048,512]{2,1,0:T(8,128)(2,1)}) custom-call(s32[3]{0:T(128)S(1)} %copy-done.8, bf16[2048,1024]{1,0:T(8,128)(2,1)} %get-tuple-element.206.hid_ref, bf16[2048,512]{1,0:T(8,128)(2,1)} %copy-done.66, ...), custom_call_target="tpu_custom_call" | custom-call | flops 8589934592 | bytes 25165824 | tf_op jit(solution)/shard_map/pallas_call | solution.py:526
  382.1 10.5 %collective-permute-start.38 = (bf16[4,256,256]{2,1,0:T(8,128)(2,1)}, bf16[4,256,256]{2,1,0:T(8,128)(2,1)S(1)}, u32[]{:S(2)}, u32[]{:S(2)}) collective-permute-start(bf16[4,256,256]{2,1,0:T(8,128)(2,1)} %get-tuple-element.332), channel_id=1, source_target_pairs={{0,8},{8,0},{16,24},{24,16},{1,9},{9,1},{17,25},{25,17},{2,10},{10... | collective-permute-start | bytes 1572872 | tf_op jit(solution)/shard_map/ppermute | solution.py:36
  395.5 27.2 %shard_map.256 = (bf16[2,4,528,512]{3,2,1,0:T(8,128)(2,1)}, bf16[1024,1024]{1,0:T(8,128)(2,1)}, bf16[1024,1024]{1,0:T(8,128)(2,1)}) custom-call(s32[3]{0:T(128)} %pad_add_fusion.idx, bf16[4,4,512,512]{3,2,1,0:T(8,128)(2,1)} %bitcast.362, f32[2048,1024]{1,0:T(8,128)} %get-tuple-element.174.refs_1_, f32[2048,1024]{1,0:T(8,128)} %get-tuple-element.175.refs_2_, ...), custom_call_target="tpu_custom_call" | custom-call | flops 12884901888 | bytes 41943040 | tf_op jit(solution)/shard_map/pallas_call | solution.py:401
  427.6 27.5 %shard_map.257 = (bf16[2,4,528,512]{3,2,1,0:T(8,128)(2,1)}, bf16[1024,1024]{1,0:T(8,128)(2,1)}, bf16[1024,1024]{1,0:T(8,128)(2,1)}) custom-call(s32[3]{0:T(128)} %pad_add_fusion.idx, bf16[4,4,512,512]{3,2,1,0:T(8,128)(2,1)} %bitcast.363, f32[2048,1024]{1,0:T(8,128)} %get-tuple-element.174.refs_1_, f32[2048,1024]{1,0:T(8,128)} %get-tuple-element.175.refs_2_, ...), custom_call_target="tpu_custom_call" | custom-call | flops 12884901888 | bytes 41943040 | tf_op jit(solution)/shard_map/pallas_call | solution.py:401
  455.9 3.9 fusion.37
  465.3 23.4 %shard_map.258 = (bf16[4,2,4,256,256]{4,3,2,1,0:T(8,128)(2,1)}, bf16[4,2,4,256,256]{4,3,2,1,0:T(8,128)(2,1)}) custom-call(s32[3]{0:T(128)S(1)} %copy-done.9, bf16[2048,2048]{1,0:T(8,128)(2,1)} %get-tuple-element.194.m_ref, bf16[1024,1024]{1,0:T(8,128)(2,1)S(1)} %copy-done.13, bf16[1024,1024]{1,0:T(8,128)(2,1)S(1)} %copy-done.12, ...), custom_call_target="tpu_custom_call" | custom-call | flops 17179869184 | bytes 25165824 | tf_op jit(solution)/shard_map/pallas_call | solution.py:574
  488.7 8.3 collective-permute-done.43
  509.3 17.2 %shard_map.259 = bf16[4,4,512,512]{3,2,1,0:T(8,128)(2,1)} custom-call(s32[3]{0:T(128)S(1)} %copy-done.9, bf16[2048,1024]{1,0:T(8,128)(2,1)} %get-tuple-element.206.hid_ref, bf16[4,4,256,256]{3,2,1,0:T(8,128)(2,1)S(1)} %copy-done.1, bf16[4,4,256,256]{3,2,1,0:T(8,128)(2,1)S(1)} %copy-done.11), custom_call_target="tpu_custom_call" | custom-call | flops 8589934592 | bytes 16777216 | tf_op jit(solution)/shard_map/pallas_call | solution.py:461
  536.2 21.4 %collective-permute-done.50 = bf16[1,528,512]{2,1,0:T(8,128)(2,1)} collective-permute-done((bf16[1,528,512]{2,1,0:T(8,128)(2,1)}, bf16[1,528,512]{2,1,0:T(8,128)(2,1)}, u32[]{:S(2)}, u32[]{:S(2)}) %collective-permute-start.50) | collective-permute-done | bytes 540704 | tf_op jit(solution)/shard_map/ppermute | solution.py:36
  566.8 3.9 add_convert_fusion
  578.4 13.3 %collective-permute-done.54 = bf16[512,512]{1,0:T(8,128)(2,1)S(1)} collective-permute-done((bf16[512,512]{1,0:T(8,128)(2,1)S(1)}, bf16[512,512]{1,0:T(8,128)(2,1)S(1)}, u32[]{:S(2)}, u32[]{:S(2)}) %collective-permute-start.54) | collective-permute-done | bytes 524320 | tf_op jit(solution)/shard_map/ppermute | solution.py:36
  595.1 7.6 collective-permute-done.56
  605.6 15.2 %collective-permute-done.58.refs_1_ = bf16[2,4,256,256]{3,2,1,0:T(8,128)(2,1)S(1)} collective-permute-done((bf16[2,4,256,256]{3,2,1,0:T(8,128)(2,1)S(1)}, bf16[2,4,256,256]{3,2,1,0:T(8,128)(2,1)S(1)}, u32[]{:S(2)}, u32[]{:S(2)}) %collective-permute-start.58) | collective-permute-done | bytes 1048608 | tf_op jit(solution)/shard_map/ppermute | solution.py:36
  632.4 15.5 %collective-permute-done.60.refs_3_ = bf16[2,4,256,256]{3,2,1,0:T(8,128)(2,1)S(1)} collective-permute-done((bf16[2,4,256,256]{3,2,1,0:T(8,128)(2,1)S(1)}, bf16[2,4,256,256]{3,2,1,0:T(8,128)(2,1)S(1)}, u32[]{:S(2)}, u32[]{:S(2)}) %collective-permute-start.60) | collective-permute-done | bytes 1048608 | tf_op jit(solution)/shard_map/ppermute | solution.py:36
  653.8 3.0 maximum_add_fusion.1
  674.0 21.1 %collective-permute-start.64 = (f32[19,512]{1,0:T(8,128)S(1)}, f32[19,512]{1,0:T(8,128)S(1)}, u32[]{:S(2)}, u32[]{:S(2)}) collective-permute-start(f32[19,512]{1,0:T(8,128)S(1)} %fusion.94), channel_id=1, source_target_pairs={{0,8},{8,0},{16,24},{24,16},{1,9},{9,1},{17,25},{25,17},{2,10},{10... | collective-permute-start | bytes 116744 | tf_op jit(solution)/shard_map/ppermute | solution.py:36
  700.7 7.9 collective-permute-done.65
  708.7 5.7 convolution_convert_fusion
  714.4 8.5 %pad_maximum_fusion = bf16[2048,2048]{0,1:T(8,128)(2,1)} fusion(bf16[2048,512]{0,1:T(8,128)(2,1)} %convolution_convert_fusion.1, bf16[2048,1536]{0,1:T(8,128)(2,1)} %convolution_convert_fusion), kind=kLoop, calls=%fused_computation.2 | loop fusion | flops 16777216 | bytes 16777216 | tf_op jit(solution)/shard_map/concatenate | solution.py:878
  722.9 6.7 fusion.8
  733.1 8.2 collective-permute-done.66
  753.4 12.7 %collective-permute-done.69 = bf16[256,512]{1,0:T(8,128)(2,1)S(1)} collective-permute-done((bf16[256,512]{1,0:T(8,128)(2,1)S(1)}, bf16[256,512]{1,0:T(8,128)(2,1)S(1)}, u32[]{:S(2)}, u32[]{:S(2)}) %collective-permute-start.69) | collective-permute-done | bytes 262176 | tf_op jit(solution)/shard_map/ppermute | solution.py:36
  767.6 5.0 collective-permute-done.72
  783.9 3.2 constant_dynamic-update-slice_fusion.10
  799.2 6.6 shard_map.260
  807.2 3.2 collective-permute-done.83
  (497 shorter events, 267.1 us)
Async XLA Ops:
  7.2 76.4 %all-gather.3.cloned.1.call-start = ((), (), s32[]{:S(2)}) async-start(), calls=%async_computation.3 | async-start | bytes 7667712 | tf_op jit(solution)/shard_map/all_gather | solution.py:656
  11.6 119.7 %all-gather.5.cloned.1.call-start = ((), (), s32[]{:S(2)}) async-start(), calls=%async_computation.4 | async-start | bytes 2359296 | tf_op jit(solution)/shard_map/all_gather | solution.py:672
  84.9 566.7 %reduce-scatter.10.cloned.1.call-start = ((), (), s32[]{:S(2)}) async-start(), calls=%async_computation.7 | async-start | bytes 10485760
  97.8 36.8 %collective-permute-start.6 = (bf16[512,512]{1,0:T(8,128)(2,1)}, bf16[512,512]{1,0:T(8,128)(2,1)}, u32[]{:S(2)}, u32[]{:S(2)}) collective-permute-start(bf16[512,512]{1,0:T(8,128)(2,1)} %constant_dynamic-slice_fusion.12), channel_id=1, source_target_pairs={{0,16},{8,24},{16,0},{24,8},{1,17},{9,25},{17,1},{25,9},{2,18},{10... | collective-permute-start | bytes 1572872 | tf_op jit(solution)/shard_map/ppermute | solution.py:36
  98.9 35.9 %collective-permute-start.5 = (bf16[512,512]{1,0:T(8,128)(2,1)}, bf16[512,512]{1,0:T(8,128)(2,1)}, u32[]{:S(2)}, u32[]{:S(2)}) collective-permute-start(bf16[512,512]{1,0:T(8,128)(2,1)} %constant_dynamic-slice_fusion.12), channel_id=1, source_target_pairs={{0,8},{8,0},{16,24},{24,16},{1,9},{9,1},{17,25},{25,17},{2,10},{10... | collective-permute-start | bytes 1572872 | tf_op jit(solution)/shard_map/ppermute | solution.py:36
  142.4 26.7 %collective-permute-start.15 = (bf16[512,512]{1,0:T(8,128)(2,1)}, bf16[512,512]{1,0:T(8,128)(2,1)S(1)}, u32[]{:S(2)}, u32[]{:S(2)}) collective-permute-start(bf16[512,512]{1,0:T(8,128)(2,1)} %collective-permute-done.6), channel_id=1, source_target_pairs={{0,8},{8,0},{16,24},{24,16},{1,9},{9,1},{17,25},{25,17},{2,10},{10... | collective-permute-start | bytes 1572872 | tf_op jit(solution)/shard_map/ppermute | solution.py:36
  153.9 24.3 %collective-permute-start.13 = (bf16[4,256,256]{2,1,0:T(8,128)(2,1)S(1)}, bf16[4,256,256]{2,1,0:T(8,128)(2,1)S(1)}, u32[]{:S(2)}, u32[]{:S(2)}) collective-permute-start(bf16[4,256,256]{2,1,0:T(8,128)(2,1)S(1)} %get-tuple-element.342), channel_id=1, source_target_pairs={{0,8},{8,0},{16,24},{24,16},{1,9},{9,1},{17,25},{25,17},{2,10},{10... | collective-permute-start | bytes 1572872 | tf_op jit(solution)/shard_map/ppermute | solution.py:36
  157.2 24.6 %collective-permute-start.14 = (bf16[4,256,256]{2,1,0:T(8,128)(2,1)S(1)}, bf16[4,256,256]{2,1,0:T(8,128)(2,1)S(1)}, u32[]{:S(2)}, u32[]{:S(2)}) collective-permute-start(bf16[4,256,256]{2,1,0:T(8,128)(2,1)S(1)} %get-tuple-element.341), channel_id=1, source_target_pairs={{0,16},{8,24},{16,0},{24,8},{1,17},{9,25},{17,1},{25,9},{2,18},{10... | collective-permute-start | bytes 1572872 | tf_op jit(solution)/shard_map/ppermute | solution.py:36
  184.2 43.8 %collective-permute-start.19 = (bf16[2048,512]{1,0:T(8,128)(2,1)S(1)}, bf16[2048,512]{1,0:T(8,128)(2,1)}, u32[]{:S(2)}, u32[]{:S(2)}) collective-permute-start(bf16[2048,512]{1,0:T(8,128)(2,1)S(1)} %constant_dynamic-update-slice_fusion.refs_0_), channel_id=1, source_target_pairs={{0,1},{1,0},{2,3},{3,2},{4,5},{5,4},{6,7},{7,6},{8,9},{9,8},{10,11... | collective-permute-start | bytes 6291464 | tf_op jit(solution)/shard_map/ppermute | solution.py:36
  184.9 43.2 %collective-permute-start.20 = (bf16[2048,512]{1,0:T(8,128)(2,1)S(1)}, bf16[2048,512]{1,0:T(8,128)(2,1)}, u32[]{:S(2)}, u32[]{:S(2)}) collective-permute-start(bf16[2048,512]{1,0:T(8,128)(2,1)S(1)} %constant_dynamic-update-slice_fusion.refs_0_), channel_id=1, source_target_pairs={{0,2},{1,3},{2,0},{3,1},{4,6},{5,7},{6,4},{7,5},{8,10},{9,11},{10,... | collective-permute-start | bytes 6291464 | tf_op jit(solution)/shard_map/ppermute | solution.py:36
  186.5 21.0 %collective-permute-start.17 = (bf16[512,512]{1,0:T(8,128)(2,1)S(1)}, bf16[512,512]{1,0:T(8,128)(2,1)S(1)}, u32[]{:S(2)}, u32[]{:S(2)}) collective-permute-start(bf16[512,512]{1,0:T(8,128)(2,1)S(1)} %multiply_convert_fusion.2), channel_id=1, source_target_pairs={{0,16},{8,24},{16,0},{24,8},{1,17},{9,25},{17,1},{25,9},{2,18},{10... | collective-permute-start | bytes 1572872 | tf_op jit(solution)/shard_map/ppermute | solution.py:36
  186.8 21.3 %collective-permute-start.16 = (bf16[512,512]{1,0:T(8,128)(2,1)S(1)}, bf16[512,512]{1,0:T(8,128)(2,1)S(1)}, u32[]{:S(2)}, u32[]{:S(2)}) collective-permute-start(bf16[512,512]{1,0:T(8,128)(2,1)S(1)} %multiply_convert_fusion.2), channel_id=1, source_target_pairs={{0,8},{8,0},{16,24},{24,16},{1,9},{9,1},{17,25},{25,17},{2,10},{10... | collective-permute-start | bytes 1572872 | tf_op jit(solution)/shard_map/ppermute | solution.py:36
  231.5 43.7 %collective-permute-start.24 = (bf16[2048,512]{1,0:T(8,128)(2,1)}, bf16[2048,512]{1,0:T(8,128)(2,1)}, u32[]{:S(2)}, u32[]{:S(2)}) collective-permute-start(bf16[2048,512]{1,0:T(8,128)(2,1)} %constant_dynamic-update-slice_fusion.4.refs_6_), channel_id=1, source_target_pairs={{0,1},{1,0},{2,3},{3,2},{4,5},{5,4},{6,7},{7,6},{8,9},{9,8},{10,11... | collective-permute-start | bytes 6291464 | tf_op jit(solution)/shard_map/ppermute | solution.py:36
  233.1 44.6 %collective-permute-start.25 = (bf16[2048,512]{1,0:T(8,128)(2,1)}, bf16[2048,512]{1,0:T(8,128)(2,1)}, u32[]{:S(2)}, u32[]{:S(2)}) collective-permute-start(bf16[2048,512]{1,0:T(8,128)(2,1)} %constant_dynamic-update-slice_fusion.4.refs_6_), channel_id=1, source_target_pairs={{0,2},{1,3},{2,0},{3,1},{4,6},{5,7},{6,4},{7,5},{8,10},{9,11},{10,... | collective-permute-start | bytes 6291464 | tf_op jit(solution)/shard_map/ppermute | solution.py:36
  234.8 20.1 %collective-permute-start.22 = (bf16[4,256,256]{2,1,0:T(8,128)(2,1)S(1)}, bf16[4,256,256]{2,1,0:T(8,128)(2,1)S(1)}, u32[]{:S(2)}, u32[]{:S(2)}) collective-permute-start(bf16[4,256,256]{2,1,0:T(8,128)(2,1)S(1)} %get-tuple-element.339), channel_id=1, source_target_pairs={{0,8},{8,0},{16,24},{24,16},{1,9},{9,1},{17,25},{25,17},{2,10},{10... | collective-permute-start | bytes 1572872 | tf_op jit(solution)/shard_map/ppermute | solution.py:36
  236.9 38.2 %collective-permute-start.23 = (bf16[4,256,256]{2,1,0:T(8,128)(2,1)S(1)}, bf16[4,256,256]{2,1,0:T(8,128)(2,1)S(1)}, u32[]{:S(2)}, u32[]{:S(2)}) collective-permute-start(bf16[4,256,256]{2,1,0:T(8,128)(2,1)S(1)} %get-tuple-element.338), channel_id=1, source_target_pairs={{0,16},{8,24},{16,0},{24,8},{1,17},{9,25},{17,1},{25,9},{2,18},{10... | collective-permute-start | bytes 1572872 | tf_op jit(solution)/shard_map/ppermute | solution.py:36
  239.9 35.3 %collective-permute-start.21 = (bf16[4,256,256]{2,1,0:T(8,128)(2,1)S(1)}, bf16[4,256,256]{2,1,0:T(8,128)(2,1)S(1)}, u32[]{:S(2)}, u32[]{:S(2)}) collective-permute-start(bf16[4,256,256]{2,1,0:T(8,128)(2,1)S(1)} %constant_dynamic-slice_fusion.8), channel_id=1, source_target_pairs={{0,24},{8,16},{16,8},{24,0},{1,25},{9,17},{17,9},{25,1},{2,26},{10... | collective-permute-start | bytes 1572872 | tf_op jit(solution)/shard_map/ppermute | solution.py:36
  279.0 18.9 %collective-permute-start.28 = (bf16[1024,512]{1,0:T(8,128)(2,1)S(1)}, bf16[1024,512]{1,0:T(8,128)(2,1)S(1)}, u32[]{:S(2)}, u32[]{:S(2)}) collective-permute-start(bf16[1024,512]{1,0:T(8,128)(2,1)S(1)} %slice.333), channel_id=1, source_target_pairs={{0,2},{1,3},{2,0},{3,1},{4,6},{5,7},{6,4},{7,5},{8,10},{9,11},{10,... | collective-permute-start | bytes 3145736 | tf_op jit(solution)/shard_map/ppermute | solution.py:36
  288.7 33.0 %collective-permute-start.26 = (bf16[4,4,256,256]{3,2,1,0:T(8,128)(2,1)}, bf16[4,4,256,256]{3,2,1,0:T(8,128)(2,1)}, u32[]{:S(2)}, u32[]{:S(2)}) collective-permute-start(bf16[4,4,256,256]{3,2,1,0:T(8,128)(2,1)} %pad_maximum_fusion.1.refs_2_.refs_5_), channel_id=1, source_target_pairs={{0,4},{4,0},{1,5},{5,1},{2,6},{6,2},{3,7},{7,3},{8,12},{12,8},{9,1... | collective-permute-start | bytes 6291464 | tf_op jit(solution)/shard_map/ppermute | solution.py:36
  299.9 23.9 %collective-permute-start.30 = (bf16[4,4,256,256]{3,2,1,0:T(8,128)(2,1)}, bf16[4,4,256,256]{3,2,1,0:T(8,128)(2,1)}, u32[]{:S(2)}, u32[]{:S(2)}) collective-permute-start(bf16[4,4,256,256]{3,2,1,0:T(8,128)(2,1)} %pad_maximum_fusion.2.refs_4_.refs_7_), channel_id=1, source_target_pairs={{0,4},{4,0},{1,5},{5,1},{2,6},{6,2},{3,7},{7,3},{8,12},{12,8},{9,1... | collective-permute-start | bytes 6291464 | tf_op jit(solution)/shard_map/ppermute | solution.py:36
  305.3 55.2 %collective-permute-start.35 = (bf16[1024,512]{1,0:T(8,128)(2,1)S(1)}, bf16[1024,512]{1,0:T(8,128)(2,1)S(1)}, u32[]{:S(2)}, u32[]{:S(2)}) collective-permute-start(bf16[1024,512]{1,0:T(8,128)(2,1)S(1)} %slice.336), channel_id=1, source_target_pairs={{0,1},{1,0},{2,3},{3,2},{4,5},{5,4},{6,7},{7,6},{8,9},{9,8},{10,11... | collective-permute-start | bytes 3145736 | tf_op jit(solution)/shard_map/ppermute | solution.py:36
  308.2 52.3 %collective-permute-start.34 = (bf16[1024,512]{1,0:T(8,128)(2,1)}, bf16[1024,512]{1,0:T(8,128)(2,1)S(1)}, u32[]{:S(2)}, u32[]{:S(2)}) collective-permute-start(bf16[1024,512]{1,0:T(8,128)(2,1)} %slice.335), channel_id=1, source_target_pairs={{0,2},{1,3},{2,0},{3,1},{4,6},{5,7},{6,4},{7,5},{8,10},{9,11},{10,... | collective-permute-start | bytes 3145736 | tf_op jit(solution)/shard_map/ppermute | solution.py:36
  310.1 47.4 %collective-permute-start.31 = (bf16[4,256,256]{2,1,0:T(8,128)(2,1)}, bf16[4,256,256]{2,1,0:T(8,128)(2,1)S(1)}, u32[]{:S(2)}, u32[]{:S(2)}) collective-permute-start(bf16[4,256,256]{2,1,0:T(8,128)(2,1)} %get-tuple-element.336), channel_id=1, source_target_pairs={{0,8},{8,0},{16,24},{24,16},{1,9},{9,1},{17,25},{25,17},{2,10},{10... | collective-permute-start | bytes 1572872 | tf_op jit(solution)/shard_map/ppermute | solution.py:36
  321.7 38.8 %collective-permute-start.32 = (bf16[4,256,256]{2,1,0:T(8,128)(2,1)}, bf16[4,256,256]{2,1,0:T(8,128)(2,1)S(1)}, u32[]{:S(2)}, u32[]{:S(2)}) collective-permute-start(bf16[4,256,256]{2,1,0:T(8,128)(2,1)} %get-tuple-element.335), channel_id=1, source_target_pairs={{0,16},{8,24},{16,0},{24,8},{1,17},{9,25},{17,1},{25,9},{2,18},{10... | collective-permute-start | bytes 1572872 | tf_op jit(solution)/shard_map/ppermute | solution.py:36
  323.7 36.8 %collective-permute-start.33 = (bf16[4,256,256]{2,1,0:T(8,128)(2,1)S(1)}, bf16[4,256,256]{2,1,0:T(8,128)(2,1)S(1)}, u32[]{:S(2)}, u32[]{:S(2)}) collective-permute-start(bf16[4,256,256]{2,1,0:T(8,128)(2,1)S(1)} %get-tuple-element.334), channel_id=1, source_target_pairs={{0,24},{8,16},{16,8},{24,0},{1,25},{9,17},{17,9},{25,1},{2,26},{10... | collective-permute-start | bytes 1572872 | tf_op jit(solution)/shard_map/ppermute | solution.py:36
  382.1 45.4 %collective-permute-start.38 = (bf16[4,256,256]{2,1,0:T(8,128)(2,1)}, bf16[4,256,256]{2,1,0:T(8,128)(2,1)S(1)}, u32[]{:S(2)}, u32[]{:S(2)}) collective-permute-start(bf16[4,256,256]{2,1,0:T(8,128)(2,1)} %get-tuple-element.332), channel_id=1, source_target_pairs={{0,8},{8,0},{16,24},{24,16},{1,9},{9,1},{17,25},{25,17},{2,10},{10... | collective-permute-start | bytes 1572872 | tf_op jit(solution)/shard_map/ppermute | solution.py:36
  392.6 35.0 %collective-permute-start.39 = (bf16[4,256,256]{2,1,0:T(8,128)(2,1)}, bf16[4,256,256]{2,1,0:T(8,128)(2,1)S(1)}, u32[]{:S(2)}, u32[]{:S(2)}) collective-permute-start(bf16[4,256,256]{2,1,0:T(8,128)(2,1)} %get-tuple-element.331), channel_id=1, source_target_pairs={{0,16},{8,24},{16,0},{24,8},{1,17},{9,25},{17,1},{25,9},{2,18},{10... | collective-permute-start | bytes 1572872 | tf_op jit(solution)/shard_map/ppermute | solution.py:36
  424.4 30.7 %collective-permute-start.40 = (bf16[2,528,512]{2,1,0:T(8,128)(2,1)S(1)}, bf16[2,528,512]{2,1,0:T(8,128)(2,1)S(1)}, u32[]{:S(2)}, u32[]{:S(2)}) collective-permute-start(bf16[2,528,512]{2,1,0:T(8,128)(2,1)S(1)} %get-tuple-element.319), channel_id=1, source_target_pairs={{0,1},{1,0},{2,3},{3,2},{4,5},{5,4},{6,7},{7,6},{8,9},{9,8},{10,11... | collective-permute-start | bytes 3244040 | tf_op jit(solution)/shard_map/ppermute | solution.py:36
  425.0 30.1 %collective-permute-start.41 = (bf16[2,528,512]{2,1,0:T(8,128)(2,1)S(1)}, bf16[2,528,512]{2,1,0:T(8,128)(2,1)S(1)}, u32[]{:S(2)}, u32[]{:S(2)}) collective-permute-start(bf16[2,528,512]{2,1,0:T(8,128)(2,1)S(1)} %get-tuple-element.318), channel_id=1, source_target_pairs={{0,2},{1,3},{2,0},{3,1},{4,6},{5,7},{6,4},{7,5},{8,10},{9,11},{10,... | collective-permute-start | bytes 3244040 | tf_op jit(solution)/shard_map/ppermute | solution.py:36
  426.1 28.9 %collective-permute-start.42 = (bf16[4,256,256]{2,1,0:T(8,128)(2,1)}, bf16[4,256,256]{2,1,0:T(8,128)(2,1)S(1)}, u32[]{:S(2)}, u32[]{:S(2)}) collective-permute-start(bf16[4,256,256]{2,1,0:T(8,128)(2,1)} %get-tuple-element.330), channel_id=1, source_target_pairs={{0,24},{8,16},{16,8},{24,0},{1,25},{9,17},{17,9},{25,1},{2,26},{10... | collective-permute-start | bytes 1572872 | tf_op jit(solution)/shard_map/ppermute | solution.py:36
  459.7 29.0 %collective-permute-start.45 = (bf16[528,512]{1,0:T(8,128)(2,1)}, bf16[528,512]{1,0:T(8,128)(2,1)S(1)}, u32[]{:S(2)}, u32[]{:S(2)}) collective-permute-start(bf16[528,512]{1,0:T(8,128)(2,1)} %get-tuple-element.315), channel_id=1, source_target_pairs={{0,2},{1,3},{2,0},{3,1},{4,6},{5,7},{6,4},{7,5},{8,10},{9,11},{10,... | collective-permute-start | bytes 1622024 | tf_op jit(solution)/shard_map/ppermute | solution.py:36
  460.7 28.0 %collective-permute-start.46 = (bf16[528,512]{1,0:T(8,128)(2,1)}, bf16[528,512]{1,0:T(8,128)(2,1)}, u32[]{:S(2)}, u32[]{:S(2)}) collective-permute-start(bf16[528,512]{1,0:T(8,128)(2,1)} %get-tuple-element.314), channel_id=1, source_target_pairs={{0,1},{1,0},{2,3},{3,2},{4,5},{5,4},{6,7},{7,6},{8,9},{9,8},{10,11... | collective-permute-start | bytes 1622024 | tf_op jit(solution)/shard_map/ppermute | solution.py:36
  463.7 33.3 %collective-permute-start.43 = (bf16[2,528,512]{2,1,0:T(8,128)(2,1)}, bf16[2,528,512]{2,1,0:T(8,128)(2,1)S(1)}, u32[]{:S(2)}, u32[]{:S(2)}) collective-permute-start(bf16[2,528,512]{2,1,0:T(8,128)(2,1)} %get-tuple-element.317), channel_id=1, source_target_pairs={{0,1},{1,0},{2,3},{3,2},{4,5},{5,4},{6,7},{7,6},{8,9},{9,8},{10,11... | collective-permute-start | bytes 3244040 | tf_op jit(solution)/shard_map/ppermute | solution.py:36
  464.2 32.8 %collective-permute-start.44 = (bf16[2,528,512]{2,1,0:T(8,128)(2,1)}, bf16[2,528,512]{2,1,0:T(8,128)(2,1)S(1)}, u32[]{:S(2)}, u32[]{:S(2)}) collective-permute-start(bf16[2,528,512]{2,1,0:T(8,128)(2,1)} %get-tuple-element.316), channel_id=1, source_target_pairs={{0,2},{1,3},{2,0},{3,1},{4,6},{5,7},{6,4},{7,5},{8,10},{9,11},{10,... | collective-permute-start | bytes 3244040 | tf_op jit(solution)/shard_map/ppermute | solution.py:36
  503.6 23.8 %collective-permute-start.47 = (bf16[2,528,512]{2,1,0:T(8,128)(2,1)}, bf16[2,528,512]{2,1,0:T(8,128)(2,1)S(1)}, u32[]{:S(2)}, u32[]{:S(2)}) collective-permute-start(bf16[2,528,512]{2,1,0:T(8,128)(2,1)} %pad_maximum_fusion.5), channel_id=1, source_target_pairs={{0,8},{8,0},{16,24},{24,16},{1,9},{9,1},{17,25},{25,17},{2,10},{10... | collective-permute-start | bytes 3244040 | tf_op jit(solution)/shard_map/ppermute | solution.py:36
  507.0 19.6 %collective-permute-start.48 = (bf16[528,512]{1,0:T(8,128)(2,1)}, bf16[528,512]{1,0:T(8,128)(2,1)}, u32[]{:S(2)}, u32[]{:S(2)}) collective-permute-start(bf16[528,512]{1,0:T(8,128)(2,1)} %get-tuple-element.311), channel_id=1, source_target_pairs={{0,2},{1,3},{2,0},{3,1},{4,6},{5,7},{6,4},{7,5},{8,10},{9,11},{10,... | collective-permute-start | bytes 1622024 | tf_op jit(solution)/shard_map/ppermute | solution.py:36
  527.4 218.7 %reduce-scatter.6.cloned.1.call-start = ((), (), s32[]{:S(2)}) async-start(), calls=%async_computation.5 | async-start | bytes 2621440 | tf_op jit(solution)/shard_map/reduce_scatter | solution.py:822
  527.4 32.5 %collective-permute-start.51 = (bf16[4,2,4,256,256]{4,3,2,1,0:T(8,128)(2,1)}, bf16[4,2,4,256,256]{4,3,2,1,0:T(8,128)(2,1)}, u32[]{:S(2)}, u32[]{:S(2)}) collective-permute-start(bf16[4,2,4,256,256]{4,3,2,1,0:T(8,128)(2,1)} %get-tuple-element.205), channel_id=1, source_target_pairs={{0,4},{4,0},{1,5},{5,1},{2,6},{6,2},{3,7},{7,3},{8,12},{12,8},{9,1... | collective-permute-start | bytes 12582920 | tf_op jit(solution)/shard_map/ppermute | solution.py:36
  531.0 26.6 %collective-permute-start.50 = (bf16[1,528,512]{2,1,0:T(8,128)(2,1)}, bf16[1,528,512]{2,1,0:T(8,128)(2,1)}, u32[]{:S(2)}, u32[]{:S(2)}) collective-permute-start(bf16[1,528,512]{2,1,0:T(8,128)(2,1)} %fusion.50), channel_id=1, source_target_pairs={{0,16},{8,24},{16,0},{24,8},{1,17},{9,25},{17,1},{25,9},{2,18},{10... | collective-permute-start | bytes 1622024 | tf_op jit(solution)/shard_map/ppermute | solution.py:36
  572.4 19.2 %collective-permute-start.54 = (bf16[512,512]{1,0:T(8,128)(2,1)S(1)}, bf16[512,512]{1,0:T(8,128)(2,1)S(1)}, u32[]{:S(2)}, u32[]{:S(2)}) collective-permute-start(bf16[512,512]{1,0:T(8,128)(2,1)S(1)} %get-tuple-element.305), channel_id=1, source_target_pairs={{0,1},{1,0},{2,3},{3,2},{4,5},{5,4},{6,7},{7,6},{8,9},{9,8},{10,11... | collective-permute-start | bytes 1572872 | tf_op jit(solution)/shard_map/ppermute | solution.py:36
  573.8 19.4 %collective-permute-start.55 = (bf16[512,512]{1,0:T(8,128)(2,1)S(1)}, bf16[512,512]{1,0:T(8,128)(2,1)S(1)}, u32[]{:S(2)}, u32[]{:S(2)}) collective-permute-start(bf16[512,512]{1,0:T(8,128)(2,1)S(1)} %get-tuple-element.305), channel_id=1, source_target_pairs={{0,2},{1,3},{2,0},{3,1},{4,6},{5,7},{6,4},{7,5},{8,10},{9,11},{10,... | collective-permute-start | bytes 1572872 | tf_op jit(solution)/shard_map/ppermute | solution.py:36
  575.3 45.4 %collective-permute-start.58 = (bf16[2,4,256,256]{3,2,1,0:T(8,128)(2,1)S(1)}, bf16[2,4,256,256]{3,2,1,0:T(8,128)(2,1)S(1)}, u32[]{:S(2)}, u32[]{:S(2)}) collective-permute-start(bf16[2,4,256,256]{3,2,1,0:T(8,128)(2,1)S(1)} %get-tuple-element.322), channel_id=1, source_target_pairs={{0,8},{8,0},{16,24},{24,16},{1,9},{9,1},{17,25},{25,17},{2,10},{10... | collective-permute-start | bytes 3145736 | tf_op jit(solution)/shard_map/ppermute | solution.py:36
  575.4 47.1 %collective-permute-start.59 = (bf16[2,4,256,256]{3,2,1,0:T(8,128)(2,1)S(1)}, bf16[2,4,256,256]{3,2,1,0:T(8,128)(2,1)S(1)}, u32[]{:S(2)}, u32[]{:S(2)}) collective-permute-start(bf16[2,4,256,256]{3,2,1,0:T(8,128)(2,1)S(1)} %get-tuple-element.321), channel_id=1, source_target_pairs={{0,16},{8,24},{16,0},{24,8},{1,17},{9,25},{17,1},{25,9},{2,18},{10... | collective-permute-start | bytes 3145736 | tf_op jit(solution)/shard_map/ppermute | solution.py:36
  623.6 24.3 %collective-permute-start.60 = (bf16[2,4,256,256]{3,2,1,0:T(8,128)(2,1)S(1)}, bf16[2,4,256,256]{3,2,1,0:T(8,128)(2,1)S(1)}, u32[]{:S(2)}, u32[]{:S(2)}) collective-permute-start(bf16[2,4,256,256]{3,2,1,0:T(8,128)(2,1)S(1)} %get-tuple-element.215), channel_id=1, source_target_pairs={{0,24},{8,16},{16,8},{24,0},{1,25},{9,17},{17,9},{25,1},{2,26},{10... | collective-permute-start | bytes 3145736 | tf_op jit(solution)/shard_map/ppermute | solution.py:36
  651.7 168.1 %reduce-scatter.8.cloned.1.call-start = ((), (), s32[]{:S(2)}) async-start(), calls=%async_computation.6 | async-start | bytes 9437184 | tf_op jit(solution)/shard_map/reduce_scatter | solution.py:879
  674.0 25.6 %collective-permute-start.64 = (f32[19,512]{1,0:T(8,128)S(1)}, f32[19,512]{1,0:T(8,128)S(1)}, u32[]{:S(2)}, u32[]{:S(2)}) collective-permute-start(f32[19,512]{1,0:T(8,128)S(1)} %fusion.94), channel_id=1, source_target_pairs={{0,8},{8,0},{16,24},{24,16},{1,9},{9,1},{17,25},{25,17},{2,10},{10... | collective-permute-start | bytes 116744 | tf_op jit(solution)/shard_map/ppermute | solution.py:36
  787.1 23.2 %collective-permute-start.76 = (bf16[512,512]{1,0:T(8,128)(2,1)}, bf16[512,512]{1,0:T(8,128)(2,1)}, u32[]{:S(2)}, u32[]{:S(2)}) collective-permute-start(bf16[512,512]{1,0:T(8,128)(2,1)} %get-tuple-element.301), channel_id=1, source_target_pairs={{0,1},{1,0},{2,3},{3,2},{4,5},{5,4},{6,7},{7,6},{8,9},{9,8},{10,11... | collective-permute-start | bytes 1572872 | tf_op jit(solution)/shard_map/ppermute | solution.py:36
  788.2 23.3 %collective-permute-start.77 = (bf16[512,512]{1,0:T(8,128)(2,1)}, bf16[512,512]{1,0:T(8,128)(2,1)}, u32[]{:S(2)}, u32[]{:S(2)}) collective-permute-start(bf16[512,512]{1,0:T(8,128)(2,1)} %get-tuple-element.301), channel_id=1, source_target_pairs={{0,2},{1,3},{2,0},{3,1},{4,6},{5,7},{6,4},{7,5},{8,10},{9,11},{10,... | collective-permute-start | bytes 1572872 | tf_op jit(solution)/shard_map/ppermute | solution.py:36
  (127 other events, 1538.7 us)
Sparse Core Ops, SparseCore 0:
  11.8 71.7 all-gather.2
  85.2 46.1 all-gather.4
  527.5 97.0 reduce-scatter.9
  651.8 63.4 reduce-scatter.5
  723.1 89.0 reduce-scatter.7

commit v4 on v3

--- a/solution.py
+++ b/solution.py
@@ -737,7 +737,8 @@
     gate_parts[-1], up_parts, m_near = held[0], held[1:nz], held[nz:]
     gate_parts = both_cores(gate_parts)
     up_parts += fetch(after(w_up, m_near[0]), last)
-    up_parts[-1], *pieces = fence(up_parts[-1], m_flat, *m_near, *spread_tensor_cross(m_near))
+    held = fence(m_flat, *m_near, *spread_tensor_cross(m_near), up_parts[-1])
+    up_parts[-1], pieces = held[-1], held[:-1]
     up_parts = both_cores(up_parts)
     down_parts = fetch(after(w_down, up_parts[0]), range(nz))
     cot_cross = spread_tensor_cross([after(x, pieces[-1]) for x in cot_near])
@@ -748,9 +749,7 @@
     act, up, hidden, probs_all, m_all = forward_call(
         idx, pieces, places, mask_all, router_q, gate_parts, up_parts, nz
     )
-    hidden, *held = fence(hidden, *down_parts, *cot_cross)
-    down_parts, cot_cross = held[:nz], held[nz:]
-    down_parts = both_cores(down_parts)
+    hidden, *cot_cross = fence(hidden, *cot_cross)
     down_keep, down_give, cot_all = down_grad_call(
         idx, [cot_flat, *cot_near, *cot_cross], hidden, own_e, nz, n
     )
@@ -760,29 +759,34 @@
         summed = (keep.astype(f32) + got.astype(f32)).astype(bf16)
         return [swap(summed[k], "z", k) for k in range(nz)]
 
+    down_give, *down_parts = fence(down_give, *down_parts)
+    down_parts = both_cores(down_parts)
     down_got = swap(down_give, "core", 1)
-    down_own = to_owners(down_keep, down_got)
     half_call = lambda first, probs: backward_call(
         idx, first, cot_all, act, up, probs, mask_all, gate_parts + up_parts + down_parts
     )
     odds, evens = range(1, nz, 2), range(0, nz, 2)
-    late = half_call(1, after(probs_all, down_own[0]))
+    late = half_call(1, after(probs_all, down_give))
     first = {k: scatter_first(late[0][k // 2], k // 2 % 2) for k in odds}
-    held = fence(late[1], *down_own[:-1])
-    down_own[:-1] = held[1:]
-    early = half_call(0, after(probs_all, *held))
-    held = fence(*early, *(first[k] for k in odds), down_own[-1])
-    early, got, down_own[-1] = held[:3], dict(zip(odds, held[3:-1])), held[-1]
+    down_own = to_owners(after(down_keep, late[1]), down_got)
+    early = half_call(0, after(probs_all, late[1], down_own[0]))
+    held = fence(*early, *down_own[:-1], *(first[k] for k in odds))
+    early, down_own[:-1] = held[:3], held[3 : 2 + nz]
+    got = dict(zip(odds, held[2 + nz :]))
     second = {k: scatter_second(late[0][k // 2], got[k], k // 2 % 2) for k in odds}
     first = {k: scatter_first(early[0][k // 2], k // 2 % 2) for k in evens}
     up_keep, up_give = up_grad_call(idx, m_all, early[1:3], late[1:3], own_e, nz, n)
     few = [second[k] for k in odds if second[k][1] is not None]
     held = fence(
-        up_keep, up_give, *(first[k] for k in evens), *(x[1] for x in few)
-    )
-    (up_keep, up_give), got = held[:2], dict(zip(evens, held[2:]))
+        up_keep,
+        up_give,
+        down_own[-1],
+        *(first[k] for k in evens),
+        *(x[1] for x in few),
+    )
+    (up_keep, up_give, down_own[-1]), got = held[:3], dict(zip(evens, held[3:]))
     if few:
-        second = {k: (second[k][0], x) for k, x in zip(odds, held[2 + nz // 2 :])}
+        second = {k: (second[k][0], x) for k, x in zip(odds, held[3 + nz // 2 :])}
     near = scatter_z_near({k: scatter_third(*second[k]) for k in odds})
     second = {k: scatter_second(early[0][k // 2], got[k], k // 2 % 2) for k in evens}
     up_got = swap(up_give, "core", 1)
@@ -819,9 +823,13 @@
     dresid_low, *up_own[:-1] = fence(dresid_low, *up_own[:-1])
     up_own[-1] = swap(after(up_last, dresid_low), "z", nz - 1)
     moe_sum = after(moe_sum, dresid_low)
-    moe_own = lax.psum_scatter(moe_sum, "z", scatter_dimension=0, tiled=False)
-
-    wo_grad = jnp.einsum("sd,sa->da", dresid_low, joined, preferred_element_type=f32)
+    moe_parts = {
+        k: lax.dynamic_index_in_dim(moe_sum, me_z ^ k, 0, keepdims=False) for k in range(nz)
+    }
+    moe_near = scatter_z_near({k: moe_parts[k] for k in range(1, nz, 2)})
+
+    wo_grad = jnp.einsum("sa,sd->ad", joined, dresid_low, preferred_element_type=f32)
+    wo_own = lax.psum_scatter(wo_grad.astype(bf16), dp, scatter_dimension=1, tiled=True)
     dout = (
         jnp.einsum("sd,ad->sa", dresid_low, wo_full, preferred_element_type=f32)
         .astype(bf16)
@@ -831,7 +839,7 @@
     dv = jnp.einsum("hqk,qhd->khd", weights_low, dout, preferred_element_type=f32)
     inner = jnp.sum(weights * dweights, -1, keepdims=True)
     dscores = (weights * (dweights - inner)).astype(bf16)
-    dscores, up_own[-1] = fence(dscores, up_own[-1])
+    dscores, up_own[-1], moe_near = fence(dscores, up_own[-1], moe_near)
     dq_rot = scale * jnp.einsum("hqk,khd->qhd", dscores, k_rot, preferred_element_type=f32)
     dk_rot = scale * jnp.einsum("hqk,qhd->khd", dscores, q_rot, preferred_element_type=f32)
     dq_norm = unrotate(dq_rot, cosine, sine).reshape(seq, local)
@@ -854,10 +862,11 @@
     smalls = jnp.concatenate(
         [q_gain_part[None], k_gain_part[None], moe_gain_part[None], router_part.T], 0
     )
-    dqkv, smalls = fence(dqkv, butterfly_sum(smalls, ("core", "z")))
+    moe_own = scatter_z_far({k: moe_parts[k].astype(f32) for k in range(0, nz, 2)}, moe_near)
+    dqkv, moe_own, smalls = fence(dqkv, moe_own, butterfly_sum(smalls, ("core", "z")))
     half = lax.dynamic_slice_in_dim(smalls[2:], me_c * slice_d, slice_d, 1)
     half = tensor_sum(jnp.where(me_t == me_z, half, 0.0))
-    mixed = gather_tensor((after(resid, dqkv) + moe_own.astype(f32)).astype(bf16))
+    mixed = gather_tensor((resid + moe_own).astype(bf16))
     wqkv_grad = jnp.einsum("sd,sa->da", a_low, dqkv, preferred_element_type=f32).astype(bf16)
     da_part = jnp.einsum("sa,da->sd", dqkv, wqkv_full, preferred_element_type=f32)
     blocks = columns_blocks(da_part.astype(bf16))
@@ -875,11 +884,10 @@
         (dresid + rate_x * (pulled_x - norm_x * inner_x)).astype(bf16)
     )
 
-    both_grads = jnp.concatenate([wqkv_grad, wo_grad.astype(bf16)], 1)
-    both_own = lax.psum_scatter(both_grads, dp, scatter_dimension=0, tiled=True)
-    tokens_grad, both_own = fence(tokens_grad, both_own)
-    both_own = both_own.astype(f32)
-    wqkv_own, wo_own = both_own[:, : 3 * local], both_own[:, 3 * local :].T
+    wqkv_grad, wo_own = fence(wqkv_grad, wo_own)
+    wqkv_own = lax.psum_scatter(wqkv_grad, dp, scatter_dimension=0, tiled=True)
+    tokens_grad, wqkv_own = fence(tokens_grad, wqkv_own)
+    wqkv_own, wo_own = wqkv_own.astype(f32), wo_own.astype(f32)
     attn_gain_grad = jnp.sum(jnp.concatenate([wq, wk, wv], 1).astype(f32) * wqkv_own, -1)
     attn_gain_grad = tensor_sum(attn_gain_grad) / attn_gain.astype(f32)
     return (

time: 846 us -> 830 us (0.981)
  starting transfers between devices: 140 us -> 114 us
  waiting for transfers between devices: 328 us -> 352 us
  other arithmetic: 85.9 us -> 74 us
    ppermute x84 -> x86, starting transfers between devices: 140 us -> 114 us  [swap(): return lax.ppermute(value, axis, [(i, i ^ mask) for i in range(n)])]
    ppermute x84 -> x86, waiting for transfers between devices: 254 us -> 278 us  [swap(): return lax.ppermute(value, axis, [(i, i ^ mask) for i in range(n)])]
    concatenate x1 -> x0, other arithmetic: 8.53 us -> none  [shards(): both_grads = jnp.concatenate([wqkv_grad, wo_grad.astype(bf16)], 1)]
    unnamed x185 -> x173, local copies, waits for them, and re-layouts: 24.9 us -> 17.2 us
  transfers between devices with their start and end apart: 89 -> 91, of which waited for: 47 -> 48; matrix products, arithmetic and copies ran while one was open for 20% -> 19% of each run, Pallas kernels for 16% -> 18%
where the time goes in v4:
time: 830 us; the launch traced here: 825 us
  waiting for transfers between devices  352 us (42%)
  Pallas kernels  150 us (18%)
  starting transfers between devices  114 us (14%)
  other arithmetic  74 us (9%)
  local copies, waits for them, and re-layouts  70.7 us (9%)
  matrix products  48.3 us (6%)
  between operations  15.9 us (2%)
    ppermute x86, waiting for transfers between devices, swap(): return lax.ppermute(value, axis, [(i, i ^ mask) for i in range(n)])  278 us
    ppermute x86, starting transfers between devices, swap(): return lax.ppermute(value, axis, [(i, i ^ mask) for i in range(n)])  114 us
    all_gather x1, waiting for transfers between devices, shards(): lax.all_gather(jnp.concatenate([wq, wk, wv, small], 1), dp, axis=0, tiled...  61.3 us
    pallas_call x2, Pallas kernels, backward_call(): pl.pallas_call(functools.partial(backward_kernel, nz, n, own_e, hid, slic...  54.7 us
    pallas_call x1, Pallas kernels, forward_call(): pl.pallas_call(functools.partial(forward_kernel, nz, n, own_e, hid, slice...  32.4 us
    pallas_call x1, Pallas kernels, up_grad_call(): pl.pallas_call(functools.partial(up_grad_kernel, nz, own_e, hid, seq, sli...  23.4 us
    pallas_call x1, Pallas kernels, output_call(): pl.pallas_call(functools.partial(output_kernel, nz, own_e, hid, slice_d,...  17.2 us
    unnamed x173, local copies, waits for them, and re-layouts  17.2 us
  transfers between devices with their start and end apart: 91, of which 48 were waited for; matrix products, arithmetic and copies ran while one was open for 19% of the time, Pallas kernels for 18%

profile of v4, /device:TPU:0, one launch (start us, length us, event | category | flops | bytes accessed | tf_op | source)
XLA Modules:
  0.0 825.1 jit_solution(7700446623471923860)
XLA Ops:
  11.7 4.1 collective-permute-start.1
  22.3 61.3 %all-gather.3.cloned.1.call-done = bf16[2048,1664]{1,0:T(8,128)(2,1)} async-done(((bf16[256,1664]{1,0:T(8,128)(2,1)}), bf16[2048,1664]{1,0:T(8,128)(2,1)}) %all-gather.3.cloned.1.call-update) | async-done | bytes 6815760 | tf_op jit(solution)/shard_map/all_gather | solution.py:656
  85.5 6.5 fusion.4
  110.4 5.0 fusion.102
  115.4 3.5 convolution_convert_fusion.5
  118.9 12.5 %all-gather.5.cloned.1.call-done = bf16[512,2048]{1,0:T(8,128)(2,1)} async-done(((bf16[512,256]{1,0:T(8,128)(2,1)}), bf16[512,2048]{1,0:T(8,128)(2,1)}) %all-gather.5.cloned.1.call-update) | async-done | bytes 2097168 | tf_op jit(solution)/shard_map/all_gather | solution.py:672
  145.3 4.4 collective-permute-done.7
  153.6 3.4 collective-permute-start.13
  168.2 10.6 %collective-permute-done.13 = bf16[4,256,256]{2,1,0:T(8,128)(2,1)S(1)} collective-permute-done((bf16[4,256,256]{2,1,0:T(8,128)(2,1)S(1)}, bf16[4,256,256]{2,1,0:T(8,128)(2,1)S(1)}, u32[]{:S(2)}, u32[]{:S(2)}) %collective-permute-start.13) | collective-permute-done | bytes 524320 | tf_op jit(solution)/shard_map/ppermute | solution.py:36
  186.6 20.8 %collective-permute-done.17 = bf16[512,512]{1,0:T(8,128)(2,1)S(1)} collective-permute-done((bf16[512,512]{1,0:T(8,128)(2,1)S(1)}, bf16[512,512]{1,0:T(8,128)(2,1)S(1)}, u32[]{:S(2)}, u32[]{:S(2)}) %collective-permute-start.17) | collective-permute-done | bytes 524320 | tf_op jit(solution)/shard_map/ppermute | solution.py:36
  207.9 12.5 %collective-permute-done.18 = bf16[512,512]{1,0:T(8,128)(2,1)S(1)} collective-permute-done((bf16[512,512]{1,0:T(8,128)(2,1)S(1)}, bf16[512,512]{1,0:T(8,128)(2,1)S(1)}, u32[]{:S(2)}, u32[]{:S(2)}) %collective-permute-start.18) | collective-permute-done | bytes 524320 | tf_op jit(solution)/shard_map/ppermute | solution.py:36
  220.3 7.7 collective-permute-done.19.refs_1_
  239.3 14.0 %collective-permute-done.22 = bf16[4,256,256]{2,1,0:T(8,128)(2,1)S(1)} collective-permute-done((bf16[4,256,256]{2,1,0:T(8,128)(2,1)S(1)}, bf16[4,256,256]{2,1,0:T(8,128)(2,1)S(1)}, u32[]{:S(2)}, u32[]{:S(2)}) %collective-permute-start.22) | collective-permute-done | bytes 524320 | tf_op jit(solution)/shard_map/ppermute | solution.py:36
  253.4 20.5 %collective-permute-done.23 = bf16[4,256,256]{2,1,0:T(8,128)(2,1)S(1)} collective-permute-done((bf16[4,256,256]{2,1,0:T(8,128)(2,1)S(1)}, bf16[4,256,256]{2,1,0:T(8,128)(2,1)S(1)}, u32[]{:S(2)}, u32[]{:S(2)}) %collective-permute-start.23) | collective-permute-done | bytes 524320 | tf_op jit(solution)/shard_map/ppermute | solution.py:36
  284.5 7.9 collective-permute-done.29
  292.4 5.8 collective-permute-done.27.refs_9_
  309.6 7.4 collective-permute-start.33
  320.9 32.4 %shard_map.254 = (f32[2048,1024]{1,0:T(8,128)}, f32[2048,1024]{1,0:T(8,128)}, bf16[2048,1024]{1,0:T(8,128)(2,1)}, f32[2048,128]{1,0:T(8,128)}, bf16[2048,2048]{1,0:T(8,128)(2,1)}) custom-call(s32[3]{0:T(128)} %pad_add_fusion.idx, f32[2048,128]{1,0:T(8,128)} %pad_convert_fusion.refs_0_.refs_4_, bf16[4,512,128]{2,1,0:T(8,128)(2,1)} %bitcast.310, ...), custom_call_target="tpu_custom_call" | custom-call | flops 17179869184 | bytes 41943040 | tf_op jit(solution)/shard_map/pallas_call | solution.py:301
  353.4 15.2 %shard_map.255 = (bf16[4,4,256,256]{3,2,1,0:T(8,128)(2,1)S(1)}, bf16[4,4,256,256]{3,2,1,0:T(8,128)(2,1)}, bf16[4,2048,512]{2,1,0:T(8,128)(2,1)}) custom-call(s32[3]{0:T(128)S(1)} %copy-done.6, bf16[2048,1024]{1,0:T(8,128)(2,1)} %get-tuple-element.210.hid_ref, bf16[2048,512]{1,0:T(8,128)(2,1)} %copy-done.64, ...), custom_call_target="tpu_custom_call" | custom-call | flops 8589934592 | bytes 25165824 | tf_op jit(solution)/shard_map/pallas_call | solution.py:526
  370.5 5.9 collective-permute-done.36.refs_10_.far
  377.8 27.2 %shard_map.256 = (bf16[2,4,528,512]{3,2,1,0:T(8,128)(2,1)}, bf16[1024,1024]{1,0:T(8,128)(2,1)}, bf16[1024,1024]{1,0:T(8,128)(2,1)}) custom-call(s32[3]{0:T(128)} %pad_add_fusion.idx, bf16[4,4,512,512]{3,2,1,0:T(8,128)(2,1)} %bitcast.359, f32[2048,1024]{1,0:T(8,128)} %get-tuple-element.178.refs_1_, f32[2048,1024]{1,0:T(8,128)} %get-tuple-element.179.refs_2_, ...), custom_call_target="tpu_custom_call" | custom-call | flops 12884901888 | bytes 41943040 | tf_op jit(solution)/shard_map/pallas_call | solution.py:401
  415.1 27.4 %shard_map.257 = (bf16[2,4,528,512]{3,2,1,0:T(8,128)(2,1)}, bf16[1024,1024]{1,0:T(8,128)(2,1)}, bf16[1024,1024]{1,0:T(8,128)(2,1)}) custom-call(s32[3]{0:T(128)} %pad_add_fusion.idx, bf16[4,4,512,512]{3,2,1,0:T(8,128)(2,1)} %bitcast.360, f32[2048,1024]{1,0:T(8,128)} %get-tuple-element.178.refs_1_, f32[2048,1024]{1,0:T(8,128)} %get-tuple-element.179.refs_2_, ...), custom_call_target="tpu_custom_call" | custom-call | flops 12884901888 | bytes 41943040 | tf_op jit(solution)/shard_map/pallas_call | solution.py:401
  442.6 4.4 collective-permute-done.39.refs_6_
  447.8 3.7 fusion.36
  455.9 23.4 %shard_map.258 = (bf16[4,2,4,256,256]{4,3,2,1,0:T(8,128)(2,1)}, bf16[4,2,4,256,256]{4,3,2,1,0:T(8,128)(2,1)}) custom-call(s32[3]{0:T(128)S(1)} %copy-done.7, bf16[2048,2048]{1,0:T(8,128)(2,1)} %get-tuple-element.198.m_ref, bf16[1024,1024]{1,0:T(8,128)(2,1)S(1)} %copy-done.11, bf16[1024,1024]{1,0:T(8,128)(2,1)S(1)} %copy-done.10, ...), custom_call_target="tpu_custom_call" | custom-call | flops 17179869184 | bytes 25165824 | tf_op jit(solution)/shard_map/pallas_call | solution.py:574
  479.3 4.4 collective-permute-done.43
  489.5 3.7 collective-permute-start.47
  497.8 17.2 %shard_map.259 = bf16[4,4,512,512]{3,2,1,0:T(8,128)(2,1)} custom-call(s32[3]{0:T(128)S(1)} %copy-done.7, bf16[2048,1024]{1,0:T(8,128)(2,1)} %get-tuple-element.210.hid_ref, bf16[4,4,256,256]{3,2,1,0:T(8,128)(2,1)S(1)} %copy-done.1, bf16[4,4,256,256]{3,2,1,0:T(8,128)(2,1)S(1)} %copy-done.9), custom_call_target="tpu_custom_call" | custom-call | flops 8589934592 | bytes 16777216 | tf_op jit(solution)/shard_map/pallas_call | solution.py:461
  517.7 3.5 collective-permute-start.50
  525.9 20.2 %collective-permute-done.50 = bf16[1,528,512]{2,1,0:T(8,128)(2,1)} collective-permute-done((bf16[1,528,512]{2,1,0:T(8,128)(2,1)}, bf16[1,528,512]{2,1,0:T(8,128)(2,1)}, u32[]{:S(2)}, u32[]{:S(2)}) %collective-permute-start.50) | collective-permute-done | bytes 540704 | tf_op jit(solution)/shard_map/ppermute | solution.py:36
  557.1 3.7 add_convert_fusion
  570.7 10.1 %collective-permute-done.54 = bf16[512,512]{1,0:T(8,128)(2,1)} collective-permute-done((bf16[512,512]{1,0:T(8,128)(2,1)}, bf16[512,512]{1,0:T(8,128)(2,1)}, u32[]{:S(2)}, u32[]{:S(2)}) %collective-permute-start.54) | collective-permute-done | bytes 524320 | tf_op jit(solution)/shard_map/ppermute | solution.py:36
  590.1 5.0 collective-permute-done.56
  595.1 3.3 collective-permute-done.57
  599.3 13.6 %collective-permute-done.58.refs_1_ = bf16[2,4,256,256]{3,2,1,0:T(8,128)(2,1)S(1)} collective-permute-done((bf16[2,4,256,256]{3,2,1,0:T(8,128)(2,1)}, bf16[2,4,256,256]{3,2,1,0:T(8,128)(2,1)S(1)}, u32[]{:S(2)}, u32[]{:S(2)}) %collective-permute-start.58) | collective-permute-done | bytes 1048608 | tf_op jit(solution)/shard_map/ppermute | solution.py:36
  624.6 4.3 convolution_convert_fusion.1
  629.0 4.1 fusion.51
  635.8 5.2 multiply_convert_fusion
  641.1 5.1 collective-permute-done.60.refs_3_
  646.2 34.5 %collective-permute-done.61 = bf16[2,512,512]{2,1,0:T(8,128)(2,1)S(1)} collective-permute-done((bf16[2,512,512]{2,1,0:T(8,128)(2,1)S(1)}, bf16[2,512,512]{2,1,0:T(8,128)(2,1)S(1)}, u32[]{:S(2)}, u32[]{:S(2)}) %collective-permute-start.61) | collective-permute-done | bytes 1048608 | tf_op jit(solution)/shard_map/ppermute | solution.py:36
  702.5 7.6 collective-permute-done.66
  713.3 11.4 %collective-permute-done.67 = f32[19,512]{1,0:T(8,128)S(1)} collective-permute-done((f32[19,512]{1,0:T(8,128)S(1)}, f32[19,512]{1,0:T(8,128)S(1)}, u32[]{:S(2)}, u32[]{:S(2)}) %collective-permute-start.67) | collective-permute-done | bytes 38944 | tf_op jit(solution)/shard_map/ppermute | solution.py:36
  727.0 5.6 convolution_convert_fusion
  736.6 6.8 fusion.8
  751.6 8.9 %collective-permute-done.68 = bf16[2,256,512]{2,1,0:T(8,128)(2,1)S(1)} collective-permute-done((bf16[2,256,512]{2,1,0:T(8,128)(2,1)S(1)}, bf16[2,256,512]{2,1,0:T(8,128)(2,1)S(1)}, u32[]{:S(2)}, u32[]{:S(2)}) %collective-permute-start.68) | collective-permute-done | bytes 524320 | tf_op jit(solution)/shard_map/ppermute | solution.py:36
  763.3 3.5 collective-permute-done.74
  766.9 4.3 collective-permute-done.69
  790.8 6.9 shard_map.260
  (491 shorter events, 268.7 us)
Async XLA Ops:
  7.2 76.4 %all-gather.3.cloned.1.call-start = ((), (), s32[]{:S(2)}) async-start(), calls=%async_computation.3 | async-start | bytes 7667712 | tf_op jit(solution)/shard_map/all_gather | solution.py:656
  11.6 119.7 %all-gather.5.cloned.1.call-start = ((), (), s32[]{:S(2)}) async-start(), calls=%async_computation.4 | async-start | bytes 2359296 | tf_op jit(solution)/shard_map/all_gather | solution.py:672
  84.9 548.4 %reduce-scatter.10.cloned.1.call-start = ((), (), s32[]{:S(2)}) async-start(), calls=%async_computation.7 | async-start | bytes 10485760
  98.3 36.5 %collective-permute-start.6 = (bf16[512,512]{1,0:T(8,128)(2,1)}, bf16[512,512]{1,0:T(8,128)(2,1)}, u32[]{:S(2)}, u32[]{:S(2)}) collective-permute-start(bf16[512,512]{1,0:T(8,128)(2,1)} %constant_dynamic-slice_fusion.14), channel_id=1, source_target_pairs={{0,16},{8,24},{16,0},{24,8},{1,17},{9,25},{17,1},{25,9},{2,18},{10... | collective-permute-start | bytes 1572872 | tf_op jit(solution)/shard_map/ppermute | solution.py:36
  99.3 35.4 %collective-permute-start.5 = (bf16[512,512]{1,0:T(8,128)(2,1)}, bf16[512,512]{1,0:T(8,128)(2,1)}, u32[]{:S(2)}, u32[]{:S(2)}) collective-permute-start(bf16[512,512]{1,0:T(8,128)(2,1)} %constant_dynamic-slice_fusion.14), channel_id=1, source_target_pairs={{0,8},{8,0},{16,24},{24,16},{1,9},{9,1},{17,25},{25,17},{2,10},{10... | collective-permute-start | bytes 1572872 | tf_op jit(solution)/shard_map/ppermute | solution.py:36
  142.5 25.8 %collective-permute-start.15 = (bf16[512,512]{1,0:T(8,128)(2,1)}, bf16[512,512]{1,0:T(8,128)(2,1)S(1)}, u32[]{:S(2)}, u32[]{:S(2)}) collective-permute-start(bf16[512,512]{1,0:T(8,128)(2,1)} %collective-permute-done.6), channel_id=1, source_target_pairs={{0,8},{8,0},{16,24},{24,16},{1,9},{9,1},{17,25},{25,17},{2,10},{10... | collective-permute-start | bytes 1572872 | tf_op jit(solution)/shard_map/ppermute | solution.py:36
  153.6 25.2 %collective-permute-start.13 = (bf16[4,256,256]{2,1,0:T(8,128)(2,1)S(1)}, bf16[4,256,256]{2,1,0:T(8,128)(2,1)S(1)}, u32[]{:S(2)}, u32[]{:S(2)}) collective-permute-start(bf16[4,256,256]{2,1,0:T(8,128)(2,1)S(1)} %get-tuple-element.298), channel_id=1, source_target_pairs={{0,8},{8,0},{16,24},{24,16},{1,9},{9,1},{17,25},{25,17},{2,10},{10... | collective-permute-start | bytes 1572872 | tf_op jit(solution)/shard_map/ppermute | solution.py:36
  157.0 24.6 %collective-permute-start.14 = (bf16[4,256,256]{2,1,0:T(8,128)(2,1)S(1)}, bf16[4,256,256]{2,1,0:T(8,128)(2,1)S(1)}, u32[]{:S(2)}, u32[]{:S(2)}) collective-permute-start(bf16[4,256,256]{2,1,0:T(8,128)(2,1)S(1)} %get-tuple-element.297), channel_id=1, source_target_pairs={{0,16},{8,24},{16,0},{24,8},{1,17},{9,25},{17,1},{25,9},{2,18},{10... | collective-permute-start | bytes 1572872 | tf_op jit(solution)/shard_map/ppermute | solution.py:36
  184.0 44.0 %collective-permute-start.19 = (bf16[2048,512]{1,0:T(8,128)(2,1)S(1)}, bf16[2048,512]{1,0:T(8,128)(2,1)}, u32[]{:S(2)}, u32[]{:S(2)}) collective-permute-start(bf16[2048,512]{1,0:T(8,128)(2,1)S(1)} %constant_dynamic-update-slice_fusion.refs_0_), channel_id=1, source_target_pairs={{0,1},{1,0},{2,3},{3,2},{4,5},{5,4},{6,7},{7,6},{8,9},{9,8},{10,11... | collective-permute-start | bytes 6291464 | tf_op jit(solution)/shard_map/ppermute | solution.py:36
  184.8 43.4 %collective-permute-start.20 = (bf16[2048,512]{1,0:T(8,128)(2,1)S(1)}, bf16[2048,512]{1,0:T(8,128)(2,1)}, u32[]{:S(2)}, u32[]{:S(2)}) collective-permute-start(bf16[2048,512]{1,0:T(8,128)(2,1)S(1)} %constant_dynamic-update-slice_fusion.refs_0_), channel_id=1, source_target_pairs={{0,2},{1,3},{2,0},{3,1},{4,6},{5,7},{6,4},{7,5},{8,10},{9,11},{10,... | collective-permute-start | bytes 6291464 | tf_op jit(solution)/shard_map/ppermute | solution.py:36
  186.4 21.0 %collective-permute-start.17 = (bf16[512,512]{1,0:T(8,128)(2,1)S(1)}, bf16[512,512]{1,0:T(8,128)(2,1)S(1)}, u32[]{:S(2)}, u32[]{:S(2)}) collective-permute-start(bf16[512,512]{1,0:T(8,128)(2,1)S(1)} %multiply_convert_fusion.2), channel_id=1, source_target_pairs={{0,16},{8,24},{16,0},{24,8},{1,17},{9,25},{17,1},{25,9},{2,18},{10... | collective-permute-start | bytes 1572872 | tf_op jit(solution)/shard_map/ppermute | solution.py:36
  186.6 21.3 %collective-permute-start.16 = (bf16[512,512]{1,0:T(8,128)(2,1)S(1)}, bf16[512,512]{1,0:T(8,128)(2,1)S(1)}, u32[]{:S(2)}, u32[]{:S(2)}) collective-permute-start(bf16[512,512]{1,0:T(8,128)(2,1)S(1)} %multiply_convert_fusion.2), channel_id=1, source_target_pairs={{0,8},{8,0},{16,24},{24,16},{1,9},{9,1},{17,25},{25,17},{2,10},{10... | collective-permute-start | bytes 1572872 | tf_op jit(solution)/shard_map/ppermute | solution.py:36
  231.5 43.2 %collective-permute-start.24 = (bf16[2048,512]{1,0:T(8,128)(2,1)}, bf16[2048,512]{1,0:T(8,128)(2,1)}, u32[]{:S(2)}, u32[]{:S(2)}) collective-permute-start(bf16[2048,512]{1,0:T(8,128)(2,1)} %constant_dynamic-update-slice_fusion.4.refs_6_), channel_id=1, source_target_pairs={{0,1},{1,0},{2,3},{3,2},{4,5},{5,4},{6,7},{7,6},{8,9},{9,8},{10,11... | collective-permute-start | bytes 6291464 | tf_op jit(solution)/shard_map/ppermute | solution.py:36
  233.2 44.6 %collective-permute-start.25 = (bf16[2048,512]{1,0:T(8,128)(2,1)}, bf16[2048,512]{1,0:T(8,128)(2,1)}, u32[]{:S(2)}, u32[]{:S(2)}) collective-permute-start(bf16[2048,512]{1,0:T(8,128)(2,1)} %constant_dynamic-update-slice_fusion.4.refs_6_), channel_id=1, source_target_pairs={{0,2},{1,3},{2,0},{3,1},{4,6},{5,7},{6,4},{7,5},{8,10},{9,11},{10,... | collective-permute-start | bytes 6291464 | tf_op jit(solution)/shard_map/ppermute | solution.py:36
  233.5 19.8 %collective-permute-start.22 = (bf16[4,256,256]{2,1,0:T(8,128)(2,1)S(1)}, bf16[4,256,256]{2,1,0:T(8,128)(2,1)S(1)}, u32[]{:S(2)}, u32[]{:S(2)}) collective-permute-start(bf16[4,256,256]{2,1,0:T(8,128)(2,1)S(1)} %get-tuple-element.295), channel_id=1, source_target_pairs={{0,8},{8,0},{16,24},{24,16},{1,9},{9,1},{17,25},{25,17},{2,10},{10... | collective-permute-start | bytes 1572872 | tf_op jit(solution)/shard_map/ppermute | solution.py:36
  235.7 38.2 %collective-permute-start.23 = (bf16[4,256,256]{2,1,0:T(8,128)(2,1)S(1)}, bf16[4,256,256]{2,1,0:T(8,128)(2,1)S(1)}, u32[]{:S(2)}, u32[]{:S(2)}) collective-permute-start(bf16[4,256,256]{2,1,0:T(8,128)(2,1)S(1)} %get-tuple-element.294), channel_id=1, source_target_pairs={{0,16},{8,24},{16,0},{24,8},{1,17},{9,25},{17,1},{25,9},{2,18},{10... | collective-permute-start | bytes 1572872 | tf_op jit(solution)/shard_map/ppermute | solution.py:36
  237.9 36.0 %collective-permute-start.21 = (bf16[4,256,256]{2,1,0:T(8,128)(2,1)S(1)}, bf16[4,256,256]{2,1,0:T(8,128)(2,1)S(1)}, u32[]{:S(2)}, u32[]{:S(2)}) collective-permute-start(bf16[4,256,256]{2,1,0:T(8,128)(2,1)S(1)} %constant_dynamic-slice_fusion.10), channel_id=1, source_target_pairs={{0,24},{8,16},{16,8},{24,0},{1,25},{9,17},{17,9},{25,1},{2,26},{10... | collective-permute-start | bytes 1572872 | tf_op jit(solution)/shard_map/ppermute | solution.py:36
  279.1 19.1 %collective-permute-start.27 = (bf16[1024,512]{1,0:T(8,128)(2,1)S(1)}, bf16[1024,512]{1,0:T(8,128)(2,1)S(1)}, u32[]{:S(2)}, u32[]{:S(2)}) collective-permute-start(bf16[1024,512]{1,0:T(8,128)(2,1)S(1)} %slice.330), channel_id=1, source_target_pairs={{0,2},{1,3},{2,0},{3,1},{4,6},{5,7},{6,4},{7,5},{8,10},{9,11},{10,... | collective-permute-start | bytes 3145736 | tf_op jit(solution)/shard_map/ppermute | solution.py:36
  284.4 32.5 %collective-permute-start.26 = (bf16[4,4,256,256]{3,2,1,0:T(8,128)(2,1)S(1)}, bf16[4,4,256,256]{3,2,1,0:T(8,128)(2,1)}, u32[]{:S(2)}, u32[]{:S(2)}) collective-permute-start(bf16[4,4,256,256]{3,2,1,0:T(8,128)(2,1)S(1)} %pad_maximum_fusion.refs_2_.refs_5_), channel_id=1, source_target_pairs={{0,4},{4,0},{1,5},{5,1},{2,6},{6,2},{3,7},{7,3},{8,12},{12,8},{9,1... | collective-permute-start | bytes 6291464 | tf_op jit(solution)/shard_map/ppermute | solution.py:36
  300.2 19.2 %collective-permute-start.30 = (bf16[4,4,256,256]{3,2,1,0:T(8,128)(2,1)}, bf16[4,4,256,256]{3,2,1,0:T(8,128)(2,1)}, u32[]{:S(2)}, u32[]{:S(2)}) collective-permute-start(bf16[4,4,256,256]{3,2,1,0:T(8,128)(2,1)} %pad_maximum_fusion.1.refs_4_.refs_7_), channel_id=1, source_target_pairs={{0,4},{4,0},{1,5},{5,1},{2,6},{6,2},{3,7},{7,3},{8,12},{12,8},{9,1... | collective-permute-start | bytes 6291464 | tf_op jit(solution)/shard_map/ppermute | solution.py:36
  305.6 47.8 %collective-permute-start.32 = (bf16[1024,512]{1,0:T(8,128)(2,1)S(1)}, bf16[1024,512]{1,0:T(8,128)(2,1)S(1)}, u32[]{:S(2)}, u32[]{:S(2)}) collective-permute-start(bf16[1024,512]{1,0:T(8,128)(2,1)S(1)} %slice.333), channel_id=1, source_target_pairs={{0,1},{1,0},{2,3},{3,2},{4,5},{5,4},{6,7},{7,6},{8,9},{9,8},{10,11... | collective-permute-start | bytes 3145736 | tf_op jit(solution)/shard_map/ppermute | solution.py:36
  307.5 45.8 %collective-permute-start.31 = (bf16[1024,512]{1,0:T(8,128)(2,1)S(1)}, bf16[1024,512]{1,0:T(8,128)(2,1)S(1)}, u32[]{:S(2)}, u32[]{:S(2)}) collective-permute-start(bf16[1024,512]{1,0:T(8,128)(2,1)S(1)} %slice.332), channel_id=1, source_target_pairs={{0,2},{1,3},{2,0},{3,1},{4,6},{5,7},{6,4},{7,5},{8,10},{9,11},{10,... | collective-permute-start | bytes 3145736 | tf_op jit(solution)/shard_map/ppermute | solution.py:36
  309.6 59.0 %collective-permute-start.33 = (bf16[4,256,256]{2,1,0:T(8,128)(2,1)}, bf16[4,256,256]{2,1,0:T(8,128)(2,1)}, u32[]{:S(2)}, u32[]{:S(2)}) collective-permute-start(bf16[4,256,256]{2,1,0:T(8,128)(2,1)} %get-tuple-element.292), channel_id=1, source_target_pairs={{0,8},{8,0},{16,24},{24,16},{1,9},{9,1},{17,25},{25,17},{2,10},{10... | collective-permute-start | bytes 1572872 | tf_op jit(solution)/shard_map/ppermute | solution.py:36
  317.4 51.3 %collective-permute-start.34 = (bf16[4,256,256]{2,1,0:T(8,128)(2,1)S(1)}, bf16[4,256,256]{2,1,0:T(8,128)(2,1)S(1)}, u32[]{:S(2)}, u32[]{:S(2)}) collective-permute-start(bf16[4,256,256]{2,1,0:T(8,128)(2,1)S(1)} %get-tuple-element.291), channel_id=1, source_target_pairs={{0,16},{8,24},{16,0},{24,8},{1,17},{9,25},{17,1},{25,9},{2,18},{10... | collective-permute-start | bytes 1572872 | tf_op jit(solution)/shard_map/ppermute | solution.py:36
  319.3 49.3 %collective-permute-start.35 = (bf16[4,256,256]{2,1,0:T(8,128)(2,1)S(1)}, bf16[4,256,256]{2,1,0:T(8,128)(2,1)S(1)}, u32[]{:S(2)}, u32[]{:S(2)}) collective-permute-start(bf16[4,256,256]{2,1,0:T(8,128)(2,1)S(1)} %get-tuple-element.290), channel_id=1, source_target_pairs={{0,24},{8,16},{16,8},{24,0},{1,25},{9,17},{17,9},{25,1},{2,26},{10... | collective-permute-start | bytes 1572872 | tf_op jit(solution)/shard_map/ppermute | solution.py:36
  370.0 35.0 %collective-permute-start.37 = (bf16[4,4,256,256]{3,2,1,0:T(8,128)(2,1)}, bf16[4,4,256,256]{3,2,1,0:T(8,128)(2,1)}, u32[]{:S(2)}, u32[]{:S(2)}) collective-permute-start(bf16[4,4,256,256]{3,2,1,0:T(8,128)(2,1)} %get-tuple-element.183), channel_id=1, source_target_pairs={{0,4},{4,0},{1,5},{5,1},{2,6},{6,2},{3,7},{7,3},{8,12},{12,8},{9,1... | collective-permute-start | bytes 6291464 | tf_op jit(solution)/shard_map/ppermute | solution.py:36
  408.4 34.2 %collective-permute-start.38 = (bf16[4,256,256]{2,1,0:T(8,128)(2,1)S(1)}, bf16[4,256,256]{2,1,0:T(8,128)(2,1)S(1)}, u32[]{:S(2)}, u32[]{:S(2)}) collective-permute-start(bf16[4,256,256]{2,1,0:T(8,128)(2,1)S(1)} %get-tuple-element.288), channel_id=1, source_target_pairs={{0,8},{8,0},{16,24},{24,16},{1,9},{9,1},{17,25},{25,17},{2,10},{10... | collective-permute-start | bytes 1572872 | tf_op jit(solution)/shard_map/ppermute | solution.py:36
  408.8 38.2 %collective-permute-start.39 = (bf16[4,256,256]{2,1,0:T(8,128)(2,1)S(1)}, bf16[4,256,256]{2,1,0:T(8,128)(2,1)S(1)}, u32[]{:S(2)}, u32[]{:S(2)}) collective-permute-start(bf16[4,256,256]{2,1,0:T(8,128)(2,1)S(1)} %get-tuple-element.287), channel_id=1, source_target_pairs={{0,16},{8,24},{16,0},{24,8},{1,17},{9,25},{17,1},{25,9},{2,18},{10... | collective-permute-start | bytes 1572872 | tf_op jit(solution)/shard_map/ppermute | solution.py:36
  411.4 35.6 %collective-permute-start.40 = (bf16[2,528,512]{2,1,0:T(8,128)(2,1)S(1)}, bf16[2,528,512]{2,1,0:T(8,128)(2,1)S(1)}, u32[]{:S(2)}, u32[]{:S(2)}) collective-permute-start(bf16[2,528,512]{2,1,0:T(8,128)(2,1)S(1)} %get-tuple-element.273), channel_id=1, source_target_pairs={{0,1},{1,0},{2,3},{3,2},{4,5},{5,4},{6,7},{7,6},{8,9},{9,8},{10,11... | collective-permute-start | bytes 3244040 | tf_op jit(solution)/shard_map/ppermute | solution.py:36
  412.3 34.7 %collective-permute-start.41 = (bf16[2,528,512]{2,1,0:T(8,128)(2,1)S(1)}, bf16[2,528,512]{2,1,0:T(8,128)(2,1)S(1)}, u32[]{:S(2)}, u32[]{:S(2)}) collective-permute-start(bf16[2,528,512]{2,1,0:T(8,128)(2,1)S(1)} %get-tuple-element.272), channel_id=1, source_target_pairs={{0,2},{1,3},{2,0},{3,1},{4,6},{5,7},{6,4},{7,5},{8,10},{9,11},{10,... | collective-permute-start | bytes 3244040 | tf_op jit(solution)/shard_map/ppermute | solution.py:36
  413.6 65.7 %collective-permute-start.42 = (bf16[4,256,256]{2,1,0:T(8,128)(2,1)}, bf16[4,256,256]{2,1,0:T(8,128)(2,1)S(1)}, u32[]{:S(2)}, u32[]{:S(2)}) collective-permute-start(bf16[4,256,256]{2,1,0:T(8,128)(2,1)} %get-tuple-element.286), channel_id=1, source_target_pairs={{0,24},{8,16},{16,8},{24,0},{1,25},{9,17},{17,9},{25,1},{2,26},{10... | collective-permute-start | bytes 1572872 | tf_op jit(solution)/shard_map/ppermute | solution.py:36
  451.6 27.7 %collective-permute-start.45 = (bf16[528,512]{1,0:T(8,128)(2,1)}, bf16[528,512]{1,0:T(8,128)(2,1)}, u32[]{:S(2)}, u32[]{:S(2)}) collective-permute-start(bf16[528,512]{1,0:T(8,128)(2,1)} %get-tuple-element.269), channel_id=1, source_target_pairs={{0,2},{1,3},{2,0},{3,1},{4,6},{5,7},{6,4},{7,5},{8,10},{9,11},{10,... | collective-permute-start | bytes 1622024 | tf_op jit(solution)/shard_map/ppermute | solution.py:36
  452.5 26.8 %collective-permute-start.46 = (bf16[528,512]{1,0:T(8,128)(2,1)S(1)}, bf16[528,512]{1,0:T(8,128)(2,1)}, u32[]{:S(2)}, u32[]{:S(2)}) collective-permute-start(bf16[528,512]{1,0:T(8,128)(2,1)S(1)} %get-tuple-element.268), channel_id=1, source_target_pairs={{0,1},{1,0},{2,3},{3,2},{4,5},{5,4},{6,7},{7,6},{8,9},{9,8},{10,11... | collective-permute-start | bytes 1622024 | tf_op jit(solution)/shard_map/ppermute | solution.py:36
  453.9 29.8 %collective-permute-start.43 = (bf16[2,528,512]{2,1,0:T(8,128)(2,1)S(1)}, bf16[2,528,512]{2,1,0:T(8,128)(2,1)S(1)}, u32[]{:S(2)}, u32[]{:S(2)}) collective-permute-start(bf16[2,528,512]{2,1,0:T(8,128)(2,1)S(1)} %get-tuple-element.271), channel_id=1, source_target_pairs={{0,1},{1,0},{2,3},{3,2},{4,5},{5,4},{6,7},{7,6},{8,9},{9,8},{10,11... | collective-permute-start | bytes 3244040 | tf_op jit(solution)/shard_map/ppermute | solution.py:36
  454.8 29.0 %collective-permute-start.44 = (bf16[2,528,512]{2,1,0:T(8,128)(2,1)S(1)}, bf16[2,528,512]{2,1,0:T(8,128)(2,1)S(1)}, u32[]{:S(2)}, u32[]{:S(2)}) collective-permute-start(bf16[2,528,512]{2,1,0:T(8,128)(2,1)S(1)} %get-tuple-element.270), channel_id=1, source_target_pairs={{0,2},{1,3},{2,0},{3,1},{4,6},{5,7},{6,4},{7,5},{8,10},{9,11},{10,... | collective-permute-start | bytes 3244040 | tf_op jit(solution)/shard_map/ppermute | solution.py:36
  489.5 25.5 %collective-permute-start.47 = (bf16[2,528,512]{2,1,0:T(8,128)(2,1)}, bf16[2,528,512]{2,1,0:T(8,128)(2,1)}, u32[]{:S(2)}, u32[]{:S(2)}) collective-permute-start(bf16[2,528,512]{2,1,0:T(8,128)(2,1)} %pad_maximum_fusion.4), channel_id=1, source_target_pairs={{0,8},{8,0},{16,24},{24,16},{1,9},{9,1},{17,25},{25,17},{2,10},{10... | collective-permute-start | bytes 3244040 | tf_op jit(solution)/shard_map/ppermute | solution.py:36
  495.8 19.2 %collective-permute-start.48 = (bf16[528,512]{1,0:T(8,128)(2,1)}, bf16[528,512]{1,0:T(8,128)(2,1)}, u32[]{:S(2)}, u32[]{:S(2)}) collective-permute-start(bf16[528,512]{1,0:T(8,128)(2,1)} %get-tuple-element.265), channel_id=1, source_target_pairs={{0,2},{1,3},{2,0},{3,1},{4,6},{5,7},{6,4},{7,5},{8,10},{9,11},{10,... | collective-permute-start | bytes 1622024 | tf_op jit(solution)/shard_map/ppermute | solution.py:36
  497.0 18.0 %collective-permute-start.49 = (bf16[528,512]{1,0:T(8,128)(2,1)}, bf16[528,512]{1,0:T(8,128)(2,1)}, u32[]{:S(2)}, u32[]{:S(2)}) collective-permute-start(bf16[528,512]{1,0:T(8,128)(2,1)} %get-tuple-element.264), channel_id=1, source_target_pairs={{0,1},{1,0},{2,3},{3,2},{4,5},{5,4},{6,7},{7,6},{8,9},{9,8},{10,11... | collective-permute-start | bytes 1622024 | tf_op jit(solution)/shard_map/ppermute | solution.py:36
  515.1 217.6 %reduce-scatter.6.cloned.1.call-start = ((), (), s32[]{:S(2)}) async-start(), calls=%async_computation.5 | async-start | bytes 2359296 | tf_op jit(solution)/shard_map/reduce_scatter | solution.py:832
  515.1 34.4 %collective-permute-start.51 = (bf16[4,2,4,256,256]{4,3,2,1,0:T(8,128)(2,1)}, bf16[4,2,4,256,256]{4,3,2,1,0:T(8,128)(2,1)}, u32[]{:S(2)}, u32[]{:S(2)}) collective-permute-start(bf16[4,2,4,256,256]{4,3,2,1,0:T(8,128)(2,1)} %get-tuple-element.209), channel_id=1, source_target_pairs={{0,4},{4,0},{1,5},{5,1},{2,6},{6,2},{3,7},{7,3},{8,12},{12,8},{9,1... | collective-permute-start | bytes 12582920 | tf_op jit(solution)/shard_map/ppermute | solution.py:36
  517.7 28.4 %collective-permute-start.50 = (bf16[1,528,512]{2,1,0:T(8,128)(2,1)}, bf16[1,528,512]{2,1,0:T(8,128)(2,1)}, u32[]{:S(2)}, u32[]{:S(2)}) collective-permute-start(bf16[1,528,512]{2,1,0:T(8,128)(2,1)} %fusion.48), channel_id=1, source_target_pairs={{0,16},{8,24},{16,0},{24,8},{1,17},{9,25},{17,1},{25,9},{2,18},{10... | collective-permute-start | bytes 1622024 | tf_op jit(solution)/shard_map/ppermute | solution.py:36
  564.1 19.2 %collective-permute-start.55 = (bf16[512,512]{1,0:T(8,128)(2,1)}, bf16[512,512]{1,0:T(8,128)(2,1)}, u32[]{:S(2)}, u32[]{:S(2)}) collective-permute-start(bf16[512,512]{1,0:T(8,128)(2,1)} %get-tuple-element.259), channel_id=1, source_target_pairs={{0,2},{1,3},{2,0},{3,1},{4,6},{5,7},{6,4},{7,5},{8,10},{9,11},{10,... | collective-permute-start | bytes 1572872 | tf_op jit(solution)/shard_map/ppermute | solution.py:36
  566.9 46.0 %collective-permute-start.58 = (bf16[2,4,256,256]{3,2,1,0:T(8,128)(2,1)}, bf16[2,4,256,256]{3,2,1,0:T(8,128)(2,1)S(1)}, u32[]{:S(2)}, u32[]{:S(2)}) collective-permute-start(bf16[2,4,256,256]{3,2,1,0:T(8,128)(2,1)} %get-tuple-element.276), channel_id=1, source_target_pairs={{0,8},{8,0},{16,24},{24,16},{1,9},{9,1},{17,25},{25,17},{2,10},{10... | collective-permute-start | bytes 3145736 | tf_op jit(solution)/shard_map/ppermute | solution.py:36
  567.8 47.0 %collective-permute-start.59 = (bf16[2,4,256,256]{3,2,1,0:T(8,128)(2,1)}, bf16[2,4,256,256]{3,2,1,0:T(8,128)(2,1)}, u32[]{:S(2)}, u32[]{:S(2)}) collective-permute-start(bf16[2,4,256,256]{3,2,1,0:T(8,128)(2,1)} %get-tuple-element.275), channel_id=1, source_target_pairs={{0,16},{8,24},{16,0},{24,8},{1,17},{9,25},{17,1},{25,9},{2,18},{10... | collective-permute-start | bytes 3145736 | tf_op jit(solution)/shard_map/ppermute | solution.py:36
  614.9 31.3 %collective-permute-start.60 = (bf16[2,4,256,256]{3,2,1,0:T(8,128)(2,1)}, bf16[2,4,256,256]{3,2,1,0:T(8,128)(2,1)}, u32[]{:S(2)}, u32[]{:S(2)}) collective-permute-start(bf16[2,4,256,256]{3,2,1,0:T(8,128)(2,1)} %get-tuple-element.219), channel_id=1, source_target_pairs={{0,24},{8,16},{16,8},{24,0},{1,25},{9,17},{17,9},{25,1},{2,26},{10... | collective-permute-start | bytes 3145736 | tf_op jit(solution)/shard_map/ppermute | solution.py:36
  633.1 176.0 %reduce-scatter.8.cloned.1.call-start = ((), (), s32[]{:S(2)}) async-start(), calls=%async_computation.6 | async-start | bytes 7077888 | tf_op jit(solution)/shard_map/reduce_scatter | solution.py:888
  634.9 45.8 %collective-permute-start.61 = (bf16[2,512,512]{2,1,0:T(8,128)(2,1)S(1)}, bf16[2,512,512]{2,1,0:T(8,128)(2,1)S(1)}, u32[]{:S(2)}, u32[]{:S(2)}) collective-permute-start(bf16[2,512,512]{2,1,0:T(8,128)(2,1)S(1)} %pad_maximum_fusion.5), channel_id=1, source_target_pairs={{0,8},{8,0},{16,24},{24,16},{1,9},{9,1},{17,25},{25,17},{2,10},{10... | collective-permute-start | bytes 3145736 | tf_op jit(solution)/shard_map/ppermute | solution.py:36
  699.0 25.8 %collective-permute-start.64 = (bf16[1,512,512]{2,1,0:T(8,128)(2,1)S(1)}, bf16[1,512,512]{2,1,0:T(8,128)(2,1)S(1)}, u32[]{:S(2)}, u32[]{:S(2)}) collective-permute-start(bf16[1,512,512]{2,1,0:T(8,128)(2,1)S(1)} %add_convert_fusion.4), channel_id=1, source_target_pairs={{0,16},{8,24},{16,0},{24,8},{1,17},{9,25},{17,1},{25,9},{2,18},{10... | collective-permute-start | bytes 1572872 | tf_op jit(solution)/shard_map/ppermute | solution.py:36
  (126 other events, 1315.6 us)
Sparse Core Ops, SparseCore 0:
  11.8 71.7 all-gather.2
  85.2 46.1 all-gather.4
  515.2 99.1 reduce-scatter.9
  633.2 44.6 reduce-scatter.5
  732.8 67.9 reduce-scatter.7

commit v5 on v4

--- a/solution.py
+++ b/solution.py
@@ -829,7 +829,6 @@
     moe_near = scatter_z_near({k: moe_parts[k] for k in range(1, nz, 2)})
 
     wo_grad = jnp.einsum("sa,sd->ad", joined, dresid_low, preferred_element_type=f32)
-    wo_own = lax.psum_scatter(wo_grad.astype(bf16), dp, scatter_dimension=1, tiled=True)
     dout = (
         jnp.einsum("sd,ad->sa", dresid_low, wo_full, preferred_element_type=f32)
         .astype(bf16)
@@ -840,6 +839,8 @@
     inner = jnp.sum(weights * dweights, -1, keepdims=True)
     dscores = (weights * (dweights - inner)).astype(bf16)
     dscores, up_own[-1], moe_near = fence(dscores, up_own[-1], moe_near)
+    wo_grad = after(wo_grad.astype(bf16), dscores)
+    wo_own = lax.psum_scatter(wo_grad, dp, scatter_dimension=1, tiled=True)
     dq_rot = scale * jnp.einsum("hqk,khd->qhd", dscores, k_rot, preferred_element_type=f32)
     dk_rot = scale * jnp.einsum("hqk,qhd->khd", dscores, q_rot, preferred_element_type=f32)
     dq_norm = unrotate(dq_rot, cosine, sine).reshape(seq, local)
@@ -889,7 +890,10 @@
     tokens_grad, wqkv_own = fence(tokens_grad, wqkv_own)
     wqkv_own, wo_own = wqkv_own.astype(f32), wo_own.astype(f32)
     attn_gain_grad = jnp.sum(jnp.concatenate([wq, wk, wv], 1).astype(f32) * wqkv_own, -1)
-    attn_gain_grad = tensor_sum(attn_gain_grad) / attn_gain.astype(f32)
+    attn_gain_grad = [attn_gain_grad] + [swap(attn_gain_grad, "tensor", k) for k in range(1, n)]
+    while len(attn_gain_grad) > 1:
+        attn_gain_grad = [a + b for a, b in zip(attn_gain_grad[::2], attn_gain_grad[1::2])]
+    attn_gain_grad = attn_gain_grad[0] / attn_gain.astype(f32)
     return (
         mixed,
         tokens_grad,

time: 830 us -> 824 us (level)
    ppermute x86 -> x87, waiting for transfers between devices: 278 us -> 271 us  [swap(): return lax.ppermute(value, axis, [(i, i ^ mask) for i in range(n)])]
    ppermute x86 -> x87, starting transfers between devices: 114 us -> 116 us  [swap(): return lax.ppermute(value, axis, [(i, i ^ mask) for i in range(n)])]
    unnamed x173 -> x177, local copies, waits for them, and re-layouts: 17.2 us -> 15.4 us
  transfers between devices with their start and end apart: 91 -> 92, of which waited for: 48 -> 50; matrix products, arithmetic and copies ran while one was open for 19% -> 19% of each run, Pallas kernels for 18% -> 18%
where the time goes in v5:
time: 824 us; the launch traced here: 819 us
  waiting for transfers between devices  345 us (42%)
  Pallas kernels  149 us (18%)
  starting transfers between devices  117 us (14%)
  other arithmetic  75.8 us (9%)
  local copies, waits for them, and re-layouts  65.1 us (8%)
  matrix products  51.6 us (6%)
  between operations  15.9 us (2%)
    ppermute x87, waiting for transfers between devices, swap(): return lax.ppermute(value, axis, [(i, i ^ mask) for i in range(n)])  271 us
    ppermute x87, starting transfers between devices, swap(): return lax.ppermute(value, axis, [(i, i ^ mask) for i in range(n)])  116 us
    all_gather x1, waiting for transfers between devices, shards(): lax.all_gather(jnp.concatenate([wq, wk, wv, small], 1), dp, axis=0, tiled...  61.3 us
    pallas_call x2, Pallas kernels, backward_call(): pl.pallas_call(functools.partial(backward_kernel, nz, n, own_e, hid, slic...  54.6 us
    pallas_call x1, Pallas kernels, forward_call(): pl.pallas_call(functools.partial(forward_kernel, nz, n, own_e, hid, slice...  32.4 us
    pallas_call x1, Pallas kernels, up_grad_call(): pl.pallas_call(functools.partial(up_grad_kernel, nz, own_e, hid, seq, sli...  23 us
    pallas_call x1, Pallas kernels, output_call(): pl.pallas_call(functools.partial(output_kernel, nz, own_e, hid, slice_d,...  17.2 us
  transfers between devices with their start and end apart: 92, of which 50 were waited for; matrix products, arithmetic and copies ran while one was open for 19% of the time, Pallas kernels for 18%

profile of v5, /device:TPU:0, one launch (start us, length us, event | category | flops | bytes accessed | tf_op | source)
XLA Modules:
  0.0 819.5 jit_solution(16776441350991385981)
XLA Ops:
  11.7 4.1 collective-permute-start.1
  22.3 61.3 %all-gather.3.cloned.1.call-done = bf16[2048,1664]{1,0:T(8,128)(2,1)} async-done(((bf16[256,1664]{1,0:T(8,128)(2,1)}), bf16[2048,1664]{1,0:T(8,128)(2,1)}) %all-gather.3.cloned.1.call-update) | async-done | bytes 6815760 | tf_op jit(solution)/shard_map/all_gather | solution.py:656
  85.5 6.5 fusion.4
  110.4 5.0 fusion.102
  115.4 3.5 convolution_convert_fusion.5
  118.9 12.4 %all-gather.5.cloned.1.call-done = bf16[512,2048]{1,0:T(8,128)(2,1)} async-done(((bf16[512,256]{1,0:T(8,128)(2,1)}), bf16[512,2048]{1,0:T(8,128)(2,1)}) %all-gather.5.cloned.1.call-update) | async-done | bytes 2097168 | tf_op jit(solution)/shard_map/all_gather | solution.py:672
  145.3 4.4 collective-permute-done.7
  153.6 3.4 collective-permute-start.13
  168.3 10.6 %collective-permute-done.13 = bf16[4,256,256]{2,1,0:T(8,128)(2,1)S(1)} collective-permute-done((bf16[4,256,256]{2,1,0:T(8,128)(2,1)S(1)}, bf16[4,256,256]{2,1,0:T(8,128)(2,1)S(1)}, u32[]{:S(2)}, u32[]{:S(2)}) %collective-permute-start.13) | collective-permute-done | bytes 524320 | tf_op jit(solution)/shard_map/ppermute | solution.py:36
  186.6 20.8 %collective-permute-done.17 = bf16[512,512]{1,0:T(8,128)(2,1)S(1)} collective-permute-done((bf16[512,512]{1,0:T(8,128)(2,1)S(1)}, bf16[512,512]{1,0:T(8,128)(2,1)S(1)}, u32[]{:S(2)}, u32[]{:S(2)}) %collective-permute-start.17) | collective-permute-done | bytes 524320 | tf_op jit(solution)/shard_map/ppermute | solution.py:36
  207.8 12.5 %collective-permute-done.18 = bf16[512,512]{1,0:T(8,128)(2,1)S(1)} collective-permute-done((bf16[512,512]{1,0:T(8,128)(2,1)S(1)}, bf16[512,512]{1,0:T(8,128)(2,1)S(1)}, u32[]{:S(2)}, u32[]{:S(2)}) %collective-permute-start.18) | collective-permute-done | bytes 524320 | tf_op jit(solution)/shard_map/ppermute | solution.py:36
  220.3 7.8 collective-permute-done.19.refs_1_
  239.3 14.0 %collective-permute-done.22 = bf16[4,256,256]{2,1,0:T(8,128)(2,1)S(1)} collective-permute-done((bf16[4,256,256]{2,1,0:T(8,128)(2,1)S(1)}, bf16[4,256,256]{2,1,0:T(8,128)(2,1)S(1)}, u32[]{:S(2)}, u32[]{:S(2)}) %collective-permute-start.22) | collective-permute-done | bytes 524320 | tf_op jit(solution)/shard_map/ppermute | solution.py:36
  253.4 20.5 %collective-permute-done.23 = bf16[4,256,256]{2,1,0:T(8,128)(2,1)S(1)} collective-permute-done((bf16[4,256,256]{2,1,0:T(8,128)(2,1)S(1)}, bf16[4,256,256]{2,1,0:T(8,128)(2,1)S(1)}, u32[]{:S(2)}, u32[]{:S(2)}) %collective-permute-start.23) | collective-permute-done | bytes 524320 | tf_op jit(solution)/shard_map/ppermute | solution.py:36
  274.7 3.1 collective-permute-done.25.refs_8_
  284.5 7.9 collective-permute-done.29
  292.4 5.8 collective-permute-done.27.refs_9_
  309.7 7.3 collective-permute-start.33
  321.0 32.4 %shard_map.254 = (f32[2048,1024]{1,0:T(8,128)}, f32[2048,1024]{1,0:T(8,128)}, bf16[2048,1024]{1,0:T(8,128)(2,1)}, f32[2048,128]{1,0:T(8,128)}, bf16[2048,2048]{1,0:T(8,128)(2,1)}) custom-call(s32[3]{0:T(128)} %pad_add_fusion.idx, f32[2048,128]{1,0:T(8,128)} %pad_convert_fusion.refs_0_.refs_4_, bf16[4,512,128]{2,1,0:T(8,128)(2,1)} %bitcast.310, ...), custom_call_target="tpu_custom_call" | custom-call | flops 17179869184 | bytes 41943040 | tf_op jit(solution)/shard_map/pallas_call | solution.py:301
  353.4 15.3 %shard_map.255 = (bf16[4,4,256,256]{3,2,1,0:T(8,128)(2,1)S(1)}, bf16[4,4,256,256]{3,2,1,0:T(8,128)(2,1)}, bf16[4,2048,512]{2,1,0:T(8,128)(2,1)}) custom-call(s32[3]{0:T(128)S(1)} %copy-done.6, bf16[2048,1024]{1,0:T(8,128)(2,1)} %get-tuple-element.211.hid_ref, bf16[2048,512]{1,0:T(8,128)(2,1)} %copy-done.66, ...), custom_call_target="tpu_custom_call" | custom-call | flops 8589934592 | bytes 25165824 | tf_op jit(solution)/shard_map/pallas_call | solution.py:526
  370.6 5.9 collective-permute-done.36.refs_10_.far
  377.8 27.2 %shard_map.256 = (bf16[2,4,528,512]{3,2,1,0:T(8,128)(2,1)}, bf16[1024,1024]{1,0:T(8,128)(2,1)}, bf16[1024,1024]{1,0:T(8,128)(2,1)}) custom-call(s32[3]{0:T(128)} %pad_add_fusion.idx, bf16[4,4,512,512]{3,2,1,0:T(8,128)(2,1)} %bitcast.359, f32[2048,1024]{1,0:T(8,128)} %get-tuple-element.179.refs_1_, f32[2048,1024]{1,0:T(8,128)} %get-tuple-element.180.refs_2_, ...), custom_call_target="tpu_custom_call" | custom-call | flops 12884901888 | bytes 41943040 | tf_op jit(solution)/shard_map/pallas_call | solution.py:401
  415.1 27.4 %shard_map.257 = (bf16[2,4,528,512]{3,2,1,0:T(8,128)(2,1)}, bf16[1024,1024]{1,0:T(8,128)(2,1)}, bf16[1024,1024]{1,0:T(8,128)(2,1)}) custom-call(s32[3]{0:T(128)} %pad_add_fusion.idx, bf16[4,4,512,512]{3,2,1,0:T(8,128)(2,1)} %bitcast.360, f32[2048,1024]{1,0:T(8,128)} %get-tuple-element.179.refs_1_, f32[2048,1024]{1,0:T(8,128)} %get-tuple-element.180.refs_2_, ...), custom_call_target="tpu_custom_call" | custom-call | flops 12884901888 | bytes 41943040 | tf_op jit(solution)/shard_map/pallas_call | solution.py:401
  442.6 4.5 collective-permute-done.39.refs_6_
  447.9 3.7 fusion.36
  455.9 23.0 %shard_map.258 = (bf16[4,2,4,256,256]{4,3,2,1,0:T(8,128)(2,1)}, bf16[4,2,4,256,256]{4,3,2,1,0:T(8,128)(2,1)}) custom-call(s32[3]{0:T(128)S(1)} %copy-done.7, bf16[2048,2048]{1,0:T(8,128)(2,1)} %get-tuple-element.199.m_ref, bf16[1024,1024]{1,0:T(8,128)(2,1)S(1)} %copy-done.11, bf16[1024,1024]{1,0:T(8,128)(2,1)S(1)} %copy-done.10, ...), custom_call_target="tpu_custom_call" | custom-call | flops 17179869184 | bytes 25165824 | tf_op jit(solution)/shard_map/pallas_call | solution.py:574
  479.0 4.7 collective-permute-done.43
  489.5 3.7 collective-permute-start.47
  497.8 17.2 %shard_map.259 = bf16[4,4,512,512]{3,2,1,0:T(8,128)(2,1)} custom-call(s32[3]{0:T(128)S(1)} %copy-done.7, bf16[2048,1024]{1,0:T(8,128)(2,1)} %get-tuple-element.211.hid_ref, bf16[4,4,256,256]{3,2,1,0:T(8,128)(2,1)S(1)} %copy-done.1, bf16[4,4,256,256]{3,2,1,0:T(8,128)(2,1)S(1)} %copy-done.9), custom_call_target="tpu_custom_call" | custom-call | flops 8589934592 | bytes 16777216 | tf_op jit(solution)/shard_map/pallas_call | solution.py:461
  518.2 3.5 collective-permute-start.50
  526.4 20.1 %collective-permute-done.50 = bf16[1,528,512]{2,1,0:T(8,128)(2,1)} collective-permute-done((bf16[1,528,512]{2,1,0:T(8,128)(2,1)}, bf16[1,528,512]{2,1,0:T(8,128)(2,1)}, u32[]{:S(2)}, u32[]{:S(2)}) %collective-permute-start.50) | collective-permute-done | bytes 540704 | tf_op jit(solution)/shard_map/ppermute | solution.py:36
  557.4 3.7 add_convert_fusion
  570.9 9.9 %collective-permute-done.54 = bf16[512,512]{1,0:T(8,128)(2,1)} collective-permute-done((bf16[512,512]{1,0:T(8,128)(2,1)}, bf16[512,512]{1,0:T(8,128)(2,1)}, u32[]{:S(2)}, u32[]{:S(2)}) %collective-permute-start.54) | collective-permute-done | bytes 524320 | tf_op jit(solution)/shard_map/ppermute | solution.py:36
  590.1 5.4 collective-permute-done.56
  599.3 13.9 %collective-permute-done.58.refs_1_ = bf16[2,4,256,256]{3,2,1,0:T(8,128)(2,1)S(1)} collective-permute-done((bf16[2,4,256,256]{3,2,1,0:T(8,128)(2,1)}, bf16[2,4,256,256]{3,2,1,0:T(8,128)(2,1)S(1)}, u32[]{:S(2)}, u32[]{:S(2)}) %collective-permute-start.58) | collective-permute-done | bytes 1048608 | tf_op jit(solution)/shard_map/ppermute | solution.py:36
  624.9 4.3 convolution_convert_fusion.1
  629.2 4.1 fusion.51
  635.8 5.0 multiply_convert_fusion
  643.4 18.0 %collective-permute-done.61 = bf16[2,512,512]{2,1,0:T(8,128)(2,1)S(1)} collective-permute-done((bf16[2,512,512]{2,1,0:T(8,128)(2,1)S(1)}, bf16[2,512,512]{2,1,0:T(8,128)(2,1)S(1)}, u32[]{:S(2)}, u32[]{:S(2)}) %collective-permute-start.61) | collective-permute-done | bytes 1048608 | tf_op jit(solution)/shard_map/ppermute | solution.py:36
  688.0 16.8 %collective-permute-done.66 = f32[19,512]{1,0:T(8,128)S(1)} collective-permute-done((f32[19,512]{1,0:T(8,128)S(1)}, f32[19,512]{1,0:T(8,128)S(1)}, u32[]{:S(2)}, u32[]{:S(2)}) %collective-permute-start.66) | collective-permute-done | bytes 38944 | tf_op jit(solution)/shard_map/ppermute | solution.py:36
  707.3 11.1 %collective-permute-done.67 = f32[19,512]{1,0:T(8,128)S(1)} collective-permute-done((f32[19,512]{1,0:T(8,128)S(1)}, f32[19,512]{1,0:T(8,128)S(1)}, u32[]{:S(2)}, u32[]{:S(2)}) %collective-permute-start.67) | collective-permute-done | bytes 38944 | tf_op jit(solution)/shard_map/ppermute | solution.py:36
  720.7 5.6 convolution_convert_fusion
  730.9 7.1 fusion.8
  745.9 8.3 %collective-permute-done.68 = bf16[2,256,512]{2,1,0:T(8,128)(2,1)S(1)} collective-permute-done((bf16[2,256,512]{2,1,0:T(8,128)(2,1)S(1)}, bf16[2,256,512]{2,1,0:T(8,128)(2,1)S(1)}, u32[]{:S(2)}, u32[]{:S(2)}) %collective-permute-start.68) | collective-permute-done | bytes 524320 | tf_op jit(solution)/shard_map/ppermute | solution.py:36
  757.7 3.5 collective-permute-done.74
  761.2 3.6 collective-permute-done.69
  776.5 3.1 constant_dynamic-update-slice_fusion.10
  783.1 6.9 shard_map.260
  (496 shorter events, 273.7 us)
Async XLA Ops:
  7.2 76.4 %all-gather.3.cloned.1.call-start = ((), (), s32[]{:S(2)}) async-start(), calls=%async_computation.3 | async-start | bytes 7667712 | tf_op jit(solution)/shard_map/all_gather | solution.py:656
  11.6 119.7 %all-gather.5.cloned.1.call-start = ((), (), s32[]{:S(2)}) async-start(), calls=%async_computation.4 | async-start | bytes 2359296 | tf_op jit(solution)/shard_map/all_gather | solution.py:672
  84.9 548.4 %reduce-scatter.10.cloned.1.call-start = ((), (), s32[]{:S(2)}) async-start(), calls=%async_computation.7 | async-start | bytes 10485760
  98.3 36.5 %collective-permute-start.6 = (bf16[512,512]{1,0:T(8,128)(2,1)}, bf16[512,512]{1,0:T(8,128)(2,1)}, u32[]{:S(2)}, u32[]{:S(2)}) collective-permute-start(bf16[512,512]{1,0:T(8,128)(2,1)} %constant_dynamic-slice_fusion.14), channel_id=1, source_target_pairs={{0,16},{8,24},{16,0},{24,8},{1,17},{9,25},{17,1},{25,9},{2,18},{10... | collective-permute-start | bytes 1572872 | tf_op jit(solution)/shard_map/ppermute | solution.py:36
  99.4 35.4 %collective-permute-start.5 = (bf16[512,512]{1,0:T(8,128)(2,1)}, bf16[512,512]{1,0:T(8,128)(2,1)}, u32[]{:S(2)}, u32[]{:S(2)}) collective-permute-start(bf16[512,512]{1,0:T(8,128)(2,1)} %constant_dynamic-slice_fusion.14), channel_id=1, source_target_pairs={{0,8},{8,0},{16,24},{24,16},{1,9},{9,1},{17,25},{25,17},{2,10},{10... | collective-permute-start | bytes 1572872 | tf_op jit(solution)/shard_map/ppermute | solution.py:36
  142.5 25.8 %collective-permute-start.15 = (bf16[512,512]{1,0:T(8,128)(2,1)}, bf16[512,512]{1,0:T(8,128)(2,1)S(1)}, u32[]{:S(2)}, u32[]{:S(2)}) collective-permute-start(bf16[512,512]{1,0:T(8,128)(2,1)} %collective-permute-done.6), channel_id=1, source_target_pairs={{0,8},{8,0},{16,24},{24,16},{1,9},{9,1},{17,25},{25,17},{2,10},{10... | collective-permute-start | bytes 1572872 | tf_op jit(solution)/shard_map/ppermute | solution.py:36
  153.6 25.2 %collective-permute-start.13 = (bf16[4,256,256]{2,1,0:T(8,128)(2,1)S(1)}, bf16[4,256,256]{2,1,0:T(8,128)(2,1)S(1)}, u32[]{:S(2)}, u32[]{:S(2)}) collective-permute-start(bf16[4,256,256]{2,1,0:T(8,128)(2,1)S(1)} %get-tuple-element.300), channel_id=1, source_target_pairs={{0,8},{8,0},{16,24},{24,16},{1,9},{9,1},{17,25},{25,17},{2,10},{10... | collective-permute-start | bytes 1572872 | tf_op jit(solution)/shard_map/ppermute | solution.py:36
  157.0 24.6 %collective-permute-start.14 = (bf16[4,256,256]{2,1,0:T(8,128)(2,1)S(1)}, bf16[4,256,256]{2,1,0:T(8,128)(2,1)S(1)}, u32[]{:S(2)}, u32[]{:S(2)}) collective-permute-start(bf16[4,256,256]{2,1,0:T(8,128)(2,1)S(1)} %get-tuple-element.299), channel_id=1, source_target_pairs={{0,16},{8,24},{16,0},{24,8},{1,17},{9,25},{17,1},{25,9},{2,18},{10... | collective-permute-start | bytes 1572872 | tf_op jit(solution)/shard_map/ppermute | solution.py:36
  184.0 44.0 %collective-permute-start.19 = (bf16[2048,512]{1,0:T(8,128)(2,1)S(1)}, bf16[2048,512]{1,0:T(8,128)(2,1)}, u32[]{:S(2)}, u32[]{:S(2)}) collective-permute-start(bf16[2048,512]{1,0:T(8,128)(2,1)S(1)} %constant_dynamic-update-slice_fusion.refs_0_), channel_id=1, source_target_pairs={{0,1},{1,0},{2,3},{3,2},{4,5},{5,4},{6,7},{7,6},{8,9},{9,8},{10,11... | collective-permute-start | bytes 6291464 | tf_op jit(solution)/shard_map/ppermute | solution.py:36
  184.8 43.4 %collective-permute-start.20 = (bf16[2048,512]{1,0:T(8,128)(2,1)S(1)}, bf16[2048,512]{1,0:T(8,128)(2,1)}, u32[]{:S(2)}, u32[]{:S(2)}) collective-permute-start(bf16[2048,512]{1,0:T(8,128)(2,1)S(1)} %constant_dynamic-update-slice_fusion.refs_0_), channel_id=1, source_target_pairs={{0,2},{1,3},{2,0},{3,1},{4,6},{5,7},{6,4},{7,5},{8,10},{9,11},{10,... | collective-permute-start | bytes 6291464 | tf_op jit(solution)/shard_map/ppermute | solution.py:36
  186.4 21.0 %collective-permute-start.17 = (bf16[512,512]{1,0:T(8,128)(2,1)S(1)}, bf16[512,512]{1,0:T(8,128)(2,1)S(1)}, u32[]{:S(2)}, u32[]{:S(2)}) collective-permute-start(bf16[512,512]{1,0:T(8,128)(2,1)S(1)} %multiply_convert_fusion.2), channel_id=1, source_target_pairs={{0,16},{8,24},{16,0},{24,8},{1,17},{9,25},{17,1},{25,9},{2,18},{10... | collective-permute-start | bytes 1572872 | tf_op jit(solution)/shard_map/ppermute | solution.py:36
  186.6 21.2 %collective-permute-start.16 = (bf16[512,512]{1,0:T(8,128)(2,1)S(1)}, bf16[512,512]{1,0:T(8,128)(2,1)S(1)}, u32[]{:S(2)}, u32[]{:S(2)}) collective-permute-start(bf16[512,512]{1,0:T(8,128)(2,1)S(1)} %multiply_convert_fusion.2), channel_id=1, source_target_pairs={{0,8},{8,0},{16,24},{24,16},{1,9},{9,1},{17,25},{25,17},{2,10},{10... | collective-permute-start | bytes 1572872 | tf_op jit(solution)/shard_map/ppermute | solution.py:36
  231.5 43.2 %collective-permute-start.24 = (bf16[2048,512]{1,0:T(8,128)(2,1)}, bf16[2048,512]{1,0:T(8,128)(2,1)}, u32[]{:S(2)}, u32[]{:S(2)}) collective-permute-start(bf16[2048,512]{1,0:T(8,128)(2,1)} %constant_dynamic-update-slice_fusion.4.refs_6_), channel_id=1, source_target_pairs={{0,1},{1,0},{2,3},{3,2},{4,5},{5,4},{6,7},{7,6},{8,9},{9,8},{10,11... | collective-permute-start | bytes 6291464 | tf_op jit(solution)/shard_map/ppermute | solution.py:36
  233.2 44.6 %collective-permute-start.25 = (bf16[2048,512]{1,0:T(8,128)(2,1)}, bf16[2048,512]{1,0:T(8,128)(2,1)}, u32[]{:S(2)}, u32[]{:S(2)}) collective-permute-start(bf16[2048,512]{1,0:T(8,128)(2,1)} %constant_dynamic-update-slice_fusion.4.refs_6_), channel_id=1, source_target_pairs={{0,2},{1,3},{2,0},{3,1},{4,6},{5,7},{6,4},{7,5},{8,10},{9,11},{10,... | collective-permute-start | bytes 6291464 | tf_op jit(solution)/shard_map/ppermute | solution.py:36
  233.6 19.8 %collective-permute-start.22 = (bf16[4,256,256]{2,1,0:T(8,128)(2,1)S(1)}, bf16[4,256,256]{2,1,0:T(8,128)(2,1)S(1)}, u32[]{:S(2)}, u32[]{:S(2)}) collective-permute-start(bf16[4,256,256]{2,1,0:T(8,128)(2,1)S(1)} %get-tuple-element.297), channel_id=1, source_target_pairs={{0,8},{8,0},{16,24},{24,16},{1,9},{9,1},{17,25},{25,17},{2,10},{10... | collective-permute-start | bytes 1572872 | tf_op jit(solution)/shard_map/ppermute | solution.py:36
  235.7 38.2 %collective-permute-start.23 = (bf16[4,256,256]{2,1,0:T(8,128)(2,1)S(1)}, bf16[4,256,256]{2,1,0:T(8,128)(2,1)S(1)}, u32[]{:S(2)}, u32[]{:S(2)}) collective-permute-start(bf16[4,256,256]{2,1,0:T(8,128)(2,1)S(1)} %get-tuple-element.296), channel_id=1, source_target_pairs={{0,16},{8,24},{16,0},{24,8},{1,17},{9,25},{17,1},{25,9},{2,18},{10... | collective-permute-start | bytes 1572872 | tf_op jit(solution)/shard_map/ppermute | solution.py:36
  237.9 36.0 %collective-permute-start.21 = (bf16[4,256,256]{2,1,0:T(8,128)(2,1)S(1)}, bf16[4,256,256]{2,1,0:T(8,128)(2,1)S(1)}, u32[]{:S(2)}, u32[]{:S(2)}) collective-permute-start(bf16[4,256,256]{2,1,0:T(8,128)(2,1)S(1)} %constant_dynamic-slice_fusion.10), channel_id=1, source_target_pairs={{0,24},{8,16},{16,8},{24,0},{1,25},{9,17},{17,9},{25,1},{2,26},{10... | collective-permute-start | bytes 1572872 | tf_op jit(solution)/shard_map/ppermute | solution.py:36
  279.1 19.1 %collective-permute-start.27 = (bf16[1024,512]{1,0:T(8,128)(2,1)S(1)}, bf16[1024,512]{1,0:T(8,128)(2,1)S(1)}, u32[]{:S(2)}, u32[]{:S(2)}) collective-permute-start(bf16[1024,512]{1,0:T(8,128)(2,1)S(1)} %slice.330), channel_id=1, source_target_pairs={{0,2},{1,3},{2,0},{3,1},{4,6},{5,7},{6,4},{7,5},{8,10},{9,11},{10,... | collective-permute-start | bytes 3145736 | tf_op jit(solution)/shard_map/ppermute | solution.py:36
  284.4 33.0 %collective-permute-start.26 = (bf16[4,4,256,256]{3,2,1,0:T(8,128)(2,1)S(1)}, bf16[4,4,256,256]{3,2,1,0:T(8,128)(2,1)}, u32[]{:S(2)}, u32[]{:S(2)}) collective-permute-start(bf16[4,4,256,256]{3,2,1,0:T(8,128)(2,1)S(1)} %pad_maximum_fusion.refs_2_.refs_5_), channel_id=1, source_target_pairs={{0,4},{4,0},{1,5},{5,1},{2,6},{6,2},{3,7},{7,3},{8,12},{12,8},{9,1... | collective-permute-start | bytes 6291464 | tf_op jit(solution)/shard_map/ppermute | solution.py:36
  300.2 19.2 %collective-permute-start.30 = (bf16[4,4,256,256]{3,2,1,0:T(8,128)(2,1)}, bf16[4,4,256,256]{3,2,1,0:T(8,128)(2,1)}, u32[]{:S(2)}, u32[]{:S(2)}) collective-permute-start(bf16[4,4,256,256]{3,2,1,0:T(8,128)(2,1)} %pad_maximum_fusion.1.refs_4_.refs_7_), channel_id=1, source_target_pairs={{0,4},{4,0},{1,5},{5,1},{2,6},{6,2},{3,7},{7,3},{8,12},{12,8},{9,1... | collective-permute-start | bytes 6291464 | tf_op jit(solution)/shard_map/ppermute | solution.py:36
  305.7 47.7 %collective-permute-start.32 = (bf16[1024,512]{1,0:T(8,128)(2,1)S(1)}, bf16[1024,512]{1,0:T(8,128)(2,1)S(1)}, u32[]{:S(2)}, u32[]{:S(2)}) collective-permute-start(bf16[1024,512]{1,0:T(8,128)(2,1)S(1)} %slice.333), channel_id=1, source_target_pairs={{0,1},{1,0},{2,3},{3,2},{4,5},{5,4},{6,7},{7,6},{8,9},{9,8},{10,11... | collective-permute-start | bytes 3145736 | tf_op jit(solution)/shard_map/ppermute | solution.py:36
  307.6 45.8 %collective-permute-start.31 = (bf16[1024,512]{1,0:T(8,128)(2,1)S(1)}, bf16[1024,512]{1,0:T(8,128)(2,1)S(1)}, u32[]{:S(2)}, u32[]{:S(2)}) collective-permute-start(bf16[1024,512]{1,0:T(8,128)(2,1)S(1)} %slice.332), channel_id=1, source_target_pairs={{0,2},{1,3},{2,0},{3,1},{4,6},{5,7},{6,4},{7,5},{8,10},{9,11},{10,... | collective-permute-start | bytes 3145736 | tf_op jit(solution)/shard_map/ppermute | solution.py:36
  309.7 58.9 %collective-permute-start.33 = (bf16[4,256,256]{2,1,0:T(8,128)(2,1)}, bf16[4,256,256]{2,1,0:T(8,128)(2,1)}, u32[]{:S(2)}, u32[]{:S(2)}) collective-permute-start(bf16[4,256,256]{2,1,0:T(8,128)(2,1)} %get-tuple-element.294), channel_id=1, source_target_pairs={{0,8},{8,0},{16,24},{24,16},{1,9},{9,1},{17,25},{25,17},{2,10},{10... | collective-permute-start | bytes 1572872 | tf_op jit(solution)/shard_map/ppermute | solution.py:36
  317.4 51.3 %collective-permute-start.34 = (bf16[4,256,256]{2,1,0:T(8,128)(2,1)S(1)}, bf16[4,256,256]{2,1,0:T(8,128)(2,1)S(1)}, u32[]{:S(2)}, u32[]{:S(2)}) collective-permute-start(bf16[4,256,256]{2,1,0:T(8,128)(2,1)S(1)} %get-tuple-element.293), channel_id=1, source_target_pairs={{0,16},{8,24},{16,0},{24,8},{1,17},{9,25},{17,1},{25,9},{2,18},{10... | collective-permute-start | bytes 1572872 | tf_op jit(solution)/shard_map/ppermute | solution.py:36
  319.4 49.3 %collective-permute-start.35 = (bf16[4,256,256]{2,1,0:T(8,128)(2,1)S(1)}, bf16[4,256,256]{2,1,0:T(8,128)(2,1)S(1)}, u32[]{:S(2)}, u32[]{:S(2)}) collective-permute-start(bf16[4,256,256]{2,1,0:T(8,128)(2,1)S(1)} %get-tuple-element.292), channel_id=1, source_target_pairs={{0,24},{8,16},{16,8},{24,0},{1,25},{9,17},{17,9},{25,1},{2,26},{10... | collective-permute-start | bytes 1572872 | tf_op jit(solution)/shard_map/ppermute | solution.py:36
  370.1 35.0 %collective-permute-start.37 = (bf16[4,4,256,256]{3,2,1,0:T(8,128)(2,1)}, bf16[4,4,256,256]{3,2,1,0:T(8,128)(2,1)}, u32[]{:S(2)}, u32[]{:S(2)}) collective-permute-start(bf16[4,4,256,256]{3,2,1,0:T(8,128)(2,1)} %get-tuple-element.184), channel_id=1, source_target_pairs={{0,4},{4,0},{1,5},{5,1},{2,6},{6,2},{3,7},{7,3},{8,12},{12,8},{9,1... | collective-permute-start | bytes 6291464 | tf_op jit(solution)/shard_map/ppermute | solution.py:36
  408.4 34.1 %collective-permute-start.38 = (bf16[4,256,256]{2,1,0:T(8,128)(2,1)S(1)}, bf16[4,256,256]{2,1,0:T(8,128)(2,1)S(1)}, u32[]{:S(2)}, u32[]{:S(2)}) collective-permute-start(bf16[4,256,256]{2,1,0:T(8,128)(2,1)S(1)} %get-tuple-element.290), channel_id=1, source_target_pairs={{0,8},{8,0},{16,24},{24,16},{1,9},{9,1},{17,25},{25,17},{2,10},{10... | collective-permute-start | bytes 1572872 | tf_op jit(solution)/shard_map/ppermute | solution.py:36
  408.8 38.2 %collective-permute-start.39 = (bf16[4,256,256]{2,1,0:T(8,128)(2,1)S(1)}, bf16[4,256,256]{2,1,0:T(8,128)(2,1)S(1)}, u32[]{:S(2)}, u32[]{:S(2)}) collective-permute-start(bf16[4,256,256]{2,1,0:T(8,128)(2,1)S(1)} %get-tuple-element.289), channel_id=1, source_target_pairs={{0,16},{8,24},{16,0},{24,8},{1,17},{9,25},{17,1},{25,9},{2,18},{10... | collective-permute-start | bytes 1572872 | tf_op jit(solution)/shard_map/ppermute | solution.py:36
  411.5 35.5 %collective-permute-start.40 = (bf16[2,528,512]{2,1,0:T(8,128)(2,1)S(1)}, bf16[2,528,512]{2,1,0:T(8,128)(2,1)S(1)}, u32[]{:S(2)}, u32[]{:S(2)}) collective-permute-start(bf16[2,528,512]{2,1,0:T(8,128)(2,1)S(1)} %get-tuple-element.275), channel_id=1, source_target_pairs={{0,1},{1,0},{2,3},{3,2},{4,5},{5,4},{6,7},{7,6},{8,9},{9,8},{10,11... | collective-permute-start | bytes 3244040 | tf_op jit(solution)/shard_map/ppermute | solution.py:36
  412.3 34.7 %collective-permute-start.41 = (bf16[2,528,512]{2,1,0:T(8,128)(2,1)S(1)}, bf16[2,528,512]{2,1,0:T(8,128)(2,1)S(1)}, u32[]{:S(2)}, u32[]{:S(2)}) collective-permute-start(bf16[2,528,512]{2,1,0:T(8,128)(2,1)S(1)} %get-tuple-element.274), channel_id=1, source_target_pairs={{0,2},{1,3},{2,0},{3,1},{4,6},{5,7},{6,4},{7,5},{8,10},{9,11},{10,... | collective-permute-start | bytes 3244040 | tf_op jit(solution)/shard_map/ppermute | solution.py:36
  413.6 65.3 %collective-permute-start.42 = (bf16[4,256,256]{2,1,0:T(8,128)(2,1)}, bf16[4,256,256]{2,1,0:T(8,128)(2,1)S(1)}, u32[]{:S(2)}, u32[]{:S(2)}) collective-permute-start(bf16[4,256,256]{2,1,0:T(8,128)(2,1)} %get-tuple-element.288), channel_id=1, source_target_pairs={{0,24},{8,16},{16,8},{24,0},{1,25},{9,17},{17,9},{25,1},{2,26},{10... | collective-permute-start | bytes 1572872 | tf_op jit(solution)/shard_map/ppermute | solution.py:36
  451.6 27.3 %collective-permute-start.45 = (bf16[528,512]{1,0:T(8,128)(2,1)}, bf16[528,512]{1,0:T(8,128)(2,1)}, u32[]{:S(2)}, u32[]{:S(2)}) collective-permute-start(bf16[528,512]{1,0:T(8,128)(2,1)} %get-tuple-element.271), channel_id=1, source_target_pairs={{0,2},{1,3},{2,0},{3,1},{4,6},{5,7},{6,4},{7,5},{8,10},{9,11},{10,... | collective-permute-start | bytes 1622024 | tf_op jit(solution)/shard_map/ppermute | solution.py:36
  452.5 26.4 %collective-permute-start.46 = (bf16[528,512]{1,0:T(8,128)(2,1)S(1)}, bf16[528,512]{1,0:T(8,128)(2,1)}, u32[]{:S(2)}, u32[]{:S(2)}) collective-permute-start(bf16[528,512]{1,0:T(8,128)(2,1)S(1)} %get-tuple-element.270), channel_id=1, source_target_pairs={{0,1},{1,0},{2,3},{3,2},{4,5},{5,4},{6,7},{7,6},{8,9},{9,8},{10,11... | collective-permute-start | bytes 1622024 | tf_op jit(solution)/shard_map/ppermute | solution.py:36
  453.9 29.8 %collective-permute-start.43 = (bf16[2,528,512]{2,1,0:T(8,128)(2,1)S(1)}, bf16[2,528,512]{2,1,0:T(8,128)(2,1)S(1)}, u32[]{:S(2)}, u32[]{:S(2)}) collective-permute-start(bf16[2,528,512]{2,1,0:T(8,128)(2,1)S(1)} %get-tuple-element.273), channel_id=1, source_target_pairs={{0,1},{1,0},{2,3},{3,2},{4,5},{5,4},{6,7},{7,6},{8,9},{9,8},{10,11... | collective-permute-start | bytes 3244040 | tf_op jit(solution)/shard_map/ppermute | solution.py:36
  454.8 28.9 %collective-permute-start.44 = (bf16[2,528,512]{2,1,0:T(8,128)(2,1)S(1)}, bf16[2,528,512]{2,1,0:T(8,128)(2,1)S(1)}, u32[]{:S(2)}, u32[]{:S(2)}) collective-permute-start(bf16[2,528,512]{2,1,0:T(8,128)(2,1)S(1)} %get-tuple-element.272), channel_id=1, source_target_pairs={{0,2},{1,3},{2,0},{3,1},{4,6},{5,7},{6,4},{7,5},{8,10},{9,11},{10,... | collective-permute-start | bytes 3244040 | tf_op jit(solution)/shard_map/ppermute | solution.py:36
  489.5 25.6 %collective-permute-start.47 = (bf16[2,528,512]{2,1,0:T(8,128)(2,1)}, bf16[2,528,512]{2,1,0:T(8,128)(2,1)}, u32[]{:S(2)}, u32[]{:S(2)}) collective-permute-start(bf16[2,528,512]{2,1,0:T(8,128)(2,1)} %pad_maximum_fusion.4), channel_id=1, source_target_pairs={{0,8},{8,0},{16,24},{24,16},{1,9},{9,1},{17,25},{25,17},{2,10},{10... | collective-permute-start | bytes 3244040 | tf_op jit(solution)/shard_map/ppermute | solution.py:36
  495.8 19.2 %collective-permute-start.48 = (bf16[528,512]{1,0:T(8,128)(2,1)}, bf16[528,512]{1,0:T(8,128)(2,1)}, u32[]{:S(2)}, u32[]{:S(2)}) collective-permute-start(bf16[528,512]{1,0:T(8,128)(2,1)} %get-tuple-element.267), channel_id=1, source_target_pairs={{0,2},{1,3},{2,0},{3,1},{4,6},{5,7},{6,4},{7,5},{8,10},{9,11},{10,... | collective-permute-start | bytes 1622024 | tf_op jit(solution)/shard_map/ppermute | solution.py:36
  515.1 211.2 %reduce-scatter.6.cloned.1.call-start = ((), (), s32[]{:S(2)}) async-start(), calls=%async_computation.5 | async-start | bytes 2359296 | tf_op jit(solution)/shard_map/reduce_scatter | solution.py:843
  515.6 34.3 %collective-permute-start.51 = (bf16[4,2,4,256,256]{4,3,2,1,0:T(8,128)(2,1)}, bf16[4,2,4,256,256]{4,3,2,1,0:T(8,128)(2,1)}, u32[]{:S(2)}, u32[]{:S(2)}) collective-permute-start(bf16[4,2,4,256,256]{4,3,2,1,0:T(8,128)(2,1)} %get-tuple-element.210), channel_id=1, source_target_pairs={{0,4},{4,0},{1,5},{5,1},{2,6},{6,2},{3,7},{7,3},{8,12},{12,8},{9,1... | collective-permute-start | bytes 12582920 | tf_op jit(solution)/shard_map/ppermute | solution.py:36
  518.2 28.3 %collective-permute-start.50 = (bf16[1,528,512]{2,1,0:T(8,128)(2,1)}, bf16[1,528,512]{2,1,0:T(8,128)(2,1)}, u32[]{:S(2)}, u32[]{:S(2)}) collective-permute-start(bf16[1,528,512]{2,1,0:T(8,128)(2,1)} %fusion.48), channel_id=1, source_target_pairs={{0,16},{8,24},{16,0},{24,8},{1,17},{9,25},{17,1},{25,9},{2,18},{10... | collective-permute-start | bytes 1622024 | tf_op jit(solution)/shard_map/ppermute | solution.py:36
  564.4 18.9 %collective-permute-start.55 = (bf16[512,512]{1,0:T(8,128)(2,1)}, bf16[512,512]{1,0:T(8,128)(2,1)}, u32[]{:S(2)}, u32[]{:S(2)}) collective-permute-start(bf16[512,512]{1,0:T(8,128)(2,1)} %get-tuple-element.261), channel_id=1, source_target_pairs={{0,2},{1,3},{2,0},{3,1},{4,6},{5,7},{6,4},{7,5},{8,10},{9,11},{10,... | collective-permute-start | bytes 1572872 | tf_op jit(solution)/shard_map/ppermute | solution.py:36
  567.2 46.0 %collective-permute-start.58 = (bf16[2,4,256,256]{3,2,1,0:T(8,128)(2,1)}, bf16[2,4,256,256]{3,2,1,0:T(8,128)(2,1)S(1)}, u32[]{:S(2)}, u32[]{:S(2)}) collective-permute-start(bf16[2,4,256,256]{3,2,1,0:T(8,128)(2,1)} %get-tuple-element.278), channel_id=1, source_target_pairs={{0,8},{8,0},{16,24},{24,16},{1,9},{9,1},{17,25},{25,17},{2,10},{10... | collective-permute-start | bytes 3145736 | tf_op jit(solution)/shard_map/ppermute | solution.py:36
  568.1 47.1 %collective-permute-start.59 = (bf16[2,4,256,256]{3,2,1,0:T(8,128)(2,1)}, bf16[2,4,256,256]{3,2,1,0:T(8,128)(2,1)}, u32[]{:S(2)}, u32[]{:S(2)}) collective-permute-start(bf16[2,4,256,256]{3,2,1,0:T(8,128)(2,1)} %get-tuple-element.277), channel_id=1, source_target_pairs={{0,16},{8,24},{16,0},{24,8},{1,17},{9,25},{17,1},{25,9},{2,18},{10... | collective-permute-start | bytes 3145736 | tf_op jit(solution)/shard_map/ppermute | solution.py:36
  615.2 28.2 %collective-permute-start.60 = (bf16[2,4,256,256]{3,2,1,0:T(8,128)(2,1)}, bf16[2,4,256,256]{3,2,1,0:T(8,128)(2,1)}, u32[]{:S(2)}, u32[]{:S(2)}) collective-permute-start(bf16[2,4,256,256]{3,2,1,0:T(8,128)(2,1)} %get-tuple-element.220), channel_id=1, source_target_pairs={{0,24},{8,16},{16,8},{24,0},{1,25},{9,17},{17,9},{25,1},{2,26},{10... | collective-permute-start | bytes 3145736 | tf_op jit(solution)/shard_map/ppermute | solution.py:36
  634.8 26.5 %collective-permute-start.61 = (bf16[2,512,512]{2,1,0:T(8,128)(2,1)S(1)}, bf16[2,512,512]{2,1,0:T(8,128)(2,1)S(1)}, u32[]{:S(2)}, u32[]{:S(2)}) collective-permute-start(bf16[2,512,512]{2,1,0:T(8,128)(2,1)S(1)} %pad_maximum_fusion.5), channel_id=1, source_target_pairs={{0,8},{8,0},{16,24},{24,16},{1,9},{9,1},{17,25},{25,17},{2,10},{10... | collective-permute-start | bytes 3145736 | tf_op jit(solution)/shard_map/ppermute | solution.py:36
  664.1 140.4 %reduce-scatter.8.cloned.1.call-start = ((), (), s32[]{:S(2)}) async-start(), calls=%async_computation.6 | async-start | bytes 7077888 | tf_op jit(solution)/shard_map/reduce_scatter | solution.py:889
  684.6 33.9 %collective-permute-start.64 = (bf16[1,512,512]{2,1,0:T(8,128)(2,1)S(1)}, bf16[1,512,512]{2,1,0:T(8,128)(2,1)S(1)}, u32[]{:S(2)}, u32[]{:S(2)}) collective-permute-start(bf16[1,512,512]{2,1,0:T(8,128)(2,1)S(1)} %add_convert_fusion.4), channel_id=1, source_target_pairs={{0,16},{8,24},{16,0},{24,8},{1,17},{9,25},{17,1},{25,9},{2,18},{10... | collective-permute-start | bytes 1572872 | tf_op jit(solution)/shard_map/ppermute | solution.py:36
  685.6 19.1 %collective-permute-start.66 = (f32[19,512]{1,0:T(8,128)S(1)}, f32[19,512]{1,0:T(8,128)S(1)}, u32[]{:S(2)}, u32[]{:S(2)}) collective-permute-start(f32[19,512]{1,0:T(8,128)S(1)} %fusion.92), channel_id=1, source_target_pairs={{0,8},{8,0},{16,24},{24,16},{1,9},{9,1},{17,25},{25,17},{2,10},{10... | collective-permute-start | bytes 116744 | tf_op jit(solution)/shard_map/ppermute | solution.py:36
  (129 other events, 1300.5 us)
Sparse Core Ops, SparseCore 0:
  11.8 71.7 all-gather.2
  85.2 46.0 all-gather.4
  515.2 98.6 reduce-scatter.9
  664.3 40.3 reduce-scatter.5
  726.5 69.3 reduce-scatter.7

commit v6 on v4

--- a/solution.py
+++ b/solution.py
@@ -49,7 +49,10 @@
 
 
 def tensor_sum(value):
-    return butterfly_sum(value, ("tensor",))
+    parts = [value] + [swap(value, "tensor", k) for k in range(1, lax.axis_size("tensor"))]
+    while len(parts) > 1:
+        parts = [a + b for a, b in zip(parts[::2], parts[1::2])]
+    return parts[0]
 
 
 def rope_tables(length, head_dim):
@@ -829,7 +832,6 @@
     moe_near = scatter_z_near({k: moe_parts[k] for k in range(1, nz, 2)})
 
     wo_grad = jnp.einsum("sa,sd->ad", joined, dresid_low, preferred_element_type=f32)
-    wo_own = lax.psum_scatter(wo_grad.astype(bf16), dp, scatter_dimension=1, tiled=True)
     dout = (
         jnp.einsum("sd,ad->sa", dresid_low, wo_full, preferred_element_type=f32)
         .astype(bf16)
@@ -840,6 +842,8 @@
     inner = jnp.sum(weights * dweights, -1, keepdims=True)
     dscores = (weights * (dweights - inner)).astype(bf16)
     dscores, up_own[-1], moe_near = fence(dscores, up_own[-1], moe_near)
+    wo_grad = after(wo_grad.astype(bf16), dscores)
+    wo_own = lax.psum_scatter(wo_grad, dp, scatter_dimension=1, tiled=True)
     dq_rot = scale * jnp.einsum("hqk,khd->qhd", dscores, k_rot, preferred_element_type=f32)
     dk_rot = scale * jnp.einsum("hqk,qhd->khd", dscores, q_rot, preferred_element_type=f32)
     dq_norm = unrotate(dq_rot, cosine, sine).reshape(seq, local)

time: 830 us -> 827 us (level)
    ppermute x86 -> x93, waiting for transfers between devices: 278 us -> 276 us  [swap(): return lax.ppermute(value, axis, [(i, i ^ mask) for i in range(n)])]
    unnamed x173 -> x181, local copies, waits for them, and re-layouts: 17.2 us -> 18.5 us
    ppermute x86 -> x93, starting transfers between devices: 114 us -> 115 us  [swap(): return lax.ppermute(value, axis, [(i, i ^ mask) for i in range(n)])]
  transfers between devices with their start and end apart: 91 -> 98, of which waited for: 48 -> 47; matrix products, arithmetic and copies ran while one was open for 19% -> 19% of each run, Pallas kernels for 18% -> 18%
where the time goes in v6:
time: 827 us; the launch traced here: 822 us
  waiting for transfers between devices  350 us (42%)
  Pallas kernels  149 us (18%)
  starting transfers between devices  116 us (14%)
  other arithmetic  74 us (9%)
  local copies, waits for them, and re-layouts  65.7 us (8%)
  matrix products  51.8 us (6%)
  between operations  15.6 us (2%)
    ppermute x93, waiting for transfers between devices, swap(): return lax.ppermute(value, axis, [(i, i ^ mask) for i in range(n)])  276 us
    ppermute x93, starting transfers between devices, swap(): return lax.ppermute(value, axis, [(i, i ^ mask) for i in range(n)])  115 us
    all_gather x1, waiting for transfers between devices, shards(): lax.all_gather(jnp.concatenate([wq, wk, wv, small], 1), dp, axis=0, tiled...  60.4 us
    pallas_call x2, Pallas kernels, backward_call(): pl.pallas_call(functools.partial(backward_kernel, nz, n, own_e, hid, slic...  54.7 us
    pallas_call x1, Pallas kernels, forward_call(): pl.pallas_call(functools.partial(forward_kernel, nz, n, own_e, hid, slice...  32.1 us
    pallas_call x1, Pallas kernels, up_grad_call(): pl.pallas_call(functools.partial(up_grad_kernel, nz, own_e, hid, seq, sli...  23 us
    unnamed x181, local copies, waits for them, and re-layouts  18.5 us
    pallas_call x1, Pallas kernels, output_call(): pl.pallas_call(functools.partial(output_kernel, nz, own_e, hid, slice_d,...  17.2 us
  transfers between devices with their start and end apart: 98, of which 47 were waited for; matrix products, arithmetic and copies ran while one was open for 19% of the time, Pallas kernels for 18%

profile of v6, /device:TPU:0, one launch (start us, length us, event | category | flops | bytes accessed | tf_op | source)
XLA Modules:
  0.0 821.8 jit_solution(3487141651594650230)
XLA Ops:
  11.7 4.1 collective-permute-start.1
  23.1 60.4 %all-gather.3.cloned.1.call-done = bf16[2048,1664]{1,0:T(8,128)(2,1)} async-done(((bf16[256,1664]{1,0:T(8,128)(2,1)}), bf16[2048,1664]{1,0:T(8,128)(2,1)}) %all-gather.3.cloned.1.call-update) | async-done | bytes 6815760 | tf_op jit(solution)/shard_map/all_gather | solution.py:659
  85.5 6.5 fusion.4
  110.2 5.0 fusion.100
  115.2 3.6 convolution_convert_fusion.5
  118.8 13.1 %all-gather.5.cloned.1.call-done = bf16[512,2048]{1,0:T(8,128)(2,1)} async-done(((bf16[512,256]{1,0:T(8,128)(2,1)}), bf16[512,2048]{1,0:T(8,128)(2,1)}) %all-gather.5.cloned.1.call-update) | async-done | bytes 2097168 | tf_op jit(solution)/shard_map/all_gather | solution.py:675
  145.5 4.8 collective-permute-done.8
  170.8 6.8 collective-permute-done.15
  177.6 4.1 collective-permute-done.16
  186.8 20.2 %collective-permute-done.19 = bf16[512,512]{1,0:T(8,128)(2,1)S(1)} collective-permute-done((bf16[512,512]{1,0:T(8,128)(2,1)S(1)}, bf16[512,512]{1,0:T(8,128)(2,1)S(1)}, u32[]{:S(2)}, u32[]{:S(2)}) %collective-permute-start.19) | collective-permute-done | bytes 524320 | tf_op jit(solution)/shard_map/ppermute | solution.py:36
  208.9 11.9 %collective-permute-done.20 = bf16[512,512]{1,0:T(8,128)(2,1)S(1)} collective-permute-done((bf16[512,512]{1,0:T(8,128)(2,1)S(1)}, bf16[512,512]{1,0:T(8,128)(2,1)S(1)}, u32[]{:S(2)}, u32[]{:S(2)}) %collective-permute-start.20) | collective-permute-done | bytes 524320 | tf_op jit(solution)/shard_map/ppermute | solution.py:36
  220.8 7.9 collective-permute-done.21.refs_1_
  241.1 13.6 %collective-permute-done.24 = bf16[4,256,256]{2,1,0:T(8,128)(2,1)S(1)} collective-permute-done((bf16[4,256,256]{2,1,0:T(8,128)(2,1)S(1)}, bf16[4,256,256]{2,1,0:T(8,128)(2,1)S(1)}, u32[]{:S(2)}, u32[]{:S(2)}) %collective-permute-start.24) | collective-permute-done | bytes 524320 | tf_op jit(solution)/shard_map/ppermute | solution.py:36
  254.8 19.2 %collective-permute-done.25 = bf16[4,256,256]{2,1,0:T(8,128)(2,1)S(1)} collective-permute-done((bf16[4,256,256]{2,1,0:T(8,128)(2,1)S(1)}, bf16[4,256,256]{2,1,0:T(8,128)(2,1)S(1)}, u32[]{:S(2)}, u32[]{:S(2)}) %collective-permute-start.25) | collective-permute-done | bytes 524320 | tf_op jit(solution)/shard_map/ppermute | solution.py:36
  273.9 3.8 collective-permute-done.26.refs_7_
  285.4 10.1 %collective-permute-done.31 = bf16[4,256,256]{2,1,0:T(8,128)(2,1)S(1)} collective-permute-done((bf16[4,256,256]{2,1,0:T(8,128)(2,1)S(1)}, bf16[4,256,256]{2,1,0:T(8,128)(2,1)S(1)}, u32[]{:S(2)}, u32[]{:S(2)}) %collective-permute-start.31) | collective-permute-done | bytes 524320 | tf_op jit(solution)/shard_map/ppermute | solution.py:36
  295.5 4.9 collective-permute-done.29.refs_9_
  314.3 4.4 collective-permute-start.35
  321.6 32.1 %shard_map.254 = (f32[2048,1024]{1,0:T(8,128)}, f32[2048,1024]{1,0:T(8,128)}, bf16[2048,1024]{1,0:T(8,128)(2,1)}, f32[2048,128]{1,0:T(8,128)}, bf16[2048,2048]{1,0:T(8,128)(2,1)}) custom-call(s32[3]{0:T(128)} %pad_add_fusion.idx, f32[2048,128]{1,0:T(8,128)} %pad_convert_fusion.refs_0_.refs_4_, bf16[4,512,128]{2,1,0:T(8,128)(2,1)} %bitcast.310, ...), custom_call_target="tpu_custom_call" | custom-call | flops 17179869184 | bytes 41943040 | tf_op jit(solution)/shard_map/pallas_call | solution.py:304
  353.8 15.2 %shard_map.255 = (bf16[4,4,256,256]{3,2,1,0:T(8,128)(2,1)S(1)}, bf16[4,4,256,256]{3,2,1,0:T(8,128)(2,1)}, bf16[4,2048,512]{2,1,0:T(8,128)(2,1)}) custom-call(s32[3]{0:T(128)S(1)} %copy-done.6, bf16[2048,1024]{1,0:T(8,128)(2,1)} %get-tuple-element.211.hid_ref, bf16[2048,512]{1,0:T(8,128)(2,1)} %copy-done.68, ...), custom_call_target="tpu_custom_call" | custom-call | flops 8589934592 | bytes 25165824 | tf_op jit(solution)/shard_map/pallas_call | solution.py:529
  371.0 5.9 collective-permute-done.38.refs_10_.far
  378.2 27.2 %shard_map.256 = (bf16[2,4,528,512]{3,2,1,0:T(8,128)(2,1)}, bf16[1024,1024]{1,0:T(8,128)(2,1)}, bf16[1024,1024]{1,0:T(8,128)(2,1)}) custom-call(s32[3]{0:T(128)} %pad_add_fusion.idx, bf16[4,4,512,512]{3,2,1,0:T(8,128)(2,1)} %bitcast.355, f32[2048,1024]{1,0:T(8,128)} %get-tuple-element.179.refs_1_, f32[2048,1024]{1,0:T(8,128)} %get-tuple-element.180.refs_2_, ...), custom_call_target="tpu_custom_call" | custom-call | flops 12884901888 | bytes 41943040 | tf_op jit(solution)/shard_map/pallas_call | solution.py:404
  415.2 27.5 %shard_map.257 = (bf16[2,4,528,512]{3,2,1,0:T(8,128)(2,1)}, bf16[1024,1024]{1,0:T(8,128)(2,1)}, bf16[1024,1024]{1,0:T(8,128)(2,1)}) custom-call(s32[3]{0:T(128)} %pad_add_fusion.idx, bf16[4,4,512,512]{3,2,1,0:T(8,128)(2,1)} %bitcast.356, f32[2048,1024]{1,0:T(8,128)} %get-tuple-element.179.refs_1_, f32[2048,1024]{1,0:T(8,128)} %get-tuple-element.180.refs_2_, ...), custom_call_target="tpu_custom_call" | custom-call | flops 12884901888 | bytes 41943040 | tf_op jit(solution)/shard_map/pallas_call | solution.py:404
  442.6 4.8 collective-permute-done.41.refs_6_
  448.2 3.7 fusion.36
  456.3 23.0 %shard_map.258 = (bf16[4,2,4,256,256]{4,3,2,1,0:T(8,128)(2,1)}, bf16[4,2,4,256,256]{4,3,2,1,0:T(8,128)(2,1)}) custom-call(s32[3]{0:T(128)S(1)} %copy-done.7, bf16[2048,2048]{1,0:T(8,128)(2,1)} %get-tuple-element.199.m_ref, bf16[1024,1024]{1,0:T(8,128)(2,1)S(1)} %copy-done.11, bf16[1024,1024]{1,0:T(8,128)(2,1)S(1)} %copy-done.10, ...), custom_call_target="tpu_custom_call" | custom-call | flops 17179869184 | bytes 25165824 | tf_op jit(solution)/shard_map/pallas_call | solution.py:577
  479.3 4.6 collective-permute-done.45
  489.7 4.1 collective-permute-start.49
  498.0 17.2 %shard_map.259 = bf16[4,4,512,512]{3,2,1,0:T(8,128)(2,1)} custom-call(s32[3]{0:T(128)S(1)} %copy-done.7, bf16[2048,1024]{1,0:T(8,128)(2,1)} %get-tuple-element.211.hid_ref, bf16[4,4,256,256]{3,2,1,0:T(8,128)(2,1)S(1)} %copy-done.1, bf16[4,4,256,256]{3,2,1,0:T(8,128)(2,1)S(1)} %copy-done.9), custom_call_target="tpu_custom_call" | custom-call | flops 8589934592 | bytes 16777216 | tf_op jit(solution)/shard_map/pallas_call | solution.py:464
  526.6 20.1 %collective-permute-done.52 = bf16[1,528,512]{2,1,0:T(8,128)(2,1)} collective-permute-done((bf16[1,528,512]{2,1,0:T(8,128)(2,1)}, bf16[1,528,512]{2,1,0:T(8,128)(2,1)}, u32[]{:S(2)}, u32[]{:S(2)}) %collective-permute-start.52) | collective-permute-done | bytes 540704 | tf_op jit(solution)/shard_map/ppermute | solution.py:36
  556.2 3.9 add_convert_fusion
  569.9 11.0 %collective-permute-done.57 = bf16[512,512]{1,0:T(8,128)(2,1)} collective-permute-done((bf16[512,512]{1,0:T(8,128)(2,1)}, bf16[512,512]{1,0:T(8,128)(2,1)}, u32[]{:S(2)}, u32[]{:S(2)}) %collective-permute-start.57) | collective-permute-done | bytes 524320 | tf_op jit(solution)/shard_map/ppermute | solution.py:36
  590.2 5.1 collective-permute-done.59
  599.4 13.2 %collective-permute-done.61.refs_1_ = bf16[2,4,256,256]{3,2,1,0:T(8,128)(2,1)S(1)} collective-permute-done((bf16[2,4,256,256]{3,2,1,0:T(8,128)(2,1)}, bf16[2,4,256,256]{3,2,1,0:T(8,128)(2,1)S(1)}, u32[]{:S(2)}, u32[]{:S(2)}) %collective-permute-start.61) | collective-permute-done | bytes 1048608 | tf_op jit(solution)/shard_map/ppermute | solution.py:36
  622.9 4.3 convolution_convert_fusion.1
  627.3 4.1 fusion.51
  633.8 5.0 multiply_convert_fusion
  638.9 4.0 collective-permute-done.63.refs_3_
  642.9 18.6 %collective-permute-done.64 = bf16[2,512,512]{2,1,0:T(8,128)(2,1)S(1)} collective-permute-done((bf16[2,512,512]{2,1,0:T(8,128)(2,1)S(1)}, bf16[2,512,512]{2,1,0:T(8,128)(2,1)S(1)}, u32[]{:S(2)}, u32[]{:S(2)}) %collective-permute-start.64) | collective-permute-done | bytes 1048608 | tf_op jit(solution)/shard_map/ppermute | solution.py:36
  686.9 17.2 %collective-permute-done.70 = f32[19,512]{1,0:T(8,128)S(1)} collective-permute-done((f32[19,512]{1,0:T(8,128)S(1)}, f32[19,512]{1,0:T(8,128)S(1)}, u32[]{:S(2)}, u32[]{:S(2)}) %collective-permute-start.70) | collective-permute-done | bytes 38944 | tf_op jit(solution)/shard_map/ppermute | solution.py:36
  707.2 11.1 %collective-permute-done.71 = f32[19,512]{1,0:T(8,128)S(1)} collective-permute-done((f32[19,512]{1,0:T(8,128)S(1)}, f32[19,512]{1,0:T(8,128)S(1)}, u32[]{:S(2)}, u32[]{:S(2)}) %collective-permute-start.71) | collective-permute-done | bytes 38944 | tf_op jit(solution)/shard_map/ppermute | solution.py:36
  720.6 5.6 convolution_convert_fusion
  730.1 7.1 fusion.8
  745.1 8.9 %collective-permute-done.72 = bf16[2,256,512]{2,1,0:T(8,128)(2,1)S(1)} collective-permute-done((bf16[2,256,512]{2,1,0:T(8,128)(2,1)S(1)}, bf16[2,256,512]{2,1,0:T(8,128)(2,1)S(1)}, u32[]{:S(2)}, u32[]{:S(2)}) %collective-permute-start.72) | collective-permute-done | bytes 524320 | tf_op jit(solution)/shard_map/ppermute | solution.py:36
  756.9 3.6 collective-permute-done.78
  760.6 4.3 collective-permute-done.73
  773.3 6.9 shard_map.260
  790.4 6.3 collective-permute-done.90
  (506 shorter events, 275.9 us)
Async XLA Ops:
  7.2 76.4 %all-gather.3.cloned.1.call-start = ((), (), s32[]{:S(2)}) async-start(), calls=%async_computation.3 | async-start | bytes 7667712 | tf_op jit(solution)/shard_map/all_gather | solution.py:659
  11.6 120.2 %all-gather.5.cloned.1.call-start = ((), (), s32[]{:S(2)}) async-start(), calls=%async_computation.4 | async-start | bytes 2359296 | tf_op jit(solution)/shard_map/all_gather | solution.py:675
  84.9 546.4 %reduce-scatter.10.cloned.1.call-start = ((), (), s32[]{:S(2)}) async-start(), calls=%async_computation.7 | async-start | bytes 10485760
  96.6 38.3 %collective-permute-start.7 = (bf16[512,512]{1,0:T(8,128)(2,1)}, bf16[512,512]{1,0:T(8,128)(2,1)}, u32[]{:S(2)}, u32[]{:S(2)}) collective-permute-start(bf16[512,512]{1,0:T(8,128)(2,1)} %constant_dynamic-slice_fusion.14), channel_id=1, source_target_pairs={{0,16},{8,24},{16,0},{24,8},{1,17},{9,25},{17,1},{25,9},{2,18},{10... | collective-permute-start | bytes 1572872 | tf_op jit(solution)/shard_map/ppermute | solution.py:36
  97.7 37.3 %collective-permute-start.6 = (bf16[512,512]{1,0:T(8,128)(2,1)}, bf16[512,512]{1,0:T(8,128)(2,1)}, u32[]{:S(2)}, u32[]{:S(2)}) collective-permute-start(bf16[512,512]{1,0:T(8,128)(2,1)} %constant_dynamic-slice_fusion.14), channel_id=1, source_target_pairs={{0,8},{8,0},{16,24},{24,16},{1,9},{9,1},{17,25},{25,17},{2,10},{10... | collective-permute-start | bytes 1572872 | tf_op jit(solution)/shard_map/ppermute | solution.py:36
  142.3 28.5 %collective-permute-start.17 = (bf16[512,512]{1,0:T(8,128)(2,1)}, bf16[512,512]{1,0:T(8,128)(2,1)S(1)}, u32[]{:S(2)}, u32[]{:S(2)}) collective-permute-start(bf16[512,512]{1,0:T(8,128)(2,1)} %collective-permute-done.7), channel_id=1, source_target_pairs={{0,8},{8,0},{16,24},{24,16},{1,9},{9,1},{17,25},{25,17},{2,10},{10... | collective-permute-start | bytes 1572872 | tf_op jit(solution)/shard_map/ppermute | solution.py:36
  153.9 23.7 %collective-permute-start.15 = (bf16[4,256,256]{2,1,0:T(8,128)(2,1)S(1)}, bf16[4,256,256]{2,1,0:T(8,128)(2,1)S(1)}, u32[]{:S(2)}, u32[]{:S(2)}) collective-permute-start(bf16[4,256,256]{2,1,0:T(8,128)(2,1)S(1)} %get-tuple-element.300), channel_id=1, source_target_pairs={{0,8},{8,0},{16,24},{24,16},{1,9},{9,1},{17,25},{25,17},{2,10},{10... | collective-permute-start | bytes 1572872 | tf_op jit(solution)/shard_map/ppermute | solution.py:36
  157.1 24.6 %collective-permute-start.16 = (bf16[4,256,256]{2,1,0:T(8,128)(2,1)S(1)}, bf16[4,256,256]{2,1,0:T(8,128)(2,1)S(1)}, u32[]{:S(2)}, u32[]{:S(2)}) collective-permute-start(bf16[4,256,256]{2,1,0:T(8,128)(2,1)S(1)} %get-tuple-element.299), channel_id=1, source_target_pairs={{0,16},{8,24},{16,0},{24,8},{1,17},{9,25},{17,1},{25,9},{2,18},{10... | collective-permute-start | bytes 1572872 | tf_op jit(solution)/shard_map/ppermute | solution.py:36
  184.2 44.4 %collective-permute-start.21 = (bf16[2048,512]{1,0:T(8,128)(2,1)S(1)}, bf16[2048,512]{1,0:T(8,128)(2,1)}, u32[]{:S(2)}, u32[]{:S(2)}) collective-permute-start(bf16[2048,512]{1,0:T(8,128)(2,1)S(1)} %constant_dynamic-update-slice_fusion.refs_0_), channel_id=1, source_target_pairs={{0,1},{1,0},{2,3},{3,2},{4,5},{5,4},{6,7},{7,6},{8,9},{9,8},{10,11... | collective-permute-start | bytes 6291464 | tf_op jit(solution)/shard_map/ppermute | solution.py:36
  185.1 45.0 %collective-permute-start.22 = (bf16[2048,512]{1,0:T(8,128)(2,1)S(1)}, bf16[2048,512]{1,0:T(8,128)(2,1)}, u32[]{:S(2)}, u32[]{:S(2)}) collective-permute-start(bf16[2048,512]{1,0:T(8,128)(2,1)S(1)} %constant_dynamic-update-slice_fusion.refs_0_), channel_id=1, source_target_pairs={{0,2},{1,3},{2,0},{3,1},{4,6},{5,7},{6,4},{7,5},{8,10},{9,11},{10,... | collective-permute-start | bytes 6291464 | tf_op jit(solution)/shard_map/ppermute | solution.py:36
  186.5 20.5 %collective-permute-start.19 = (bf16[512,512]{1,0:T(8,128)(2,1)S(1)}, bf16[512,512]{1,0:T(8,128)(2,1)S(1)}, u32[]{:S(2)}, u32[]{:S(2)}) collective-permute-start(bf16[512,512]{1,0:T(8,128)(2,1)S(1)} %multiply_convert_fusion.2), channel_id=1, source_target_pairs={{0,16},{8,24},{16,0},{24,8},{1,17},{9,25},{17,1},{25,9},{2,18},{10... | collective-permute-start | bytes 1572872 | tf_op jit(solution)/shard_map/ppermute | solution.py:36
  186.8 22.1 %collective-permute-start.18 = (bf16[512,512]{1,0:T(8,128)(2,1)S(1)}, bf16[512,512]{1,0:T(8,128)(2,1)S(1)}, u32[]{:S(2)}, u32[]{:S(2)}) collective-permute-start(bf16[512,512]{1,0:T(8,128)(2,1)S(1)} %multiply_convert_fusion.2), channel_id=1, source_target_pairs={{0,8},{8,0},{16,24},{24,16},{1,9},{9,1},{17,25},{25,17},{2,10},{10... | collective-permute-start | bytes 1572872 | tf_op jit(solution)/shard_map/ppermute | solution.py:36
  233.4 44.3 %collective-permute-start.26 = (bf16[2048,512]{1,0:T(8,128)(2,1)}, bf16[2048,512]{1,0:T(8,128)(2,1)}, u32[]{:S(2)}, u32[]{:S(2)}) collective-permute-start(bf16[2048,512]{1,0:T(8,128)(2,1)} %constant_dynamic-update-slice_fusion.4.refs_6_), channel_id=1, source_target_pairs={{0,1},{1,0},{2,3},{3,2},{4,5},{5,4},{6,7},{7,6},{8,9},{9,8},{10,11... | collective-permute-start | bytes 6291464 | tf_op jit(solution)/shard_map/ppermute | solution.py:36
  233.8 44.6 %collective-permute-start.27 = (bf16[2048,512]{1,0:T(8,128)(2,1)}, bf16[2048,512]{1,0:T(8,128)(2,1)}, u32[]{:S(2)}, u32[]{:S(2)}) collective-permute-start(bf16[2048,512]{1,0:T(8,128)(2,1)} %constant_dynamic-update-slice_fusion.4.refs_6_), channel_id=1, source_target_pairs={{0,2},{1,3},{2,0},{3,1},{4,6},{5,7},{6,4},{7,5},{8,10},{9,11},{10,... | collective-permute-start | bytes 6291464 | tf_op jit(solution)/shard_map/ppermute | solution.py:36
  235.5 19.2 %collective-permute-start.24 = (bf16[4,256,256]{2,1,0:T(8,128)(2,1)S(1)}, bf16[4,256,256]{2,1,0:T(8,128)(2,1)S(1)}, u32[]{:S(2)}, u32[]{:S(2)}) collective-permute-start(bf16[4,256,256]{2,1,0:T(8,128)(2,1)S(1)} %get-tuple-element.297), channel_id=1, source_target_pairs={{0,8},{8,0},{16,24},{24,16},{1,9},{9,1},{17,25},{25,17},{2,10},{10... | collective-permute-start | bytes 1572872 | tf_op jit(solution)/shard_map/ppermute | solution.py:36
  235.6 38.3 %collective-permute-start.25 = (bf16[4,256,256]{2,1,0:T(8,128)(2,1)S(1)}, bf16[4,256,256]{2,1,0:T(8,128)(2,1)S(1)}, u32[]{:S(2)}, u32[]{:S(2)}) collective-permute-start(bf16[4,256,256]{2,1,0:T(8,128)(2,1)S(1)} %get-tuple-element.296), channel_id=1, source_target_pairs={{0,16},{8,24},{16,0},{24,8},{1,17},{9,25},{17,1},{25,9},{2,18},{10... | collective-permute-start | bytes 1572872 | tf_op jit(solution)/shard_map/ppermute | solution.py:36
  237.9 36.0 %collective-permute-start.23 = (bf16[4,256,256]{2,1,0:T(8,128)(2,1)S(1)}, bf16[4,256,256]{2,1,0:T(8,128)(2,1)S(1)}, u32[]{:S(2)}, u32[]{:S(2)}) collective-permute-start(bf16[4,256,256]{2,1,0:T(8,128)(2,1)S(1)} %constant_dynamic-slice_fusion.10), channel_id=1, source_target_pairs={{0,24},{8,16},{16,8},{24,0},{1,25},{9,17},{17,9},{25,1},{2,26},{10... | collective-permute-start | bytes 1572872 | tf_op jit(solution)/shard_map/ppermute | solution.py:36
  279.7 20.7 %collective-permute-start.29 = (bf16[1024,512]{1,0:T(8,128)(2,1)S(1)}, bf16[1024,512]{1,0:T(8,128)(2,1)S(1)}, u32[]{:S(2)}, u32[]{:S(2)}) collective-permute-start(bf16[1024,512]{1,0:T(8,128)(2,1)S(1)} %slice.330), channel_id=1, source_target_pairs={{0,2},{1,3},{2,0},{3,1},{4,6},{5,7},{6,4},{7,5},{8,10},{9,11},{10,... | collective-permute-start | bytes 3145736 | tf_op jit(solution)/shard_map/ppermute | solution.py:36
  282.7 19.6 %collective-permute-start.30 = (bf16[1024,512]{1,0:T(8,128)(2,1)S(1)}, bf16[1024,512]{1,0:T(8,128)(2,1)S(1)}, u32[]{:S(2)}, u32[]{:S(2)}) collective-permute-start(bf16[1024,512]{1,0:T(8,128)(2,1)S(1)} %slice.331), channel_id=1, source_target_pairs={{0,1},{1,0},{2,3},{3,2},{4,5},{5,4},{6,7},{7,6},{8,9},{9,8},{10,11... | collective-permute-start | bytes 3145736 | tf_op jit(solution)/shard_map/ppermute | solution.py:36
  285.3 33.3 %collective-permute-start.28 = (bf16[4,4,256,256]{3,2,1,0:T(8,128)(2,1)S(1)}, bf16[4,4,256,256]{3,2,1,0:T(8,128)(2,1)}, u32[]{:S(2)}, u32[]{:S(2)}) collective-permute-start(bf16[4,4,256,256]{3,2,1,0:T(8,128)(2,1)S(1)} %pad_maximum_fusion.refs_2_.refs_5_), channel_id=1, source_target_pairs={{0,4},{4,0},{1,5},{5,1},{2,6},{6,2},{3,7},{7,3},{8,12},{12,8},{9,1... | collective-permute-start | bytes 6291464 | tf_op jit(solution)/shard_map/ppermute | solution.py:36
  309.5 44.3 %collective-permute-start.34 = (bf16[1024,512]{1,0:T(8,128)(2,1)S(1)}, bf16[1024,512]{1,0:T(8,128)(2,1)S(1)}, u32[]{:S(2)}, u32[]{:S(2)}) collective-permute-start(bf16[1024,512]{1,0:T(8,128)(2,1)S(1)} %slice.333), channel_id=1, source_target_pairs={{0,1},{1,0},{2,3},{3,2},{4,5},{5,4},{6,7},{7,6},{8,9},{9,8},{10,11... | collective-permute-start | bytes 3145736 | tf_op jit(solution)/shard_map/ppermute | solution.py:36
  312.3 41.5 %collective-permute-start.33 = (bf16[1024,512]{1,0:T(8,128)(2,1)S(1)}, bf16[1024,512]{1,0:T(8,128)(2,1)S(1)}, u32[]{:S(2)}, u32[]{:S(2)}) collective-permute-start(bf16[1024,512]{1,0:T(8,128)(2,1)S(1)} %slice.332), channel_id=1, source_target_pairs={{0,2},{1,3},{2,0},{3,1},{4,6},{5,7},{6,4},{7,5},{8,10},{9,11},{10,... | collective-permute-start | bytes 3145736 | tf_op jit(solution)/shard_map/ppermute | solution.py:36
  314.3 54.8 %collective-permute-start.35 = (bf16[4,256,256]{2,1,0:T(8,128)(2,1)}, bf16[4,256,256]{2,1,0:T(8,128)(2,1)}, u32[]{:S(2)}, u32[]{:S(2)}) collective-permute-start(bf16[4,256,256]{2,1,0:T(8,128)(2,1)} %get-tuple-element.294), channel_id=1, source_target_pairs={{0,8},{8,0},{16,24},{24,16},{1,9},{9,1},{17,25},{25,17},{2,10},{10... | collective-permute-start | bytes 1572872 | tf_op jit(solution)/shard_map/ppermute | solution.py:36
  318.6 50.4 %collective-permute-start.36 = (bf16[4,256,256]{2,1,0:T(8,128)(2,1)S(1)}, bf16[4,256,256]{2,1,0:T(8,128)(2,1)S(1)}, u32[]{:S(2)}, u32[]{:S(2)}) collective-permute-start(bf16[4,256,256]{2,1,0:T(8,128)(2,1)S(1)} %get-tuple-element.293), channel_id=1, source_target_pairs={{0,16},{8,24},{16,0},{24,8},{1,17},{9,25},{17,1},{25,9},{2,18},{10... | collective-permute-start | bytes 1572872 | tf_op jit(solution)/shard_map/ppermute | solution.py:36
  320.1 49.0 %collective-permute-start.37 = (bf16[4,256,256]{2,1,0:T(8,128)(2,1)S(1)}, bf16[4,256,256]{2,1,0:T(8,128)(2,1)S(1)}, u32[]{:S(2)}, u32[]{:S(2)}) collective-permute-start(bf16[4,256,256]{2,1,0:T(8,128)(2,1)S(1)} %get-tuple-element.292), channel_id=1, source_target_pairs={{0,24},{8,16},{16,8},{24,0},{1,25},{9,17},{17,9},{25,1},{2,26},{10... | collective-permute-start | bytes 1572872 | tf_op jit(solution)/shard_map/ppermute | solution.py:36
  370.5 34.9 %collective-permute-start.39 = (bf16[4,4,256,256]{3,2,1,0:T(8,128)(2,1)}, bf16[4,4,256,256]{3,2,1,0:T(8,128)(2,1)}, u32[]{:S(2)}, u32[]{:S(2)}) collective-permute-start(bf16[4,4,256,256]{3,2,1,0:T(8,128)(2,1)} %get-tuple-element.184), channel_id=1, source_target_pairs={{0,4},{4,0},{1,5},{5,1},{2,6},{6,2},{3,7},{7,3},{8,12},{12,8},{9,1... | collective-permute-start | bytes 6291464 | tf_op jit(solution)/shard_map/ppermute | solution.py:36
  408.8 33.8 %collective-permute-start.40 = (bf16[4,256,256]{2,1,0:T(8,128)(2,1)S(1)}, bf16[4,256,256]{2,1,0:T(8,128)(2,1)S(1)}, u32[]{:S(2)}, u32[]{:S(2)}) collective-permute-start(bf16[4,256,256]{2,1,0:T(8,128)(2,1)S(1)} %get-tuple-element.290), channel_id=1, source_target_pairs={{0,8},{8,0},{16,24},{24,16},{1,9},{9,1},{17,25},{25,17},{2,10},{10... | collective-permute-start | bytes 1572872 | tf_op jit(solution)/shard_map/ppermute | solution.py:36
  409.2 38.2 %collective-permute-start.41 = (bf16[4,256,256]{2,1,0:T(8,128)(2,1)S(1)}, bf16[4,256,256]{2,1,0:T(8,128)(2,1)S(1)}, u32[]{:S(2)}, u32[]{:S(2)}) collective-permute-start(bf16[4,256,256]{2,1,0:T(8,128)(2,1)S(1)} %get-tuple-element.289), channel_id=1, source_target_pairs={{0,16},{8,24},{16,0},{24,8},{1,17},{9,25},{17,1},{25,9},{2,18},{10... | collective-permute-start | bytes 1572872 | tf_op jit(solution)/shard_map/ppermute | solution.py:36
  411.8 35.6 %collective-permute-start.42 = (bf16[2,528,512]{2,1,0:T(8,128)(2,1)S(1)}, bf16[2,528,512]{2,1,0:T(8,128)(2,1)S(1)}, u32[]{:S(2)}, u32[]{:S(2)}) collective-permute-start(bf16[2,528,512]{2,1,0:T(8,128)(2,1)S(1)} %get-tuple-element.275), channel_id=1, source_target_pairs={{0,1},{1,0},{2,3},{3,2},{4,5},{5,4},{6,7},{7,6},{8,9},{9,8},{10,11... | collective-permute-start | bytes 3244040 | tf_op jit(solution)/shard_map/ppermute | solution.py:36
  412.5 34.9 %collective-permute-start.43 = (bf16[2,528,512]{2,1,0:T(8,128)(2,1)S(1)}, bf16[2,528,512]{2,1,0:T(8,128)(2,1)S(1)}, u32[]{:S(2)}, u32[]{:S(2)}) collective-permute-start(bf16[2,528,512]{2,1,0:T(8,128)(2,1)S(1)} %get-tuple-element.274), channel_id=1, source_target_pairs={{0,2},{1,3},{2,0},{3,1},{4,6},{5,7},{6,4},{7,5},{8,10},{9,11},{10,... | collective-permute-start | bytes 3244040 | tf_op jit(solution)/shard_map/ppermute | solution.py:36
  413.6 65.6 %collective-permute-start.44 = (bf16[4,256,256]{2,1,0:T(8,128)(2,1)}, bf16[4,256,256]{2,1,0:T(8,128)(2,1)S(1)}, u32[]{:S(2)}, u32[]{:S(2)}) collective-permute-start(bf16[4,256,256]{2,1,0:T(8,128)(2,1)} %get-tuple-element.288), channel_id=1, source_target_pairs={{0,24},{8,16},{16,8},{24,0},{1,25},{9,17},{17,9},{25,1},{2,26},{10... | collective-permute-start | bytes 1572872 | tf_op jit(solution)/shard_map/ppermute | solution.py:36
  452.0 27.3 %collective-permute-start.47 = (bf16[528,512]{1,0:T(8,128)(2,1)}, bf16[528,512]{1,0:T(8,128)(2,1)}, u32[]{:S(2)}, u32[]{:S(2)}) collective-permute-start(bf16[528,512]{1,0:T(8,128)(2,1)} %get-tuple-element.271), channel_id=1, source_target_pairs={{0,2},{1,3},{2,0},{3,1},{4,6},{5,7},{6,4},{7,5},{8,10},{9,11},{10,... | collective-permute-start | bytes 1622024 | tf_op jit(solution)/shard_map/ppermute | solution.py:36
  453.0 26.3 %collective-permute-start.48 = (bf16[528,512]{1,0:T(8,128)(2,1)S(1)}, bf16[528,512]{1,0:T(8,128)(2,1)}, u32[]{:S(2)}, u32[]{:S(2)}) collective-permute-start(bf16[528,512]{1,0:T(8,128)(2,1)S(1)} %get-tuple-element.270), channel_id=1, source_target_pairs={{0,1},{1,0},{2,3},{3,2},{4,5},{5,4},{6,7},{7,6},{8,9},{9,8},{10,11... | collective-permute-start | bytes 1622024 | tf_op jit(solution)/shard_map/ppermute | solution.py:36
  453.9 30.1 %collective-permute-start.45 = (bf16[2,528,512]{2,1,0:T(8,128)(2,1)S(1)}, bf16[2,528,512]{2,1,0:T(8,128)(2,1)S(1)}, u32[]{:S(2)}, u32[]{:S(2)}) collective-permute-start(bf16[2,528,512]{2,1,0:T(8,128)(2,1)S(1)} %get-tuple-element.273), channel_id=1, source_target_pairs={{0,1},{1,0},{2,3},{3,2},{4,5},{5,4},{6,7},{7,6},{8,9},{9,8},{10,11... | collective-permute-start | bytes 3244040 | tf_op jit(solution)/shard_map/ppermute | solution.py:36
  455.2 28.7 %collective-permute-start.46 = (bf16[2,528,512]{2,1,0:T(8,128)(2,1)S(1)}, bf16[2,528,512]{2,1,0:T(8,128)(2,1)S(1)}, u32[]{:S(2)}, u32[]{:S(2)}) collective-permute-start(bf16[2,528,512]{2,1,0:T(8,128)(2,1)S(1)} %get-tuple-element.272), channel_id=1, source_target_pairs={{0,2},{1,3},{2,0},{3,1},{4,6},{5,7},{6,4},{7,5},{8,10},{9,11},{10,... | collective-permute-start | bytes 3244040 | tf_op jit(solution)/shard_map/ppermute | solution.py:36
  489.7 25.5 %collective-permute-start.49 = (bf16[2,528,512]{2,1,0:T(8,128)(2,1)}, bf16[2,528,512]{2,1,0:T(8,128)(2,1)}, u32[]{:S(2)}, u32[]{:S(2)}) collective-permute-start(bf16[2,528,512]{2,1,0:T(8,128)(2,1)} %pad_maximum_fusion.4), channel_id=1, source_target_pairs={{0,8},{8,0},{16,24},{24,16},{1,9},{9,1},{17,25},{25,17},{2,10},{10... | collective-permute-start | bytes 3244040 | tf_op jit(solution)/shard_map/ppermute | solution.py:36
  496.4 18.8 %collective-permute-start.50 = (bf16[528,512]{1,0:T(8,128)(2,1)}, bf16[528,512]{1,0:T(8,128)(2,1)}, u32[]{:S(2)}, u32[]{:S(2)}) collective-permute-start(bf16[528,512]{1,0:T(8,128)(2,1)} %get-tuple-element.267), channel_id=1, source_target_pairs={{0,2},{1,3},{2,0},{3,1},{4,6},{5,7},{6,4},{7,5},{8,10},{9,11},{10,... | collective-permute-start | bytes 1622024 | tf_op jit(solution)/shard_map/ppermute | solution.py:36
  515.3 210.9 %reduce-scatter.6.cloned.1.call-start = ((), (), s32[]{:S(2)}) async-start(), calls=%async_computation.5 | async-start | bytes 2359296 | tf_op jit(solution)/shard_map/reduce_scatter | solution.py:846
  515.7 34.3 %collective-permute-start.53 = (bf16[4,2,4,256,256]{4,3,2,1,0:T(8,128)(2,1)}, bf16[4,2,4,256,256]{4,3,2,1,0:T(8,128)(2,1)}, u32[]{:S(2)}, u32[]{:S(2)}) collective-permute-start(bf16[4,2,4,256,256]{4,3,2,1,0:T(8,128)(2,1)} %get-tuple-element.210), channel_id=1, source_target_pairs={{0,4},{4,0},{1,5},{5,1},{2,6},{6,2},{3,7},{7,3},{8,12},{12,8},{9,1... | collective-permute-start | bytes 12582920 | tf_op jit(solution)/shard_map/ppermute | solution.py:36
  518.3 28.4 %collective-permute-start.52 = (bf16[1,528,512]{2,1,0:T(8,128)(2,1)}, bf16[1,528,512]{2,1,0:T(8,128)(2,1)}, u32[]{:S(2)}, u32[]{:S(2)}) collective-permute-start(bf16[1,528,512]{2,1,0:T(8,128)(2,1)} %fusion.48), channel_id=1, source_target_pairs={{0,16},{8,24},{16,0},{24,8},{1,17},{9,25},{17,1},{25,9},{2,18},{10... | collective-permute-start | bytes 1622024 | tf_op jit(solution)/shard_map/ppermute | solution.py:36
  564.1 19.4 %collective-permute-start.58 = (bf16[512,512]{1,0:T(8,128)(2,1)}, bf16[512,512]{1,0:T(8,128)(2,1)}, u32[]{:S(2)}, u32[]{:S(2)}) collective-permute-start(bf16[512,512]{1,0:T(8,128)(2,1)} %get-tuple-element.261), channel_id=1, source_target_pairs={{0,2},{1,3},{2,0},{3,1},{4,6},{5,7},{6,4},{7,5},{8,10},{9,11},{10,... | collective-permute-start | bytes 1572872 | tf_op jit(solution)/shard_map/ppermute | solution.py:36
  566.8 45.9 %collective-permute-start.61 = (bf16[2,4,256,256]{3,2,1,0:T(8,128)(2,1)}, bf16[2,4,256,256]{3,2,1,0:T(8,128)(2,1)S(1)}, u32[]{:S(2)}, u32[]{:S(2)}) collective-permute-start(bf16[2,4,256,256]{3,2,1,0:T(8,128)(2,1)} %get-tuple-element.278), channel_id=1, source_target_pairs={{0,8},{8,0},{16,24},{24,16},{1,9},{9,1},{17,25},{25,17},{2,10},{10... | collective-permute-start | bytes 3145736 | tf_op jit(solution)/shard_map/ppermute | solution.py:36
  566.8 47.9 %collective-permute-start.62 = (bf16[2,4,256,256]{3,2,1,0:T(8,128)(2,1)}, bf16[2,4,256,256]{3,2,1,0:T(8,128)(2,1)}, u32[]{:S(2)}, u32[]{:S(2)}) collective-permute-start(bf16[2,4,256,256]{3,2,1,0:T(8,128)(2,1)} %get-tuple-element.277), channel_id=1, source_target_pairs={{0,16},{8,24},{16,0},{24,8},{1,17},{9,25},{17,1},{25,9},{2,18},{10... | collective-permute-start | bytes 3145736 | tf_op jit(solution)/shard_map/ppermute | solution.py:36
  614.7 28.2 %collective-permute-start.63 = (bf16[2,4,256,256]{3,2,1,0:T(8,128)(2,1)}, bf16[2,4,256,256]{3,2,1,0:T(8,128)(2,1)}, u32[]{:S(2)}, u32[]{:S(2)}) collective-permute-start(bf16[2,4,256,256]{3,2,1,0:T(8,128)(2,1)} %get-tuple-element.220), channel_id=1, source_target_pairs={{0,24},{8,16},{16,8},{24,0},{1,25},{9,17},{17,9},{25,1},{2,26},{10... | collective-permute-start | bytes 3145736 | tf_op jit(solution)/shard_map/ppermute | solution.py:36
  632.9 28.6 %collective-permute-start.64 = (bf16[2,512,512]{2,1,0:T(8,128)(2,1)S(1)}, bf16[2,512,512]{2,1,0:T(8,128)(2,1)S(1)}, u32[]{:S(2)}, u32[]{:S(2)}) collective-permute-start(bf16[2,512,512]{2,1,0:T(8,128)(2,1)S(1)} %pad_maximum_fusion.5), channel_id=1, source_target_pairs={{0,8},{8,0},{16,24},{24,16},{1,9},{9,1},{17,25},{25,17},{2,10},{10... | collective-permute-start | bytes 3145736 | tf_op jit(solution)/shard_map/ppermute | solution.py:36
  664.3 142.9 %reduce-scatter.8.cloned.1.call-start = ((), (), s32[]{:S(2)}) async-start(), calls=%async_computation.6 | async-start | bytes 7077888 | tf_op jit(solution)/shard_map/reduce_scatter | solution.py:892
  683.3 35.0 %collective-permute-start.68 = (bf16[1,512,512]{2,1,0:T(8,128)(2,1)S(1)}, bf16[1,512,512]{2,1,0:T(8,128)(2,1)S(1)}, u32[]{:S(2)}, u32[]{:S(2)}) collective-permute-start(bf16[1,512,512]{2,1,0:T(8,128)(2,1)S(1)} %add_convert_fusion.4), channel_id=1, source_target_pairs={{0,16},{8,24},{16,0},{24,8},{1,17},{9,25},{17,1},{25,9},{2,18},{10... | collective-permute-start | bytes 1572872 | tf_op jit(solution)/shard_map/ppermute | solution.py:36
  684.2 19.9 %collective-permute-start.70 = (f32[19,512]{1,0:T(8,128)S(1)}, f32[19,512]{1,0:T(8,128)S(1)}, u32[]{:S(2)}, u32[]{:S(2)}) collective-permute-start(f32[19,512]{1,0:T(8,128)S(1)} %fusion.90), channel_id=1, source_target_pairs={{0,8},{8,0},{16,24},{24,16},{1,9},{9,1},{17,25},{25,17},{2,10},{10... | collective-permute-start | bytes 116744 | tf_op jit(solution)/shard_map/ppermute | solution.py:36
  (137 other events, 1377.3 us)
Sparse Core Ops, SparseCore 0:
  11.8 71.7 all-gather.2
  85.2 46.6 all-gather.4
  515.4 99.4 reduce-scatter.9
  664.4 38.9 reduce-scatter.5
  726.3 68.9 reduce-scatter.7
